TPU v7x, 512 devices: a whole 4x8x8 slice. The times are simulated.
512 devices in a mesh: row: 16 (over y, core), col: 32 (over z, x).
Axes of the slice: x: 4, y: 8, z: 8, core: 2. Of those that a mesh axis runs over, the one named last changes fastest.
Arguments:
- root_inverse: float32 [8192, 8192], P('row', 'col'), may hold values from -6 to 6
- boundary_map: int32 [4096], replicated, may hold values from 2 to 8191, as said below
- lower_factor: float32 [4096, 4096], P('row', 'col'), may hold values from -0.09375 to 0.09375
- upper_factor: float32 [4096, 4096], P('row', 'col'), may hold values from -0.09375 to 0.09375
- diagonal_inverse: float32 [4096, 4096], P('row', 'col'), may hold values from -6 to 6
Outputs:
- sigma_bs: float32 [4096, 4096], P('row', 'col')
- sigma_sb: float32 [4096, 4096], P('row', 'col')
- sigma_ss: float32 [4096, 4096], P('row', 'col')
Inputs may be any that keep to these rules, and one draw needn't show every extreme that they name: `boundary_map`: root unknowns come four to a lattice site (two spin components, real and imaginary part each), site s holding indices 4 s to 4 s + 3. The child's boundary is the projected half-spinor of every root site: entries 2 q and 2 q + 1 are the real and imaginary unknown of the second spin component of one site, 4 s + 2 and 4 s + 3. Entry p lies in [256 * (p // 128), 256 * (p // 128 + 1)); each root site appears once, in the child's own order of sites within each block of 256 root indices.
All inputs are finite; a program needn't handle non-finite values.
Results may differ from a plain program's by a relative error of at most 0.000084.
Values sent between devices are 32-bit elements; how exact they have to be, the bound alone decides.
No kernel may reach another device: no remote copies, remote signals or barrier semaphores. Data moves between devices by JAX's collectives and lax.ppermute only.
A program may use at most 64 MiB of HBM per device.

v0:
```python
import jax
import jax.numpy as jnp
from jax import lax
from jax.sharding import PartitionSpec as P


def shards(root_inverse, boundary_map, lower_factor, upper_factor, diagonal_inverse):
    row_rank = lax.axis_index("row")
    col_rank = lax.axis_index("col")
    width = root_inverse.shape[1]
    half = width // 2
    row_pick = (
        lax.dynamic_slice_in_dim(boundary_map, row_rank * width, width) - row_rank * 2 * width
    )
    col_pick = lax.dynamic_slice_in_dim(boundary_map, col_rank * half, half) - col_rank * width
    local_sigma = jnp.take(jnp.take(root_inverse, row_pick, axis=0), col_pick, axis=1)
    lower_cols = lax.all_gather(lower_factor, "row", axis=0, tiled=True)
    sigma_bs = -jnp.dot(
        lax.all_gather(local_sigma, "col", axis=1, tiled=True),
        lower_cols,
        preferred_element_type=jnp.float32,
        precision=lax.Precision.HIGHEST,
    )
    sigma_cols = lax.all_gather(local_sigma, "row", axis=0, tiled=True)
    upper_rows = lax.all_gather(upper_factor, "col", axis=1, tiled=True)
    sigma_sb = -jnp.dot(
        upper_rows, sigma_cols, preferred_element_type=jnp.float32, precision=lax.Precision.HIGHEST
    )
    coupling = lax.all_gather(sigma_bs, "row", axis=0, tiled=True)
    sigma_ss = diagonal_inverse - jnp.dot(
        upper_rows, coupling, preferred_element_type=jnp.float32, precision=lax.Precision.HIGHEST
    )
    return (sigma_bs, sigma_sb, sigma_ss)


def solution(mesh):
    return jax.shard_map(
        shards,
        mesh=mesh,
        in_specs=(P("row", "col"), P(), P("row", "col"), P("row", "col"), P("row", "col")),
        out_specs=(P("row", "col"), P("row", "col"), P("row", "col")),
        check_vma=False,
    )
```

profile of v0, /device:TPU:1, one launch (start us, length us, event | category | flops | bytes accessed | tf_op | source)
XLA Modules:
  0.0 339.4 jit_solution(5394015697026516421)
XLA Ops:
  7.2 0.0 copy-start
  7.2 0.0 all-gather.8.cloned.1.call-start
  7.2 0.7 all-gather.8.cloned.1.call-update
  7.9 0.0 all-gather.6.cloned.1.call-start
  8.0 0.8 compare_and_fusion
  8.7 0.0 copy-done
  8.8 1.0 gather_fusion
  9.7 0.1 broadcast_select_fusion
  9.8 0.1 copy.8
  10.0 0.8 compare_and_fusion.1
  10.8 0.8 gather_fusion.1
  11.5 0.7 select_bitcast_fusion
  12.3 0.0 all-gather.6.cloned.1.call-update
  12.3 0.0 all-gather.10.cloned.1.call-start
  12.3 0.7 all-gather.10.cloned.1.call-update
  13.0 0.0 all-gather.12.cloned.1.call-start
  13.1 0.5 all-gather.12.cloned.1.call-update
  13.6 0.0 copy-start.1
  13.6 0.0 all-gather.14.cloned.1.call-start
  13.7 44.3 %all-gather.8.cloned.1.call-done = f32[4096,128]{1,0:T(8,128)} async-done(((f32[256,128]{1,0:T(8,128)}), f32[4096,128]{1,0:T(8,128)}) %all-gather.8.cloned.1.call-update) | async-done | bytes 2097168 | tf_op jit(solution)/shard_map/all_gather | solution.py:17
  58.0 87.4 %all-gather.6.cloned.1.call-done = f32[256,4096]{0,1:T(8,128)} async-done(((f32[256,128]{0,1:T(8,128)}), f32[256,4096]{0,1:T(8,128)}) %all-gather.6.cloned.1.call-update) | async-done | bytes 4194320 | tf_op jit(solution)/shard_map/all_gather | solution.py:19
  145.4 10.2 %convolution_negate_fusion.1 = f32[256,128]{1,0:T(8,128)} fusion(f32[256,4096]{0,1:T(8,128)} %all-gather.6.cloned.1.call-done, f32[4096,128]{1,0:T(8,128)} %all-gather.8.cloned.1.call-done), kind=kOutput, calls=%fused_computation.6 | convolution fusion | flops 1610645504 | bytes 6422528 | tf_op jit(solution)/shard_map/dot_general | solution.py:18
  155.5 0.0 all-gather.14.cloned.1.call-update
  155.6 0.0 copy-done.1
  155.6 0.1 copy.9
  155.7 34.4 %all-gather.10.cloned.1.call-done = f32[4096,128]{0,1:T(8,128)} async-done(((f32[256,128]{0,1:T(8,128)}), f32[4096,128]{0,1:T(8,128)}) %all-gather.10.cloned.1.call-update) | async-done | bytes 2097168 | tf_op jit(solution)/shard_map/all_gather | solution.py:24
  190.1 87.7 %all-gather.12.cloned.1.call-done = f32[256,4096]{1,0:T(8,128)} async-done(((f32[256,128]{1,0:T(8,128)}), f32[256,4096]{1,0:T(8,128)}) %all-gather.12.cloned.1.call-update) | async-done | bytes 4194320 | tf_op jit(solution)/shard_map/all_gather | solution.py:25
  277.8 7.1 %fusion.1 = f32[256,128]{0,1:T(8,128)S(1)} fusion(f32[4096,128]{0,1:T(8,128)} %all-gather.10.cloned.1.call-done, f32[256,4096]{1,0:T(8,128)} %all-gather.12.cloned.1.call-done), kind=kOutput, calls=%fused_computation.5 | convolution fusion | flops 1610645504 | bytes 6422528 | tf_op jit(solution)/shard_map/dot_general | solution.py:26
  285.0 0.8 copy.10
  285.7 40.1 %all-gather.14.cloned.1.call-done = f32[4096,128]{1,0:T(8,128)} async-done(((f32[256,128]{1,0:T(8,128)}), f32[4096,128]{1,0:T(8,128)}) %all-gather.14.cloned.1.call-update) | async-done | bytes 2097168 | tf_op jit(solution)/shard_map/all_gather | solution.py:29
  325.8 6.3 %fusion = f32[256,128]{0,1:T(8,128)S(1)} fusion(f32[256,128]{0,1:T(8,128)S(1)} %copy.9, f32[4096,128]{1,0:T(8,128)} %all-gather.14.cloned.1.call-done, f32[256,4096]{1,0:T(8,128)} %all-gather.12.cloned.1.call-done), kind=kOutput, calls=%fused_computation.3 | convolution fusion | flops 1610645504 | bytes 6553600 | tf_op jit(solution)/shard_map/dot_general | solution.py:30
  332.1 0.8 copy.11
  (2 shorter events, 0.0 us)
Async XLA Ops:
  7.2 1.6 copy-start
  7.2 50.8 %all-gather.8.cloned.1.call-start = ((), (), s32[]{:S(2)}) async-start(), calls=%async_computation.1 | async-start | bytes 2228224 | tf_op jit(solution)/shard_map/all_gather | solution.py:17
  7.9 137.4 %all-gather.6.cloned.1.call-start = ((), (), s32[]{:S(2)}) async-start(), calls=%async_computation | async-start | bytes 4325376 | tf_op jit(solution)/shard_map/all_gather | solution.py:19
  12.3 177.8 %all-gather.10.cloned.1.call-start = ((), (), s32[]{:S(2)}) async-start(), calls=%async_computation.2 | async-start | bytes 2228224 | tf_op jit(solution)/shard_map/all_gather | solution.py:24
  13.0 264.8 %all-gather.12.cloned.1.call-start = ((), (), s32[]{:S(2)}) async-start(), calls=%async_computation.3 | async-start | bytes 4325376 | tf_op jit(solution)/shard_map/all_gather | solution.py:25
  13.6 142.0 %copy-start.1 = (f32[256,128]{1,0:T(8,128)S(1)}, f32[256,128]{1,0:T(8,128)}, u32[]{:S(2)}) copy-start(f32[256,128]{1,0:T(8,128)} %param.9) | copy-start | bytes 393220
  13.6 312.2 %all-gather.14.cloned.1.call-start = ((), (), s32[]{:S(2)}) async-start(), calls=%async_computation.4 | async-start | bytes 2228224 | tf_op jit(solution)/shard_map/all_gather | solution.py:29
Sparse Core Ops, SparseCore 0:
  10.1 47.7 all-gather.7
  61.7 83.6 all-gather.5
  148.1 41.9 all-gather.9
  193.0 84.8 all-gather.11
  280.4 45.3 all-gather.13
where the time goes:
time: 340 us; the launch traced here: 339 us
  waiting for transfers between devices  296 us (87%)
  matrix products  23.6 us (7%)
  between operations  13.9 us (4%)
  local copies, waits for them, and re-layouts  3.47 us (1%)
    all_gather x1, waiting for transfers between devices, shards(): upper_rows = lax.all_gather(upper_factor, 'col', axis=1, tiled=True)  87.7 us
    all_gather x1, waiting for transfers between devices, shards(): lax.all_gather(local_sigma, 'col', axis=1, tiled=True)  87.4 us
    all_gather x1, waiting for transfers between devices, shards(): lower_cols = lax.all_gather(lower_factor, 'row', axis=0, tiled=True)  44.3 us
    all_gather x1, waiting for transfers between devices, shards(): coupling = lax.all_gather(sigma_bs, 'row', axis=0, tiled=True)  40.1 us
    all_gather x1, waiting for transfers between devices, shards(): sigma_cols = lax.all_gather(local_sigma, 'row', axis=0, tiled=True)  34.4 us
    dot_general x1, matrix products, shards(): jnp.dot(lax.all_gather(local_sigma, 'col', axis=1, tiled=True), lower_col...  10.2 us
    dot_general x1, matrix products, shards(): jnp.dot(upper_rows, sigma_cols, preferred_element_type=jnp.float32, preci...  7.1 us
  transfers between devices with their start and end apart: 5, of which 5 were waited for; matrix products, arithmetic and copies ran while one was open for 7% of the time, Pallas kernels for 0%

commit v1 on v0

v1 whole, which is shorter than its diff:
```python
import jax
import jax.numpy as jnp
import numpy as np
from jax import lax
from jax.experimental import pallas as pl
from jax.experimental.pallas import tpu as pltpu
from jax.sharding import Mesh, PartitionSpec as P

F32 = jnp.float32
BF16 = jnp.bfloat16
VMEM = pl.BlockSpec(memory_space=pltpu.VMEM)
PARAMS = pltpu.CompilerParams(vmem_limit_bytes=40 * 1024 * 1024)


def split2(v):
    hi = v.astype(BF16)
    return hi, (v - hi.astype(F32)).astype(BF16)


def dot(a, b):
    return lax.dot_general(a, b, (((1,), (0,)), ((), ())), preferred_element_type=F32)


def pick_kernel(rows_ref, cols_ref, root_ref, lower_ref, upper_ref, su_ref, send_ref):
    iota = lax.broadcasted_iota(jnp.int32, (256, 128), 0)
    col_hot = jnp.where(cols_ref[...] == iota, 1.0, 0.0).astype(BF16)
    for part in range(2):
        row_hot = jnp.where(rows_ref[part : part + 1, :] == iota, 1.0, 0.0).astype(BF16)
        left = root_ref[256 * part : 256 * (part + 1), :]
        picked = None
        for _ in range(3):
            piece = left.astype(BF16)
            left = left - piece.astype(F32)
            across = lax.dot_general(
                row_hot, piece, (((0,), (0,)), ((), ())), preferred_element_type=F32
            )
            value = dot(across.astype(BF16), col_hot)
            picked = value if picked is None else picked + value
        su_ref[128 * part : 128 * (part + 1), :] = picked
        for core in range(2):
            send_ref[core, part, 0] = picked[64 * core : 64 * (core + 1), :]
            start = 128 * part + 64 * core
            send_ref[core, part, 1] = lower_ref[start : start + 64, :]
    su_ref[256:512, :] = upper_ref[...]


def pick(rows, cols, root, lower, upper):
    return pl.pallas_call(
        pick_kernel,
        out_shape=(
            jax.ShapeDtypeStruct((512, 128), F32),
            jax.ShapeDtypeStruct((2, 2, 2, 64, 128), F32),
        ),
        in_specs=[VMEM] * 5,
        out_specs=(VMEM, VMEM),
        compiler_params=PARAMS,
    )(rows, cols, root, lower, upper)


def three_pass(ah, al, bh, bl):
    return dot(ah[...], bh) + (dot(ah[...], bl) + dot(al[...], bh))


def coupling_kernel(core_ref, su_ref, own_ref, other_ref, out_ref, ah, al, bh, bl):
    core = core_ref[0]
    for z in range(8):
        hi, lo = split2(su_ref[z, 256:512, :])
        ah[:, 128 * z : 128 * (z + 1)] = hi
        al[:, 128 * z : 128 * (z + 1)] = lo
        first = pl.multiple_of(128 * z + 64 * core, 64)
        second = pl.multiple_of(128 * z + 64 * (1 - core), 64)
        for x in range(4):
            hi, lo = split2(own_ref[z, x])
            bh[pl.ds(first, 64), 128 * x : 128 * (x + 1)] = hi
            bl[pl.ds(first, 64), 128 * x : 128 * (x + 1)] = lo
            hi, lo = split2(other_ref[z, x])
            bh[pl.ds(second, 64), 128 * x : 128 * (x + 1)] = hi
            bl[pl.ds(second, 64), 128 * x : 128 * (x + 1)] = lo
    for n in range(2):
        cols = slice(256 * n, 256 * (n + 1))
        part = three_pass(ah, al, bh[:, cols], bl[:, cols])
        out_ref[2 * n] = part[:, :128]
        out_ref[2 * n + 1] = part[:, 128:]


def couple(core, gathered, own, other):
    return pl.pallas_call(
        coupling_kernel,
        out_shape=jax.ShapeDtypeStruct((4, 256, 128), F32),
        in_specs=[pl.BlockSpec(memory_space=pltpu.SMEM)] + [VMEM] * 3,
        out_specs=VMEM,
        scratch_shapes=[
            pltpu.VMEM((256, 1024), BF16),
            pltpu.VMEM((256, 1024), BF16),
            pltpu.VMEM((1024, 512), BF16),
            pltpu.VMEM((1024, 512), BF16),
        ],
        compiler_params=PARAMS,
    )(core, gathered, own, other)


def pair_kernel(su_ref, w_ref, lower_ref, out_ref, ah, al, bh, bl):
    for z in range(8):
        cols = slice(128 * z, 128 * (z + 1))
        ah[:256, cols], al[:256, cols] = split2(su_ref[z, :256, :])
        ah[256:, cols], al[256:, cols] = split2(w_ref[z])
        for core in range(2):
            start = 128 * z + 64 * core
            for x in range(4):
                hi, lo = split2(lower_ref[z, core, x])
                bh[start : start + 64, 128 * x : 128 * (x + 1)] = hi
                bl[start : start + 64, 128 * x : 128 * (x + 1)] = lo
    for n in range(2):
        cols = slice(256 * n, 256 * (n + 1))
        part = three_pass(ah, al, bh[:, cols], bl[:, cols])
        for i in range(2):
            for k in range(2):
                out_ref[2 * n + i, k] = part[256 * k : 256 * (k + 1), 128 * i : 128 * (i + 1)]


def pair(gathered, w, lower):
    return pl.pallas_call(
        pair_kernel,
        out_shape=jax.ShapeDtypeStruct((4, 2, 256, 128), F32),
        in_specs=[VMEM] * 3,
        out_specs=VMEM,
        scratch_shapes=[
            pltpu.VMEM((512, 1024), BF16),
            pltpu.VMEM((512, 1024), BF16),
            pltpu.VMEM((1024, 512), BF16),
            pltpu.VMEM((1024, 512), BF16),
        ],
        compiler_params=PARAMS,
    )(gathered, w, lower)


def exchange(v, axis):
    return lax.all_to_all(v, axis, 0, 0, tiled=True)


def spread(v, axis, count):
    return exchange(jnp.broadcast_to(v[None], (count,) + v.shape), axis)


def shards(root_inverse, boundary_map, lower_factor, upper_factor, diagonal_inverse):
    y, c, z, x = (lax.axis_index(name) for name in ("y", "c", "z", "x"))
    blocks = boundary_map.reshape(32, 128)
    row, col = 2 * y + c, 4 * z + x
    rows = lax.dynamic_slice_in_dim(blocks, 2 * row, 2) - 256 * (
        2 * row + jnp.arange(2, dtype=jnp.int32)[:, None]
    )
    cols = lax.dynamic_slice_in_dim(blocks, col, 1) - 256 * col
    su, send = pick(rows, cols, root_inverse, lower_factor, upper_factor)
    gathered = lax.all_gather(su, "z", axis=0, tiled=False)
    moved = exchange(send, "c").reshape(4, 2, 64, 128)
    moved = exchange(moved, "x")
    lower_all = lax.all_gather(moved[:, 1].reshape(256, 128), ("y", "c"), axis=0, tiled=True)
    lower_all = lower_all.reshape(8, 2, 4, 64, 128)
    own = spread(moved[:, 0], "y", 8)
    other = lax.ppermute(own, "c", [(0, 1), (1, 0)])
    part = couple(c.astype(jnp.int32).reshape(1), gathered, own, other)
    w = exchange(part, "x").sum(axis=0)
    w_all = spread(w, "z", 8)
    both = exchange(pair(gathered, w_all, lower_all), "x").sum(axis=0)
    return (-both[0], -w, diagonal_inverse + both[1])


def solution(mesh):
    grid = Mesh(np.asarray(mesh.devices).reshape(8, 2, 8, 4), ("y", "c", "z", "x"))
    block = P(("y", "c"), ("z", "x"))
    return jax.shard_map(
        shards,
        mesh=grid,
        in_specs=(block, P(), block, block, block),
        out_specs=(block, block, block),
        check_vma=False,
    )
```

time: 340 us -> 157 us (0.46)
  waiting for transfers between devices: 296 us -> 72.4 us
  blocking collectives: 0 us -> 30.9 us
  matrix products: 23.6 us -> 0 us
  starting transfers between devices: 0.19 us -> 20.7 us
  local copies, waits for them, and re-layouts: 3.47 us -> 9.84 us
  Pallas kernels: 0 us -> 4.82 us
    all_gather x5 -> x2, waiting for transfers between devices: 294 us -> 10.5 us  [the longest x1 10.5 us: shards(): lax.all_gather(moved[:, 1].reshape(256, 128), ('y', 'c'), axis=0, tiled=T...]
    all_to_all x0 -> x3, waiting for transfers between devices: none -> 58.9 us  [exchange(): return lax.all_to_all(v, axis, 0, 0, tiled=True)]
    all_to_all x0 -> x3, blocking collectives: none -> 30.9 us  [exchange(): return lax.all_to_all(v, axis, 0, 0, tiled=True)]
    dot_general x3 -> x0, matrix products: 23.6 us -> none  [the longest x1 10.2 us: shards(): jnp.dot(lax.all_gather(local_sigma, 'col', axis=1, tiled=True), lower_col...]
    all_to_all x0 -> x3, starting transfers between devices: none -> 16.1 us  [exchange(): return lax.all_to_all(v, axis, 0, 0, tiled=True)]
    unnamed x7 -> x16, local copies, waits for them, and re-layouts: 1.62 us -> 7.02 us
    pallas_call x0 -> x3, Pallas kernels: none -> 4.82 us  [the longest x1 1.95 us: pair(): pl.pallas_call(pair_kernel, out_shape=jax.ShapeDtypeStruct((4, 2, 256, 12...]
    ppermute x0 -> x1, starting transfers between devices: none -> 4.55 us  [shards(): other = lax.ppermute(own, 'c', [(0, 1), (1, 0)])]
  transfers between devices with their start and end apart: 5 -> 6, of which waited for: 5 -> 5; matrix products, arithmetic and copies ran while one was open for 7% -> 2% of each run, Pallas kernels for 0% -> 1%
where the time goes in v1:
time: 157 us; the launch traced here: 156 us
  waiting for transfers between devices  72.4 us (46%)
  blocking collectives  30.9 us (20%)
  starting transfers between devices  20.7 us (13%)
  between operations  14.1 us (9%)
  local copies, waits for them, and re-layouts  9.84 us (6%)
  Pallas kernels  4.82 us (3%)
  other arithmetic  3.56 us (2%)
    all_to_all x3, waiting for transfers between devices, exchange(): return lax.all_to_all(v, axis, 0, 0, tiled=True)  58.9 us
    all_to_all x3, blocking collectives, exchange(): return lax.all_to_all(v, axis, 0, 0, tiled=True)  30.9 us
    all_to_all x3, starting transfers between devices, exchange(): return lax.all_to_all(v, axis, 0, 0, tiled=True)  16.1 us
    all_gather x1, waiting for transfers between devices, shards(): lax.all_gather(moved[:, 1].reshape(256, 128), ('y', 'c'), axis=0, tiled=T...  10.5 us
    unnamed x16, local copies, waits for them, and re-layouts  7.02 us
    ppermute x1, starting transfers between devices, shards(): other = lax.ppermute(own, 'c', [(0, 1), (1, 0)])  4.55 us
  transfers between devices with their start and end apart: 6, of which 5 were waited for; matrix products, arithmetic and copies ran while one was open for 2% of the time, Pallas kernels for 1%

profile of v1, /device:TPU:1, one launch (start us, length us, event | category | flops | bytes accessed | tf_op | source)
XLA Modules:
  0.0 156.3 jit_solution(10142824240547121438)
XLA Ops:
  7.2 0.0 all-gather.6.cloned.1.call-start
  7.2 0.8 dynamic-slice_subtract_fusion.rows_ref
  8.0 0.7 dynamic-slice_subtract_fusion.1.cols_ref
  8.7 0.0 copy-start.4
  8.7 1.0 copy-done.4
  9.7 0.0 copy-start.5
  9.7 0.9 copy-done.5
  10.6 0.0 copy-start.6
  10.6 0.9 copy-done.6
  11.5 1.5 shard_map.76
  13.1 0.0 all-gather.6.cloned.1.call-update
  13.1 10.5 %all_to_all.30 = f32[2,2,2,64,128]{4,3,2,1,0:T(8,128)S(1)} all-to-all(f32[2,2,2,64,128]{4,3,2,1,0:T(8,128)S(1)} %get-tuple-element.6), channel_id=1, replica_groups=mesh['y'=8,'c'=2,'z'=8,'x'=4] {'c'}, dimensions={0} | all-to-all | bytes 524288 | tf_op jit(solution)/shard_map/all_to_all | solution.py:138
  23.6 8.8 %all_to_all.31 = f32[4,2,64,128]{3,2,1,0:T(8,128)S(1)} all-to-all(f32[4,2,64,128]{3,2,1,0:T(8,128)S(1)} %bitcast.17), channel_id=1, replica_groups=mesh['y'=8,'c'=2,'z'=8,'x'=4] {'x'}, dimensions={0} | all-to-all | bytes 524288 | tf_op jit(solution)/shard_map/all_to_all | solution.py:138
  32.4 0.7 fusion.2
  33.0 1.1 broadcast_in_dim.7
  34.1 3.6 %all-to-all-start.2 = ((f32[8,4,64,128]{3,2,1,0:T(8,128)}), f32[8,4,64,128]{3,2,1,0:T(8,128)S(1)}, u32[]{:S(2)}, u32[]{:S(2)}) async-start(f32[8,4,64,128]{3,2,1,0:T(8,128)} %broadcast_in_dim.7), calls=%async_computation.2 | async-start | bytes 2097152 | tf_op jit(solution)/shard_map/all_to_all | solution.py:138
  37.7 0.0 all-gather.4.cloned.1.call-start
  37.8 0.7 all-gather.4.cloned.1.call-update
  38.5 26.2 %all-to-all-done.2.own_ref = f32[8,4,64,128]{3,2,1,0:T(8,128)S(1)} async-done(((f32[8,4,64,128]{3,2,1,0:T(8,128)}), f32[8,4,64,128]{3,2,1,0:T(8,128)S(1)}, u32[]{:S(2)}, u32[]{:S(2)}) %all-to-all-start.2) | async-done | bytes 1048608 | tf_op jit(solution)/shard_map/all_to_all | solution.py:138
  64.6 4.6 %collective-permute-start = (f32[8,4,64,128]{3,2,1,0:T(8,128)S(1)}, f32[8,4,64,128]{3,2,1,0:T(8,128)S(1)}, u32[]{:S(2)}, u32[]{:S(2)}) collective-permute-start(f32[8,4,64,128]{3,2,1,0:T(8,128)S(1)} %all-to-all-done.2.own_ref), channel_id=1, source_target_pairs={{0,32},{32,0},{1,33},{33,1},{2,34},{34,2},{3,35},{35,3},{4,36},{36... | collective-permute-start | bytes 3145736 | tf_op jit(solution)/shard_map/ppermute | solution.py:160
  69.2 2.3 %collective-permute-done.other_ref = f32[8,4,64,128]{3,2,1,0:T(8,128)S(1)} collective-permute-done((f32[8,4,64,128]{3,2,1,0:T(8,128)S(1)}, f32[8,4,64,128]{3,2,1,0:T(8,128)S(1)}, u32[]{:S(2)}, u32[]{:S(2)}) %collective-permute-start) | collective-permute-done | bytes 1048608 | tf_op jit(solution)/shard_map/ppermute | solution.py:160
  71.5 0.0 all-gather.6.cloned.1.call-done
  71.5 0.0 copy-start
  71.5 1.6 %copy-done = f32[4096,128]{1,0:T(8,128)S(1)} copy-done((f32[4096,128]{1,0:T(8,128)S(1)}, f32[4096,128]{1,0:T(8,128)}, u32[]{:S(2)}) %copy-start) | copy-done | bytes 2097176
  73.1 1.3 shard_map.77
  74.4 11.6 %all_to_all.32 = f32[4,256,128]{2,1,0:T(8,128)S(1)} all-to-all(f32[4,256,128]{2,1,0:T(8,128)S(1)} %shard_map.77), channel_id=1, replica_groups=mesh['y'=8,'c'=2,'z'=8,'x'=4] {'x'}, dimensions={0} | all-to-all | bytes 1048576 | tf_op jit(solution)/shard_map/all_to_all | solution.py:138
  86.0 0.0 copy-start.1
  86.1 1.0 broadcast_in_dim.16
  87.1 8.9 %all-to-all-start.4 = ((f32[8,256,128]{2,1,0:T(8,128)}), f32[8,256,128]{2,1,0:T(8,128)S(1)}, u32[]{:S(2)}, u32[]{:S(2)}) async-start(f32[8,256,128]{2,1,0:T(8,128)} %broadcast_in_dim.16), calls=%async_computation.4 | async-start | bytes 2097152 | tf_op jit(solution)/shard_map/all_to_all | solution.py:138
  96.0 10.5 %all-gather.4.cloned.1.call-done = f32[4096,128]{1,0:T(8,128)} async-done(((f32[256,128]{1,0:T(8,128)}), f32[4096,128]{1,0:T(8,128)}) %all-gather.4.cloned.1.call-update) | async-done | bytes 2097168 | tf_op jit(solution)/shard_map/all_gather | solution.py:157
  106.5 18.7 %all-to-all-done.4.w_ref = f32[8,256,128]{2,1,0:T(8,128)S(1)} async-done(((f32[8,256,128]{2,1,0:T(8,128)}), f32[8,256,128]{2,1,0:T(8,128)S(1)}, u32[]{:S(2)}, u32[]{:S(2)}) %all-to-all-start.4) | async-done | bytes 1048608 | tf_op jit(solution)/shard_map/all_to_all | solution.py:138
  125.2 0.0 copy-done.1
  125.2 0.0 copy-start.3
  125.2 1.6 %copy-done.3 = f32[4096,128]{1,0:T(8,128)S(1)} copy-done((f32[4096,128]{1,0:T(8,128)S(1)}, f32[4096,128]{1,0:T(8,128)}, u32[]{:S(2)}) %copy-start.3) | copy-done | bytes 2097176
  126.8 1.9 %shard_map.78 = f32[4,2,256,128]{3,2,1,0:T(8,128)S(1)} custom-call(f32[8,512,128]{2,1,0:T(8,128)S(1)} %bitcast.15, f32[8,256,128]{2,1,0:T(8,128)S(1)} %all-to-all-done.4.w_ref, f32[8,2,4,64,128]{4,3,2,1,0:T(8,128)S(1)} %bitcast.16), custom_call_target="tpu_custom_call" | custom-call | tf_op jit(solution)/shard_map/pallas_call | solution.py:122
  128.7 0.0 copy-start.2
  128.7 1.0 copy-done.2
  129.7 0.0 copy-start.7
  129.7 3.6 %all-to-all-start.5 = ((f32[4,2,256,128]{3,2,1,0:T(8,128)}), f32[4,2,256,128]{3,2,1,0:T(8,128)S(1)}, u32[]{:S(2)}, u32[]{:S(2)}) async-start(f32[4,2,256,128]{3,2,1,0:T(8,128)} %copy-done.2), calls=%async_computation.5 | async-start | bytes 2097152 | tf_op jit(solution)/shard_map/all_to_all | solution.py:138
  133.4 0.7 neg.11
  134.0 14.0 %all-to-all-done.5 = f32[4,2,256,128]{3,2,1,0:T(8,128)S(1)} async-done(((f32[4,2,256,128]{3,2,1,0:T(8,128)}), f32[4,2,256,128]{3,2,1,0:T(8,128)S(1)}, u32[]{:S(2)}, u32[]{:S(2)}) %all-to-all-start.5) | async-done | bytes 1048608 | tf_op jit(solution)/shard_map/all_to_all | solution.py:138
  148.1 0.1 reduce_sum.19
  148.1 0.7 fusion.1
  148.8 0.0 copy-done.7
  148.8 0.7 fusion
  (2 shorter events, 0.0 us)
Async XLA Ops:
  7.2 64.3 %all-gather.6.cloned.1.call-start = ((), (), s32[]{:S(2)}) async-start(), calls=%async_computation.7 | async-start | bytes 2359296 | tf_op jit(solution)/shard_map/all_gather | solution.py:154
  8.7 1.0 copy-start.4
  9.7 0.9 copy-start.5
  10.6 0.9 copy-start.6
  34.1 30.5 %all-to-all-start.2 = ((f32[8,4,64,128]{3,2,1,0:T(8,128)}), f32[8,4,64,128]{3,2,1,0:T(8,128)S(1)}, u32[]{:S(2)}, u32[]{:S(2)}) async-start(f32[8,4,64,128]{3,2,1,0:T(8,128)} %broadcast_in_dim.7), calls=%async_computation.2 | async-start | bytes 2097152 | tf_op jit(solution)/shard_map/all_to_all | solution.py:138
  37.7 68.8 %all-gather.4.cloned.1.call-start = ((), (), s32[]{:S(2)}) async-start(), calls=%async_computation.6 | async-start | bytes 2228224 | tf_op jit(solution)/shard_map/all_gather | solution.py:157
  64.6 6.8 %collective-permute-start = (f32[8,4,64,128]{3,2,1,0:T(8,128)S(1)}, f32[8,4,64,128]{3,2,1,0:T(8,128)S(1)}, u32[]{:S(2)}, u32[]{:S(2)}) collective-permute-start(f32[8,4,64,128]{3,2,1,0:T(8,128)S(1)} %all-to-all-done.2.own_ref), channel_id=1, source_target_pairs={{0,32},{32,0},{1,33},{33,1},{2,34},{34,2},{3,35},{35,3},{4,36},{36... | collective-permute-start | bytes 3145736 | tf_op jit(solution)/shard_map/ppermute | solution.py:160
  71.5 1.6 %copy-start = (f32[4096,128]{1,0:T(8,128)S(1)}, f32[4096,128]{1,0:T(8,128)}, u32[]{:S(2)}) copy-start(f32[4096,128]{1,0:T(8,128)} %all-gather.6.cloned.1.call-done) | copy-start | bytes 6291460
  86.0 39.1 %copy-start.1 = (f32[4096,128]{1,0:T(8,128)S(1)}, f32[4096,128]{1,0:T(8,128)}, u32[]{:S(2)}) copy-start(f32[4096,128]{1,0:T(8,128)} %all-gather.6.cloned.1.call-done) | copy-start | bytes 6291460
  87.1 38.1 %all-to-all-start.4 = ((f32[8,256,128]{2,1,0:T(8,128)}), f32[8,256,128]{2,1,0:T(8,128)S(1)}, u32[]{:S(2)}, u32[]{:S(2)}) async-start(f32[8,256,128]{2,1,0:T(8,128)} %broadcast_in_dim.16), calls=%async_computation.4 | async-start | bytes 2097152 | tf_op jit(solution)/shard_map/all_to_all | solution.py:138
  125.2 1.6 %copy-start.3 = (f32[4096,128]{1,0:T(8,128)S(1)}, f32[4096,128]{1,0:T(8,128)}, u32[]{:S(2)}) copy-start(f32[4096,128]{1,0:T(8,128)} %all-gather.4.cloned.1.call-done) | copy-start | bytes 6291460
  128.7 1.0 copy-start.2
  129.7 19.1 %copy-start.7 = (f32[256,128]{1,0:T(8,128)S(1)}, f32[256,128]{1,0:T(8,128)}, u32[]{:S(2)}) copy-start(f32[256,128]{1,0:T(8,128)} %param.9) | copy-start | bytes 393220
  129.7 18.3 %all-to-all-start.5 = ((f32[4,2,256,128]{3,2,1,0:T(8,128)}), f32[4,2,256,128]{3,2,1,0:T(8,128)S(1)}, u32[]{:S(2)}, u32[]{:S(2)}) async-start(f32[4,2,256,128]{3,2,1,0:T(8,128)} %copy-done.2), calls=%async_computation.5 | async-start | bytes 2097152 | tf_op jit(solution)/shard_map/all_to_all | solution.py:138
Sparse Core Ops, SparseCore 0:
  13.2 46.0 all-gather.5
  62.0 44.4 all-gather.3

commit v2 on v0

v2 whole, which is shorter than its diff:
```python
import jax
import jax.numpy as jnp
import numpy as np
from jax import lax
from jax.experimental import pallas as pl
from jax.experimental.pallas import tpu as pltpu
from jax.sharding import Mesh, PartitionSpec as P

F32 = jnp.float32
BF16 = jnp.bfloat16
VMEM = pl.BlockSpec(memory_space=pltpu.VMEM)
SMEM = pl.BlockSpec(memory_space=pltpu.SMEM)
HBM = pl.BlockSpec(memory_space=pltpu.HBM)
PARAMS = pltpu.CompilerParams(vmem_limit_bytes=32 * 1024 * 1024)
DMA = pltpu.SemaphoreType.DMA


def shape(*dims, dtype=F32):
    return jax.ShapeDtypeStruct(dims, dtype)


def split2(v):
    hi = v.astype(BF16)
    return hi, (v - hi.astype(F32)).astype(BF16)


def dot(a, b):
    return lax.dot_general(a, b, (((1,), (0,)), ((), ())), preferred_element_type=F32)


def three_pass(ah, al, bh, bl):
    return dot(ah, bh) + (dot(ah, bl) + dot(al, bh))


def pick_kernel(
    at_ref, map_hbm, root_hbm, lower_hbm, upper_hbm, su_ref, first_ref, second_ref, picks, root, lower, sems
):
    loads = [
        pltpu.make_async_copy(map_hbm, picks, sems.at[0]),
        pltpu.make_async_copy(root_hbm, root, sems.at[1]),
        pltpu.make_async_copy(lower_hbm, lower, sems.at[2]),
        pltpu.make_async_copy(upper_hbm, su_ref.at[256:512], sems.at[3]),
    ]
    for load in loads:
        load.start()
    row, col, odd = at_ref[0], at_ref[1], at_ref[3]
    iota = lax.broadcasted_iota(jnp.int32, (256, 128), 0)
    loads[0].wait()
    cols = picks[pl.ds(col, 1), :] - 256 * col
    col_hot = jnp.where(cols == iota, 1.0, 0.0).astype(BF16)
    hots = []
    for part in range(2):
        block = 2 * row + part
        rows = picks[pl.ds(block, 1), :] - 256 * block
        hots.append(jnp.where(rows == iota, 1.0, 0.0).astype(BF16))
    loads[1].wait()
    for part in range(2):
        left = root[256 * part : 256 * (part + 1), :]
        picked = None
        for _ in range(3):
            piece = left.astype(BF16)
            left = left - piece.astype(F32)
            across = lax.dot_general(
                hots[part], piece, (((0,), (0,)), ((), ())), preferred_element_type=F32
            )
            value = dot(across.astype(BF16), col_hot)
            picked = value if picked is None else picked + value
        su_ref[128 * part : 128 * (part + 1), :] = picked
    for load in loads[2:]:
        load.wait()
    near = pl.multiple_of(128 * odd, 128)
    far = pl.multiple_of(128 - 128 * odd, 128)
    first_ref[0] = su_ref[pl.ds(near, 128), :]
    first_ref[1] = lower[pl.ds(near, 128), :]
    second_ref[0] = su_ref[pl.ds(far, 128), :]
    second_ref[1] = lower[pl.ds(far, 128), :]


def pick(at, blocks, root, lower, upper):
    return pl.pallas_call(
        pick_kernel,
        out_shape=(shape(512, 128), shape(2, 128, 128), shape(2, 128, 128)),
        in_specs=[SMEM] + [HBM] * 4,
        out_specs=(VMEM, VMEM, VMEM),
        scratch_shapes=[
            pltpu.VMEM((32, 128), jnp.int32),
            pltpu.VMEM((512, 256), F32),
            pltpu.VMEM((256, 128), F32),
            DMA((4,)),
        ],
        compiler_params=pltpu.CompilerParams(vmem_limit_bytes=62 * 1024 * 1024),
    )(at, blocks, root, lower, upper)


def fan_kernel(first_ref, second_ref, copies_ref, lower_ref):
    for t, ref in enumerate((first_ref, second_ref)):
        lower_ref[128 * t : 128 * (t + 1), :] = ref[1]
        value = ref[0]
        for i in range(8):
            copies_ref[i, t] = value


def fan(first, second):
    return pl.pallas_call(
        fan_kernel,
        out_shape=(shape(8, 2, 128, 128), shape(256, 128)),
        in_specs=[VMEM] * 2,
        out_specs=(VMEM, VMEM),
        compiler_params=PARAMS,
    )(first, second)


def couple(at, gathered, columns, before=None):
    def kernel(at_ref, su_hbm, columns_ref, *refs):
        before_ref, (out_ref, upper, ah, al, bh, bl, sem) = (
            (None, refs) if before is None else (refs[0], refs[1:])
        )
        load = pltpu.make_async_copy(su_hbm.at[:, 256:512], upper, sem)
        load.start()
        for z in range(8):
            rows = slice(128 * z, 128 * (z + 1))
            for t in range(2):
                cols = slice(128 * t, 128 * (t + 1))
                bh[rows, cols], bl[rows, cols] = split2(columns_ref[z, t])
        load.wait()
        for z in range(8):
            rows = slice(128 * z, 128 * (z + 1))
            ah[:, rows], al[:, rows] = split2(upper[z])
        part = three_pass(ah[...], al[...], bh[...], bl[...])
        if before is None:
            out_ref[0] = part[:, :128]
            out_ref[1] = part[:, 128:]
        else:
            core, odd = at_ref[2], at_ref[3]
            out_ref[2 * core + odd] = before_ref[0]
            out_ref[2 * core + 1 - odd] = before_ref[1]
            out_ref[2 * (1 - core) + odd] = part[:, :128]
            out_ref[2 * (1 - core) + 1 - odd] = part[:, 128:]

    more = () if before is None else (before,)
    return pl.pallas_call(
        kernel,
        out_shape=shape(2 + 2 * len(more), 256, 128),
        in_specs=[SMEM, HBM, VMEM] + [VMEM] * len(more),
        out_specs=VMEM,
        scratch_shapes=[
            pltpu.VMEM((8, 256, 128), F32),
            pltpu.VMEM((256, 1024), BF16),
            pltpu.VMEM((256, 1024), BF16),
            pltpu.VMEM((1024, 256), BF16),
            pltpu.VMEM((1024, 256), BF16),
            DMA,
        ],
        compiler_params=PARAMS,
        cost_estimate=pl.CostEstimate(flops=3 << 28, bytes_accessed=3 << 20, transcendentals=0),
    )(at, gathered, columns, *more)


def lower_columns(odd, lower, bh, bl):
    for z in range(8):
        rows = slice(128 * z, 128 * (z + 1))
        for core in range(2):
            for t in range(2):
                cols = slice(256 * core + 128 * t, 256 * core + 128 * (t + 1))
                place = 128 * jnp.where(odd == 0, t, 1 - t)
                value = lower[2 * z + core, pl.ds(pl.multiple_of(place, 128), 128), :]
                bh[rows, cols], bl[rows, cols] = split2(value)


def side_kernel(at_ref, su_hbm, lower, s0, s1, s2, s3, sigma, ah, al, bh, bl, out, sem):
    load = pltpu.make_async_copy(su_hbm.at[:, 0:256], sigma, sem)
    load.start()
    lower_columns(at_ref[3], lower, bh, bl)
    load.wait()
    for z in range(8):
        rows = slice(128 * z, 128 * (z + 1))
        ah[:, rows], al[:, rows] = split2(sigma[z])
    for n in range(2):
        cols = slice(256 * n, 256 * (n + 1))
        part = three_pass(ah[...], al[...], bh[:, cols], bl[:, cols])
        out[2 * n] = part[:, :128]
        out[2 * n + 1] = part[:, 128:]
    for k, ref in enumerate((s0, s1, s2, s3)):
        ref[...] = out[(at_ref[4] + k) & 3]


def side(at, gathered, lower):
    return pl.pallas_call(
        side_kernel,
        out_shape=(shape(256, 128),) * 4,
        in_specs=[SMEM, HBM, VMEM],
        out_specs=(VMEM,) * 4,
        scratch_shapes=[
            pltpu.VMEM((8, 256, 128), F32),
            pltpu.VMEM((256, 1024), BF16),
            pltpu.VMEM((256, 1024), BF16),
            pltpu.VMEM((1024, 512), BF16),
            pltpu.VMEM((1024, 512), BF16),
            pltpu.VMEM((4, 256, 128), F32),
            DMA,
        ],
        compiler_params=PARAMS,
        cost_estimate=pl.CostEstimate(flops=6 << 28, bytes_accessed=6 << 20, transcendentals=0),
    )(at, gathered, lower)


def last_kernel(at_ref, w_ref, lower, out_ref, ah, al, bh, bl):
    lower_columns(at_ref[3], lower, bh, bl)
    for z in range(8):
        rows = slice(128 * z, 128 * (z + 1))
        ah[:, rows], al[:, rows] = split2(w_ref[z])
    for n in range(2):
        cols = slice(256 * n, 256 * (n + 1))
        part = three_pass(ah[...], al[...], bh[:, cols], bl[:, cols])
        out_ref[2 * n] = part[:, :128]
        out_ref[2 * n + 1] = part[:, 128:]


def last(at, w, lower):
    return pl.pallas_call(
        last_kernel,
        out_shape=shape(4, 256, 128),
        in_specs=[SMEM, VMEM, VMEM],
        out_specs=VMEM,
        scratch_shapes=[
            pltpu.VMEM((256, 1024), BF16),
            pltpu.VMEM((256, 1024), BF16),
            pltpu.VMEM((1024, 512), BF16),
            pltpu.VMEM((1024, 512), BF16),
        ],
        compiler_params=PARAMS,
    )(at, w, lower)


def exchange(v, axis):
    return lax.all_to_all(v, axis, 0, 0, tiled=True)


def deal(v, t):
    moves = [(4 * c + x, 4 * (x >> 1) + 2 * c + ((x & 1) ^ t)) for c in range(2) for x in range(4)]
    return lax.ppermute(v, ("c", "x"), moves)


def shards(root_inverse, boundary_map, lower_factor, upper_factor, diagonal_inverse):
    y, c, z, x = (lax.axis_index(name) for name in ("y", "c", "z", "x"))
    at = jnp.stack([2 * y + c, 4 * z + x, c, x & 1, x]).astype(jnp.int32)
    su, first, second = pick(
        at, boundary_map.reshape(32, 128), root_inverse, lower_factor, upper_factor
    )
    gathered = lax.all_gather(su, "z", axis=0, tiled=False)
    copies, lower = fan(deal(first, 0), deal(second, 1))
    lower = lax.all_gather(lower, ("y", "c"), axis=0, tiled=False)
    own = exchange(copies, "y")
    other = lax.ppermute(own, "c", [(0, 1), (1, 0)])
    part = couple(at, gathered, other, couple(at, gathered, own))
    w = exchange(part, "x").sum(axis=0)
    w_all = exchange(jnp.broadcast_to(w[None], (8, 256, 128)), "z")
    pieces = side(at, gathered, lower)
    total = pieces[0]
    for k in range(1, 4):
        total = total + lax.ppermute(pieces[k], "x", [(i, (i + k) & 3) for i in range(4)])
    total, w_all = lax.optimization_barrier((-total, w_all))
    product = exchange(last(at, w_all, lower), "x").sum(axis=0)
    return (total, -w, diagonal_inverse + product)


def solution(mesh):
    grid = Mesh(np.asarray(mesh.devices).reshape(8, 2, 8, 4), ("y", "c", "z", "x"))
    block = P(("y", "c"), ("z", "x"))
    return jax.shard_map(
        shards,
        mesh=grid,
        in_specs=(block, P(), block, block, block),
        out_specs=(block, block, block),
        check_vma=False,
    )
```

time: 340 us -> 147 us (0.43)
  waiting for transfers between devices: 296 us -> 57.8 us
  starting transfers between devices: 0.19 us -> 41.3 us
  matrix products: 23.6 us -> 0 us
  Pallas kernels: 0 us -> 12.2 us
  blocking collectives: 0 us -> 11.4 us
    all_gather x5 -> x2, waiting for transfers between devices: 294 us -> 15 us  [the longest x1 15 us: shards(): lower = lax.all_gather(lower, ('y', 'c'), axis=0, tiled=False)]
    all_to_all x0 -> x3, waiting for transfers between devices: none -> 33.9 us  [exchange(): return lax.all_to_all(v, axis, 0, 0, tiled=True)]
    dot_general x3 -> x0, matrix products: 23.6 us -> none  [the longest x1 10.2 us: shards(): jnp.dot(lax.all_gather(local_sigma, 'col', axis=1, tiled=True), lower_col...]
    ppermute x0 -> x6, starting transfers between devices: none -> 21.3 us  [the longest x3 10.5 us: shards(): lax.ppermute(pieces[k], 'x', [(i, i + k & 3) for i in range(4)])]
    all_to_all x0 -> x3, starting transfers between devices: none -> 19.9 us  [exchange(): return lax.all_to_all(v, axis, 0, 0, tiled=True)]
    pallas_call x0 -> x6, Pallas kernels: none -> 12.2 us  [the longest x1 3.49 us: pick(): pl.pallas_call(pick_kernel, out_shape=(shape(512, 128), shape(2, 128, 128...]
    all_to_all x0 -> x1, blocking collectives: none -> 11.4 us  [exchange(): return lax.all_to_all(v, axis, 0, 0, tiled=True)]
    ppermute x0 -> x6, waiting for transfers between devices: none -> 8.21 us  [the longest x2 5.21 us: deal(): return lax.ppermute(v, ('c', 'x'), moves)]
  transfers between devices with their start and end apart: 5 -> 11, of which waited for: 5 -> 7; matrix products, arithmetic and copies ran while one was open for 7% -> 2% of each run, Pallas kernels for 0% -> 4%
where the time goes in v2:
time: 147 us; the launch traced here: 145 us
  waiting for transfers between devices  57.8 us (39%)
  starting transfers between devices  41.3 us (28%)
  between operations  14.2 us (10%)
  Pallas kernels  12.2 us (8%)
  blocking collectives  11.4 us (8%)
  local copies, waits for them, and re-layouts  6.5 us (4%)
  other arithmetic  2.07 us (1%)
    all_to_all x3, waiting for transfers between devices, exchange(): return lax.all_to_all(v, axis, 0, 0, tiled=True)  33.9 us
    all_to_all x3, starting transfers between devices, exchange(): return lax.all_to_all(v, axis, 0, 0, tiled=True)  19.9 us
    all_gather x1, waiting for transfers between devices, shards(): lower = lax.all_gather(lower, ('y', 'c'), axis=0, tiled=False)  15 us
    all_to_all x1, blocking collectives, exchange(): return lax.all_to_all(v, axis, 0, 0, tiled=True)  11.4 us
    ppermute x3, starting transfers between devices, shards(): lax.ppermute(pieces[k], 'x', [(i, i + k & 3) for i in range(4)])  10.5 us
    ppermute x2, starting transfers between devices, deal(): return lax.ppermute(v, ('c', 'x'), moves)  8.53 us
    ppermute x2, waiting for transfers between devices, deal(): return lax.ppermute(v, ('c', 'x'), moves)  5.21 us
    unnamed x12, local copies, waits for them, and re-layouts  4.78 us
  transfers between devices with their start and end apart: 11, of which 7 were waited for; matrix products, arithmetic and copies ran while one was open for 2% of the time, Pallas kernels for 4%

profile of v2, /device:TPU:1, one launch (start us, length us, event | category | flops | bytes accessed | tf_op | source)
XLA Modules:
  0.0 145.4 jit_solution(8232081738919339587)
XLA Ops:
  7.2 0.0 all-gather.5.cloned.1.call-start
  7.2 0.7 stack.23.at_ref
  7.9 0.0 copy-start.4
  7.9 3.5 %shard_map.76 = (f32[512,128]{1,0:T(8,128)}, f32[2,128,128]{2,1,0:T(8,128)}, f32[2,128,128]{2,1,0:T(8,128)}) custom-call(s32[5]{0:T(128)} %stack.23.at_ref, s32[32,128]{1,0:T(8,128)} %bitcast.13, f32[512,256]{1,0:T(8,128)} %root_hbm.1, f32[256,128]{1,0:T(8,128)} %lower_hbm.1, f32[256,128]{1,0:T(8,128)} %upper_hbm.1), custom_call_target="tpu_custom_call" | custom-call | tf_op jit(solution)/shard_map/pallas_call | solution.py:80
  11.4 0.0 all-gather.5.cloned.1.call-update
  11.4 6.0 %collective-permute-start = (f32[2,128,128]{2,1,0:T(8,128)}, f32[2,128,128]{2,1,0:T(8,128)S(1)}, u32[]{:S(2)}, u32[]{:S(2)}) collective-permute-start(f32[2,128,128]{2,1,0:T(8,128)} %get-tuple-element.15), channel_id=1, source_target_pairs={{0,0},{1,1},{2,32},{3,33},{32,2},{33,3},{34,34},{35,35},{4,4},{5,5... | collective-permute-start | bytes 393224 | tf_op jit(solution)/shard_map/ppermute | solution.py:241
  17.5 2.5 %collective-permute-start.1 = (f32[2,128,128]{2,1,0:T(8,128)}, f32[2,128,128]{2,1,0:T(8,128)S(1)}, u32[]{:S(2)}, u32[]{:S(2)}) collective-permute-start(f32[2,128,128]{2,1,0:T(8,128)} %get-tuple-element.16), channel_id=1, source_target_pairs={{0,1},{1,0},{2,33},{3,32},{32,3},{33,2},{34,35},{35,34},{4,5},{5,4... | collective-permute-start | bytes 393224 | tf_op jit(solution)/shard_map/ppermute | solution.py:241
  20.0 0.4 collective-permute-done.first_ref
  20.3 4.9 %collective-permute-done.1.second_ref = f32[2,128,128]{2,1,0:T(8,128)S(1)} collective-permute-done((f32[2,128,128]{2,1,0:T(8,128)}, f32[2,128,128]{2,1,0:T(8,128)S(1)}, u32[]{:S(2)}, u32[]{:S(2)}) %collective-permute-start.1) | collective-permute-done | bytes 131104 | tf_op jit(solution)/shard_map/ppermute | solution.py:241
  25.2 1.1 shard_map.77
  26.3 6.8 %all-to-all-start = ((f32[8,2,128,128]{3,2,1,0:T(8,128)}), f32[8,2,128,128]{3,2,1,0:T(8,128)S(1)}, u32[]{:S(2)}, u32[]{:S(2)}) async-start(f32[8,2,128,128]{3,2,1,0:T(8,128)} %get-tuple-element.22), calls=%async_computation | async-start | bytes 2097152 | tf_op jit(solution)/shard_map/all_to_all | solution.py:236
  33.1 0.0 all-gather.7.cloned.1.call-start
  33.1 0.7 all-gather.7.cloned.1.call-update
  33.8 27.3 %all-to-all-done.columns_ref = f32[8,2,128,128]{3,2,1,0:T(8,128)S(1)} async-done(((f32[8,2,128,128]{3,2,1,0:T(8,128)}), f32[8,2,128,128]{3,2,1,0:T(8,128)S(1)}, u32[]{:S(2)}, u32[]{:S(2)}) %all-to-all-start) | async-done | bytes 1048608 | tf_op jit(solution)/shard_map/all_to_all | solution.py:236
  61.1 2.3 %collective-permute-start.5 = (f32[8,2,128,128]{3,2,1,0:T(8,128)S(1)}, f32[8,2,128,128]{3,2,1,0:T(8,128)S(1)}, u32[]{:S(2)}, u32[]{:S(2)}) collective-permute-start(f32[8,2,128,128]{3,2,1,0:T(8,128)S(1)} %all-to-all-done.columns_ref), channel_id=1, source_target_pairs={{0,32},{32,0},{1,33},{33,1},{2,34},{34,2},{3,35},{35,3},{4,36},{36... | collective-permute-start | bytes 3145736 | tf_op jit(solution)/shard_map/ppermute | solution.py:254
  63.4 0.0 all-gather.5.cloned.1.call-done
  63.5 0.0 copy-done.4
  63.5 0.0 copy-start
  63.5 1.6 %copy-done = f32[4096,128]{1,0:T(8,128)S(1)} copy-done((f32[4096,128]{1,0:T(8,128)S(1)}, f32[4096,128]{1,0:T(8,128)}, u32[]{:S(2)}) %copy-start) | copy-done | bytes 2097176
  65.1 1.4 shard_map.79.refs_0_
  66.5 0.0 collective-permute-done.5.columns_ref
  66.5 1.4 shard_map.80
  67.9 11.4 %all_to_all.20 = f32[4,256,128]{2,1,0:T(8,128)S(1)} all-to-all(f32[4,256,128]{2,1,0:T(8,128)S(1)} %shard_map.80), channel_id=1, replica_groups=mesh['y'=8,'c'=2,'z'=8,'x'=4] {'x'}, dimensions={0} | all-to-all | bytes 1048576 | tf_op jit(solution)/shard_map/all_to_all | solution.py:236
  79.3 0.0 copy-start.1
  79.4 1.0 broadcast_in_dim.2
  80.4 9.5 %all-to-all-start.2 = ((f32[8,256,128]{2,1,0:T(8,128)}), f32[8,256,128]{2,1,0:T(8,128)S(1)}, u32[]{:S(2)}, u32[]{:S(2)}) async-start(f32[8,256,128]{2,1,0:T(8,128)} %broadcast_in_dim.2), calls=%async_computation.2 | async-start | bytes 2097152 | tf_op jit(solution)/shard_map/all_to_all | solution.py:236
  89.9 15.0 %all-gather.7.cloned.1.call-done = f32[4096,128]{1,0:T(8,128)} async-done(((f32[256,128]{1,0:T(8,128)}), f32[4096,128]{1,0:T(8,128)}) %all-gather.7.cloned.1.call-update) | async-done | bytes 2097168 | tf_op jit(solution)/shard_map/all_gather | solution.py:252
  104.8 0.0 copy-done.1
  104.8 0.0 copy-start.2
  104.8 1.6 %copy-done.2 = f32[4096,128]{1,0:T(8,128)S(1)} copy-done((f32[4096,128]{1,0:T(8,128)S(1)}, f32[4096,128]{1,0:T(8,128)}, u32[]{:S(2)}) %copy-start.2) | copy-done | bytes 2097176
  106.4 2.0 %shard_map.78 = (f32[256,128]{1,0:T(8,128)S(1)}, f32[256,128]{1,0:T(8,128)S(1)}, f32[256,128]{1,0:T(8,128)S(1)}, f32[256,128]{1,0:T(8,128)S(1)}) custom-call(s32[5]{0:T(128)S(1)} %copy-done.4, f32[8,512,128]{2,1,0:T(8,128)S(1)} %bitcast.10, f32[16,256,128]{2,1,0:T(8,128)S(1)} %bitcast.11), custom_call_target="tpu_custom_call" | custom-call | flops 1610612736 | bytes 6291456 | tf_op jit(solution)/shard_map/pallas_call | solution.py:188
  108.5 3.1 %collective-permute-start.2 = (f32[256,128]{1,0:T(8,128)S(1)}, f32[256,128]{1,0:T(8,128)S(1)}, u32[]{:S(2)}, u32[]{:S(2)}) collective-permute-start(f32[256,128]{1,0:T(8,128)S(1)} %get-tuple-element.19), channel_id=1, source_target_pairs={{0,1},{1,2},{2,3},{3,0},{4,5},{5,6},{6,7},{7,4},{8,9},{9,10},{10,1... | collective-permute-start | bytes 393224 | tf_op jit(solution)/shard_map/ppermute | solution.py:261
  111.6 4.3 %collective-permute-start.3 = (f32[256,128]{1,0:T(8,128)S(1)}, f32[256,128]{1,0:T(8,128)S(1)}, u32[]{:S(2)}, u32[]{:S(2)}) collective-permute-start(f32[256,128]{1,0:T(8,128)S(1)} %get-tuple-element.20), channel_id=1, source_target_pairs={{0,2},{1,3},{2,0},{3,1},{4,6},{5,7},{6,4},{7,5},{8,10},{9,11},{10,... | collective-permute-start | bytes 393224 | tf_op jit(solution)/shard_map/ppermute | solution.py:261
  115.9 3.1 %collective-permute-start.4 = (f32[256,128]{1,0:T(8,128)S(1)}, f32[256,128]{1,0:T(8,128)S(1)}, u32[]{:S(2)}, u32[]{:S(2)}) collective-permute-start(f32[256,128]{1,0:T(8,128)S(1)} %get-tuple-element.21), channel_id=1, source_target_pairs={{0,3},{1,0},{2,1},{3,2},{4,7},{5,4},{6,5},{7,6},{8,11},{9,8},{10,9... | collective-permute-start | bytes 393224 | tf_op jit(solution)/shard_map/ppermute | solution.py:261
  119.0 0.0 collective-permute-done.2
  119.0 1.2 collective-permute-done.3
  120.2 1.8 %collective-permute-done.4 = f32[256,128]{1,0:T(8,128)S(1)} collective-permute-done((f32[256,128]{1,0:T(8,128)S(1)}, f32[256,128]{1,0:T(8,128)S(1)}, u32[]{:S(2)}, u32[]{:S(2)}) %collective-permute-start.4) | collective-permute-done | bytes 131104 | tf_op jit(solution)/shard_map/ppermute | solution.py:261
  122.0 0.7 add_negate_fusion
  122.7 0.0 all-to-all-done.2.w_ref
  122.7 0.0 copy-start.3
  122.7 1.6 %copy-done.3 = f32[4096,128]{1,0:T(8,128)S(1)} copy-done((f32[4096,128]{1,0:T(8,128)S(1)}, f32[4096,128]{1,0:T(8,128)}, u32[]{:S(2)}) %copy-start.3) | copy-done | bytes 2097176
  124.3 0.0 copy-start.5
  124.3 2.7 %shard_map.81 = f32[4,256,128]{2,1,0:T(8,128)} custom-call(s32[5]{0:T(128)S(1)} %copy-done.4, f32[8,256,128]{2,1,0:T(8,128)S(1)} %all-to-all-done.2.w_ref, f32[16,256,128]{2,1,0:T(8,128)S(1)} %bitcast.12), custom_call_target="tpu_custom_call" | custom-call | tf_op jit(solution)/shard_map/pallas_call | solution.py:220
  127.0 3.7 %all-to-all-start.3 = ((f32[4,256,128]{2,1,0:T(8,128)}), f32[4,256,128]{2,1,0:T(8,128)S(1)}, u32[]{:S(2)}, u32[]{:S(2)}) async-start(f32[4,256,128]{2,1,0:T(8,128)} %shard_map.81), calls=%async_computation.3 | async-start | bytes 1048576 | tf_op jit(solution)/shard_map/all_to_all | solution.py:236
  130.7 0.7 neg.7
  131.3 6.6 %all-to-all-done.3 = f32[4,256,128]{2,1,0:T(8,128)S(1)} async-done(((f32[4,256,128]{2,1,0:T(8,128)}), f32[4,256,128]{2,1,0:T(8,128)S(1)}, u32[]{:S(2)}, u32[]{:S(2)}) %all-to-all-start.3) | async-done | bytes 524320 | tf_op jit(solution)/shard_map/all_to_all | solution.py:236
  137.9 0.0 copy-done.5
  137.9 0.7 add.23
  (2 shorter events, 0.1 us)
Async XLA Ops:
  7.2 56.3 %all-gather.5.cloned.1.call-start = ((), (), s32[]{:S(2)}) async-start(), calls=%async_computation.4 | async-start | bytes 2359296 | tf_op jit(solution)/shard_map/all_gather | solution.py:250
  7.9 55.6 %copy-start.4 = (s32[5]{0:T(128)S(1)}, s32[5]{0:T(128)}, u32[]{:S(2)}) copy-start(s32[5]{0:T(128)} %stack.23.at_ref) | copy-start | bytes 64
  11.4 8.9 %collective-permute-start = (f32[2,128,128]{2,1,0:T(8,128)}, f32[2,128,128]{2,1,0:T(8,128)S(1)}, u32[]{:S(2)}, u32[]{:S(2)}) collective-permute-start(f32[2,128,128]{2,1,0:T(8,128)} %get-tuple-element.15), channel_id=1, source_target_pairs={{0,0},{1,1},{2,32},{3,33},{32,2},{33,3},{34,34},{35,35},{4,4},{5,5... | collective-permute-start | bytes 393224 | tf_op jit(solution)/shard_map/ppermute | solution.py:241
  17.5 7.7 %collective-permute-start.1 = (f32[2,128,128]{2,1,0:T(8,128)}, f32[2,128,128]{2,1,0:T(8,128)S(1)}, u32[]{:S(2)}, u32[]{:S(2)}) collective-permute-start(f32[2,128,128]{2,1,0:T(8,128)} %get-tuple-element.16), channel_id=1, source_target_pairs={{0,1},{1,0},{2,33},{3,32},{32,3},{33,2},{34,35},{35,34},{4,5},{5,4... | collective-permute-start | bytes 393224 | tf_op jit(solution)/shard_map/ppermute | solution.py:241
  26.3 34.9 %all-to-all-start = ((f32[8,2,128,128]{3,2,1,0:T(8,128)}), f32[8,2,128,128]{3,2,1,0:T(8,128)S(1)}, u32[]{:S(2)}, u32[]{:S(2)}) async-start(f32[8,2,128,128]{3,2,1,0:T(8,128)} %get-tuple-element.22), calls=%async_computation | async-start | bytes 2097152 | tf_op jit(solution)/shard_map/all_to_all | solution.py:236
  33.1 71.7 %all-gather.7.cloned.1.call-start = ((), (), s32[]{:S(2)}) async-start(), calls=%async_computation.5 | async-start | bytes 2228224 | tf_op jit(solution)/shard_map/all_gather | solution.py:252
  61.1 5.3 %collective-permute-start.5 = (f32[8,2,128,128]{3,2,1,0:T(8,128)S(1)}, f32[8,2,128,128]{3,2,1,0:T(8,128)S(1)}, u32[]{:S(2)}, u32[]{:S(2)}) collective-permute-start(f32[8,2,128,128]{3,2,1,0:T(8,128)S(1)} %all-to-all-done.columns_ref), channel_id=1, source_target_pairs={{0,32},{32,0},{1,33},{33,1},{2,34},{34,2},{3,35},{35,3},{4,36},{36... | collective-permute-start | bytes 3145736 | tf_op jit(solution)/shard_map/ppermute | solution.py:254
  63.5 1.6 %copy-start = (f32[4096,128]{1,0:T(8,128)S(1)}, f32[4096,128]{1,0:T(8,128)}, u32[]{:S(2)}) copy-start(f32[4096,128]{1,0:T(8,128)} %all-gather.5.cloned.1.call-done) | copy-start | bytes 6291460
  79.3 25.5 %copy-start.1 = (f32[4096,128]{1,0:T(8,128)S(1)}, f32[4096,128]{1,0:T(8,128)}, u32[]{:S(2)}) copy-start(f32[4096,128]{1,0:T(8,128)} %all-gather.5.cloned.1.call-done) | copy-start | bytes 6291460
  80.4 42.3 %all-to-all-start.2 = ((f32[8,256,128]{2,1,0:T(8,128)}), f32[8,256,128]{2,1,0:T(8,128)S(1)}, u32[]{:S(2)}, u32[]{:S(2)}) async-start(f32[8,256,128]{2,1,0:T(8,128)} %broadcast_in_dim.2), calls=%async_computation.2 | async-start | bytes 2097152 | tf_op jit(solution)/shard_map/all_to_all | solution.py:236
  104.8 1.6 %copy-start.2 = (f32[4096,128]{1,0:T(8,128)S(1)}, f32[4096,128]{1,0:T(8,128)}, u32[]{:S(2)}) copy-start(f32[4096,128]{1,0:T(8,128)} %all-gather.7.cloned.1.call-done) | copy-start | bytes 6291460
  108.5 10.5 %collective-permute-start.2 = (f32[256,128]{1,0:T(8,128)S(1)}, f32[256,128]{1,0:T(8,128)S(1)}, u32[]{:S(2)}, u32[]{:S(2)}) collective-permute-start(f32[256,128]{1,0:T(8,128)S(1)} %get-tuple-element.19), channel_id=1, source_target_pairs={{0,1},{1,2},{2,3},{3,0},{4,5},{5,6},{6,7},{7,4},{8,9},{9,10},{10,1... | collective-permute-start | bytes 393224 | tf_op jit(solution)/shard_map/ppermute | solution.py:261
  111.6 8.6 %collective-permute-start.3 = (f32[256,128]{1,0:T(8,128)S(1)}, f32[256,128]{1,0:T(8,128)S(1)}, u32[]{:S(2)}, u32[]{:S(2)}) collective-permute-start(f32[256,128]{1,0:T(8,128)S(1)} %get-tuple-element.20), channel_id=1, source_target_pairs={{0,2},{1,3},{2,0},{3,1},{4,6},{5,7},{6,4},{7,5},{8,10},{9,11},{10,... | collective-permute-start | bytes 393224 | tf_op jit(solution)/shard_map/ppermute | solution.py:261
  115.9 6.1 %collective-permute-start.4 = (f32[256,128]{1,0:T(8,128)S(1)}, f32[256,128]{1,0:T(8,128)S(1)}, u32[]{:S(2)}, u32[]{:S(2)}) collective-permute-start(f32[256,128]{1,0:T(8,128)S(1)} %get-tuple-element.21), channel_id=1, source_target_pairs={{0,3},{1,0},{2,1},{3,2},{4,7},{5,4},{6,5},{7,6},{8,11},{9,8},{10,9... | collective-permute-start | bytes 393224 | tf_op jit(solution)/shard_map/ppermute | solution.py:261
  122.7 1.6 %copy-start.3 = (f32[4096,128]{1,0:T(8,128)S(1)}, f32[4096,128]{1,0:T(8,128)}, u32[]{:S(2)}) copy-start(f32[4096,128]{1,0:T(8,128)} %all-gather.7.cloned.1.call-done) | copy-start | bytes 6291460
  124.3 13.6 %copy-start.5 = (f32[256,128]{1,0:T(8,128)S(1)}, f32[256,128]{1,0:T(8,128)}, u32[]{:S(2)}) copy-start(f32[256,128]{1,0:T(8,128)} %param.9) | copy-start | bytes 393220
  127.0 10.9 %all-to-all-start.3 = ((f32[4,256,128]{2,1,0:T(8,128)}), f32[4,256,128]{2,1,0:T(8,128)S(1)}, u32[]{:S(2)}, u32[]{:S(2)}) async-start(f32[4,256,128]{2,1,0:T(8,128)} %shard_map.81), calls=%async_computation.3 | async-start | bytes 1048576 | tf_op jit(solution)/shard_map/all_to_all | solution.py:236
Sparse Core Ops, SparseCore 0:
  11.5 46.0 all-gather.4
  60.3 44.4 all-gather.6

commit v3 on v2

v3 whole, which is shorter than its diff:
```python
import jax
import jax.numpy as jnp
import numpy as np
from jax import lax
from jax.experimental import pallas as pl
from jax.experimental.pallas import tpu as pltpu
from jax.sharding import Mesh, PartitionSpec as P

F32 = jnp.float32
BF16 = jnp.bfloat16
VMEM = pl.BlockSpec(memory_space=pltpu.VMEM)
SMEM = pl.BlockSpec(memory_space=pltpu.SMEM)
HBM = pl.BlockSpec(memory_space=pltpu.HBM)
PARAMS = pltpu.CompilerParams(vmem_limit_bytes=32 * 1024 * 1024)
WIDE = pltpu.CompilerParams(vmem_limit_bytes=62 * 1024 * 1024)
MIDDLE = pltpu.CompilerParams(vmem_limit_bytes=52 * 1024 * 1024)
DMA = pltpu.SemaphoreType.DMA


def shape(*dims, dtype=F32):
    return jax.ShapeDtypeStruct(dims, dtype)


def split2(v):
    hi = v.astype(BF16)
    return hi, (v - hi.astype(F32)).astype(BF16)


def dot(a, b):
    return lax.dot_general(a, b, (((1,), (0,)), ((), ())), preferred_element_type=F32)


def three_pass(ah, al, bh, bl):
    return dot(ah, bh) + (dot(ah, bl) + dot(al, bh))


def device(ref):
    number = ref[0]
    return number >> 5, number & 31, (number >> 5) & 1, (number >> 2) & 7, number & 3


def pick_kernel(
    at_ref, map_hbm, root_hbm, lower_hbm, sigma_ref, first_ref, second_ref, picks, root, lower, sems
):
    loads = [
        pltpu.make_async_copy(map_hbm, picks, sems.at[0]),
        pltpu.make_async_copy(root_hbm, root, sems.at[1]),
        pltpu.make_async_copy(lower_hbm, lower, sems.at[2]),
    ]
    for load in loads:
        load.start()
    row, col, _, _, x = device(at_ref)
    odd = x & 1
    iota = lax.broadcasted_iota(jnp.int32, (256, 128), 0)
    loads[0].wait()
    cols = picks[pl.ds(col, 1), :] - 256 * col
    col_hot = jnp.where(cols == iota, 1.0, 0.0).astype(BF16)
    hots = []
    for part in range(2):
        block = 2 * row + part
        rows = picks[pl.ds(block, 1), :] - 256 * block
        hots.append(jnp.where(rows == iota, 1.0, 0.0).astype(BF16))
    loads[1].wait()
    stack = []
    for part in range(2):
        left = root[256 * part : 256 * (part + 1), :]
        pieces = []
        for _ in range(3):
            piece = left.astype(BF16)
            left = left - piece.astype(F32)
            pieces.append(piece)
        across = lax.dot_general(
            hots[part],
            jnp.concatenate(pieces, axis=1),
            (((0,), (0,)), ((), ())),
            preferred_element_type=F32,
        ).astype(BF16)
        stack += [across[:, 256 * i : 256 * (i + 1)] for i in range(3)]
    value = dot(jnp.concatenate(stack, axis=0), col_hot)
    for part in range(2):
        v = [value[128 * (3 * part + i) : 128 * (3 * part + i + 1), :] for i in range(3)]
        sigma_ref[128 * part : 128 * (part + 1), :] = (v[0] + v[1]) + v[2]
    loads[2].wait()
    near = pl.multiple_of(128 * odd, 128)
    far = pl.multiple_of(128 - 128 * odd, 128)
    first_ref[0] = sigma_ref[pl.ds(near, 128), :]
    first_ref[1] = lower[pl.ds(near, 128), :]
    second_ref[0] = sigma_ref[pl.ds(far, 128), :]
    second_ref[1] = lower[pl.ds(far, 128), :]


def pick(at, blocks, root, lower):
    return pl.pallas_call(
        pick_kernel,
        out_shape=(shape(256, 128), shape(2, 128, 128), shape(2, 128, 128)),
        in_specs=[SMEM] + [HBM] * 3,
        out_specs=(VMEM, VMEM, VMEM),
        scratch_shapes=[
            pltpu.VMEM((32, 128), jnp.int32),
            pltpu.VMEM((512, 256), F32),
            pltpu.VMEM((256, 128), F32),
            DMA((3,)),
        ],
        compiler_params=WIDE,
    )(at, blocks, root, lower)


def fan_kernel(first_ref, second_ref, copies_ref, lower_ref):
    for t, ref in enumerate((first_ref, second_ref)):
        lower_ref[128 * t : 128 * (t + 1), :] = ref[1]
        value = ref[0]
        for i in range(8):
            copies_ref[i, t] = value


def fan(first, second):
    return pl.pallas_call(
        fan_kernel,
        out_shape=(shape(8, 2, 128, 128), shape(256, 128)),
        in_specs=[VMEM] * 2,
        out_specs=(VMEM, VMEM),
        compiler_params=PARAMS,
    )(first, second)


def couple(at, upper, columns, before=None):
    def kernel(at_ref, upper_hbm, columns_hbm, *refs):
        before_ref, (out_ref, left, right, ah, al, bh, bl, sems) = (
            (None, refs) if before is None else (refs[0], refs[1:])
        )
        loads = [
            pltpu.make_async_copy(columns_hbm, right, sems.at[0]),
            pltpu.make_async_copy(upper_hbm, left, sems.at[1]),
        ]
        for load in loads:
            load.start()
        loads[0].wait()
        for z in range(8):
            rows = slice(128 * z, 128 * (z + 1))
            for t in range(2):
                cols = slice(128 * t, 128 * (t + 1))
                bh[rows, cols], bl[rows, cols] = split2(right[z, t])
        loads[1].wait()
        for z in range(8):
            rows = slice(128 * z, 128 * (z + 1))
            ah[:, rows], al[:, rows] = split2(left[z])
        part = three_pass(ah[...], al[...], bh[...], bl[...])
        if before is None:
            out_ref[0] = part[:, :128]
            out_ref[1] = part[:, 128:]
        else:
            _, _, core, _, x = device(at_ref)
            odd = x & 1
            out_ref[2 * core + odd] = before_ref[0]
            out_ref[2 * core + 1 - odd] = before_ref[1]
            out_ref[2 * (1 - core) + odd] = part[:, :128]
            out_ref[2 * (1 - core) + 1 - odd] = part[:, 128:]

    more = () if before is None else (before,)
    return pl.pallas_call(
        kernel,
        out_shape=shape(2 + 2 * len(more), 256, 128),
        in_specs=[SMEM, HBM, HBM] + [VMEM] * len(more),
        out_specs=VMEM,
        scratch_shapes=[
            pltpu.VMEM((8, 256, 128), F32),
            pltpu.VMEM((8, 2, 128, 128), F32),
            pltpu.VMEM((256, 1024), BF16),
            pltpu.VMEM((256, 1024), BF16),
            pltpu.VMEM((1024, 256), BF16),
            pltpu.VMEM((1024, 256), BF16),
            DMA((2,)),
        ],
        compiler_params=PARAMS,
        cost_estimate=pl.CostEstimate(flops=3 << 28, bytes_accessed=3 << 20, transcendentals=0),
    )(at, upper, columns, *more)


def side_kernel(at_ref, lower_hbm, *refs):
    blocks, sums, (bh, bl, lower, ah, al, out, sem) = refs[:8], refs[8:12], refs[12:]
    load = pltpu.make_async_copy(lower_hbm, lower, sem)
    load.start()
    _, _, _, z, x = device(at_ref)
    odd = x & 1
    for k, ref in enumerate(blocks):
        cols = pl.ds(pl.multiple_of(128 * ((z - k) & 7), 128), 128)
        ah[:, cols], al[:, cols] = split2(ref[...])
    load.wait()
    for i in range(8):
        rows = slice(128 * i, 128 * (i + 1))
        for core in range(2):
            for t in range(2):
                cols = slice(256 * core + 128 * t, 256 * core + 128 * (t + 1))
                place = 128 * (odd if t == 0 else 1 - odd)
                value = lower[2 * i + core, pl.ds(pl.multiple_of(place, 128), 128), :]
                bh[rows, cols], bl[rows, cols] = split2(value)
    for n in range(2):
        cols = slice(256 * n, 256 * (n + 1))
        part = three_pass(ah[...], al[...], bh[:, cols], bl[:, cols])
        out[2 * n] = part[:, :128]
        out[2 * n + 1] = part[:, 128:]
    for k, ref in enumerate(sums):
        ref[...] = out[(x + k) & 3]


def side(at, lower, blocks):
    return pl.pallas_call(
        side_kernel,
        out_shape=(shape(256, 128),) * 4 + (shape(1024, 512, dtype=BF16),) * 2,
        in_specs=[SMEM, HBM] + [VMEM] * 8,
        out_specs=(VMEM,) * 6,
        scratch_shapes=[
            pltpu.VMEM((16, 256, 128), F32),
            pltpu.VMEM((256, 1024), BF16),
            pltpu.VMEM((256, 1024), BF16),
            pltpu.VMEM((4, 256, 128), F32),
            DMA,
        ],
        compiler_params=WIDE,
        cost_estimate=pl.CostEstimate(flops=6 << 28, bytes_accessed=6 << 20, transcendentals=0),
    )(at, lower, *blocks)


def last_kernel(w_hbm, hi_hbm, lo_hbm, out_ref, w, ah, al, bh, bl, sems):
    loads = [
        pltpu.make_async_copy(w_hbm, w, sems.at[0]),
        pltpu.make_async_copy(hi_hbm, bh, sems.at[1]),
        pltpu.make_async_copy(lo_hbm, bl, sems.at[2]),
    ]
    for load in loads:
        load.start()
    loads[0].wait()
    for z in range(8):
        rows = slice(128 * z, 128 * (z + 1))
        ah[:, rows], al[:, rows] = split2(w[z])
    for load in loads[1:]:
        load.wait()
    for n in range(2):
        cols = slice(256 * n, 256 * (n + 1))
        part = three_pass(ah[...], al[...], bh[:, cols], bl[:, cols])
        out_ref[2 * n] = part[:, :128]
        out_ref[2 * n + 1] = part[:, 128:]


def last(w, hi, lo):
    return pl.pallas_call(
        last_kernel,
        out_shape=shape(4, 256, 128),
        in_specs=[HBM] * 3,
        out_specs=VMEM,
        scratch_shapes=[
            pltpu.VMEM((8, 256, 128), F32),
            pltpu.VMEM((256, 1024), BF16),
            pltpu.VMEM((256, 1024), BF16),
            pltpu.VMEM((1024, 512), BF16),
            pltpu.VMEM((1024, 512), BF16),
            DMA((3,)),
        ],
        compiler_params=MIDDLE,
    )(w, hi, lo)


def exchange(v, axis):
    return lax.all_to_all(v, axis, 0, 0, tiled=True)


def deal(v, t):
    moves = [(4 * c + x, 4 * (x >> 1) + 2 * c + ((x & 1) ^ t)) for c in range(2) for x in range(4)]
    return lax.ppermute(v, ("c", "x"), moves)


def turn(v, axis, size, k):
    return lax.ppermute(v, axis, [(i, (i + k) % size) for i in range(size)])


def shards(root_inverse, boundary_map, lower_factor, upper_factor, diagonal_inverse):
    at = lax.axis_index(("y", "c", "z", "x")).astype(jnp.int32).reshape(1)
    upper = lax.all_gather(upper_factor, "z", axis=0, tiled=False)
    sigma, first, second = pick(at, boundary_map.reshape(32, 128), root_inverse, lower_factor)
    copies, lower = fan(deal(first, 0), deal(second, 1))
    lower = lax.all_gather(lower, ("y", "c"), axis=0, tiled=False)
    own = exchange(copies, "y")
    blocks = [sigma] + [turn(sigma, "z", 8, k) for k in range(1, 8)]
    own, blocks = lax.optimization_barrier((own, blocks))
    other = turn(own, "c", 2, 1)
    part = couple(at, upper, other, couple(at, upper, own))
    w = exchange(part, "x").sum(axis=0)
    w_all = exchange(jnp.broadcast_to(w[None], (8, 256, 128)), "z")
    *sums, hi, lo = side(at, lower, blocks)
    total = sums[0]
    for k in range(1, 4):
        total = total + turn(sums[k], "x", 4, k)
    total, w_all = lax.optimization_barrier((-total, w_all))
    product = exchange(last(w_all, hi, lo), "x").sum(axis=0)
    return (total, -w, diagonal_inverse + product)


def solution(mesh):
    grid = Mesh(np.asarray(mesh.devices).reshape(8, 2, 8, 4), ("y", "c", "z", "x"))
    block = P(("y", "c"), ("z", "x"))
    return jax.shard_map(
        shards,
        mesh=grid,
        in_specs=(block, P(), block, block, block),
        out_specs=(block, block, block),
        check_vma=False,
    )
```

time: 147 us -> 159 us (1.082)
  starting transfers between devices: 41.3 us -> 67.3 us
  waiting for transfers between devices: 57.8 us -> 44.5 us
  local copies, waits for them, and re-layouts: 6.5 us -> 3.52 us
  Pallas kernels: 12.2 us -> 13.8 us
    ppermute x4 -> x11, starting transfers between devices: 12.8 us -> 43.2 us  [turn(): return lax.ppermute(v, axis, [(i, (i + k) % size) for i in range(size)])]
    all_to_all x3, waiting for transfers between devices: 33.9 us -> 7.45 us  [exchange(): return lax.all_to_all(v, axis, 0, 0, tiled=True)]
    ppermute x4 -> x11, waiting for transfers between devices: 3 us -> 18.7 us  [turn(): return lax.ppermute(v, axis, [(i, (i + k) % size) for i in range(size)])]
    all_to_all x3, starting transfers between devices: 19.9 us -> 15.4 us  [exchange(): return lax.all_to_all(v, axis, 0, 0, tiled=True)]
    all_gather x1, waiting for transfers between devices: 15 us -> 11.7 us  [shards(): lower = lax.all_gather(lower, ('y', 'c'), axis=0, tiled=False)]
    pallas_call x3, Pallas kernels: 8.24 us -> 10.9 us  [the longest x1 5.15 us: side(): pl.pallas_call(side_kernel, out_shape=(shape(256, 128),) * 4 + (shape(102...]
    unnamed x12 -> x20, local copies, waits for them, and re-layouts: 4.78 us -> 2.46 us
  transfers between devices with their start and end apart: 11 -> 18, of which waited for: 7 -> 12; matrix products, arithmetic and copies ran while one was open for 2% -> 2% of each run, Pallas kernels for 4% -> 7%
where the time goes in v3:
time: 159 us; the launch traced here: 158 us
  starting transfers between devices  67.3 us (42%)
  waiting for transfers between devices  44.5 us (28%)
  between operations  14.3 us (9%)
  Pallas kernels  13.8 us (9%)
  blocking collectives  11.6 us (7%)
  local copies, waits for them, and re-layouts  3.52 us (2%)
  other arithmetic  2.99 us (2%)
    ppermute x11, starting transfers between devices, turn(): return lax.ppermute(v, axis, [(i, (i + k) % size) for i in range(size)])  43.2 us
    ppermute x11, waiting for transfers between devices, turn(): return lax.ppermute(v, axis, [(i, (i + k) % size) for i in range(size)])  18.7 us
    all_to_all x3, starting transfers between devices, exchange(): return lax.all_to_all(v, axis, 0, 0, tiled=True)  15.4 us
    all_gather x1, waiting for transfers between devices, shards(): lower = lax.all_gather(lower, ('y', 'c'), axis=0, tiled=False)  11.7 us
    all_to_all x1, blocking collectives, exchange(): return lax.all_to_all(v, axis, 0, 0, tiled=True)  11.6 us
    ppermute x2, starting transfers between devices, deal(): return lax.ppermute(v, ('c', 'x'), moves)  8.66 us
    all_to_all x3, waiting for transfers between devices, exchange(): return lax.all_to_all(v, axis, 0, 0, tiled=True)  7.45 us
    ppermute x2, waiting for transfers between devices, deal(): return lax.ppermute(v, ('c', 'x'), moves)  5.21 us
  transfers between devices with their start and end apart: 18, of which 12 were waited for; matrix products, arithmetic and copies ran while one was open for 2% of the time, Pallas kernels for 7%

profile of v3, /device:TPU:1, one launch (start us, length us, event | category | flops | bytes accessed | tf_op | source)
XLA Modules:
  0.0 158.1 jit_solution(17610170716949031593)
XLA Ops:
  7.2 0.0 all-gather.7.cloned.1.call-start
  7.2 0.7 all-gather.7.cloned.1.call-update
  7.9 2.3 %shard_map.76 = (f32[256,128]{1,0:T(8,128)}, f32[2,128,128]{2,1,0:T(8,128)}, f32[2,128,128]{2,1,0:T(8,128)}) custom-call(s32[1]{0:T(128)} %bitcast.at_ref, s32[32,128]{1,0:T(8,128)} %bitcast.6, f32[512,256]{1,0:T(8,128)} %root_hbm.1, f32[256,128]{1,0:T(8,128)} %lower_hbm.1), custom_call_target="tpu_custom_call" | custom-call | tf_op jit(solution)/shard_map/pallas_call | solution.py:93
  10.2 0.0 copy-start.2
  10.2 6.2 %collective-permute-start = (f32[2,128,128]{2,1,0:T(8,128)}, f32[2,128,128]{2,1,0:T(8,128)S(1)}, u32[]{:S(2)}, u32[]{:S(2)}) collective-permute-start(f32[2,128,128]{2,1,0:T(8,128)} %get-tuple-element.25), channel_id=1, source_target_pairs={{0,0},{1,1},{2,32},{3,33},{32,2},{33,3},{34,34},{35,35},{4,4},{5,5... | collective-permute-start | bytes 393224 | tf_op jit(solution)/shard_map/ppermute | solution.py:269
  16.4 2.5 %collective-permute-start.1 = (f32[2,128,128]{2,1,0:T(8,128)}, f32[2,128,128]{2,1,0:T(8,128)S(1)}, u32[]{:S(2)}, u32[]{:S(2)}) collective-permute-start(f32[2,128,128]{2,1,0:T(8,128)} %get-tuple-element.26), channel_id=1, source_target_pairs={{0,1},{1,0},{2,33},{3,32},{32,3},{33,2},{34,35},{35,34},{4,5},{5,4... | collective-permute-start | bytes 393224 | tf_op jit(solution)/shard_map/ppermute | solution.py:269
  18.9 0.4 collective-permute-done.first_ref
  19.3 4.9 %collective-permute-done.1.second_ref = f32[2,128,128]{2,1,0:T(8,128)S(1)} collective-permute-done((f32[2,128,128]{2,1,0:T(8,128)}, f32[2,128,128]{2,1,0:T(8,128)S(1)}, u32[]{:S(2)}, u32[]{:S(2)}) %collective-permute-start.1) | collective-permute-done | bytes 131104 | tf_op jit(solution)/shard_map/ppermute | solution.py:269
  24.1 1.1 shard_map.77
  25.2 6.8 %all-to-all-start = ((f32[8,2,128,128]{3,2,1,0:T(8,128)}), f32[8,2,128,128]{3,2,1,0:T(8,128)S(1)}, u32[]{:S(2)}, u32[]{:S(2)}) async-start(f32[8,2,128,128]{3,2,1,0:T(8,128)} %get-tuple-element.28), calls=%async_computation | async-start | bytes 2097152 | tf_op jit(solution)/shard_map/all_to_all | solution.py:264
  32.0 0.0 all-gather.5.cloned.1.call-start
  32.1 0.7 all-gather.5.cloned.1.call-update
  32.8 4.0 %collective-permute-start.2 = (f32[256,128]{1,0:T(8,128)S(1)}, f32[256,128]{1,0:T(8,128)S(1)}, u32[]{:S(2)}, u32[]{:S(2)}) collective-permute-start(f32[256,128]{1,0:T(8,128)S(1)} %copy-done.2), channel_id=1, source_target_pairs={{0,4},{4,8},{8,12},{12,16},{16,20},{20,24},{24,28},{28,0},{1,5},{5... | collective-permute-start | bytes 393224 | tf_op jit(solution)/shard_map/ppermute | solution.py:273
  36.8 5.8 %collective-permute-start.3 = (f32[256,128]{1,0:T(8,128)S(1)}, f32[256,128]{1,0:T(8,128)S(1)}, u32[]{:S(2)}, u32[]{:S(2)}) collective-permute-start(f32[256,128]{1,0:T(8,128)S(1)} %copy-done.2), channel_id=1, source_target_pairs={{0,8},{4,12},{8,16},{12,20},{16,24},{20,28},{24,0},{28,4},{1,9},{5... | collective-permute-start | bytes 393224 | tf_op jit(solution)/shard_map/ppermute | solution.py:273
  42.6 7.0 %collective-permute-start.4 = (f32[256,128]{1,0:T(8,128)S(1)}, f32[256,128]{1,0:T(8,128)S(1)}, u32[]{:S(2)}, u32[]{:S(2)}) collective-permute-start(f32[256,128]{1,0:T(8,128)S(1)} %copy-done.2), channel_id=1, source_target_pairs={{0,12},{4,16},{8,20},{12,24},{16,28},{20,0},{24,4},{28,8},{1,13},{... | collective-permute-start | bytes 393224 | tf_op jit(solution)/shard_map/ppermute | solution.py:273
  49.7 2.8 %collective-permute-start.5 = (f32[256,128]{1,0:T(8,128)S(1)}, f32[256,128]{1,0:T(8,128)S(1)}, u32[]{:S(2)}, u32[]{:S(2)}) collective-permute-start(f32[256,128]{1,0:T(8,128)S(1)} %copy-done.2), channel_id=1, source_target_pairs={{0,16},{4,20},{8,24},{12,28},{16,0},{20,4},{24,8},{28,12},{1,17},{... | collective-permute-start | bytes 393224 | tf_op jit(solution)/shard_map/ppermute | solution.py:273
  52.5 6.4 %collective-permute-start.6 = (f32[256,128]{1,0:T(8,128)S(1)}, f32[256,128]{1,0:T(8,128)S(1)}, u32[]{:S(2)}, u32[]{:S(2)}) collective-permute-start(f32[256,128]{1,0:T(8,128)S(1)} %copy-done.2), channel_id=1, source_target_pairs={{0,20},{4,24},{8,28},{12,0},{16,4},{20,8},{24,12},{28,16},{1,21},{... | collective-permute-start | bytes 393224 | tf_op jit(solution)/shard_map/ppermute | solution.py:273
  58.9 3.4 %collective-permute-start.7 = (f32[256,128]{1,0:T(8,128)S(1)}, f32[256,128]{1,0:T(8,128)S(1)}, u32[]{:S(2)}, u32[]{:S(2)}) collective-permute-start(f32[256,128]{1,0:T(8,128)S(1)} %copy-done.2), channel_id=1, source_target_pairs={{0,24},{4,28},{8,0},{12,4},{16,8},{20,12},{24,16},{28,20},{1,25},{... | collective-permute-start | bytes 393224 | tf_op jit(solution)/shard_map/ppermute | solution.py:273
  62.3 2.2 %collective-permute-start.8 = (f32[256,128]{1,0:T(8,128)S(1)}, f32[256,128]{1,0:T(8,128)S(1)}, u32[]{:S(2)}, u32[]{:S(2)}) collective-permute-start(f32[256,128]{1,0:T(8,128)S(1)} %copy-done.2), channel_id=1, source_target_pairs={{0,28},{4,0},{8,4},{12,8},{16,12},{20,16},{24,20},{28,24},{1,29},{... | collective-permute-start | bytes 393224 | tf_op jit(solution)/shard_map/ppermute | solution.py:273
  64.5 3.2 %collective-permute-done.4.refs_3_ = f32[256,128]{1,0:T(8,128)S(1)} collective-permute-done((f32[256,128]{1,0:T(8,128)S(1)}, f32[256,128]{1,0:T(8,128)S(1)}, u32[]{:S(2)}, u32[]{:S(2)}) %collective-permute-start.4) | collective-permute-done | bytes 131104 | tf_op jit(solution)/shard_map/ppermute | solution.py:273
  67.7 1.3 collective-permute-done.5.refs_4_
  69.1 3.0 %collective-permute-done.6.refs_5_ = f32[256,128]{1,0:T(8,128)S(1)} collective-permute-done((f32[256,128]{1,0:T(8,128)S(1)}, f32[256,128]{1,0:T(8,128)S(1)}, u32[]{:S(2)}, u32[]{:S(2)}) %collective-permute-start.6) | collective-permute-done | bytes 131104 | tf_op jit(solution)/shard_map/ppermute | solution.py:273
  72.1 4.6 %collective-permute-done.7.refs_6_ = f32[256,128]{1,0:T(8,128)S(1)} collective-permute-done((f32[256,128]{1,0:T(8,128)S(1)}, f32[256,128]{1,0:T(8,128)S(1)}, u32[]{:S(2)}, u32[]{:S(2)}) %collective-permute-start.7) | collective-permute-done | bytes 131104 | tf_op jit(solution)/shard_map/ppermute | solution.py:273
  76.6 0.1 collective-permute-done.8.refs_7_
  76.7 0.6 copy-done.8
  77.3 0.7 copy-done.9
  78.0 2.3 %collective-permute-start.12 = (f32[8,2,128,128]{3,2,1,0:T(8,128)S(1)}, f32[8,2,128,128]{3,2,1,0:T(8,128)S(1)}, u32[]{:S(2)}, u32[]{:S(2)}) collective-permute-start(f32[8,2,128,128]{3,2,1,0:T(8,128)S(1)} %all-to-all-done.columns_hbm), channel_id=1, source_target_pairs={{0,32},{32,0},{1,33},{33,1},{2,34},{34,2},{3,35},{35,3},{4,36},{36... | collective-permute-start | bytes 3145736 | tf_op jit(solution)/shard_map/ppermute | solution.py:273
  80.3 0.0 all-gather.7.cloned.1.call-done
  80.3 1.2 copy-done
  81.6 0.9 shard_map.79.refs_0_
  82.5 0.1 collective-permute-done.12.columns_hbm
  82.6 0.9 shard_map.80
  83.6 11.6 %all_to_all.20 = f32[4,256,128]{2,1,0:T(8,128)S(1)} all-to-all(f32[4,256,128]{2,1,0:T(8,128)S(1)} %shard_map.80), channel_id=1, replica_groups=mesh['y'=8,'c'=2,'z'=8,'x'=4] {'x'}, dimensions={0} | all-to-all | bytes 1048576 | tf_op jit(solution)/shard_map/all_to_all | solution.py:264
  95.2 1.1 broadcast_in_dim.2
  96.3 5.1 %all-to-all-start.2 = ((f32[8,256,128]{2,1,0:T(8,128)}), f32[8,256,128]{2,1,0:T(8,128)S(1)}, u32[]{:S(2)}, u32[]{:S(2)}) async-start(f32[8,256,128]{2,1,0:T(8,128)} %broadcast_in_dim.2), calls=%async_computation.2 | async-start | bytes 2097152 | tf_op jit(solution)/shard_map/all_to_all | solution.py:264
  101.3 11.7 %all-gather.5.cloned.1.call-done = f32[4096,128]{1,0:T(8,128)} async-done(((f32[256,128]{1,0:T(8,128)}), f32[4096,128]{1,0:T(8,128)}) %all-gather.5.cloned.1.call-update) | async-done | bytes 2097168 | tf_op jit(solution)/shard_map/all_gather | solution.py:281
  113.0 5.2 %shard_map.78 = (f32[256,128]{1,0:T(8,128)}, f32[256,128]{1,0:T(8,128)}, f32[256,128]{1,0:T(8,128)}, f32[256,128]{1,0:T(8,128)}, bf16[1024,512]{1,0:T(8,128)(2,1)}, /*index=5*/bf16[1024,512]{1,0:T(8,128)(2,1)}) custom-call(s32[1]{0:T(128)} %bitcast.at_ref, f32[16,256,128]{2,1,0:T(8,128)} %bitcast.7, f32[256,128]{1,0:T(8,128)} %get-tuple-element.30.refs_0_, ...), custom_call_target="tpu_custom_call" | custom-call | flops 1610612736 | bytes 6291456 | tf_op jit(solution)/shard_map/pallas_call | solution.py:207
  118.2 4.3 %collective-permute-start.11 = (f32[256,128]{1,0:T(8,128)}, f32[256,128]{1,0:T(8,128)S(1)}, u32[]{:S(2)}, u32[]{:S(2)}) collective-permute-start(f32[256,128]{1,0:T(8,128)} %get-tuple-element.41), channel_id=1, source_target_pairs={{0,3},{1,0},{2,1},{3,2},{4,7},{5,4},{6,5},{7,6},{8,11},{9,8},{10,9... | collective-permute-start | bytes 393224 | tf_op jit(solution)/shard_map/ppermute | solution.py:273
  122.5 2.5 %collective-permute-start.10 = (f32[256,128]{1,0:T(8,128)}, f32[256,128]{1,0:T(8,128)S(1)}, u32[]{:S(2)}, u32[]{:S(2)}) collective-permute-start(f32[256,128]{1,0:T(8,128)} %get-tuple-element.40), channel_id=1, source_target_pairs={{0,2},{1,3},{2,0},{3,1},{4,6},{5,7},{6,4},{7,5},{8,10},{9,11},{10,... | collective-permute-start | bytes 393224 | tf_op jit(solution)/shard_map/ppermute | solution.py:273
  125.0 2.5 %collective-permute-start.9 = (f32[256,128]{1,0:T(8,128)}, f32[256,128]{1,0:T(8,128)S(1)}, u32[]{:S(2)}, u32[]{:S(2)}) collective-permute-start(f32[256,128]{1,0:T(8,128)} %get-tuple-element.39), channel_id=1, source_target_pairs={{0,1},{1,2},{2,3},{3,0},{4,5},{5,6},{6,7},{7,4},{8,9},{9,10},{10,1... | collective-permute-start | bytes 393224 | tf_op jit(solution)/shard_map/ppermute | solution.py:273
  127.5 3.1 %collective-permute-done.10 = f32[256,128]{1,0:T(8,128)S(1)} collective-permute-done((f32[256,128]{1,0:T(8,128)}, f32[256,128]{1,0:T(8,128)S(1)}, u32[]{:S(2)}, u32[]{:S(2)}) %collective-permute-start.10) | collective-permute-done | bytes 131104 | tf_op jit(solution)/shard_map/ppermute | solution.py:273
  130.7 3.3 %collective-permute-done.9 = f32[256,128]{1,0:T(8,128)S(1)} collective-permute-done((f32[256,128]{1,0:T(8,128)}, f32[256,128]{1,0:T(8,128)S(1)}, u32[]{:S(2)}, u32[]{:S(2)}) %collective-permute-start.9) | collective-permute-done | bytes 131104 | tf_op jit(solution)/shard_map/ppermute | solution.py:273
  133.9 1.6 %add_negate_fusion = f32[256,128]{1,0:T(8,128)} fusion(f32[256,128]{1,0:T(8,128)S(1)} %collective-permute-done.11, f32[256,128]{1,0:T(8,128)S(1)} %collective-permute-done.10, f32[256,128]{1,0:T(8,128)} %get-tuple-element.38, f32[256,128]{1,0:T(8,128)S(1)} %collective-permute-done.9), kind=kLoop, calls=%fused_computation | loop fusion | flops 131072 | bytes 655360 | tf_op jit(solution)/shard_map/neg | solution.py:293
  135.5 3.4 %shard_map.81 = f32[4,256,128]{2,1,0:T(8,128)} custom-call(f32[8,256,128]{2,1,0:T(8,128)S(1)} %all-to-all-done.2.w_hbm, bf16[1024,512]{1,0:T(8,128)(2,1)} %get-tuple-element.45.hi_hbm, bf16[1024,512]{1,0:T(8,128)(2,1)} %get-tuple-element.46.lo_hbm), custom_call_target="tpu_custom_call" | custom-call | tf_op jit(solution)/shard_map/pallas_call | solution.py:246
  139.0 3.5 %all-to-all-start.3 = ((f32[4,256,128]{2,1,0:T(8,128)}), f32[4,256,128]{2,1,0:T(8,128)S(1)}, u32[]{:S(2)}, u32[]{:S(2)}) async-start(f32[4,256,128]{2,1,0:T(8,128)} %shard_map.81), calls=%async_computation.3 | async-start | bytes 1048576 | tf_op jit(solution)/shard_map/all_to_all | solution.py:264
  142.5 0.7 neg.7
  143.1 7.4 %all-to-all-done.3 = f32[4,256,128]{2,1,0:T(8,128)S(1)} async-done(((f32[4,256,128]{2,1,0:T(8,128)}), f32[4,256,128]{2,1,0:T(8,128)S(1)}, u32[]{:S(2)}, u32[]{:S(2)}) %all-to-all-start.3) | async-done | bytes 524320 | tf_op jit(solution)/shard_map/all_to_all | solution.py:264
  150.6 0.7 add.27
  (23 shorter events, 0.1 us)
Async XLA Ops:
  7.2 73.2 %all-gather.7.cloned.1.call-start = ((), (), s32[]{:S(2)}) async-start(), calls=%async_computation.5 | async-start | bytes 1179648 | tf_op jit(solution)/shard_map/all_gather | solution.py:278
  10.2 22.6 %copy-start.2 = (f32[256,128]{1,0:T(8,128)S(1)}, f32[256,128]{1,0:T(8,128)}, u32[]{:S(2)}) copy-start(f32[256,128]{1,0:T(8,128)} %get-tuple-element.30.refs_0_) | copy-start | bytes 393220
  10.2 9.0 %collective-permute-start = (f32[2,128,128]{2,1,0:T(8,128)}, f32[2,128,128]{2,1,0:T(8,128)S(1)}, u32[]{:S(2)}, u32[]{:S(2)}) collective-permute-start(f32[2,128,128]{2,1,0:T(8,128)} %get-tuple-element.25), channel_id=1, source_target_pairs={{0,0},{1,1},{2,32},{3,33},{32,2},{33,3},{34,34},{35,35},{4,4},{5,5... | collective-permute-start | bytes 393224 | tf_op jit(solution)/shard_map/ppermute | solution.py:269
  16.4 7.7 %collective-permute-start.1 = (f32[2,128,128]{2,1,0:T(8,128)}, f32[2,128,128]{2,1,0:T(8,128)S(1)}, u32[]{:S(2)}, u32[]{:S(2)}) collective-permute-start(f32[2,128,128]{2,1,0:T(8,128)} %get-tuple-element.26), channel_id=1, source_target_pairs={{0,1},{1,0},{2,33},{3,32},{32,3},{33,2},{34,35},{35,34},{4,5},{5,4... | collective-permute-start | bytes 393224 | tf_op jit(solution)/shard_map/ppermute | solution.py:269
  25.2 52.7 %all-to-all-start = ((f32[8,2,128,128]{3,2,1,0:T(8,128)}), f32[8,2,128,128]{3,2,1,0:T(8,128)S(1)}, u32[]{:S(2)}, u32[]{:S(2)}) async-start(f32[8,2,128,128]{3,2,1,0:T(8,128)} %get-tuple-element.28), calls=%async_computation | async-start | bytes 2097152 | tf_op jit(solution)/shard_map/all_to_all | solution.py:264
  32.0 81.0 %all-gather.5.cloned.1.call-start = ((), (), s32[]{:S(2)}) async-start(), calls=%async_computation.4 | async-start | bytes 2228224 | tf_op jit(solution)/shard_map/all_gather | solution.py:281
  32.8 26.1 %collective-permute-start.2 = (f32[256,128]{1,0:T(8,128)S(1)}, f32[256,128]{1,0:T(8,128)S(1)}, u32[]{:S(2)}, u32[]{:S(2)}) collective-permute-start(f32[256,128]{1,0:T(8,128)S(1)} %copy-done.2), channel_id=1, source_target_pairs={{0,4},{4,8},{8,12},{12,16},{16,20},{20,24},{24,28},{28,0},{1,5},{5... | collective-permute-start | bytes 393224 | tf_op jit(solution)/shard_map/ppermute | solution.py:273
  36.8 25.5 %collective-permute-start.3 = (f32[256,128]{1,0:T(8,128)S(1)}, f32[256,128]{1,0:T(8,128)S(1)}, u32[]{:S(2)}, u32[]{:S(2)}) collective-permute-start(f32[256,128]{1,0:T(8,128)S(1)} %copy-done.2), channel_id=1, source_target_pairs={{0,8},{4,12},{8,16},{12,20},{16,24},{20,28},{24,0},{28,4},{1,9},{5... | collective-permute-start | bytes 393224 | tf_op jit(solution)/shard_map/ppermute | solution.py:273
  42.6 25.1 %collective-permute-start.4 = (f32[256,128]{1,0:T(8,128)S(1)}, f32[256,128]{1,0:T(8,128)S(1)}, u32[]{:S(2)}, u32[]{:S(2)}) collective-permute-start(f32[256,128]{1,0:T(8,128)S(1)} %copy-done.2), channel_id=1, source_target_pairs={{0,12},{4,16},{8,20},{12,24},{16,28},{20,0},{24,4},{28,8},{1,13},{... | collective-permute-start | bytes 393224 | tf_op jit(solution)/shard_map/ppermute | solution.py:273
  49.7 19.4 %collective-permute-start.5 = (f32[256,128]{1,0:T(8,128)S(1)}, f32[256,128]{1,0:T(8,128)S(1)}, u32[]{:S(2)}, u32[]{:S(2)}) collective-permute-start(f32[256,128]{1,0:T(8,128)S(1)} %copy-done.2), channel_id=1, source_target_pairs={{0,16},{4,20},{8,24},{12,28},{16,0},{20,4},{24,8},{28,12},{1,17},{... | collective-permute-start | bytes 393224 | tf_op jit(solution)/shard_map/ppermute | solution.py:273
  52.5 19.6 %collective-permute-start.6 = (f32[256,128]{1,0:T(8,128)S(1)}, f32[256,128]{1,0:T(8,128)S(1)}, u32[]{:S(2)}, u32[]{:S(2)}) collective-permute-start(f32[256,128]{1,0:T(8,128)S(1)} %copy-done.2), channel_id=1, source_target_pairs={{0,20},{4,24},{8,28},{12,0},{16,4},{20,8},{24,12},{28,16},{1,21},{... | collective-permute-start | bytes 393224 | tf_op jit(solution)/shard_map/ppermute | solution.py:273
  58.9 24.6 %copy-start.3 = (f32[256,128]{1,0:T(8,128)}, f32[256,128]{1,0:T(8,128)S(1)}, u32[]{:S(2)}) copy-start(f32[256,128]{1,0:T(8,128)S(1)} %collective-permute-done.2.refs_1_) | copy-start | bytes 393220
  58.9 17.7 %collective-permute-start.7 = (f32[256,128]{1,0:T(8,128)S(1)}, f32[256,128]{1,0:T(8,128)S(1)}, u32[]{:S(2)}, u32[]{:S(2)}) collective-permute-start(f32[256,128]{1,0:T(8,128)S(1)} %copy-done.2), channel_id=1, source_target_pairs={{0,24},{4,28},{8,0},{12,4},{16,8},{20,12},{24,16},{28,20},{1,25},{... | collective-permute-start | bytes 393224 | tf_op jit(solution)/shard_map/ppermute | solution.py:273
  62.3 21.2 %copy-start.4 = (f32[256,128]{1,0:T(8,128)}, f32[256,128]{1,0:T(8,128)S(1)}, u32[]{:S(2)}) copy-start(f32[256,128]{1,0:T(8,128)S(1)} %collective-permute-done.3.refs_2_) | copy-start | bytes 393220
  62.3 14.4 %collective-permute-start.8 = (f32[256,128]{1,0:T(8,128)S(1)}, f32[256,128]{1,0:T(8,128)S(1)}, u32[]{:S(2)}, u32[]{:S(2)}) collective-permute-start(f32[256,128]{1,0:T(8,128)S(1)} %copy-done.2), channel_id=1, source_target_pairs={{0,28},{4,0},{8,4},{12,8},{16,12},{20,16},{24,20},{28,24},{1,29},{... | collective-permute-start | bytes 393224 | tf_op jit(solution)/shard_map/ppermute | solution.py:273
  67.7 15.8 %copy-start.5 = (f32[256,128]{1,0:T(8,128)}, f32[256,128]{1,0:T(8,128)S(1)}, u32[]{:S(2)}) copy-start(f32[256,128]{1,0:T(8,128)S(1)} %collective-permute-done.4.refs_3_) | copy-start | bytes 393220
  69.1 14.5 %copy-start.6 = (f32[256,128]{1,0:T(8,128)}, f32[256,128]{1,0:T(8,128)S(1)}, u32[]{:S(2)}) copy-start(f32[256,128]{1,0:T(8,128)S(1)} %collective-permute-done.5.refs_4_) | copy-start | bytes 393220
  72.1 11.5 %copy-start.7 = (f32[256,128]{1,0:T(8,128)}, f32[256,128]{1,0:T(8,128)S(1)}, u32[]{:S(2)}) copy-start(f32[256,128]{1,0:T(8,128)S(1)} %collective-permute-done.6.refs_5_) | copy-start | bytes 393220
  76.6 0.7 copy-start.8
  77.3 0.7 copy-start.9
  78.0 4.6 %collective-permute-start.12 = (f32[8,2,128,128]{3,2,1,0:T(8,128)S(1)}, f32[8,2,128,128]{3,2,1,0:T(8,128)S(1)}, u32[]{:S(2)}, u32[]{:S(2)}) collective-permute-start(f32[8,2,128,128]{3,2,1,0:T(8,128)S(1)} %all-to-all-done.columns_hbm), channel_id=1, source_target_pairs={{0,32},{32,0},{1,33},{33,1},{2,34},{34,2},{3,35},{35,3},{4,36},{36... | collective-permute-start | bytes 3145736 | tf_op jit(solution)/shard_map/ppermute | solution.py:273
  80.3 1.2 copy-start
  96.3 39.3 %all-to-all-start.2 = ((f32[8,256,128]{2,1,0:T(8,128)}), f32[8,256,128]{2,1,0:T(8,128)S(1)}, u32[]{:S(2)}, u32[]{:S(2)}) async-start(f32[8,256,128]{2,1,0:T(8,128)} %broadcast_in_dim.2), calls=%async_computation.2 | async-start | bytes 2097152 | tf_op jit(solution)/shard_map/all_to_all | solution.py:264
  118.2 9.3 %collective-permute-start.11 = (f32[256,128]{1,0:T(8,128)}, f32[256,128]{1,0:T(8,128)S(1)}, u32[]{:S(2)}, u32[]{:S(2)}) collective-permute-start(f32[256,128]{1,0:T(8,128)} %get-tuple-element.41), channel_id=1, source_target_pairs={{0,3},{1,0},{2,1},{3,2},{4,7},{5,4},{6,5},{7,6},{8,11},{9,8},{10,9... | collective-permute-start | bytes 393224 | tf_op jit(solution)/shard_map/ppermute | solution.py:273
  122.5 8.1 %collective-permute-start.10 = (f32[256,128]{1,0:T(8,128)}, f32[256,128]{1,0:T(8,128)S(1)}, u32[]{:S(2)}, u32[]{:S(2)}) collective-permute-start(f32[256,128]{1,0:T(8,128)} %get-tuple-element.40), channel_id=1, source_target_pairs={{0,2},{1,3},{2,0},{3,1},{4,6},{5,7},{6,4},{7,5},{8,10},{9,11},{10,... | collective-permute-start | bytes 393224 | tf_op jit(solution)/shard_map/ppermute | solution.py:273
  125.0 8.9 %collective-permute-start.9 = (f32[256,128]{1,0:T(8,128)}, f32[256,128]{1,0:T(8,128)S(1)}, u32[]{:S(2)}, u32[]{:S(2)}) collective-permute-start(f32[256,128]{1,0:T(8,128)} %get-tuple-element.39), channel_id=1, source_target_pairs={{0,1},{1,2},{2,3},{3,0},{4,5},{5,6},{6,7},{7,4},{8,9},{9,10},{10,1... | collective-permute-start | bytes 393224 | tf_op jit(solution)/shard_map/ppermute | solution.py:273
  135.5 15.1 %copy-start.1 = (f32[256,128]{1,0:T(8,128)S(1)}, f32[256,128]{1,0:T(8,128)}, u32[]{:S(2)}) copy-start(f32[256,128]{1,0:T(8,128)} %param.9) | copy-start | bytes 393220
  139.0 11.6 %all-to-all-start.3 = ((f32[4,256,128]{2,1,0:T(8,128)}), f32[4,256,128]{2,1,0:T(8,128)S(1)}, u32[]{:S(2)}, u32[]{:S(2)}) async-start(f32[4,256,128]{2,1,0:T(8,128)} %shard_map.81), calls=%async_computation.3 | async-start | bytes 1048576 | tf_op jit(solution)/shard_map/all_to_all | solution.py:264
Sparse Core Ops, SparseCore 0:
  10.1 46.8 all-gather.6
  59.6 53.3 all-gather.4

commit v4 on v3

--- a/solution.py
+++ b/solution.py
@@ -13,7 +13,7 @@
 HBM = pl.BlockSpec(memory_space=pltpu.HBM)
 PARAMS = pltpu.CompilerParams(vmem_limit_bytes=32 * 1024 * 1024)
 WIDE = pltpu.CompilerParams(vmem_limit_bytes=62 * 1024 * 1024)
-MIDDLE = pltpu.CompilerParams(vmem_limit_bytes=52 * 1024 * 1024)
+MIDDLE = pltpu.CompilerParams(vmem_limit_bytes=51 * 1024 * 1024)
 DMA = pltpu.SemaphoreType.DMA
 
 
@@ -40,12 +40,13 @@
 
 
 def pick_kernel(
-    at_ref, map_hbm, root_hbm, lower_hbm, sigma_ref, first_ref, second_ref, picks, root, lower, sems
+    at_ref, map_hbm, root_hbm, lower_hbm, upper_hbm, su_ref, first_ref, second_ref, picks, root, lower, sems
 ):
     loads = [
         pltpu.make_async_copy(map_hbm, picks, sems.at[0]),
         pltpu.make_async_copy(root_hbm, root, sems.at[1]),
         pltpu.make_async_copy(lower_hbm, lower, sems.at[2]),
+        pltpu.make_async_copy(upper_hbm, su_ref.at[256:512], sems.at[3]),
     ]
     for load in loads:
         load.start()
@@ -79,30 +80,31 @@
     value = dot(jnp.concatenate(stack, axis=0), col_hot)
     for part in range(2):
         v = [value[128 * (3 * part + i) : 128 * (3 * part + i + 1), :] for i in range(3)]
-        sigma_ref[128 * part : 128 * (part + 1), :] = (v[0] + v[1]) + v[2]
-    loads[2].wait()
+        su_ref[128 * part : 128 * (part + 1), :] = (v[0] + v[1]) + v[2]
+    for load in loads[2:]:
+        load.wait()
     near = pl.multiple_of(128 * odd, 128)
     far = pl.multiple_of(128 - 128 * odd, 128)
-    first_ref[0] = sigma_ref[pl.ds(near, 128), :]
+    first_ref[0] = su_ref[pl.ds(near, 128), :]
     first_ref[1] = lower[pl.ds(near, 128), :]
-    second_ref[0] = sigma_ref[pl.ds(far, 128), :]
+    second_ref[0] = su_ref[pl.ds(far, 128), :]
     second_ref[1] = lower[pl.ds(far, 128), :]
 
 
-def pick(at, blocks, root, lower):
+def pick(at, blocks, root, lower, upper):
     return pl.pallas_call(
         pick_kernel,
-        out_shape=(shape(256, 128), shape(2, 128, 128), shape(2, 128, 128)),
-        in_specs=[SMEM] + [HBM] * 3,
+        out_shape=(shape(512, 128), shape(2, 128, 128), shape(2, 128, 128)),
+        in_specs=[SMEM] + [HBM] * 4,
         out_specs=(VMEM, VMEM, VMEM),
         scratch_shapes=[
             pltpu.VMEM((32, 128), jnp.int32),
             pltpu.VMEM((512, 256), F32),
             pltpu.VMEM((256, 128), F32),
-            DMA((3,)),
+            DMA((4,)),
         ],
         compiler_params=WIDE,
-    )(at, blocks, root, lower)
+    )(at, blocks, root, lower, upper)
 
 
 def fan_kernel(first_ref, second_ref, copies_ref, lower_ref):
@@ -130,7 +132,7 @@
         )
         loads = [
             pltpu.make_async_copy(columns_hbm, right, sems.at[0]),
-            pltpu.make_async_copy(upper_hbm, left, sems.at[1]),
+            pltpu.make_async_copy(upper_hbm.at[:, 256:512], left, sems.at[1]),
         ]
         for load in loads:
             load.start()
@@ -176,56 +178,59 @@
     )(at, upper, columns, *more)
 
 
-def side_kernel(at_ref, lower_hbm, *refs):
-    blocks, sums, (bh, bl, lower, ah, al, out, sem) = refs[:8], refs[8:12], refs[12:]
-    load = pltpu.make_async_copy(lower_hbm, lower, sem)
-    load.start()
-    _, _, _, z, x = device(at_ref)
+def side_kernel(at_ref, su_hbm, lower_hbm, out_ref, bh, bl, sigma, lower, ah, al, sems):
+    loads = [
+        pltpu.make_async_copy(su_hbm.at[:, 0:256], sigma, sems.at[0]),
+        pltpu.make_async_copy(lower_hbm, lower, sems.at[1]),
+    ]
+    for load in loads:
+        load.start()
+    _, _, _, _, x = device(at_ref)
     odd = x & 1
-    for k, ref in enumerate(blocks):
-        cols = pl.ds(pl.multiple_of(128 * ((z - k) & 7), 128), 128)
-        ah[:, cols], al[:, cols] = split2(ref[...])
-    load.wait()
-    for i in range(8):
-        rows = slice(128 * i, 128 * (i + 1))
+    loads[0].wait()
+    for z in range(8):
+        rows = slice(128 * z, 128 * (z + 1))
+        ah[:, rows], al[:, rows] = split2(sigma[z])
+    loads[1].wait()
+    for z in range(8):
+        rows = slice(128 * z, 128 * (z + 1))
         for core in range(2):
             for t in range(2):
                 cols = slice(256 * core + 128 * t, 256 * core + 128 * (t + 1))
                 place = 128 * (odd if t == 0 else 1 - odd)
-                value = lower[2 * i + core, pl.ds(pl.multiple_of(place, 128), 128), :]
+                value = lower[2 * z + core, pl.ds(pl.multiple_of(place, 128), 128), :]
                 bh[rows, cols], bl[rows, cols] = split2(value)
     for n in range(2):
         cols = slice(256 * n, 256 * (n + 1))
         part = three_pass(ah[...], al[...], bh[:, cols], bl[:, cols])
-        out[2 * n] = part[:, :128]
-        out[2 * n + 1] = part[:, 128:]
-    for k, ref in enumerate(sums):
-        ref[...] = out[(x + k) & 3]
-
-
-def side(at, lower, blocks):
+        out_ref[2 * n] = part[:, :128]
+        out_ref[2 * n + 1] = part[:, 128:]
+
+
+def side(at, gathered, lower):
     return pl.pallas_call(
         side_kernel,
-        out_shape=(shape(256, 128),) * 4 + (shape(1024, 512, dtype=BF16),) * 2,
-        in_specs=[SMEM, HBM] + [VMEM] * 8,
-        out_specs=(VMEM,) * 6,
+        out_shape=(shape(4, 256, 128),) + (shape(1024, 512, dtype=BF16),) * 2,
+        in_specs=[SMEM, HBM, HBM],
+        out_specs=(VMEM,) * 3,
         scratch_shapes=[
+            pltpu.VMEM((8, 256, 128), F32),
             pltpu.VMEM((16, 256, 128), F32),
             pltpu.VMEM((256, 1024), BF16),
             pltpu.VMEM((256, 1024), BF16),
-            pltpu.VMEM((4, 256, 128), F32),
-            DMA,
+            DMA((2,)),
         ],
         compiler_params=WIDE,
         cost_estimate=pl.CostEstimate(flops=6 << 28, bytes_accessed=6 << 20, transcendentals=0),
-    )(at, lower, *blocks)
-
-
-def last_kernel(w_hbm, hi_hbm, lo_hbm, out_ref, w, ah, al, bh, bl, sems):
+    )(at, gathered, lower)
+
+
+def last_kernel(w_hbm, hi_hbm, lo_hbm, side_hbm, out_ref, w, ah, al, bh, bl, sems):
     loads = [
         pltpu.make_async_copy(w_hbm, w, sems.at[0]),
         pltpu.make_async_copy(hi_hbm, bh, sems.at[1]),
         pltpu.make_async_copy(lo_hbm, bl, sems.at[2]),
+        pltpu.make_async_copy(side_hbm, out_ref.at[:, 0], sems.at[3]),
     ]
     for load in loads:
         load.start()
@@ -233,20 +238,21 @@
     for z in range(8):
         rows = slice(128 * z, 128 * (z + 1))
         ah[:, rows], al[:, rows] = split2(w[z])
-    for load in loads[1:]:
+    for load in loads[1:3]:
         load.wait()
     for n in range(2):
         cols = slice(256 * n, 256 * (n + 1))
         part = three_pass(ah[...], al[...], bh[:, cols], bl[:, cols])
-        out_ref[2 * n] = part[:, :128]
-        out_ref[2 * n + 1] = part[:, 128:]
-
-
-def last(w, hi, lo):
+        out_ref[2 * n, 1] = part[:, :128]
+        out_ref[2 * n + 1, 1] = part[:, 128:]
+    loads[3].wait()
+
+
+def last(w, hi, lo, sides):
     return pl.pallas_call(
         last_kernel,
-        out_shape=shape(4, 256, 128),
-        in_specs=[HBM] * 3,
+        out_shape=shape(4, 2, 256, 128),
+        in_specs=[HBM] * 4,
         out_specs=VMEM,
         scratch_shapes=[
             pltpu.VMEM((8, 256, 128), F32),
@@ -254,10 +260,10 @@
             pltpu.VMEM((256, 1024), BF16),
             pltpu.VMEM((1024, 512), BF16),
             pltpu.VMEM((1024, 512), BF16),
-            DMA((3,)),
+            DMA((4,)),
         ],
         compiler_params=MIDDLE,
-    )(w, hi, lo)
+    )(w, hi, lo, sides)
 
 
 def exchange(v, axis):
@@ -275,24 +281,20 @@
 
 def shards(root_inverse, boundary_map, lower_factor, upper_factor, diagonal_inverse):
     at = lax.axis_index(("y", "c", "z", "x")).astype(jnp.int32).reshape(1)
-    upper = lax.all_gather(upper_factor, "z", axis=0, tiled=False)
-    sigma, first, second = pick(at, boundary_map.reshape(32, 128), root_inverse, lower_factor)
+    su, first, second = pick(
+        at, boundary_map.reshape(32, 128), root_inverse, lower_factor, upper_factor
+    )
+    gathered = lax.all_gather(su, "z", axis=0, tiled=False)
     copies, lower = fan(deal(first, 0), deal(second, 1))
     lower = lax.all_gather(lower, ("y", "c"), axis=0, tiled=False)
     own = exchange(copies, "y")
-    blocks = [sigma] + [turn(sigma, "z", 8, k) for k in range(1, 8)]
-    own, blocks = lax.optimization_barrier((own, blocks))
     other = turn(own, "c", 2, 1)
-    part = couple(at, upper, other, couple(at, upper, own))
+    part = couple(at, gathered, other, couple(at, gathered, own))
     w = exchange(part, "x").sum(axis=0)
     w_all = exchange(jnp.broadcast_to(w[None], (8, 256, 128)), "z")
-    *sums, hi, lo = side(at, lower, blocks)
-    total = sums[0]
-    for k in range(1, 4):
-        total = total + turn(sums[k], "x", 4, k)
-    total, w_all = lax.optimization_barrier((-total, w_all))
-    product = exchange(last(w_all, hi, lo), "x").sum(axis=0)
-    return (total, -w, diagonal_inverse + product)
+    sides, hi, lo = side(at, gathered, lower)
+    both = exchange(last(w_all, hi, lo, sides), "x").sum(axis=0)
+    return (-both[0], -w, diagonal_inverse + both[1])
 
 
 def solution(mesh):

time: 159 us -> 148 us (0.931)
  starting transfers between devices: 67.3 us -> 31.2 us
  waiting for transfers between devices: 44.5 us -> 72.7 us
    all_to_all x3, waiting for transfers between devices: 7.45 us -> 50.5 us  [exchange(): return lax.all_to_all(v, axis, 0, 0, tiled=True)]
    ppermute x11 -> x1, starting transfers between devices: 43.2 us -> 2.29 us  [turn(): return lax.ppermute(v, axis, [(i, (i + k) % size) for i in range(size)])]
    ppermute x11 -> x1, waiting for transfers between devices: 18.7 us -> 0.01 us  [turn(): return lax.ppermute(v, axis, [(i, (i + k) % size) for i in range(size)])]
    all_to_all x3, starting transfers between devices: 15.4 us -> 20.3 us  [exchange(): return lax.all_to_all(v, axis, 0, 0, tiled=True)]
    all_gather x1, waiting for transfers between devices: 11.7 us -> 16.2 us  [shards(): lower = lax.all_gather(lower, ('y', 'c'), axis=0, tiled=False)]
  transfers between devices with their start and end apart: 18 -> 8, of which waited for: 12 -> 6; matrix products, arithmetic and copies ran while one was open for 2% -> 1% of each run, Pallas kernels for 7% -> 5%
where the time goes in v4:
time: 148 us
  waiting for transfers between devices  72.7 us (49%)
  starting transfers between devices  31.2 us (21%)
  between operations  14.2 us (10%)
  Pallas kernels  12.7 us (9%)
  blocking collectives  11 us (7%)
  local copies, waits for them, and re-layouts  3.7 us (2%)
  other arithmetic  2.1 us (1%)
    all_to_all x3, waiting for transfers between devices, exchange(): return lax.all_to_all(v, axis, 0, 0, tiled=True)  50.5 us
    all_to_all x3, starting transfers between devices, exchange(): return lax.all_to_all(v, axis, 0, 0, tiled=True)  20.3 us
    all_gather x1, waiting for transfers between devices, shards(): lower = lax.all_gather(lower, ('y', 'c'), axis=0, tiled=False)  16.2 us
    all_to_all x1, blocking collectives, exchange(): return lax.all_to_all(v, axis, 0, 0, tiled=True)  11 us
    ppermute x2, starting transfers between devices, deal(): return lax.ppermute(v, ('c', 'x'), moves)  8.53 us
    ppermute x2, waiting for transfers between devices, deal(): return lax.ppermute(v, ('c', 'x'), moves)  5.21 us
    pallas_call x1, Pallas kernels, side(): pl.pallas_call(side_kernel, out_shape=(shape(4, 256, 128),) + (shape(1024...  3.76 us
    pallas_call x1, Pallas kernels, last(): pl.pallas_call(last_kernel, out_shape=shape(4, 2, 256, 128), in_specs=[HB...  3.6 us
  transfers between devices with their start and end apart: 8, of which 6 were waited for; matrix products, arithmetic and copies ran while one was open for 1% of the time, Pallas kernels for 5%

profile of v4, /device:TPU:1, one launch (start us, length us, event | category | flops | bytes accessed | tf_op | source)
XLA Modules:
  0.0 147.6 jit_solution(7238160992138525228)
XLA Ops:
  7.2 0.0 all-gather.5.cloned.1.call-start
  7.2 2.4 %shard_map.76 = (f32[512,128]{1,0:T(8,128)}, f32[2,128,128]{2,1,0:T(8,128)}, f32[2,128,128]{2,1,0:T(8,128)}) custom-call(s32[1]{0:T(128)} %bitcast.at_ref, s32[32,128]{1,0:T(8,128)} %bitcast.13, f32[512,256]{1,0:T(8,128)} %root_hbm.1, f32[256,128]{1,0:T(8,128)} %lower_hbm.1, f32[256,128]{1,0:T(8,128)} %upper_hbm.1), custom_call_target="tpu_custom_call" | custom-call | tf_op jit(solution)/shard_map/pallas_call | solution.py:95
  9.6 0.0 all-gather.5.cloned.1.call-update
  9.6 6.0 %collective-permute-start = (f32[2,128,128]{2,1,0:T(8,128)}, f32[2,128,128]{2,1,0:T(8,128)S(1)}, u32[]{:S(2)}, u32[]{:S(2)}) collective-permute-start(f32[2,128,128]{2,1,0:T(8,128)} %get-tuple-element.12), channel_id=1, source_target_pairs={{0,0},{1,1},{2,32},{3,33},{32,2},{33,3},{34,34},{35,35},{4,4},{5,5... | collective-permute-start | bytes 393224 | tf_op jit(solution)/shard_map/ppermute | solution.py:275
  15.7 2.5 %collective-permute-start.1 = (f32[2,128,128]{2,1,0:T(8,128)}, f32[2,128,128]{2,1,0:T(8,128)S(1)}, u32[]{:S(2)}, u32[]{:S(2)}) collective-permute-start(f32[2,128,128]{2,1,0:T(8,128)} %get-tuple-element.13), channel_id=1, source_target_pairs={{0,1},{1,0},{2,33},{3,32},{32,3},{33,2},{34,35},{35,34},{4,5},{5,4... | collective-permute-start | bytes 393224 | tf_op jit(solution)/shard_map/ppermute | solution.py:275
  18.1 0.4 collective-permute-done.first_ref
  18.5 4.9 %collective-permute-done.1.second_ref = f32[2,128,128]{2,1,0:T(8,128)S(1)} collective-permute-done((f32[2,128,128]{2,1,0:T(8,128)}, f32[2,128,128]{2,1,0:T(8,128)S(1)}, u32[]{:S(2)}, u32[]{:S(2)}) %collective-permute-start.1) | collective-permute-done | bytes 131104 | tf_op jit(solution)/shard_map/ppermute | solution.py:275
  23.4 1.1 shard_map.77
  24.5 6.8 %all-to-all-start = ((f32[8,2,128,128]{3,2,1,0:T(8,128)}), f32[8,2,128,128]{3,2,1,0:T(8,128)S(1)}, u32[]{:S(2)}, u32[]{:S(2)}) async-start(f32[8,2,128,128]{3,2,1,0:T(8,128)} %get-tuple-element.14), calls=%async_computation | async-start | bytes 2097152 | tf_op jit(solution)/shard_map/all_to_all | solution.py:270
  31.3 0.0 all-gather.7.cloned.1.call-start
  31.3 0.7 all-gather.7.cloned.1.call-update
  32.0 27.3 %all-to-all-done.columns_hbm = f32[8,2,128,128]{3,2,1,0:T(8,128)S(1)} async-done(((f32[8,2,128,128]{3,2,1,0:T(8,128)}), f32[8,2,128,128]{3,2,1,0:T(8,128)S(1)}, u32[]{:S(2)}, u32[]{:S(2)}) %all-to-all-start) | async-done | bytes 1048608 | tf_op jit(solution)/shard_map/all_to_all | solution.py:270
  59.3 2.3 %collective-permute-start.2 = (f32[8,2,128,128]{3,2,1,0:T(8,128)S(1)}, f32[8,2,128,128]{3,2,1,0:T(8,128)S(1)}, u32[]{:S(2)}, u32[]{:S(2)}) collective-permute-start(f32[8,2,128,128]{3,2,1,0:T(8,128)S(1)} %all-to-all-done.columns_hbm), channel_id=1, source_target_pairs={{0,32},{32,0},{1,33},{33,1},{2,34},{34,2},{3,35},{35,3},{4,36},{36... | collective-permute-start | bytes 3145736 | tf_op jit(solution)/shard_map/ppermute | solution.py:279
  61.6 0.0 all-gather.5.cloned.1.call-done
  61.7 0.0 copy-start
  61.7 1.6 %copy-done = f32[4096,128]{1,0:T(8,128)S(1)} copy-done((f32[4096,128]{1,0:T(8,128)S(1)}, f32[4096,128]{1,0:T(8,128)}, u32[]{:S(2)}) %copy-start) | copy-done | bytes 2097176
  63.2 0.9 shard_map.78.refs_0_
  64.2 0.0 collective-permute-done.2.columns_hbm
  64.2 0.9 shard_map.79
  65.1 11.0 %all_to_all.20 = f32[4,256,128]{2,1,0:T(8,128)S(1)} all-to-all(f32[4,256,128]{2,1,0:T(8,128)S(1)} %shard_map.79), channel_id=1, replica_groups=mesh['y'=8,'c'=2,'z'=8,'x'=4] {'x'}, dimensions={0} | all-to-all | bytes 1048576 | tf_op jit(solution)/shard_map/all_to_all | solution.py:270
  76.2 1.1 broadcast_in_dim.2
  77.3 9.9 %all-to-all-start.2 = ((f32[8,256,128]{2,1,0:T(8,128)}), f32[8,256,128]{2,1,0:T(8,128)S(1)}, u32[]{:S(2)}, u32[]{:S(2)}) async-start(f32[8,256,128]{2,1,0:T(8,128)} %broadcast_in_dim.2), calls=%async_computation.2 | async-start | bytes 2097152 | tf_op jit(solution)/shard_map/all_to_all | solution.py:270
  87.1 16.2 %all-gather.7.cloned.1.call-done = f32[4096,128]{1,0:T(8,128)} async-done(((f32[256,128]{1,0:T(8,128)}), f32[4096,128]{1,0:T(8,128)}) %all-gather.7.cloned.1.call-update) | async-done | bytes 2097168 | tf_op jit(solution)/shard_map/all_gather | solution.py:289
  103.4 3.8 %shard_map.80 = (f32[4,256,128]{2,1,0:T(8,128)}, bf16[1024,512]{1,0:T(8,128)(2,1)}, bf16[1024,512]{1,0:T(8,128)(2,1)}) custom-call(s32[1]{0:T(128)} %bitcast.at_ref, f32[8,512,128]{2,1,0:T(8,128)} %bitcast.10, f32[16,256,128]{2,1,0:T(8,128)} %bitcast.14), custom_call_target="tpu_custom_call" | custom-call | flops 1610612736 | bytes 6291456 | tf_op jit(solution)/shard_map/pallas_call | solution.py:211
  107.1 9.2 %all-to-all-done.2.w_hbm = f32[8,256,128]{2,1,0:T(8,128)S(1)} async-done(((f32[8,256,128]{2,1,0:T(8,128)}), f32[8,256,128]{2,1,0:T(8,128)S(1)}, u32[]{:S(2)}, u32[]{:S(2)}) %all-to-all-start.2) | async-done | bytes 1048608 | tf_op jit(solution)/shard_map/all_to_all | solution.py:270
  116.3 0.0 copy-start.1
  116.3 1.0 copy-done.1
  117.4 3.6 %shard_map.81 = f32[4,2,256,128]{3,2,1,0:T(8,128)} custom-call(f32[8,256,128]{2,1,0:T(8,128)S(1)} %all-to-all-done.2.w_hbm, bf16[1024,512]{1,0:T(8,128)(2,1)} %get-tuple-element.16.hi_hbm, bf16[1024,512]{1,0:T(8,128)(2,1)} %get-tuple-element.17.lo_hbm, f32[4,256,128]{2,1,0:T(8,128)S(1)} %copy-done.1), custom_call_target="tpu_custom_call" | custom-call | tf_op jit(solution)/shard_map/pallas_call | solution.py:252
  121.0 0.0 copy-start.2
  121.0 3.7 %all-to-all-start.3 = ((f32[4,2,256,128]{3,2,1,0:T(8,128)}), f32[4,2,256,128]{3,2,1,0:T(8,128)S(1)}, u32[]{:S(2)}, u32[]{:S(2)}) async-start(f32[4,2,256,128]{3,2,1,0:T(8,128)} %shard_map.81), calls=%async_computation.3 | async-start | bytes 2097152 | tf_op jit(solution)/shard_map/all_to_all | solution.py:270
  124.6 0.7 neg.11
  125.3 14.0 %all-to-all-done.3 = f32[4,2,256,128]{3,2,1,0:T(8,128)S(1)} async-done(((f32[4,2,256,128]{3,2,1,0:T(8,128)}), f32[4,2,256,128]{3,2,1,0:T(8,128)S(1)}, u32[]{:S(2)}, u32[]{:S(2)}) %all-to-all-start.3) | async-done | bytes 1048608 | tf_op jit(solution)/shard_map/all_to_all | solution.py:270
  139.3 0.1 reduce_sum.19
  139.4 0.7 fusion.1
  140.1 0.0 copy-done.2
  140.1 0.7 fusion
  (1 shorter events, 0.0 us)
Async XLA Ops:
  7.2 54.5 %all-gather.5.cloned.1.call-start = ((), (), s32[]{:S(2)}) async-start(), calls=%async_computation.4 | async-start | bytes 2359296 | tf_op jit(solution)/shard_map/all_gather | solution.py:287
  9.6 8.9 %collective-permute-start = (f32[2,128,128]{2,1,0:T(8,128)}, f32[2,128,128]{2,1,0:T(8,128)S(1)}, u32[]{:S(2)}, u32[]{:S(2)}) collective-permute-start(f32[2,128,128]{2,1,0:T(8,128)} %get-tuple-element.12), channel_id=1, source_target_pairs={{0,0},{1,1},{2,32},{3,33},{32,2},{33,3},{34,34},{35,35},{4,4},{5,5... | collective-permute-start | bytes 393224 | tf_op jit(solution)/shard_map/ppermute | solution.py:275
  15.7 7.7 %collective-permute-start.1 = (f32[2,128,128]{2,1,0:T(8,128)}, f32[2,128,128]{2,1,0:T(8,128)S(1)}, u32[]{:S(2)}, u32[]{:S(2)}) collective-permute-start(f32[2,128,128]{2,1,0:T(8,128)} %get-tuple-element.13), channel_id=1, source_target_pairs={{0,1},{1,0},{2,33},{3,32},{32,3},{33,2},{34,35},{35,34},{4,5},{5,4... | collective-permute-start | bytes 393224 | tf_op jit(solution)/shard_map/ppermute | solution.py:275
  24.5 34.9 %all-to-all-start = ((f32[8,2,128,128]{3,2,1,0:T(8,128)}), f32[8,2,128,128]{3,2,1,0:T(8,128)S(1)}, u32[]{:S(2)}, u32[]{:S(2)}) async-start(f32[8,2,128,128]{3,2,1,0:T(8,128)} %get-tuple-element.14), calls=%async_computation | async-start | bytes 2097152 | tf_op jit(solution)/shard_map/all_to_all | solution.py:270
  31.3 72.1 %all-gather.7.cloned.1.call-start = ((), (), s32[]{:S(2)}) async-start(), calls=%async_computation.5 | async-start | bytes 2228224 | tf_op jit(solution)/shard_map/all_gather | solution.py:289
  59.3 4.9 %collective-permute-start.2 = (f32[8,2,128,128]{3,2,1,0:T(8,128)S(1)}, f32[8,2,128,128]{3,2,1,0:T(8,128)S(1)}, u32[]{:S(2)}, u32[]{:S(2)}) collective-permute-start(f32[8,2,128,128]{3,2,1,0:T(8,128)S(1)} %all-to-all-done.columns_hbm), channel_id=1, source_target_pairs={{0,32},{32,0},{1,33},{33,1},{2,34},{34,2},{3,35},{35,3},{4,36},{36... | collective-permute-start | bytes 3145736 | tf_op jit(solution)/shard_map/ppermute | solution.py:279
  61.7 1.6 %copy-start = (f32[4096,128]{1,0:T(8,128)S(1)}, f32[4096,128]{1,0:T(8,128)}, u32[]{:S(2)}) copy-start(f32[4096,128]{1,0:T(8,128)} %all-gather.5.cloned.1.call-done) | copy-start | bytes 6291460
  77.3 39.0 %all-to-all-start.2 = ((f32[8,256,128]{2,1,0:T(8,128)}), f32[8,256,128]{2,1,0:T(8,128)S(1)}, u32[]{:S(2)}, u32[]{:S(2)}) async-start(f32[8,256,128]{2,1,0:T(8,128)} %broadcast_in_dim.2), calls=%async_computation.2 | async-start | bytes 2097152 | tf_op jit(solution)/shard_map/all_to_all | solution.py:270
  116.3 1.0 copy-start.1
  121.0 19.1 %copy-start.2 = (f32[256,128]{1,0:T(8,128)S(1)}, f32[256,128]{1,0:T(8,128)}, u32[]{:S(2)}) copy-start(f32[256,128]{1,0:T(8,128)} %param.9) | copy-start | bytes 393220
  121.0 18.3 %all-to-all-start.3 = ((f32[4,2,256,128]{3,2,1,0:T(8,128)}), f32[4,2,256,128]{3,2,1,0:T(8,128)S(1)}, u32[]{:S(2)}, u32[]{:S(2)}) async-start(f32[4,2,256,128]{3,2,1,0:T(8,128)} %shard_map.81), calls=%async_computation.3 | async-start | bytes 2097152 | tf_op jit(solution)/shard_map/all_to_all | solution.py:270
Sparse Core Ops, SparseCore 0:
  10.1 46.0 all-gather.4
  58.9 44.4 all-gather.6

commit v5 on v4

--- a/solution.py
+++ b/solution.py
@@ -13,7 +13,7 @@
 HBM = pl.BlockSpec(memory_space=pltpu.HBM)
 PARAMS = pltpu.CompilerParams(vmem_limit_bytes=32 * 1024 * 1024)
 WIDE = pltpu.CompilerParams(vmem_limit_bytes=62 * 1024 * 1024)
-MIDDLE = pltpu.CompilerParams(vmem_limit_bytes=51 * 1024 * 1024)
+MIDDLE = pltpu.CompilerParams(vmem_limit_bytes=52 * 1024 * 1024)
 DMA = pltpu.SemaphoreType.DMA
 
 
@@ -225,12 +225,11 @@
     )(at, gathered, lower)
 
 
-def last_kernel(w_hbm, hi_hbm, lo_hbm, side_hbm, out_ref, w, ah, al, bh, bl, sems):
+def last_kernel(w_hbm, hi_hbm, lo_hbm, out_ref, w, ah, al, bh, bl, sems):
     loads = [
         pltpu.make_async_copy(w_hbm, w, sems.at[0]),
         pltpu.make_async_copy(hi_hbm, bh, sems.at[1]),
         pltpu.make_async_copy(lo_hbm, bl, sems.at[2]),
-        pltpu.make_async_copy(side_hbm, out_ref.at[:, 0], sems.at[3]),
     ]
     for load in loads:
         load.start()
@@ -238,21 +237,20 @@
     for z in range(8):
         rows = slice(128 * z, 128 * (z + 1))
         ah[:, rows], al[:, rows] = split2(w[z])
-    for load in loads[1:3]:
+    for load in loads[1:]:
         load.wait()
     for n in range(2):
         cols = slice(256 * n, 256 * (n + 1))
         part = three_pass(ah[...], al[...], bh[:, cols], bl[:, cols])
-        out_ref[2 * n, 1] = part[:, :128]
-        out_ref[2 * n + 1, 1] = part[:, 128:]
-    loads[3].wait()
-
-
-def last(w, hi, lo, sides):
+        out_ref[2 * n] = part[:, :128]
+        out_ref[2 * n + 1] = part[:, 128:]
+
+
+def last(w, hi, lo):
     return pl.pallas_call(
         last_kernel,
-        out_shape=shape(4, 2, 256, 128),
-        in_specs=[HBM] * 4,
+        out_shape=shape(4, 256, 128),
+        in_specs=[HBM] * 3,
         out_specs=VMEM,
         scratch_shapes=[
             pltpu.VMEM((8, 256, 128), F32),
@@ -260,10 +258,10 @@
             pltpu.VMEM((256, 1024), BF16),
             pltpu.VMEM((1024, 512), BF16),
             pltpu.VMEM((1024, 512), BF16),
-            DMA((4,)),
+            DMA((3,)),
         ],
         compiler_params=MIDDLE,
-    )(w, hi, lo, sides)
+    )(w, hi, lo)
 
 
 def exchange(v, axis):
@@ -293,8 +291,9 @@
     w = exchange(part, "x").sum(axis=0)
     w_all = exchange(jnp.broadcast_to(w[None], (8, 256, 128)), "z")
     sides, hi, lo = side(at, gathered, lower)
-    both = exchange(last(w_all, hi, lo, sides), "x").sum(axis=0)
-    return (-both[0], -w, diagonal_inverse + both[1])
+    t = lax.psum_scatter(sides, "x", scatter_dimension=0, tiled=False)
+    product = exchange(last(w_all, hi, lo), "x").sum(axis=0)
+    return (-t, -w, diagonal_inverse + product)
 
 
 def solution(mesh):

time: 148 us -> 144 us (0.973); the launches traced: 148 us -> 142 us
  waiting for transfers between devices: 72.7 us -> 67.8 us
    all_to_all x3, waiting for transfers between devices: 50.5 us -> 37.2 us  [exchange(): return lax.all_to_all(v, axis, 0, 0, tiled=True)]
    reduce_scatter x0 -> x1, waiting for transfers between devices: none -> 8.49 us  [shards(): t = lax.psum_scatter(sides, 'x', scatter_dimension=0, tiled=False)]
  transfers between devices with their start and end apart: 8 -> 9, of which waited for: 6 -> 7; matrix products, arithmetic and copies ran while one was open for 1% -> 2% of each run, Pallas kernels for 5% -> 7%
where the time goes in v5:
time: 144 us; the launch traced here: 142 us
  waiting for transfers between devices  67.8 us (47%)
  starting transfers between devices  31.1 us (22%)
  between operations  13.9 us (10%)
  Pallas kernels  12.5 us (9%)
  blocking collectives  11 us (8%)
  other arithmetic  2.96 us (2%)
  local copies, waits for them, and re-layouts  2.66 us (2%)
    all_to_all x3, waiting for transfers between devices, exchange(): return lax.all_to_all(v, axis, 0, 0, tiled=True)  37.2 us
    all_to_all x3, starting transfers between devices, exchange(): return lax.all_to_all(v, axis, 0, 0, tiled=True)  20.2 us
    all_gather x1, waiting for transfers between devices, shards(): lower = lax.all_gather(lower, ('y', 'c'), axis=0, tiled=False)  16.2 us
    all_to_all x1, blocking collectives, exchange(): return lax.all_to_all(v, axis, 0, 0, tiled=True)  11 us
    ppermute x2, starting transfers between devices, deal(): return lax.ppermute(v, ('c', 'x'), moves)  8.53 us
    reduce_scatter x1, waiting for transfers between devices, shards(): t = lax.psum_scatter(sides, 'x', scatter_dimension=0, tiled=False)  8.49 us
    ppermute x2, waiting for transfers between devices, deal(): return lax.ppermute(v, ('c', 'x'), moves)  5.21 us
    pallas_call x1, Pallas kernels, side(): pl.pallas_call(side_kernel, out_shape=(shape(4, 256, 128),) + (shape(1024...  3.77 us
  transfers between devices with their start and end apart: 9, of which 7 were waited for; matrix products, arithmetic and copies ran while one was open for 2% of the time, Pallas kernels for 7%

profile of v5, /device:TPU:1, one launch (start us, length us, event | category | flops | bytes accessed | tf_op | source)
XLA Modules:
  0.0 141.9 jit_solution(1725304349181752732)
XLA Ops:
  7.2 0.0 all-gather.5.cloned.1.call-start
  7.2 2.4 %shard_map.76 = (f32[512,128]{1,0:T(8,128)}, f32[2,128,128]{2,1,0:T(8,128)}, f32[2,128,128]{2,1,0:T(8,128)}) custom-call(s32[1]{0:T(128)} %bitcast.at_ref, s32[32,128]{1,0:T(8,128)} %bitcast.9, f32[512,256]{1,0:T(8,128)} %root_hbm.1, f32[256,128]{1,0:T(8,128)} %lower_hbm.1, f32[256,128]{1,0:T(8,128)} %upper_hbm.1), custom_call_target="tpu_custom_call" | custom-call | tf_op jit(solution)/shard_map/pallas_call | solution.py:95
  9.6 0.0 all-gather.5.cloned.1.call-update
  9.6 6.0 %collective-permute-start = (f32[2,128,128]{2,1,0:T(8,128)}, f32[2,128,128]{2,1,0:T(8,128)S(1)}, u32[]{:S(2)}, u32[]{:S(2)}) collective-permute-start(f32[2,128,128]{2,1,0:T(8,128)} %get-tuple-element.12), channel_id=1, source_target_pairs={{0,0},{1,1},{2,32},{3,33},{32,2},{33,3},{34,34},{35,35},{4,4},{5,5... | collective-permute-start | bytes 393224 | tf_op jit(solution)/shard_map/ppermute | solution.py:273
  15.7 2.5 %collective-permute-start.1 = (f32[2,128,128]{2,1,0:T(8,128)}, f32[2,128,128]{2,1,0:T(8,128)S(1)}, u32[]{:S(2)}, u32[]{:S(2)}) collective-permute-start(f32[2,128,128]{2,1,0:T(8,128)} %get-tuple-element.13), channel_id=1, source_target_pairs={{0,1},{1,0},{2,33},{3,32},{32,3},{33,2},{34,35},{35,34},{4,5},{5,4... | collective-permute-start | bytes 393224 | tf_op jit(solution)/shard_map/ppermute | solution.py:273
  18.1 0.4 collective-permute-done.first_ref
  18.5 4.9 %collective-permute-done.1.second_ref = f32[2,128,128]{2,1,0:T(8,128)S(1)} collective-permute-done((f32[2,128,128]{2,1,0:T(8,128)}, f32[2,128,128]{2,1,0:T(8,128)S(1)}, u32[]{:S(2)}, u32[]{:S(2)}) %collective-permute-start.1) | collective-permute-done | bytes 131104 | tf_op jit(solution)/shard_map/ppermute | solution.py:273
  23.4 1.1 shard_map.77
  24.5 6.8 %all-to-all-start = ((f32[8,2,128,128]{3,2,1,0:T(8,128)}), f32[8,2,128,128]{3,2,1,0:T(8,128)S(1)}, u32[]{:S(2)}, u32[]{:S(2)}) async-start(f32[8,2,128,128]{3,2,1,0:T(8,128)} %get-tuple-element.16), calls=%async_computation.1 | async-start | bytes 2097152 | tf_op jit(solution)/shard_map/all_to_all | solution.py:268
  31.3 0.0 all-gather.7.cloned.1.call-start
  31.3 0.7 all-gather.7.cloned.1.call-update
  32.0 27.3 %all-to-all-done.columns_hbm = f32[8,2,128,128]{3,2,1,0:T(8,128)S(1)} async-done(((f32[8,2,128,128]{3,2,1,0:T(8,128)}), f32[8,2,128,128]{3,2,1,0:T(8,128)S(1)}, u32[]{:S(2)}, u32[]{:S(2)}) %all-to-all-start) | async-done | bytes 1048608 | tf_op jit(solution)/shard_map/all_to_all | solution.py:268
  59.3 2.3 %collective-permute-start.2 = (f32[8,2,128,128]{3,2,1,0:T(8,128)S(1)}, f32[8,2,128,128]{3,2,1,0:T(8,128)S(1)}, u32[]{:S(2)}, u32[]{:S(2)}) collective-permute-start(f32[8,2,128,128]{3,2,1,0:T(8,128)S(1)} %all-to-all-done.columns_hbm), channel_id=1, source_target_pairs={{0,32},{32,0},{1,33},{33,1},{2,34},{34,2},{3,35},{35,3},{4,36},{36... | collective-permute-start | bytes 3145736 | tf_op jit(solution)/shard_map/ppermute | solution.py:277
  61.6 0.0 all-gather.5.cloned.1.call-done
  61.7 0.0 copy-start
  61.7 1.6 %copy-done = f32[4096,128]{1,0:T(8,128)S(1)} copy-done((f32[4096,128]{1,0:T(8,128)S(1)}, f32[4096,128]{1,0:T(8,128)}, u32[]{:S(2)}) %copy-start) | copy-done | bytes 2097176
  63.3 0.9 shard_map.79.refs_0_
  64.2 0.0 collective-permute-done.2.columns_hbm
  64.2 0.9 shard_map.80
  65.1 11.0 %all_to_all.20 = f32[4,256,128]{2,1,0:T(8,128)S(1)} all-to-all(f32[4,256,128]{2,1,0:T(8,128)S(1)} %shard_map.80), channel_id=1, replica_groups=mesh['y'=8,'c'=2,'z'=8,'x'=4] {'x'}, dimensions={0} | all-to-all | bytes 1048576 | tf_op jit(solution)/shard_map/all_to_all | solution.py:268
  76.2 1.1 broadcast_in_dim.2
  77.3 9.9 %all-to-all-start.2 = ((f32[8,256,128]{2,1,0:T(8,128)}), f32[8,256,128]{2,1,0:T(8,128)S(1)}, u32[]{:S(2)}, u32[]{:S(2)}) async-start(f32[8,256,128]{2,1,0:T(8,128)} %broadcast_in_dim.2), calls=%async_computation.3 | async-start | bytes 2097152 | tf_op jit(solution)/shard_map/all_to_all | solution.py:268
  87.1 0.0 reduce-scatter.2.cloned.1.call-start
  87.2 16.2 %all-gather.7.cloned.1.call-done = f32[4096,128]{1,0:T(8,128)} async-done(((f32[256,128]{1,0:T(8,128)}), f32[4096,128]{1,0:T(8,128)}) %all-gather.7.cloned.1.call-update) | async-done | bytes 2097168 | tf_op jit(solution)/shard_map/all_gather | solution.py:287
  103.4 3.8 %shard_map.78 = (f32[4,256,128]{2,1,0:T(8,128)}, bf16[1024,512]{1,0:T(8,128)(2,1)}, bf16[1024,512]{1,0:T(8,128)(2,1)}) custom-call(s32[1]{0:T(128)} %bitcast.at_ref, f32[8,512,128]{2,1,0:T(8,128)} %bitcast.6, f32[16,256,128]{2,1,0:T(8,128)} %bitcast.10), custom_call_target="tpu_custom_call" | custom-call | flops 1610612736 | bytes 6291456 | tf_op jit(solution)/shard_map/pallas_call | solution.py:211
  107.1 0.0 reduce-scatter.2.cloned.1.call-update
  107.2 9.2 %all-to-all-done.2.w_hbm = f32[8,256,128]{2,1,0:T(8,128)S(1)} async-done(((f32[8,256,128]{2,1,0:T(8,128)}), f32[8,256,128]{2,1,0:T(8,128)S(1)}, u32[]{:S(2)}, u32[]{:S(2)}) %all-to-all-start.2) | async-done | bytes 1048608 | tf_op jit(solution)/shard_map/all_to_all | solution.py:268
  116.3 0.0 copy-start.1
  116.3 3.4 %shard_map.81 = f32[4,256,128]{2,1,0:T(8,128)} custom-call(f32[8,256,128]{2,1,0:T(8,128)S(1)} %all-to-all-done.2.w_hbm, bf16[1024,512]{1,0:T(8,128)(2,1)} %get-tuple-element.17.hi_hbm, bf16[1024,512]{1,0:T(8,128)(2,1)} %get-tuple-element.18.lo_hbm), custom_call_target="tpu_custom_call" | custom-call | tf_op jit(solution)/shard_map/pallas_call | solution.py:250
  119.7 3.5 %all-to-all-start.3 = ((f32[4,256,128]{2,1,0:T(8,128)}), f32[4,256,128]{2,1,0:T(8,128)S(1)}, u32[]{:S(2)}, u32[]{:S(2)}) async-start(f32[4,256,128]{2,1,0:T(8,128)} %shard_map.81), calls=%async_computation.4 | async-start | bytes 1048576 | tf_op jit(solution)/shard_map/all_to_all | solution.py:268
  123.2 0.7 neg.11
  123.9 8.5 %reduce-scatter.2.cloned.1.call-done = f32[1,256,128]{2,1,0:T(8,128)} async-done(((f32[4,256,128]{2,1,0:T(8,128)}), f32[1,256,128]{2,1,0:T(8,128)}) %reduce-scatter.2.cloned.1.call-update) | async-done | bytes 131088 | tf_op jit(solution)/shard_map/reduce_scatter | solution.py:294
  132.4 1.6 %negate_bitcast_fusion = f32[256,128]{1,0:T(8,128)} fusion(f32[1,256,128]{2,1,0:T(8,128)} %reduce-scatter.2.cloned.1.call-done), kind=kLoop, calls=%fused_computation | loop fusion | flops 32768 | bytes 262144 | tf_op jit(solution)/shard_map/neg | solution.py:296
  134.0 0.7 all-to-all-done.3
  134.7 0.0 copy-done.1
  134.7 0.7 add.17
  (2 shorter events, 0.1 us)
Async XLA Ops:
  7.2 54.5 %all-gather.5.cloned.1.call-start = ((), (), s32[]{:S(2)}) async-start(), calls=%async_computation.6 | async-start | bytes 2359296 | tf_op jit(solution)/shard_map/all_gather | solution.py:285
  9.6 8.9 %collective-permute-start = (f32[2,128,128]{2,1,0:T(8,128)}, f32[2,128,128]{2,1,0:T(8,128)S(1)}, u32[]{:S(2)}, u32[]{:S(2)}) collective-permute-start(f32[2,128,128]{2,1,0:T(8,128)} %get-tuple-element.12), channel_id=1, source_target_pairs={{0,0},{1,1},{2,32},{3,33},{32,2},{33,3},{34,34},{35,35},{4,4},{5,5... | collective-permute-start | bytes 393224 | tf_op jit(solution)/shard_map/ppermute | solution.py:273
  15.7 7.7 %collective-permute-start.1 = (f32[2,128,128]{2,1,0:T(8,128)}, f32[2,128,128]{2,1,0:T(8,128)S(1)}, u32[]{:S(2)}, u32[]{:S(2)}) collective-permute-start(f32[2,128,128]{2,1,0:T(8,128)} %get-tuple-element.13), channel_id=1, source_target_pairs={{0,1},{1,0},{2,33},{3,32},{32,3},{33,2},{34,35},{35,34},{4,5},{5,4... | collective-permute-start | bytes 393224 | tf_op jit(solution)/shard_map/ppermute | solution.py:273
  24.5 34.9 %all-to-all-start = ((f32[8,2,128,128]{3,2,1,0:T(8,128)}), f32[8,2,128,128]{3,2,1,0:T(8,128)S(1)}, u32[]{:S(2)}, u32[]{:S(2)}) async-start(f32[8,2,128,128]{3,2,1,0:T(8,128)} %get-tuple-element.16), calls=%async_computation.1 | async-start | bytes 2097152 | tf_op jit(solution)/shard_map/all_to_all | solution.py:268
  31.3 72.1 %all-gather.7.cloned.1.call-start = ((), (), s32[]{:S(2)}) async-start(), calls=%async_computation.7 | async-start | bytes 2228224 | tf_op jit(solution)/shard_map/all_gather | solution.py:287
  59.3 4.9 %collective-permute-start.2 = (f32[8,2,128,128]{3,2,1,0:T(8,128)S(1)}, f32[8,2,128,128]{3,2,1,0:T(8,128)S(1)}, u32[]{:S(2)}, u32[]{:S(2)}) collective-permute-start(f32[8,2,128,128]{3,2,1,0:T(8,128)S(1)} %all-to-all-done.columns_hbm), channel_id=1, source_target_pairs={{0,32},{32,0},{1,33},{33,1},{2,34},{34,2},{3,35},{35,3},{4,36},{36... | collective-permute-start | bytes 3145736 | tf_op jit(solution)/shard_map/ppermute | solution.py:277
  61.7 1.6 %copy-start = (f32[4096,128]{1,0:T(8,128)S(1)}, f32[4096,128]{1,0:T(8,128)}, u32[]{:S(2)}) copy-start(f32[4096,128]{1,0:T(8,128)} %all-gather.5.cloned.1.call-done) | copy-start | bytes 6291460
  77.3 39.1 %all-to-all-start.2 = ((f32[8,256,128]{2,1,0:T(8,128)}), f32[8,256,128]{2,1,0:T(8,128)S(1)}, u32[]{:S(2)}, u32[]{:S(2)}) async-start(f32[8,256,128]{2,1,0:T(8,128)} %broadcast_in_dim.2), calls=%async_computation.3 | async-start | bytes 2097152 | tf_op jit(solution)/shard_map/all_to_all | solution.py:268
  87.1 45.3 %reduce-scatter.2.cloned.1.call-start = ((), (), s32[]{:S(2)}) async-start(), calls=%async_computation.5 | async-start | bytes 655360 | tf_op jit(solution)/shard_map/reduce_scatter | solution.py:294
  116.3 18.4 %copy-start.1 = (f32[256,128]{1,0:T(8,128)S(1)}, f32[256,128]{1,0:T(8,128)}, u32[]{:S(2)}) copy-start(f32[256,128]{1,0:T(8,128)} %param.9) | copy-start | bytes 393220
  119.7 14.9 %all-to-all-start.3 = ((f32[4,256,128]{2,1,0:T(8,128)}), f32[4,256,128]{2,1,0:T(8,128)S(1)}, u32[]{:S(2)}, u32[]{:S(2)}) async-start(f32[4,256,128]{2,1,0:T(8,128)} %shard_map.81), calls=%async_computation.4 | async-start | bytes 1048576 | tf_op jit(solution)/shard_map/all_to_all | solution.py:268
Sparse Core Ops, SparseCore 0:
  10.1 46.0 all-gather.4
  58.9 44.4 all-gather.6
  107.3 25.0 reduce-scatter.1

commit v6 on v5

--- a/solution.py
+++ b/solution.py
@@ -178,11 +178,13 @@
     )(at, upper, columns, *more)
 
 
-def side_kernel(at_ref, su_hbm, lower_hbm, out_ref, bh, bl, sigma, lower, ah, al, sems):
-    loads = [
-        pltpu.make_async_copy(su_hbm.at[:, 0:256], sigma, sems.at[0]),
-        pltpu.make_async_copy(lower_hbm, lower, sems.at[1]),
-    ]
+def side_kernel(
+    at_ref, su_hbm, lower_hbm, out_hbm, hi_hbm, lo_hbm, sigma, lower, ah, al, bh, bl, out, sems
+):
+    loads = [pltpu.make_async_copy(su_hbm.at[:, 0:256], sigma, sems.at[0])]
+    for i in range(2):
+        rows = slice(8 * i, 8 * (i + 1))
+        loads.append(pltpu.make_async_copy(lower_hbm.at[rows], lower.at[rows], sems.at[1 + i]))
     for load in loads:
         load.start()
     _, _, _, _, x = device(at_ref)
@@ -191,8 +193,9 @@
     for z in range(8):
         rows = slice(128 * z, 128 * (z + 1))
         ah[:, rows], al[:, rows] = split2(sigma[z])
-    loads[1].wait()
     for z in range(8):
+        if z % 4 == 0:
+            loads[1 + z // 4].wait()
         rows = slice(128 * z, 128 * (z + 1))
         for core in range(2):
             for t in range(2):
@@ -200,11 +203,22 @@
                 place = 128 * (odd if t == 0 else 1 - odd)
                 value = lower[2 * z + core, pl.ds(pl.multiple_of(place, 128), 128), :]
                 bh[rows, cols], bl[rows, cols] = split2(value)
+    stores = [
+        pltpu.make_async_copy(bh, hi_hbm, sems.at[3]),
+        pltpu.make_async_copy(bl, lo_hbm, sems.at[4]),
+    ]
+    for store in stores:
+        store.start()
     for n in range(2):
         cols = slice(256 * n, 256 * (n + 1))
-        part = three_pass(ah[...], al[...], bh[:, cols], bl[:, cols])
-        out_ref[2 * n] = part[:, :128]
-        out_ref[2 * n + 1] = part[:, 128:]
+        part = -three_pass(ah[...], al[...], bh[:, cols], bl[:, cols])
+        out[2 * n] = part[:, :128]
+        out[2 * n + 1] = part[:, 128:]
+        pair = slice(2 * n, 2 * n + 2)
+        stores.append(pltpu.make_async_copy(out.at[pair], out_hbm.at[pair], sems.at[5 + n]))
+        stores[-1].start()
+    for store in stores:
+        store.wait()
 
 
 def side(at, gathered, lower):
@@ -212,13 +226,16 @@
         side_kernel,
         out_shape=(shape(4, 256, 128),) + (shape(1024, 512, dtype=BF16),) * 2,
         in_specs=[SMEM, HBM, HBM],
-        out_specs=(VMEM,) * 3,
+        out_specs=(HBM,) * 3,
         scratch_shapes=[
             pltpu.VMEM((8, 256, 128), F32),
             pltpu.VMEM((16, 256, 128), F32),
             pltpu.VMEM((256, 1024), BF16),
             pltpu.VMEM((256, 1024), BF16),
-            DMA((2,)),
+            pltpu.VMEM((1024, 512), BF16),
+            pltpu.VMEM((1024, 512), BF16),
+            pltpu.VMEM((4, 256, 128), F32),
+            DMA((7,)),
         ],
         compiler_params=WIDE,
         cost_estimate=pl.CostEstimate(flops=6 << 28, bytes_accessed=6 << 20, transcendentals=0),
@@ -293,7 +310,7 @@
     sides, hi, lo = side(at, gathered, lower)
     t = lax.psum_scatter(sides, "x", scatter_dimension=0, tiled=False)
     product = exchange(last(w_all, hi, lo), "x").sum(axis=0)
-    return (-t, -w, diagonal_inverse + product)
+    return (t, -w, diagonal_inverse + product)
 
 
 def solution(mesh):

time: 144 us -> 142 us (0.986); the launches traced: 142 us -> 142 us
  waiting for transfers between devices: 67.8 us -> 69.4 us
  other arithmetic: 2.96 us -> 1.39 us
    all_to_all x3, waiting for transfers between devices: 37.2 us -> 47.3 us  [exchange(): return lax.all_to_all(v, axis, 0, 0, tiled=True)]
    reduce_scatter x1, waiting for transfers between devices: 8.49 us -> 0.01 us  [shards(): t = lax.psum_scatter(sides, 'x', scatter_dimension=0, tiled=False)]
    neg x2 -> x1, other arithmetic: 2.23 us -> 0.67 us  [shards(): return (t, -w, diagonal_inverse + product)]
  transfers between devices with their start and end apart: 9 -> 9, of which waited for: 7 -> 6; matrix products, arithmetic and copies ran while one was open for 2% -> 2% of each run, Pallas kernels for 7% -> 7%
where the time goes in v6:
time: 142 us
  waiting for transfers between devices  69.4 us (49%)
  starting transfers between devices  31.1 us (22%)
  between operations  13.9 us (10%)
  Pallas kernels  12.4 us (9%)
  blocking collectives  11 us (8%)
  local copies, waits for them, and re-layouts  2.66 us (2%)
    all_to_all x3, waiting for transfers between devices, exchange(): return lax.all_to_all(v, axis, 0, 0, tiled=True)  47.3 us
    all_to_all x3, starting transfers between devices, exchange(): return lax.all_to_all(v, axis, 0, 0, tiled=True)  20.2 us
    all_gather x1, waiting for transfers between devices, shards(): lower = lax.all_gather(lower, ('y', 'c'), axis=0, tiled=False)  16.2 us
    all_to_all x1, blocking collectives, exchange(): return lax.all_to_all(v, axis, 0, 0, tiled=True)  11 us
    ppermute x2, starting transfers between devices, deal(): return lax.ppermute(v, ('c', 'x'), moves)  8.53 us
    ppermute x2, waiting for transfers between devices, deal(): return lax.ppermute(v, ('c', 'x'), moves)  5.21 us
    pallas_call x1, Pallas kernels, side(): pl.pallas_call(side_kernel, out_shape=(shape(4, 256, 128),) + (shape(1024...  3.71 us
    pallas_call x1, Pallas kernels, last(): pl.pallas_call(last_kernel, out_shape=shape(4, 256, 128), in_specs=[HBM]...  3.41 us
  transfers between devices with their start and end apart: 9, of which 6 were waited for; matrix products, arithmetic and copies ran while one was open for 2% of the time, Pallas kernels for 7%

profile of v6, /device:TPU:1, one launch (start us, length us, event | category | flops | bytes accessed | tf_op | source)
XLA Modules:
  0.0 141.9 jit_solution(13094616072910655563)
XLA Ops:
  7.2 0.0 all-gather.5.cloned.1.call-start
  7.2 2.4 %shard_map.76 = (f32[512,128]{1,0:T(8,128)}, f32[2,128,128]{2,1,0:T(8,128)}, f32[2,128,128]{2,1,0:T(8,128)}) custom-call(s32[1]{0:T(128)} %bitcast.at_ref, s32[32,128]{1,0:T(8,128)} %bitcast.8, f32[512,256]{1,0:T(8,128)} %root_hbm.1, f32[256,128]{1,0:T(8,128)} %lower_hbm.1, f32[256,128]{1,0:T(8,128)} %upper_hbm.1), custom_call_target="tpu_custom_call" | custom-call | tf_op jit(solution)/shard_map/pallas_call | solution.py:95
  9.6 0.0 all-gather.5.cloned.1.call-update
  9.6 6.0 %collective-permute-start = (f32[2,128,128]{2,1,0:T(8,128)}, f32[2,128,128]{2,1,0:T(8,128)S(1)}, u32[]{:S(2)}, u32[]{:S(2)}) collective-permute-start(f32[2,128,128]{2,1,0:T(8,128)} %get-tuple-element.12), channel_id=1, source_target_pairs={{0,0},{1,1},{2,32},{3,33},{32,2},{33,3},{34,34},{35,35},{4,4},{5,5... | collective-permute-start | bytes 393224 | tf_op jit(solution)/shard_map/ppermute | solution.py:290
  15.7 2.5 %collective-permute-start.1 = (f32[2,128,128]{2,1,0:T(8,128)}, f32[2,128,128]{2,1,0:T(8,128)S(1)}, u32[]{:S(2)}, u32[]{:S(2)}) collective-permute-start(f32[2,128,128]{2,1,0:T(8,128)} %get-tuple-element.13), channel_id=1, source_target_pairs={{0,1},{1,0},{2,33},{3,32},{32,3},{33,2},{34,35},{35,34},{4,5},{5,4... | collective-permute-start | bytes 393224 | tf_op jit(solution)/shard_map/ppermute | solution.py:290
  18.1 0.4 collective-permute-done.first_ref
  18.5 4.9 %collective-permute-done.1.second_ref = f32[2,128,128]{2,1,0:T(8,128)S(1)} collective-permute-done((f32[2,128,128]{2,1,0:T(8,128)}, f32[2,128,128]{2,1,0:T(8,128)S(1)}, u32[]{:S(2)}, u32[]{:S(2)}) %collective-permute-start.1) | collective-permute-done | bytes 131104 | tf_op jit(solution)/shard_map/ppermute | solution.py:290
  23.4 1.1 shard_map.77
  24.5 6.8 %all-to-all-start = ((f32[8,2,128,128]{3,2,1,0:T(8,128)}), f32[8,2,128,128]{3,2,1,0:T(8,128)S(1)}, u32[]{:S(2)}, u32[]{:S(2)}) async-start(f32[8,2,128,128]{3,2,1,0:T(8,128)} %get-tuple-element.16), calls=%async_computation.1 | async-start | bytes 2097152 | tf_op jit(solution)/shard_map/all_to_all | solution.py:285
  31.3 0.0 all-gather.7.cloned.1.call-start
  31.3 0.7 all-gather.7.cloned.1.call-update
  32.0 27.3 %all-to-all-done.columns_hbm = f32[8,2,128,128]{3,2,1,0:T(8,128)S(1)} async-done(((f32[8,2,128,128]{3,2,1,0:T(8,128)}), f32[8,2,128,128]{3,2,1,0:T(8,128)S(1)}, u32[]{:S(2)}, u32[]{:S(2)}) %all-to-all-start) | async-done | bytes 1048608 | tf_op jit(solution)/shard_map/all_to_all | solution.py:285
  59.3 2.3 %collective-permute-start.2 = (f32[8,2,128,128]{3,2,1,0:T(8,128)S(1)}, f32[8,2,128,128]{3,2,1,0:T(8,128)S(1)}, u32[]{:S(2)}, u32[]{:S(2)}) collective-permute-start(f32[8,2,128,128]{3,2,1,0:T(8,128)S(1)} %all-to-all-done.columns_hbm), channel_id=1, source_target_pairs={{0,32},{32,0},{1,33},{33,1},{2,34},{34,2},{3,35},{35,3},{4,36},{36... | collective-permute-start | bytes 3145736 | tf_op jit(solution)/shard_map/ppermute | solution.py:294
  61.6 0.0 all-gather.5.cloned.1.call-done
  61.7 0.0 copy-start
  61.7 1.6 %copy-done = f32[4096,128]{1,0:T(8,128)S(1)} copy-done((f32[4096,128]{1,0:T(8,128)S(1)}, f32[4096,128]{1,0:T(8,128)}, u32[]{:S(2)}) %copy-start) | copy-done | bytes 2097176
  63.3 0.9 shard_map.79.refs_0_
  64.2 0.0 collective-permute-done.2.columns_hbm
  64.2 0.9 shard_map.80
  65.1 11.0 %all_to_all.20 = f32[4,256,128]{2,1,0:T(8,128)S(1)} all-to-all(f32[4,256,128]{2,1,0:T(8,128)S(1)} %shard_map.80), channel_id=1, replica_groups=mesh['y'=8,'c'=2,'z'=8,'x'=4] {'x'}, dimensions={0} | all-to-all | bytes 1048576 | tf_op jit(solution)/shard_map/all_to_all | solution.py:285
  76.2 1.1 broadcast_in_dim.2
  77.3 9.9 %all-to-all-start.2 = ((f32[8,256,128]{2,1,0:T(8,128)}), f32[8,256,128]{2,1,0:T(8,128)S(1)}, u32[]{:S(2)}, u32[]{:S(2)}) async-start(f32[8,256,128]{2,1,0:T(8,128)} %broadcast_in_dim.2), calls=%async_computation.3 | async-start | bytes 2097152 | tf_op jit(solution)/shard_map/all_to_all | solution.py:285
  87.1 0.0 reduce-scatter.2.cloned.1.call-start
  87.2 16.2 %all-gather.7.cloned.1.call-done = f32[4096,128]{1,0:T(8,128)} async-done(((f32[256,128]{1,0:T(8,128)}), f32[4096,128]{1,0:T(8,128)}) %all-gather.7.cloned.1.call-update) | async-done | bytes 2097168 | tf_op jit(solution)/shard_map/all_gather | solution.py:304
  103.4 3.7 %shard_map.78 = (f32[4,256,128]{2,1,0:T(8,128)}, bf16[1024,512]{1,0:T(8,128)(2,1)}, bf16[1024,512]{1,0:T(8,128)(2,1)}) custom-call(s32[1]{0:T(128)} %bitcast.at_ref, f32[8,512,128]{2,1,0:T(8,128)} %bitcast.5, f32[16,256,128]{2,1,0:T(8,128)} %bitcast.9), custom_call_target="tpu_custom_call" | custom-call | flops 1610612736 | bytes 6291456 | tf_op jit(solution)/shard_map/pallas_call | solution.py:225
  107.1 0.0 reduce-scatter.2.cloned.1.call-update
  107.1 9.2 %all-to-all-done.2.w_hbm = f32[8,256,128]{2,1,0:T(8,128)S(1)} async-done(((f32[8,256,128]{2,1,0:T(8,128)}), f32[8,256,128]{2,1,0:T(8,128)S(1)}, u32[]{:S(2)}, u32[]{:S(2)}) %all-to-all-start.2) | async-done | bytes 1048608 | tf_op jit(solution)/shard_map/all_to_all | solution.py:285
  116.3 0.0 copy-start.1
  116.3 3.4 %shard_map.81 = f32[4,256,128]{2,1,0:T(8,128)} custom-call(f32[8,256,128]{2,1,0:T(8,128)S(1)} %all-to-all-done.2.w_hbm, bf16[1024,512]{1,0:T(8,128)(2,1)} %get-tuple-element.17.hi_hbm, bf16[1024,512]{1,0:T(8,128)(2,1)} %get-tuple-element.18.lo_hbm), custom_call_target="tpu_custom_call" | custom-call | tf_op jit(solution)/shard_map/pallas_call | solution.py:267
  119.7 3.5 %all-to-all-start.3 = ((f32[4,256,128]{2,1,0:T(8,128)}), f32[4,256,128]{2,1,0:T(8,128)S(1)}, u32[]{:S(2)}, u32[]{:S(2)}) async-start(f32[4,256,128]{2,1,0:T(8,128)} %shard_map.81), calls=%async_computation.4 | async-start | bytes 1048576 | tf_op jit(solution)/shard_map/all_to_all | solution.py:285
  123.2 0.7 neg.3
  123.9 10.7 %all-to-all-done.3 = f32[4,256,128]{2,1,0:T(8,128)S(1)} async-done(((f32[4,256,128]{2,1,0:T(8,128)}), f32[4,256,128]{2,1,0:T(8,128)S(1)}, u32[]{:S(2)}, u32[]{:S(2)}) %all-to-all-start.3) | async-done | bytes 524320 | tf_op jit(solution)/shard_map/all_to_all | solution.py:285
  134.7 0.0 copy-done.1
  134.7 0.7 add.17
  135.3 0.0 reduce-scatter.2.cloned.1.call-done
  (2 shorter events, 0.1 us)
Async XLA Ops:
  7.2 54.5 %all-gather.5.cloned.1.call-start = ((), (), s32[]{:S(2)}) async-start(), calls=%async_computation.6 | async-start | bytes 2359296 | tf_op jit(solution)/shard_map/all_gather | solution.py:302
  9.6 8.9 %collective-permute-start = (f32[2,128,128]{2,1,0:T(8,128)}, f32[2,128,128]{2,1,0:T(8,128)S(1)}, u32[]{:S(2)}, u32[]{:S(2)}) collective-permute-start(f32[2,128,128]{2,1,0:T(8,128)} %get-tuple-element.12), channel_id=1, source_target_pairs={{0,0},{1,1},{2,32},{3,33},{32,2},{33,3},{34,34},{35,35},{4,4},{5,5... | collective-permute-start | bytes 393224 | tf_op jit(solution)/shard_map/ppermute | solution.py:290
  15.7 7.7 %collective-permute-start.1 = (f32[2,128,128]{2,1,0:T(8,128)}, f32[2,128,128]{2,1,0:T(8,128)S(1)}, u32[]{:S(2)}, u32[]{:S(2)}) collective-permute-start(f32[2,128,128]{2,1,0:T(8,128)} %get-tuple-element.13), channel_id=1, source_target_pairs={{0,1},{1,0},{2,33},{3,32},{32,3},{33,2},{34,35},{35,34},{4,5},{5,4... | collective-permute-start | bytes 393224 | tf_op jit(solution)/shard_map/ppermute | solution.py:290
  24.5 34.9 %all-to-all-start = ((f32[8,2,128,128]{3,2,1,0:T(8,128)}), f32[8,2,128,128]{3,2,1,0:T(8,128)S(1)}, u32[]{:S(2)}, u32[]{:S(2)}) async-start(f32[8,2,128,128]{3,2,1,0:T(8,128)} %get-tuple-element.16), calls=%async_computation.1 | async-start | bytes 2097152 | tf_op jit(solution)/shard_map/all_to_all | solution.py:285
  31.3 72.1 %all-gather.7.cloned.1.call-start = ((), (), s32[]{:S(2)}) async-start(), calls=%async_computation.7 | async-start | bytes 2228224 | tf_op jit(solution)/shard_map/all_gather | solution.py:304
  59.3 4.9 %collective-permute-start.2 = (f32[8,2,128,128]{3,2,1,0:T(8,128)S(1)}, f32[8,2,128,128]{3,2,1,0:T(8,128)S(1)}, u32[]{:S(2)}, u32[]{:S(2)}) collective-permute-start(f32[8,2,128,128]{3,2,1,0:T(8,128)S(1)} %all-to-all-done.columns_hbm), channel_id=1, source_target_pairs={{0,32},{32,0},{1,33},{33,1},{2,34},{34,2},{3,35},{35,3},{4,36},{36... | collective-permute-start | bytes 3145736 | tf_op jit(solution)/shard_map/ppermute | solution.py:294
  61.7 1.6 %copy-start = (f32[4096,128]{1,0:T(8,128)S(1)}, f32[4096,128]{1,0:T(8,128)}, u32[]{:S(2)}) copy-start(f32[4096,128]{1,0:T(8,128)} %all-gather.5.cloned.1.call-done) | copy-start | bytes 6291460
  77.3 39.1 %all-to-all-start.2 = ((f32[8,256,128]{2,1,0:T(8,128)}), f32[8,256,128]{2,1,0:T(8,128)S(1)}, u32[]{:S(2)}, u32[]{:S(2)}) async-start(f32[8,256,128]{2,1,0:T(8,128)} %broadcast_in_dim.2), calls=%async_computation.3 | async-start | bytes 2097152 | tf_op jit(solution)/shard_map/all_to_all | solution.py:285
  87.1 48.2 %reduce-scatter.2.cloned.1.call-start = ((), (), s32[]{:S(2)}) async-start(), calls=%async_computation.5 | async-start | bytes 655360 | tf_op jit(solution)/shard_map/reduce_scatter | solution.py:311
  116.3 18.3 %copy-start.1 = (f32[256,128]{1,0:T(8,128)S(1)}, f32[256,128]{1,0:T(8,128)}, u32[]{:S(2)}) copy-start(f32[256,128]{1,0:T(8,128)} %param.9) | copy-start | bytes 393220
  119.7 14.9 %all-to-all-start.3 = ((f32[4,256,128]{2,1,0:T(8,128)}), f32[4,256,128]{2,1,0:T(8,128)S(1)}, u32[]{:S(2)}, u32[]{:S(2)}) async-start(f32[4,256,128]{2,1,0:T(8,128)} %shard_map.81), calls=%async_computation.4 | async-start | bytes 1048576 | tf_op jit(solution)/shard_map/all_to_all | solution.py:285
Sparse Core Ops, SparseCore 0:
  10.1 46.0 all-gather.4
  58.9 44.4 all-gather.6
  107.2 25.0 reduce-scatter.1

commit v7 on v6

--- a/solution.py
+++ b/solution.py
@@ -13,6 +13,7 @@
 HBM = pl.BlockSpec(memory_space=pltpu.HBM)
 PARAMS = pltpu.CompilerParams(vmem_limit_bytes=32 * 1024 * 1024)
 WIDE = pltpu.CompilerParams(vmem_limit_bytes=62 * 1024 * 1024)
+NEAR = pltpu.CompilerParams(vmem_limit_bytes=51 * 1024 * 1024)
 MIDDLE = pltpu.CompilerParams(vmem_limit_bytes=52 * 1024 * 1024)
 DMA = pltpu.SemaphoreType.DMA
 
@@ -40,13 +41,12 @@
 
 
 def pick_kernel(
-    at_ref, map_hbm, root_hbm, lower_hbm, upper_hbm, su_ref, first_ref, second_ref, picks, root, lower, sems
+    at_ref, map_hbm, root_hbm, upper_hbm, su_ref, first_ref, second_ref, picks, root, sems
 ):
     loads = [
         pltpu.make_async_copy(map_hbm, picks, sems.at[0]),
         pltpu.make_async_copy(root_hbm, root, sems.at[1]),
-        pltpu.make_async_copy(lower_hbm, lower, sems.at[2]),
-        pltpu.make_async_copy(upper_hbm, su_ref.at[256:512], sems.at[3]),
+        pltpu.make_async_copy(upper_hbm, su_ref.at[256:512], sems.at[2]),
     ]
     for load in loads:
         load.start()
@@ -81,36 +81,31 @@
     for part in range(2):
         v = [value[128 * (3 * part + i) : 128 * (3 * part + i + 1), :] for i in range(3)]
         su_ref[128 * part : 128 * (part + 1), :] = (v[0] + v[1]) + v[2]
-    for load in loads[2:]:
-        load.wait()
+    loads[2].wait()
     near = pl.multiple_of(128 * odd, 128)
     far = pl.multiple_of(128 - 128 * odd, 128)
-    first_ref[0] = su_ref[pl.ds(near, 128), :]
-    first_ref[1] = lower[pl.ds(near, 128), :]
-    second_ref[0] = su_ref[pl.ds(far, 128), :]
-    second_ref[1] = lower[pl.ds(far, 128), :]
-
-
-def pick(at, blocks, root, lower, upper):
+    first_ref[...] = su_ref[pl.ds(near, 128), :]
+    second_ref[...] = su_ref[pl.ds(far, 128), :]
+
+
+def pick(at, blocks, root, upper):
     return pl.pallas_call(
         pick_kernel,
-        out_shape=(shape(512, 128), shape(2, 128, 128), shape(2, 128, 128)),
-        in_specs=[SMEM] + [HBM] * 4,
+        out_shape=(shape(512, 128), shape(128, 128), shape(128, 128)),
+        in_specs=[SMEM] + [HBM] * 3,
         out_specs=(VMEM, VMEM, VMEM),
         scratch_shapes=[
             pltpu.VMEM((32, 128), jnp.int32),
             pltpu.VMEM((512, 256), F32),
-            pltpu.VMEM((256, 128), F32),
-            DMA((4,)),
+            DMA((3,)),
         ],
         compiler_params=WIDE,
-    )(at, blocks, root, lower, upper)
-
-
-def fan_kernel(first_ref, second_ref, copies_ref, lower_ref):
+    )(at, blocks, root, upper)
+
+
+def fan_kernel(first_ref, second_ref, copies_ref):
     for t, ref in enumerate((first_ref, second_ref)):
-        lower_ref[128 * t : 128 * (t + 1), :] = ref[1]
-        value = ref[0]
+        value = ref[...]
         for i in range(8):
             copies_ref[i, t] = value
 
@@ -118,9 +113,9 @@
 def fan(first, second):
     return pl.pallas_call(
         fan_kernel,
-        out_shape=(shape(8, 2, 128, 128), shape(256, 128)),
+        out_shape=shape(8, 2, 128, 128),
         in_specs=[VMEM] * 2,
-        out_specs=(VMEM, VMEM),
+        out_specs=VMEM,
         compiler_params=PARAMS,
     )(first, second)
 
@@ -136,12 +131,15 @@
         ]
         for load in loads:
             load.start()
+        _, _, core, _, x = device(at_ref)
+        odd = x & 1
+        side = core if before is None else 1 - core
         loads[0].wait()
         for z in range(8):
             rows = slice(128 * z, 128 * (z + 1))
             for t in range(2):
                 cols = slice(128 * t, 128 * (t + 1))
-                bh[rows, cols], bl[rows, cols] = split2(right[z, t])
+                bh[rows, cols], bl[rows, cols] = split2(right[z ^ (4 * side), t])
         loads[1].wait()
         for z in range(8):
             rows = slice(128 * z, 128 * (z + 1))
@@ -151,12 +149,10 @@
             out_ref[0] = part[:, :128]
             out_ref[1] = part[:, 128:]
         else:
-            _, _, core, _, x = device(at_ref)
-            odd = x & 1
-            out_ref[2 * core + odd] = before_ref[0]
-            out_ref[2 * core + 1 - odd] = before_ref[1]
-            out_ref[2 * (1 - core) + odd] = part[:, :128]
-            out_ref[2 * (1 - core) + 1 - odd] = part[:, 128:]
+            out_ref[odd] = before_ref[0]
+            out_ref[1 - odd] = before_ref[1]
+            out_ref[2 + odd] = part[:, :128]
+            out_ref[3 - odd] = part[:, 128:]
 
     more = () if before is None else (before,)
     return pl.pallas_call(
@@ -173,7 +169,7 @@
             pltpu.VMEM((1024, 256), BF16),
             DMA((2,)),
         ],
-        compiler_params=PARAMS,
+        compiler_params=NEAR,
         cost_estimate=pl.CostEstimate(flops=3 << 28, bytes_accessed=3 << 20, transcendentals=0),
     )(at, upper, columns, *more)
 
@@ -242,7 +238,7 @@
     )(at, gathered, lower)
 
 
-def last_kernel(w_hbm, hi_hbm, lo_hbm, out_ref, w, ah, al, bh, bl, sems):
+def last_kernel(at_ref, w_hbm, hi_hbm, lo_hbm, out_hbm, w, ah, al, bh, bl, out, sems):
     loads = [
         pltpu.make_async_copy(w_hbm, w, sems.at[0]),
         pltpu.make_async_copy(hi_hbm, bh, sems.at[1]),
@@ -250,39 +246,52 @@
     ]
     for load in loads:
         load.start()
+    core = device(at_ref)[2]
     loads[0].wait()
     for z in range(8):
         rows = slice(128 * z, 128 * (z + 1))
-        ah[:, rows], al[:, rows] = split2(w[z])
+        ah[:, rows], al[:, rows] = split2(w[z ^ (4 * core)])
     for load in loads[1:]:
         load.wait()
+    stores = []
     for n in range(2):
         cols = slice(256 * n, 256 * (n + 1))
         part = three_pass(ah[...], al[...], bh[:, cols], bl[:, cols])
-        out_ref[2 * n] = part[:, :128]
-        out_ref[2 * n + 1] = part[:, 128:]
-
-
-def last(w, hi, lo):
+        out[2 * n] = part[:, :128]
+        out[2 * n + 1] = part[:, 128:]
+        pair, place = slice(2 * n, 2 * n + 2), pl.ds(2 * (n ^ core), 2)
+        stores.append(pltpu.make_async_copy(out.at[pair], out_hbm.at[place], sems.at[3 + n]))
+        stores[-1].start()
+    for store in stores:
+        store.wait()
+
+
+def last(at, w, hi, lo):
     return pl.pallas_call(
         last_kernel,
         out_shape=shape(4, 256, 128),
-        in_specs=[HBM] * 3,
-        out_specs=VMEM,
+        in_specs=[SMEM] + [HBM] * 3,
+        out_specs=HBM,
         scratch_shapes=[
             pltpu.VMEM((8, 256, 128), F32),
             pltpu.VMEM((256, 1024), BF16),
             pltpu.VMEM((256, 1024), BF16),
             pltpu.VMEM((1024, 512), BF16),
             pltpu.VMEM((1024, 512), BF16),
-            DMA((3,)),
+            pltpu.VMEM((4, 256, 128), F32),
+            DMA((5,)),
         ],
         compiler_params=MIDDLE,
-    )(w, hi, lo)
-
-
-def exchange(v, axis):
-    return lax.all_to_all(v, axis, 0, 0, tiled=True)
+    )(at, w, hi, lo)
+
+
+def exchange(v, axis, size):
+    axes = (axis, "c") if axis == "y" else ("c", axis)
+    groups = [
+        [2 * p + c if axis == "y" else size * c + p for p in (i ^ (size // 2 * c) for i in range(size))]
+        for c in range(2)
+    ]
+    return lax.all_to_all(v, axes, 0, 0, tiled=True, axis_index_groups=groups)
 
 
 def deal(v, t):
@@ -296,20 +305,24 @@
 
 def shards(root_inverse, boundary_map, lower_factor, upper_factor, diagonal_inverse):
     at = lax.axis_index(("y", "c", "z", "x")).astype(jnp.int32).reshape(1)
-    su, first, second = pick(
-        at, boundary_map.reshape(32, 128), root_inverse, lower_factor, upper_factor
-    )
+    su, first, second = pick(at, boundary_map.reshape(32, 128), root_inverse, upper_factor)
     gathered = lax.all_gather(su, "z", axis=0, tiled=False)
-    copies, lower = fan(deal(first, 0), deal(second, 1))
+    copies = fan(deal(first, 0), deal(second, 1))
+    copies, lower = lax.optimization_barrier((copies, lower_factor))
+    odd = lax.axis_index("x") & 1
+    lower = [
+        deal(lax.dynamic_slice_in_dim(lower, 128 * (odd ^ t), 128), t) for t in range(2)
+    ]
+    lower = jnp.concatenate(lower, axis=0)
     lower = lax.all_gather(lower, ("y", "c"), axis=0, tiled=False)
-    own = exchange(copies, "y")
+    own = exchange(copies, "y", 8)
     other = turn(own, "c", 2, 1)
     part = couple(at, gathered, other, couple(at, gathered, own))
-    w = exchange(part, "x").sum(axis=0)
-    w_all = exchange(jnp.broadcast_to(w[None], (8, 256, 128)), "z")
+    w = exchange(part, "x", 4).sum(axis=0)
+    w_all = exchange(jnp.broadcast_to(w[None], (8, 256, 128)), "z", 8)
     sides, hi, lo = side(at, gathered, lower)
     t = lax.psum_scatter(sides, "x", scatter_dimension=0, tiled=False)
-    product = exchange(last(w_all, hi, lo), "x").sum(axis=0)
+    product = exchange(last(at, w_all, hi, lo), "x", 4).sum(axis=0)
     return (t, -w, diagonal_inverse + product)
 
 

time: 142 us -> 141 us (level)
  waiting for transfers between devices: 69.4 us -> 48.2 us
  starting transfers between devices: 31.1 us -> 51.5 us
  blocking collectives: 11 us -> 8.7 us
  Pallas kernels: 12.4 us -> 14.4 us
  local copies, waits for them, and re-layouts: 2.66 us -> 1.09 us
    all_to_all x3, waiting for transfers between devices: 47.3 us -> 20.7 us  [exchange(): return lax.all_to_all(v, axes, 0, 0, tiled=True, axis_index_groups=groups)]
    all_to_all x3, starting transfers between devices: 20.2 us -> 34.9 us  [exchange(): return lax.all_to_all(v, axes, 0, 0, tiled=True, axis_index_groups=groups)]
    ppermute x2 -> x4, starting transfers between devices: 8.53 us -> 13.5 us  [deal(): return lax.ppermute(v, ('c', 'x'), moves)]
    ppermute x2 -> x4, waiting for transfers between devices: 5.21 us -> 8.65 us  [deal(): return lax.ppermute(v, ('c', 'x'), moves)]
    all_to_all x1, blocking collectives: 11 us -> 8.7 us  [exchange(): return lax.all_to_all(v, axes, 0, 0, tiled=True, axis_index_groups=groups)]
    reduce_scatter x1, waiting for transfers between devices: 0.01 us -> 2.26 us  [shards(): t = lax.psum_scatter(sides, 'x', scatter_dimension=0, tiled=False)]
    pallas_call x2, Pallas kernels: 1.87 us -> 3.85 us  [couple(): pl.pallas_call(kernel, out_shape=shape(2 + 2 * len(more), 256, 128), in_s...]
    unnamed x4, local copies, waits for them, and re-layouts: 1.59 us -> 0.01 us
  transfers between devices with their start and end apart: 9 -> 11, of which waited for: 6 -> 9; matrix products, arithmetic and copies ran while one was open for 2% -> 2% of each run, Pallas kernels for 7% -> 9%
where the time goes in v7:
time: 141 us; the launch traced here: 140 us
  starting transfers between devices  51.5 us (37%)
  waiting for transfers between devices  48.2 us (34%)
  Pallas kernels  14.4 us (10%)
  between operations  13.9 us (10%)
  blocking collectives  8.7 us (6%)
  other arithmetic  2.05 us (1%)
    all_to_all x3, starting transfers between devices, exchange(): return lax.all_to_all(v, axes, 0, 0, tiled=True, axis_index_groups=groups)  34.9 us
    all_to_all x3, waiting for transfers between devices, exchange(): return lax.all_to_all(v, axes, 0, 0, tiled=True, axis_index_groups=groups)  20.7 us
    all_gather x1, waiting for transfers between devices, shards(): lower = lax.all_gather(lower, ('y', 'c'), axis=0, tiled=False)  16.2 us
    ppermute x4, starting transfers between devices, deal(): return lax.ppermute(v, ('c', 'x'), moves)  13.5 us
    all_to_all x1, blocking collectives, exchange(): return lax.all_to_all(v, axes, 0, 0, tiled=True, axis_index_groups=groups)  8.7 us
    ppermute x4, waiting for transfers between devices, deal(): return lax.ppermute(v, ('c', 'x'), moves)  8.65 us
    pallas_call x2, Pallas kernels, couple(): pl.pallas_call(kernel, out_shape=shape(2 + 2 * len(more), 256, 128), in_s...  3.85 us
    pallas_call x1, Pallas kernels, side(): pl.pallas_call(side_kernel, out_shape=(shape(4, 256, 128),) + (shape(1024...  3.71 us
  transfers between devices with their start and end apart: 11, of which 9 were waited for; matrix products, arithmetic and copies ran while one was open for 2% of the time, Pallas kernels for 9%

profile of v7, /device:TPU:1, one launch (start us, length us, event | category | flops | bytes accessed | tf_op | source)
XLA Modules:
  0.0 139.7 jit_solution(3366138403509539848)
XLA Ops:
  7.2 0.0 all-gather.5.cloned.1.call-start
  7.2 0.0 copy-start.1
  7.2 2.3 %shard_map.76 = (f32[512,128]{1,0:T(8,128)}, f32[128,128]{1,0:T(8,128)}, f32[128,128]{1,0:T(8,128)}) custom-call(s32[1]{0:T(128)} %bitcast.at_ref, s32[32,128]{1,0:T(8,128)} %bitcast.8, f32[512,256]{1,0:T(8,128)} %root_hbm.1, f32[256,128]{1,0:T(8,128)} %upper_hbm.1), custom_call_target="tpu_custom_call" | custom-call | tf_op jit(solution)/shard_map/pallas_call | solution.py:92
  9.6 0.0 all-gather.5.cloned.1.call-update
  9.6 6.0 %collective-permute-start = (f32[128,128]{1,0:T(8,128)}, f32[128,128]{1,0:T(8,128)S(1)}, u32[]{:S(2)}, u32[]{:S(2)}) collective-permute-start(f32[128,128]{1,0:T(8,128)} %get-tuple-element.12), channel_id=1, source_target_pairs={{0,0},{1,1},{2,32},{3,33},{32,2},{33,3},{34,34},{35,35},{4,4},{5,5... | collective-permute-start | bytes 196616 | tf_op jit(solution)/shard_map/ppermute | solution.py:299
  15.6 2.5 %collective-permute-start.1 = (f32[128,128]{1,0:T(8,128)}, f32[128,128]{1,0:T(8,128)S(1)}, u32[]{:S(2)}, u32[]{:S(2)}) collective-permute-start(f32[128,128]{1,0:T(8,128)} %get-tuple-element.13), channel_id=1, source_target_pairs={{0,1},{1,0},{2,33},{3,32},{32,3},{33,2},{34,35},{35,34},{4,5},{5,4... | collective-permute-start | bytes 196616 | tf_op jit(solution)/shard_map/ppermute | solution.py:299
  18.1 0.0 collective-permute-done.first_ref
  18.1 4.5 %collective-permute-done.1.second_ref = f32[128,128]{1,0:T(8,128)S(1)} collective-permute-done((f32[128,128]{1,0:T(8,128)}, f32[128,128]{1,0:T(8,128)S(1)}, u32[]{:S(2)}, u32[]{:S(2)}) %collective-permute-start.1) | collective-permute-done | bytes 65568 | tf_op jit(solution)/shard_map/ppermute | solution.py:299
  22.6 1.1 shard_map.77
  23.7 9.0 %all-to-all-start = ((f32[8,2,128,128]{3,2,1,0:T(8,128)}), f32[8,2,128,128]{3,2,1,0:T(8,128)S(1)}, u32[]{:S(2)}, u32[]{:S(2)}) async-start(f32[8,2,128,128]{3,2,1,0:T(8,128)} %shard_map.77), calls=%async_computation.1 | async-start | bytes 2097152 | tf_op jit(solution)/shard_map/all_to_all | solution.py:294
  32.7 0.0 all-gather.7.cloned.1.call-start
  32.7 0.0 copy-done.1
  32.7 1.9 %collective-permute-start.3 = (f32[128,128]{1,0:T(8,128)S(1)}, f32[128,128]{1,0:T(8,128)S(1)}, u32[]{:S(2)}, u32[]{:S(2)}) collective-permute-start(f32[128,128]{1,0:T(8,128)S(1)} %get-tuple-element.20), channel_id=1, source_target_pairs={{0,1},{1,0},{2,33},{3,32},{32,3},{33,2},{34,35},{35,34},{4,5},{5,4... | collective-permute-start | bytes 196616 | tf_op jit(solution)/shard_map/ppermute | solution.py:299
  34.7 3.1 %collective-permute-start.2 = (f32[128,128]{1,0:T(8,128)S(1)}, f32[128,128]{1,0:T(8,128)S(1)}, u32[]{:S(2)}, u32[]{:S(2)}) collective-permute-start(f32[128,128]{1,0:T(8,128)S(1)} %get-tuple-element.19), channel_id=1, source_target_pairs={{0,0},{1,1},{2,32},{3,33},{32,2},{33,3},{34,34},{35,35},{4,4},{5,5... | collective-permute-start | bytes 196616 | tf_op jit(solution)/shard_map/ppermute | solution.py:299
  37.7 2.2 %collective-permute-done.3 = f32[128,128]{1,0:T(8,128)S(1)} collective-permute-done((f32[128,128]{1,0:T(8,128)S(1)}, f32[128,128]{1,0:T(8,128)S(1)}, u32[]{:S(2)}, u32[]{:S(2)}) %collective-permute-start.3) | collective-permute-done | bytes 65568 | tf_op jit(solution)/shard_map/ppermute | solution.py:299
  39.9 2.0 %collective-permute-done.2 = f32[128,128]{1,0:T(8,128)S(1)} collective-permute-done((f32[128,128]{1,0:T(8,128)S(1)}, f32[128,128]{1,0:T(8,128)S(1)}, u32[]{:S(2)}, u32[]{:S(2)}) %collective-permute-start.2) | collective-permute-done | bytes 65568 | tf_op jit(solution)/shard_map/ppermute | solution.py:299
  41.9 0.7 pad_maximum_fusion
  42.6 0.0 all-gather.7.cloned.1.call-update
  42.6 10.9 %all-to-all-done.columns_hbm = f32[8,2,128,128]{3,2,1,0:T(8,128)S(1)} async-done(((f32[8,2,128,128]{3,2,1,0:T(8,128)}), f32[8,2,128,128]{3,2,1,0:T(8,128)S(1)}, u32[]{:S(2)}, u32[]{:S(2)}) %all-to-all-start) | async-done | bytes 1048608 | tf_op jit(solution)/shard_map/all_to_all | solution.py:294
  53.5 3.0 %collective-permute-start.4 = (f32[8,2,128,128]{3,2,1,0:T(8,128)S(1)}, f32[8,2,128,128]{3,2,1,0:T(8,128)S(1)}, u32[]{:S(2)}, u32[]{:S(2)}) collective-permute-start(f32[8,2,128,128]{3,2,1,0:T(8,128)S(1)} %all-to-all-done.columns_hbm), channel_id=1, source_target_pairs={{0,32},{32,0},{1,33},{33,1},{2,34},{34,2},{3,35},{35,3},{4,36},{36... | collective-permute-start | bytes 3145736 | tf_op jit(solution)/shard_map/ppermute | solution.py:303
  56.5 0.0 all-gather.5.cloned.1.call-done
  56.5 1.9 %shard_map.79.refs_0_ = f32[2,256,128]{2,1,0:T(8,128)S(1)} custom-call(s32[1]{0:T(128)} %bitcast.at_ref, f32[8,512,128]{2,1,0:T(8,128)} %bitcast.5, f32[8,2,128,128]{3,2,1,0:T(8,128)S(1)} %all-to-all-done.columns_hbm), custom_call_target="tpu_custom_call" | custom-call | flops 805306368 | bytes 3145728 | tf_op jit(solution)/shard_map/pallas_call | solution.py:158
  58.5 0.3 collective-permute-done.4.columns_hbm
  58.8 1.9 %shard_map.80 = f32[4,256,128]{2,1,0:T(8,128)S(1)} custom-call(s32[1]{0:T(128)} %bitcast.at_ref, f32[8,512,128]{2,1,0:T(8,128)} %bitcast.6, f32[8,2,128,128]{3,2,1,0:T(8,128)S(1)} %collective-permute-done.4.columns_hbm, f32[2,256,128]{2,1,0:T(8,128)S(1)} %shard_map.79.refs_0_), custom_call_target="tpu_custom_call" | custom-call | flops 805306368 | bytes 3145728 | tf_op jit(solution)/shard_map/pallas_call | solution.py:158
  60.7 8.7 %all_to_all.20 = f32[4,256,128]{2,1,0:T(8,128)S(1)} all-to-all(f32[4,256,128]{2,1,0:T(8,128)S(1)} %shard_map.80), channel_id=1, replica_groups={{0,1,2,3},{34,35,32,33},{4,5,6,7},{38,39,36,37},{8,9,10,11},{42,43,40,4..., dimensions={0} | all-to-all | bytes 1048576 | tf_op jit(solution)/shard_map/all_to_all | solution.py:294
  69.4 1.1 broadcast_in_dim.2
  70.5 16.7 %all-to-all-start.2 = ((f32[8,256,128]{2,1,0:T(8,128)}), f32[8,256,128]{2,1,0:T(8,128)S(1)}, u32[]{:S(2)}, u32[]{:S(2)}) async-start(f32[8,256,128]{2,1,0:T(8,128)} %broadcast_in_dim.2), calls=%async_computation.3 | async-start | bytes 2097152 | tf_op jit(solution)/shard_map/all_to_all | solution.py:294
  87.2 0.0 reduce-scatter.2.cloned.1.call-start
  87.2 16.2 %all-gather.7.cloned.1.call-done = f32[4096,128]{1,0:T(8,128)} async-done(((f32[256,128]{1,0:T(8,128)}), f32[4096,128]{1,0:T(8,128)}) %all-gather.7.cloned.1.call-update) | async-done | bytes 2097168 | tf_op jit(solution)/shard_map/all_gather | solution.py:317
  103.4 3.7 %shard_map.78 = (f32[4,256,128]{2,1,0:T(8,128)}, bf16[1024,512]{1,0:T(8,128)(2,1)}, bf16[1024,512]{1,0:T(8,128)(2,1)}) custom-call(s32[1]{0:T(128)} %bitcast.at_ref, f32[8,512,128]{2,1,0:T(8,128)} %bitcast.7, f32[16,256,128]{2,1,0:T(8,128)} %bitcast.9), custom_call_target="tpu_custom_call" | custom-call | flops 1610612736 | bytes 6291456 | tf_op jit(solution)/shard_map/pallas_call | solution.py:221
  107.1 0.0 reduce-scatter.2.cloned.1.call-update
  107.1 1.5 %all-to-all-done.2.w_hbm = f32[8,256,128]{2,1,0:T(8,128)S(1)} async-done(((f32[8,256,128]{2,1,0:T(8,128)}), f32[8,256,128]{2,1,0:T(8,128)S(1)}, u32[]{:S(2)}, u32[]{:S(2)}) %all-to-all-start.2) | async-done | bytes 1048608 | tf_op jit(solution)/shard_map/all_to_all | solution.py:294
  108.6 0.0 copy-start
  108.6 3.4 %shard_map.81 = f32[4,256,128]{2,1,0:T(8,128)} custom-call(s32[1]{0:T(128)} %bitcast.at_ref, f32[8,256,128]{2,1,0:T(8,128)S(1)} %all-to-all-done.2.w_hbm, bf16[1024,512]{1,0:T(8,128)(2,1)} %get-tuple-element.17.hi_hbm, bf16[1024,512]{1,0:T(8,128)(2,1)} %get-tuple-element.18.lo_hbm), custom_call_target="tpu_custom_call" | custom-call | tf_op jit(solution)/shard_map/pallas_call | solution.py:270
  112.0 9.2 %all-to-all-start.3 = ((f32[4,256,128]{2,1,0:T(8,128)}), f32[4,256,128]{2,1,0:T(8,128)S(1)}, u32[]{:S(2)}, u32[]{:S(2)}) async-start(f32[4,256,128]{2,1,0:T(8,128)} %shard_map.81), calls=%async_computation.4 | async-start | bytes 1048576 | tf_op jit(solution)/shard_map/all_to_all | solution.py:294
  121.2 0.7 neg.3
  121.8 8.4 %all-to-all-done.3 = f32[4,256,128]{2,1,0:T(8,128)S(1)} async-done(((f32[4,256,128]{2,1,0:T(8,128)}), f32[4,256,128]{2,1,0:T(8,128)S(1)}, u32[]{:S(2)}, u32[]{:S(2)}) %all-to-all-start.3) | async-done | bytes 524320 | tf_op jit(solution)/shard_map/all_to_all | solution.py:294
  130.3 0.0 copy-done
  130.3 0.7 add.25
  131.0 2.3 %reduce-scatter.2.cloned.1.call-done = f32[1,256,128]{2,1,0:T(8,128)} async-done(((f32[4,256,128]{2,1,0:T(8,128)}), f32[1,256,128]{2,1,0:T(8,128)}) %reduce-scatter.2.cloned.1.call-update) | async-done | bytes 131088 | tf_op jit(solution)/shard_map/reduce_scatter | solution.py:324
  (3 shorter events, 0.1 us)
Async XLA Ops:
  7.2 49.4 %all-gather.5.cloned.1.call-start = ((), (), s32[]{:S(2)}) async-start(), calls=%async_computation.6 | async-start | bytes 2359296 | tf_op jit(solution)/shard_map/all_gather | solution.py:309
  7.2 25.5 %copy-start.1 = (f32[256,128]{1,0:T(8,128)S(1)}, f32[256,128]{1,0:T(8,128)}, u32[]{:S(2)}) copy-start(f32[256,128]{1,0:T(8,128)} %param.7) | copy-start | bytes 393220
  9.6 8.5 %collective-permute-start = (f32[128,128]{1,0:T(8,128)}, f32[128,128]{1,0:T(8,128)S(1)}, u32[]{:S(2)}, u32[]{:S(2)}) collective-permute-start(f32[128,128]{1,0:T(8,128)} %get-tuple-element.12), channel_id=1, source_target_pairs={{0,0},{1,1},{2,32},{3,33},{32,2},{33,3},{34,34},{35,35},{4,4},{5,5... | collective-permute-start | bytes 196616 | tf_op jit(solution)/shard_map/ppermute | solution.py:299
  15.6 7.0 %collective-permute-start.1 = (f32[128,128]{1,0:T(8,128)}, f32[128,128]{1,0:T(8,128)S(1)}, u32[]{:S(2)}, u32[]{:S(2)}) collective-permute-start(f32[128,128]{1,0:T(8,128)} %get-tuple-element.13), channel_id=1, source_target_pairs={{0,1},{1,0},{2,33},{3,32},{32,3},{33,2},{34,35},{35,34},{4,5},{5,4... | collective-permute-start | bytes 196616 | tf_op jit(solution)/shard_map/ppermute | solution.py:299
  23.7 29.8 %all-to-all-start = ((f32[8,2,128,128]{3,2,1,0:T(8,128)}), f32[8,2,128,128]{3,2,1,0:T(8,128)S(1)}, u32[]{:S(2)}, u32[]{:S(2)}) async-start(f32[8,2,128,128]{3,2,1,0:T(8,128)} %shard_map.77), calls=%async_computation.1 | async-start | bytes 2097152 | tf_op jit(solution)/shard_map/all_to_all | solution.py:294
  32.7 70.6 %all-gather.7.cloned.1.call-start = ((), (), s32[]{:S(2)}) async-start(), calls=%async_computation.7 | async-start | bytes 2228224 | tf_op jit(solution)/shard_map/all_gather | solution.py:317
  32.7 7.2 %collective-permute-start.3 = (f32[128,128]{1,0:T(8,128)S(1)}, f32[128,128]{1,0:T(8,128)S(1)}, u32[]{:S(2)}, u32[]{:S(2)}) collective-permute-start(f32[128,128]{1,0:T(8,128)S(1)} %get-tuple-element.20), channel_id=1, source_target_pairs={{0,1},{1,0},{2,33},{3,32},{32,3},{33,2},{34,35},{35,34},{4,5},{5,4... | collective-permute-start | bytes 196616 | tf_op jit(solution)/shard_map/ppermute | solution.py:299
  34.7 7.2 %collective-permute-start.2 = (f32[128,128]{1,0:T(8,128)S(1)}, f32[128,128]{1,0:T(8,128)S(1)}, u32[]{:S(2)}, u32[]{:S(2)}) collective-permute-start(f32[128,128]{1,0:T(8,128)S(1)} %get-tuple-element.19), channel_id=1, source_target_pairs={{0,0},{1,1},{2,32},{3,33},{32,2},{33,3},{34,34},{35,35},{4,4},{5,5... | collective-permute-start | bytes 196616 | tf_op jit(solution)/shard_map/ppermute | solution.py:299
  53.5 5.3 %collective-permute-start.4 = (f32[8,2,128,128]{3,2,1,0:T(8,128)S(1)}, f32[8,2,128,128]{3,2,1,0:T(8,128)S(1)}, u32[]{:S(2)}, u32[]{:S(2)}) collective-permute-start(f32[8,2,128,128]{3,2,1,0:T(8,128)S(1)} %all-to-all-done.columns_hbm), channel_id=1, source_target_pairs={{0,32},{32,0},{1,33},{33,1},{2,34},{34,2},{3,35},{35,3},{4,36},{36... | collective-permute-start | bytes 3145736 | tf_op jit(solution)/shard_map/ppermute | solution.py:303
  70.5 38.0 %all-to-all-start.2 = ((f32[8,256,128]{2,1,0:T(8,128)}), f32[8,256,128]{2,1,0:T(8,128)S(1)}, u32[]{:S(2)}, u32[]{:S(2)}) async-start(f32[8,256,128]{2,1,0:T(8,128)} %broadcast_in_dim.2), calls=%async_computation.3 | async-start | bytes 2097152 | tf_op jit(solution)/shard_map/all_to_all | solution.py:294
  87.2 46.0 %reduce-scatter.2.cloned.1.call-start = ((), (), s32[]{:S(2)}) async-start(), calls=%async_computation.5 | async-start | bytes 655360 | tf_op jit(solution)/shard_map/reduce_scatter | solution.py:324
  108.6 21.7 %copy-start = (f32[256,128]{1,0:T(8,128)S(1)}, f32[256,128]{1,0:T(8,128)}, u32[]{:S(2)}) copy-start(f32[256,128]{1,0:T(8,128)} %param.9) | copy-start | bytes 393220
  112.0 18.3 %all-to-all-start.3 = ((f32[4,256,128]{2,1,0:T(8,128)}), f32[4,256,128]{2,1,0:T(8,128)S(1)}, u32[]{:S(2)}, u32[]{:S(2)}) async-start(f32[4,256,128]{2,1,0:T(8,128)} %shard_map.81), calls=%async_computation.4 | async-start | bytes 1048576 | tf_op jit(solution)/shard_map/all_to_all | solution.py:294
Sparse Core Ops, SparseCore 0:
  10.1 46.0 all-gather.4
  58.9 44.4 all-gather.6
  107.2 25.9 reduce-scatter.1

commit v8 on v7

--- a/solution.py
+++ b/solution.py
@@ -13,9 +13,9 @@
 HBM = pl.BlockSpec(memory_space=pltpu.HBM)
 PARAMS = pltpu.CompilerParams(vmem_limit_bytes=32 * 1024 * 1024)
 WIDE = pltpu.CompilerParams(vmem_limit_bytes=62 * 1024 * 1024)
-NEAR = pltpu.CompilerParams(vmem_limit_bytes=51 * 1024 * 1024)
 MIDDLE = pltpu.CompilerParams(vmem_limit_bytes=52 * 1024 * 1024)
 DMA = pltpu.SemaphoreType.DMA
+ORDER = (0, 4, 2, 6, 1, 5, 3, 7)
 
 
 def shape(*dims, dtype=F32):
@@ -41,12 +41,11 @@
 
 
 def pick_kernel(
-    at_ref, map_hbm, root_hbm, upper_hbm, su_ref, first_ref, second_ref, picks, root, sems
+    at_ref, map_hbm, root_hbm, sigma_ref, first_ref, second_ref, picks, root, sems
 ):
     loads = [
         pltpu.make_async_copy(map_hbm, picks, sems.at[0]),
         pltpu.make_async_copy(root_hbm, root, sems.at[1]),
-        pltpu.make_async_copy(upper_hbm, su_ref.at[256:512], sems.at[2]),
     ]
     for load in loads:
         load.start()
@@ -80,27 +79,26 @@
     value = dot(jnp.concatenate(stack, axis=0), col_hot)
     for part in range(2):
         v = [value[128 * (3 * part + i) : 128 * (3 * part + i + 1), :] for i in range(3)]
-        su_ref[128 * part : 128 * (part + 1), :] = (v[0] + v[1]) + v[2]
-    loads[2].wait()
+        sigma_ref[128 * part : 128 * (part + 1), :] = (v[0] + v[1]) + v[2]
     near = pl.multiple_of(128 * odd, 128)
     far = pl.multiple_of(128 - 128 * odd, 128)
-    first_ref[...] = su_ref[pl.ds(near, 128), :]
-    second_ref[...] = su_ref[pl.ds(far, 128), :]
-
-
-def pick(at, blocks, root, upper):
+    first_ref[...] = sigma_ref[pl.ds(near, 128), :]
+    second_ref[...] = sigma_ref[pl.ds(far, 128), :]
+
+
+def pick(at, blocks, root):
     return pl.pallas_call(
         pick_kernel,
-        out_shape=(shape(512, 128), shape(128, 128), shape(128, 128)),
-        in_specs=[SMEM] + [HBM] * 3,
+        out_shape=(shape(256, 128), shape(128, 128), shape(128, 128)),
+        in_specs=[SMEM] + [HBM] * 2,
         out_specs=(VMEM, VMEM, VMEM),
         scratch_shapes=[
             pltpu.VMEM((32, 128), jnp.int32),
             pltpu.VMEM((512, 256), F32),
-            DMA((3,)),
+            DMA((2,)),
         ],
         compiler_params=WIDE,
-    )(at, blocks, root, upper)
+    )(at, blocks, root)
 
 
 def fan_kernel(first_ref, second_ref, copies_ref):
@@ -127,7 +125,7 @@
         )
         loads = [
             pltpu.make_async_copy(columns_hbm, right, sems.at[0]),
-            pltpu.make_async_copy(upper_hbm.at[:, 256:512], left, sems.at[1]),
+            pltpu.make_async_copy(upper_hbm, left, sems.at[1]),
         ]
         for load in loads:
             load.start()
@@ -169,26 +167,26 @@
             pltpu.VMEM((1024, 256), BF16),
             DMA((2,)),
         ],
-        compiler_params=NEAR,
+        compiler_params=PARAMS,
         cost_estimate=pl.CostEstimate(flops=3 << 28, bytes_accessed=3 << 20, transcendentals=0),
     )(at, upper, columns, *more)
 
 
 def side_kernel(
-    at_ref, su_hbm, lower_hbm, out_hbm, hi_hbm, lo_hbm, sigma, lower, ah, al, bh, bl, out, sems
+    at_ref, sigma_hbm, lower_hbm, out_hbm, hi_hbm, lo_hbm, sigma, lower, ah, al, bh, bl, out, sems
 ):
-    loads = [pltpu.make_async_copy(su_hbm.at[:, 0:256], sigma, sems.at[0])]
+    loads = [pltpu.make_async_copy(sigma_hbm, sigma, sems.at[0])]
     for i in range(2):
         rows = slice(8 * i, 8 * (i + 1))
         loads.append(pltpu.make_async_copy(lower_hbm.at[rows], lower.at[rows], sems.at[1 + i]))
     for load in loads:
         load.start()
-    _, _, _, _, x = device(at_ref)
+    _, _, _, z_at, x = device(at_ref)
     odd = x & 1
     loads[0].wait()
-    for z in range(8):
-        rows = slice(128 * z, 128 * (z + 1))
-        ah[:, rows], al[:, rows] = split2(sigma[z])
+    for k, flip in enumerate(ORDER):
+        cols = pl.ds(pl.multiple_of(128 * (z_at ^ flip), 128), 128)
+        ah[:, cols], al[:, cols] = split2(sigma[k])
     for z in range(8):
         if z % 4 == 0:
             loads[1 + z // 4].wait()
@@ -217,7 +215,7 @@
         store.wait()
 
 
-def side(at, gathered, lower):
+def side(at, sigma, lower):
     return pl.pallas_call(
         side_kernel,
         out_shape=(shape(4, 256, 128),) + (shape(1024, 512, dtype=BF16),) * 2,
@@ -235,7 +233,7 @@
         ],
         compiler_params=WIDE,
         cost_estimate=pl.CostEstimate(flops=6 << 28, bytes_accessed=6 << 20, transcendentals=0),
-    )(at, gathered, lower)
+    )(at, sigma, lower)
 
 
 def last_kernel(at_ref, w_hbm, hi_hbm, lo_hbm, out_hbm, w, ah, al, bh, bl, out, sems):
@@ -299,28 +297,33 @@
     return lax.ppermute(v, ("c", "x"), moves)
 
 
-def turn(v, axis, size, k):
-    return lax.ppermute(v, axis, [(i, (i + k) % size) for i in range(size)])
+def flip(v, axis, size, k):
+    return lax.ppermute(v, axis, [(i, i ^ k) for i in range(size)])
 
 
 def shards(root_inverse, boundary_map, lower_factor, upper_factor, diagonal_inverse):
     at = lax.axis_index(("y", "c", "z", "x")).astype(jnp.int32).reshape(1)
-    su, first, second = pick(at, boundary_map.reshape(32, 128), root_inverse, upper_factor)
-    gathered = lax.all_gather(su, "z", axis=0, tiled=False)
+    upper = lax.all_gather(upper_factor, "z", axis=0, tiled=False)
+    sigma, first, second = pick(at, boundary_map.reshape(32, 128), root_inverse)
     copies = fan(deal(first, 0), deal(second, 1))
-    copies, lower = lax.optimization_barrier((copies, lower_factor))
+    copies, lower, sigma = lax.optimization_barrier((copies, lower_factor, sigma))
     odd = lax.axis_index("x") & 1
     lower = [
         deal(lax.dynamic_slice_in_dim(lower, 128 * (odd ^ t), 128), t) for t in range(2)
     ]
-    lower = jnp.concatenate(lower, axis=0)
-    lower = lax.all_gather(lower, ("y", "c"), axis=0, tiled=False)
+    lower = lax.all_gather(jnp.concatenate(lower, axis=0), ("y", "c"), axis=0, tiled=False)
     own = exchange(copies, "y", 8)
-    other = turn(own, "c", 2, 1)
-    part = couple(at, gathered, other, couple(at, gathered, own))
-    w = exchange(part, "x", 4).sum(axis=0)
+    sigma = sigma[None]
+    for k in (4, 2):
+        sigma = jnp.concatenate([sigma, flip(sigma, "z", 8, k)], axis=0)
+    own, sigma = lax.optimization_barrier((own, sigma))
+    other = flip(own, "c", 2, 1)
+    sigma = jnp.concatenate([sigma, flip(sigma, "z", 8, 1)], axis=0)
+    part = exchange(couple(at, upper, other, couple(at, upper, own)), "x", 4)
+    part, sigma = lax.optimization_barrier((part, sigma))
+    w = part.sum(axis=0)
     w_all = exchange(jnp.broadcast_to(w[None], (8, 256, 128)), "z", 8)
-    sides, hi, lo = side(at, gathered, lower)
+    sides, hi, lo = side(at, sigma, lower)
     t = lax.psum_scatter(sides, "x", scatter_dimension=0, tiled=False)
     product = exchange(last(at, w_all, hi, lo), "x", 4).sum(axis=0)
     return (t, -w, diagonal_inverse + product)

time: 141 us -> 147 us (1.043); the launches traced: 140 us -> 144 us
  starting transfers between devices: 51.5 us -> 63.8 us
  blocking collectives: 8.7 us -> 0 us
    ppermute x1 -> x4, starting transfers between devices: 3.03 us -> 19.3 us  [flip(): return lax.ppermute(v, axis, [(i, i ^ k) for i in range(size)])]
    ppermute x1 -> x4, waiting for transfers between devices: 0.31 us -> 13.8 us  [flip(): return lax.ppermute(v, axis, [(i, i ^ k) for i in range(size)])]
    all_gather x2, waiting for transfers between devices: 16.2 us -> 6.67 us  [the longest x1 6.65 us: shards(): lax.all_gather(jnp.concatenate(lower, axis=0), ('y', 'c'), axis=0, tiled=...]
    all_to_all x1 -> x0, blocking collectives: 8.7 us -> none  [exchange(): return lax.all_to_all(v, axes, 0, 0, tiled=True, axis_index_groups=groups)]
    all_to_all x3 -> x4, starting transfers between devices: 34.9 us -> 30.2 us  [exchange(): return lax.all_to_all(v, axes, 0, 0, tiled=True, axis_index_groups=groups)]
    reduce_scatter x1, waiting for transfers between devices: 2.26 us -> 0.01 us  [shards(): t = lax.psum_scatter(sides, 'x', scatter_dimension=0, tiled=False)]
    all_to_all x3 -> x4, waiting for transfers between devices: 20.7 us -> 18.5 us  [exchange(): return lax.all_to_all(v, axes, 0, 0, tiled=True, axis_index_groups=groups)]
  transfers between devices with their start and end apart: 11 -> 15, of which waited for: 9 -> 10; matrix products, arithmetic and copies ran while one was open for 2% -> 3% of each run, Pallas kernels for 9% -> 9%
where the time goes in v8:
time: 147 us; the launch traced here: 144 us
  starting transfers between devices  63.8 us (43%)
  waiting for transfers between devices  47.7 us (32%)
  between operations  13.9 us (9%)
  Pallas kernels  13.1 us (9%)
  other arithmetic  3.16 us (2%)
  local copies, waits for them, and re-layouts  2.3 us (2%)
    all_to_all x4, starting transfers between devices, exchange(): return lax.all_to_all(v, axes, 0, 0, tiled=True, axis_index_groups=groups)  30.2 us
    ppermute x4, starting transfers between devices, flip(): return lax.ppermute(v, axis, [(i, i ^ k) for i in range(size)])  19.3 us
    all_to_all x4, waiting for transfers between devices, exchange(): return lax.all_to_all(v, axes, 0, 0, tiled=True, axis_index_groups=groups)  18.5 us
    ppermute x4, starting transfers between devices, deal(): return lax.ppermute(v, ('c', 'x'), moves)  14.3 us
    ppermute x4, waiting for transfers between devices, flip(): return lax.ppermute(v, axis, [(i, i ^ k) for i in range(size)])  13.8 us
    ppermute x4, waiting for transfers between devices, deal(): return lax.ppermute(v, ('c', 'x'), moves)  8.01 us
    all_gather x1, waiting for transfers between devices, shards(): lax.all_gather(jnp.concatenate(lower, axis=0), ('y', 'c'), axis=0, tiled=...  6.65 us
    pallas_call x1, Pallas kernels, side(): pl.pallas_call(side_kernel, out_shape=(shape(4, 256, 128),) + (shape(1024...  3.7 us
  transfers between devices with their start and end apart: 15, of which 10 were waited for; matrix products, arithmetic and copies ran while one was open for 3% of the time, Pallas kernels for 9%

profile of v8, /device:TPU:1, one launch (start us, length us, event | category | flops | bytes accessed | tf_op | source)
XLA Modules:
  0.0 144.0 jit_solution(4506704750538655571)
XLA Ops:
  7.2 0.0 copy-start.3
  7.2 0.0 all-gather.5.cloned.1.call-start
  7.2 0.7 all-gather.5.cloned.1.call-update
  7.9 2.2 %shard_map.76 = (f32[256,128]{1,0:T(8,128)}, f32[128,128]{1,0:T(8,128)}, f32[128,128]{1,0:T(8,128)}) custom-call(s32[1]{0:T(128)} %bitcast.at_ref, s32[32,128]{1,0:T(8,128)} %bitcast.11, f32[512,256]{1,0:T(8,128)} %root_hbm.1), custom_call_target="tpu_custom_call" | custom-call | tf_op jit(solution)/shard_map/pallas_call | solution.py:90
  10.2 0.0 copy-start.1
  10.2 6.2 %collective-permute-start = (f32[128,128]{1,0:T(8,128)}, f32[128,128]{1,0:T(8,128)S(1)}, u32[]{:S(2)}, u32[]{:S(2)}) collective-permute-start(f32[128,128]{1,0:T(8,128)} %get-tuple-element.16), channel_id=1, source_target_pairs={{0,0},{1,1},{2,32},{3,33},{32,2},{33,3},{34,34},{35,35},{4,4},{5,5... | collective-permute-start | bytes 196616 | tf_op jit(solution)/shard_map/ppermute | solution.py:297
  16.4 2.5 %collective-permute-start.1 = (f32[128,128]{1,0:T(8,128)}, f32[128,128]{1,0:T(8,128)S(1)}, u32[]{:S(2)}, u32[]{:S(2)}) collective-permute-start(f32[128,128]{1,0:T(8,128)} %get-tuple-element.17), channel_id=1, source_target_pairs={{0,1},{1,0},{2,33},{3,32},{32,3},{33,2},{34,35},{35,34},{4,5},{5,4... | collective-permute-start | bytes 196616 | tf_op jit(solution)/shard_map/ppermute | solution.py:297
  18.9 0.0 collective-permute-done.first_ref
  18.9 4.5 %collective-permute-done.1.second_ref = f32[128,128]{1,0:T(8,128)S(1)} collective-permute-done((f32[128,128]{1,0:T(8,128)}, f32[128,128]{1,0:T(8,128)S(1)}, u32[]{:S(2)}, u32[]{:S(2)}) %collective-permute-start.1) | collective-permute-done | bytes 65568 | tf_op jit(solution)/shard_map/ppermute | solution.py:297
  23.4 1.0 shard_map.77
  24.4 9.0 %all-to-all-start = ((f32[8,2,128,128]{3,2,1,0:T(8,128)}), f32[8,2,128,128]{3,2,1,0:T(8,128)S(1)}, u32[]{:S(2)}, u32[]{:S(2)}) async-start(f32[8,2,128,128]{3,2,1,0:T(8,128)} %shard_map.77), calls=%async_computation | async-start | bytes 2097152 | tf_op jit(solution)/shard_map/all_to_all | solution.py:292
  33.4 0.0 all-gather.7.cloned.1.call-start
  33.4 0.0 copy-done.3
  33.5 1.9 %collective-permute-start.6 = (f32[128,128]{1,0:T(8,128)S(1)}, f32[128,128]{1,0:T(8,128)S(1)}, u32[]{:S(2)}, u32[]{:S(2)}) collective-permute-start(f32[128,128]{1,0:T(8,128)S(1)} %get-tuple-element.29), channel_id=1, source_target_pairs={{0,0},{1,1},{2,32},{3,33},{32,2},{33,3},{34,34},{35,35},{4,4},{5,5... | collective-permute-start | bytes 196616 | tf_op jit(solution)/shard_map/ppermute | solution.py:297
  35.4 3.7 %collective-permute-start.7 = (f32[128,128]{1,0:T(8,128)S(1)}, f32[128,128]{1,0:T(8,128)S(1)}, u32[]{:S(2)}, u32[]{:S(2)}) collective-permute-start(f32[128,128]{1,0:T(8,128)S(1)} %get-tuple-element.30), channel_id=1, source_target_pairs={{0,1},{1,0},{2,33},{3,32},{32,3},{33,2},{34,35},{35,34},{4,5},{5,4... | collective-permute-start | bytes 196616 | tf_op jit(solution)/shard_map/ppermute | solution.py:297
  39.1 1.8 %collective-permute-done.6 = f32[128,128]{1,0:T(8,128)S(1)} collective-permute-done((f32[128,128]{1,0:T(8,128)S(1)}, f32[128,128]{1,0:T(8,128)S(1)}, u32[]{:S(2)}, u32[]{:S(2)}) %collective-permute-start.6) | collective-permute-done | bytes 65568 | tf_op jit(solution)/shard_map/ppermute | solution.py:297
  40.8 1.7 %collective-permute-done.7 = f32[128,128]{1,0:T(8,128)S(1)} collective-permute-done((f32[128,128]{1,0:T(8,128)S(1)}, f32[128,128]{1,0:T(8,128)S(1)}, u32[]{:S(2)}, u32[]{:S(2)}) %collective-permute-start.7) | collective-permute-done | bytes 65568 | tf_op jit(solution)/shard_map/ppermute | solution.py:297
  42.6 0.7 pad_maximum_fusion.3
  43.2 0.0 all-gather.7.cloned.1.call-update
  43.3 0.0 copy-done.1
  43.3 10.6 %collective-permute-start.2 = (f32[1,256,128]{2,1,0:T(8,128)S(1)}, f32[1,256,128]{2,1,0:T(8,128)S(1)}, u32[]{:S(2)}, u32[]{:S(2)}) collective-permute-start(f32[1,256,128]{2,1,0:T(8,128)S(1)} %bitcast.8), channel_id=1, source_target_pairs={{0,16},{4,20},{8,24},{12,28},{16,0},{20,4},{24,8},{28,12},{1,17},{... | collective-permute-start | bytes 393224 | tf_op jit(solution)/shard_map/ppermute | solution.py:301
  53.9 3.6 %collective-permute-done.2 = f32[1,256,128]{2,1,0:T(8,128)S(1)} collective-permute-done((f32[1,256,128]{2,1,0:T(8,128)S(1)}, f32[1,256,128]{2,1,0:T(8,128)S(1)}, u32[]{:S(2)}, u32[]{:S(2)}) %collective-permute-start.2) | collective-permute-done | bytes 131104 | tf_op jit(solution)/shard_map/ppermute | solution.py:301
  57.4 4.9 %collective-permute-start.3 = (f32[2,256,128]{2,1,0:T(8,128)S(1)}, f32[2,256,128]{2,1,0:T(8,128)S(1)}, u32[]{:S(2)}, u32[]{:S(2)}) collective-permute-start(f32[2,256,128]{2,1,0:T(8,128)S(1)} %pad_maximum_fusion.2), channel_id=1, source_target_pairs={{0,8},{4,12},{8,0},{12,4},{16,24},{20,28},{24,16},{28,20},{1,9},{5... | collective-permute-start | bytes 786440 | tf_op jit(solution)/shard_map/ppermute | solution.py:301
  62.3 7.9 %collective-permute-done.3 = f32[2,256,128]{2,1,0:T(8,128)S(1)} collective-permute-done((f32[2,256,128]{2,1,0:T(8,128)S(1)}, f32[2,256,128]{2,1,0:T(8,128)S(1)}, u32[]{:S(2)}, u32[]{:S(2)}) %collective-permute-start.3) | collective-permute-done | bytes 262176 | tf_op jit(solution)/shard_map/ppermute | solution.py:301
  70.3 0.0 all-to-all-done.columns_hbm
  70.3 1.9 %collective-permute-start.4 = (f32[8,2,128,128]{3,2,1,0:T(8,128)S(1)}, f32[8,2,128,128]{3,2,1,0:T(8,128)S(1)}, u32[]{:S(2)}, u32[]{:S(2)}) collective-permute-start(f32[8,2,128,128]{3,2,1,0:T(8,128)S(1)} %all-to-all-done.columns_hbm), channel_id=1, source_target_pairs={{0,32},{32,0},{1,33},{33,1},{2,34},{34,2},{3,35},{35,3},{4,36},{36... | collective-permute-start | bytes 3145736 | tf_op jit(solution)/shard_map/ppermute | solution.py:301
  72.2 1.9 %collective-permute-start.5 = (f32[4,256,128]{2,1,0:T(8,128)S(1)}, f32[4,256,128]{2,1,0:T(8,128)S(1)}, u32[]{:S(2)}, u32[]{:S(2)}) collective-permute-start(f32[4,256,128]{2,1,0:T(8,128)S(1)} %pad_maximum_fusion.1), channel_id=1, source_target_pairs={{0,4},{4,0},{8,12},{12,8},{16,20},{20,16},{24,28},{28,24},{1,5},{5... | collective-permute-start | bytes 1572872 | tf_op jit(solution)/shard_map/ppermute | solution.py:301
  74.1 0.0 all-gather.5.cloned.1.call-done
  74.2 1.2 copy-done
  75.4 0.9 shard_map.78.refs_0_
  76.3 0.0 collective-permute-done.4.columns_hbm
  76.4 1.7 %shard_map.79 = f32[4,256,128]{2,1,0:T(8,128)} custom-call(s32[1]{0:T(128)} %bitcast.at_ref, f32[8,256,128]{2,1,0:T(8,128)S(1)} %bitcast.7, f32[8,2,128,128]{3,2,1,0:T(8,128)S(1)} %collective-permute-done.4.columns_hbm, f32[2,256,128]{2,1,0:T(8,128)S(1)} %shard_map.78.refs_0_), custom_call_target="tpu_custom_call" | custom-call | flops 805306368 | bytes 3145728 | tf_op jit(solution)/shard_map/pallas_call | solution.py:156
  78.1 6.7 %all-to-all-start.1 = ((f32[4,256,128]{2,1,0:T(8,128)}), f32[4,256,128]{2,1,0:T(8,128)S(1)}, u32[]{:S(2)}, u32[]{:S(2)}) async-start(f32[4,256,128]{2,1,0:T(8,128)} %shard_map.79), calls=%async_computation.1 | async-start | bytes 1048576 | tf_op jit(solution)/shard_map/all_to_all | solution.py:292
  84.8 2.3 %collective-permute-done.5 = f32[4,256,128]{2,1,0:T(8,128)S(1)} collective-permute-done((f32[4,256,128]{2,1,0:T(8,128)S(1)}, f32[4,256,128]{2,1,0:T(8,128)S(1)}, u32[]{:S(2)}, u32[]{:S(2)}) %collective-permute-start.5) | collective-permute-done | bytes 524320 | tf_op jit(solution)/shard_map/ppermute | solution.py:301
  87.1 1.1 pad_maximum_fusion.sigma_hbm
  88.2 1.8 %all-to-all-done.1 = f32[4,256,128]{2,1,0:T(8,128)S(1)} async-done(((f32[4,256,128]{2,1,0:T(8,128)}), f32[4,256,128]{2,1,0:T(8,128)S(1)}, u32[]{:S(2)}, u32[]{:S(2)}) %all-to-all-start.1) | async-done | bytes 524320 | tf_op jit(solution)/shard_map/all_to_all | solution.py:292
  90.0 1.1 broadcast_in_dim.10
  91.0 9.1 %all-to-all-start.2 = ((f32[8,256,128]{2,1,0:T(8,128)}), f32[8,256,128]{2,1,0:T(8,128)S(1)}, u32[]{:S(2)}, u32[]{:S(2)}) async-start(f32[8,256,128]{2,1,0:T(8,128)} %broadcast_in_dim.10), calls=%async_computation.3 | async-start | bytes 2097152 | tf_op jit(solution)/shard_map/all_to_all | solution.py:292
  100.1 6.6 %all-gather.7.cloned.1.call-done = f32[4096,128]{1,0:T(8,128)} async-done(((f32[256,128]{1,0:T(8,128)}), f32[4096,128]{1,0:T(8,128)}) %all-gather.7.cloned.1.call-update) | async-done | bytes 2097168 | tf_op jit(solution)/shard_map/all_gather | solution.py:314
  106.8 3.7 %shard_map.80 = (f32[4,256,128]{2,1,0:T(8,128)}, bf16[1024,512]{1,0:T(8,128)(2,1)}, bf16[1024,512]{1,0:T(8,128)(2,1)}) custom-call(s32[1]{0:T(128)} %bitcast.at_ref, f32[8,256,128]{2,1,0:T(8,128)} %pad_maximum_fusion.sigma_hbm, f32[16,256,128]{2,1,0:T(8,128)} %bitcast.12), custom_call_target="tpu_custom_call" | custom-call | flops 1610612736 | bytes 6291456 | tf_op jit(solution)/shard_map/pallas_call | solution.py:219
  110.5 0.0 reduce-scatter.2.cloned.1.call-update
  110.5 11.3 %all-to-all-done.2.w_hbm = f32[8,256,128]{2,1,0:T(8,128)S(1)} async-done(((f32[8,256,128]{2,1,0:T(8,128)}), f32[8,256,128]{2,1,0:T(8,128)S(1)}, u32[]{:S(2)}, u32[]{:S(2)}) %all-to-all-start.2) | async-done | bytes 1048608 | tf_op jit(solution)/shard_map/all_to_all | solution.py:292
  121.9 3.4 %shard_map.81 = f32[4,256,128]{2,1,0:T(8,128)} custom-call(s32[1]{0:T(128)} %bitcast.at_ref, f32[8,256,128]{2,1,0:T(8,128)S(1)} %all-to-all-done.2.w_hbm, bf16[1024,512]{1,0:T(8,128)(2,1)} %get-tuple-element.27.hi_hbm, bf16[1024,512]{1,0:T(8,128)(2,1)} %get-tuple-element.28.lo_hbm), custom_call_target="tpu_custom_call" | custom-call | tf_op jit(solution)/shard_map/pallas_call | solution.py:268
  125.3 5.4 %all-to-all-start.3 = ((f32[4,256,128]{2,1,0:T(8,128)}), f32[4,256,128]{2,1,0:T(8,128)S(1)}, u32[]{:S(2)}, u32[]{:S(2)}) async-start(f32[4,256,128]{2,1,0:T(8,128)} %shard_map.81), calls=%async_computation.4 | async-start | bytes 1048576 | tf_op jit(solution)/shard_map/all_to_all | solution.py:292
  130.7 0.7 neg.3
  131.4 5.4 %all-to-all-done.3 = f32[4,256,128]{2,1,0:T(8,128)S(1)} async-done(((f32[4,256,128]{2,1,0:T(8,128)}), f32[4,256,128]{2,1,0:T(8,128)S(1)}, u32[]{:S(2)}, u32[]{:S(2)}) %all-to-all-start.3) | async-done | bytes 524320 | tf_op jit(solution)/shard_map/all_to_all | solution.py:292
  136.8 0.0 copy-done.2
  136.8 0.7 add.25
  (9 shorter events, 0.1 us)
Async XLA Ops:
  7.2 26.3 %copy-start.3 = (f32[256,128]{1,0:T(8,128)S(1)}, f32[256,128]{1,0:T(8,128)}, u32[]{:S(2)}) copy-start(f32[256,128]{1,0:T(8,128)} %param.7) | copy-start | bytes 393220
  7.2 67.0 %all-gather.5.cloned.1.call-start = ((), (), s32[]{:S(2)}) async-start(), calls=%async_computation.6 | async-start | bytes 1179648 | tf_op jit(solution)/shard_map/all_gather | solution.py:306
  10.2 33.1 %copy-start.1 = (f32[256,128]{1,0:T(8,128)S(1)}, f32[256,128]{1,0:T(8,128)}, u32[]{:S(2)}) copy-start(f32[256,128]{1,0:T(8,128)} %get-tuple-element.20) | copy-start | bytes 393220
  10.2 8.7 %collective-permute-start = (f32[128,128]{1,0:T(8,128)}, f32[128,128]{1,0:T(8,128)S(1)}, u32[]{:S(2)}, u32[]{:S(2)}) collective-permute-start(f32[128,128]{1,0:T(8,128)} %get-tuple-element.16), channel_id=1, source_target_pairs={{0,0},{1,1},{2,32},{3,33},{32,2},{33,3},{34,34},{35,35},{4,4},{5,5... | collective-permute-start | bytes 196616 | tf_op jit(solution)/shard_map/ppermute | solution.py:297
  16.4 7.0 %collective-permute-start.1 = (f32[128,128]{1,0:T(8,128)}, f32[128,128]{1,0:T(8,128)S(1)}, u32[]{:S(2)}, u32[]{:S(2)}) collective-permute-start(f32[128,128]{1,0:T(8,128)} %get-tuple-element.17), channel_id=1, source_target_pairs={{0,1},{1,0},{2,33},{3,32},{32,3},{33,2},{34,35},{35,34},{4,5},{5,4... | collective-permute-start | bytes 196616 | tf_op jit(solution)/shard_map/ppermute | solution.py:297
  24.4 45.9 %all-to-all-start = ((f32[8,2,128,128]{3,2,1,0:T(8,128)}), f32[8,2,128,128]{3,2,1,0:T(8,128)S(1)}, u32[]{:S(2)}, u32[]{:S(2)}) async-start(f32[8,2,128,128]{3,2,1,0:T(8,128)} %shard_map.77), calls=%async_computation | async-start | bytes 2097152 | tf_op jit(solution)/shard_map/all_to_all | solution.py:292
  33.4 73.4 %all-gather.7.cloned.1.call-start = ((), (), s32[]{:S(2)}) async-start(), calls=%async_computation.7 | async-start | bytes 2228224 | tf_op jit(solution)/shard_map/all_gather | solution.py:314
  33.5 7.4 %collective-permute-start.6 = (f32[128,128]{1,0:T(8,128)S(1)}, f32[128,128]{1,0:T(8,128)S(1)}, u32[]{:S(2)}, u32[]{:S(2)}) collective-permute-start(f32[128,128]{1,0:T(8,128)S(1)} %get-tuple-element.29), channel_id=1, source_target_pairs={{0,0},{1,1},{2,32},{3,33},{32,2},{33,3},{34,34},{35,35},{4,4},{5,5... | collective-permute-start | bytes 196616 | tf_op jit(solution)/shard_map/ppermute | solution.py:297
  35.4 7.2 %collective-permute-start.7 = (f32[128,128]{1,0:T(8,128)S(1)}, f32[128,128]{1,0:T(8,128)S(1)}, u32[]{:S(2)}, u32[]{:S(2)}) collective-permute-start(f32[128,128]{1,0:T(8,128)S(1)} %get-tuple-element.30), channel_id=1, source_target_pairs={{0,1},{1,0},{2,33},{3,32},{32,3},{33,2},{34,35},{35,34},{4,5},{5,4... | collective-permute-start | bytes 196616 | tf_op jit(solution)/shard_map/ppermute | solution.py:297
  43.3 14.1 %collective-permute-start.2 = (f32[1,256,128]{2,1,0:T(8,128)S(1)}, f32[1,256,128]{2,1,0:T(8,128)S(1)}, u32[]{:S(2)}, u32[]{:S(2)}) collective-permute-start(f32[1,256,128]{2,1,0:T(8,128)S(1)} %bitcast.8), channel_id=1, source_target_pairs={{0,16},{4,20},{8,24},{12,28},{16,0},{20,4},{24,8},{28,12},{1,17},{... | collective-permute-start | bytes 393224 | tf_op jit(solution)/shard_map/ppermute | solution.py:301
  57.4 12.8 %collective-permute-start.3 = (f32[2,256,128]{2,1,0:T(8,128)S(1)}, f32[2,256,128]{2,1,0:T(8,128)S(1)}, u32[]{:S(2)}, u32[]{:S(2)}) collective-permute-start(f32[2,256,128]{2,1,0:T(8,128)S(1)} %pad_maximum_fusion.2), channel_id=1, source_target_pairs={{0,8},{4,12},{8,0},{12,4},{16,24},{20,28},{24,16},{28,20},{1,9},{5... | collective-permute-start | bytes 786440 | tf_op jit(solution)/shard_map/ppermute | solution.py:301
  70.3 6.1 %collective-permute-start.4 = (f32[8,2,128,128]{3,2,1,0:T(8,128)S(1)}, f32[8,2,128,128]{3,2,1,0:T(8,128)S(1)}, u32[]{:S(2)}, u32[]{:S(2)}) collective-permute-start(f32[8,2,128,128]{3,2,1,0:T(8,128)S(1)} %all-to-all-done.columns_hbm), channel_id=1, source_target_pairs={{0,32},{32,0},{1,33},{33,1},{2,34},{34,2},{3,35},{35,3},{4,36},{36... | collective-permute-start | bytes 3145736 | tf_op jit(solution)/shard_map/ppermute | solution.py:301
  72.2 14.9 %collective-permute-start.5 = (f32[4,256,128]{2,1,0:T(8,128)S(1)}, f32[4,256,128]{2,1,0:T(8,128)S(1)}, u32[]{:S(2)}, u32[]{:S(2)}) collective-permute-start(f32[4,256,128]{2,1,0:T(8,128)S(1)} %pad_maximum_fusion.1), channel_id=1, source_target_pairs={{0,4},{4,0},{8,12},{12,8},{16,20},{20,16},{24,28},{28,24},{1,5},{5... | collective-permute-start | bytes 1572872 | tf_op jit(solution)/shard_map/ppermute | solution.py:301
  74.2 1.2 copy-start
  78.1 11.9 %all-to-all-start.1 = ((f32[4,256,128]{2,1,0:T(8,128)}), f32[4,256,128]{2,1,0:T(8,128)S(1)}, u32[]{:S(2)}, u32[]{:S(2)}) async-start(f32[4,256,128]{2,1,0:T(8,128)} %shard_map.79), calls=%async_computation.1 | async-start | bytes 1048576 | tf_op jit(solution)/shard_map/all_to_all | solution.py:292
  91.0 30.8 %all-to-all-start.2 = ((f32[8,256,128]{2,1,0:T(8,128)}), f32[8,256,128]{2,1,0:T(8,128)S(1)}, u32[]{:S(2)}, u32[]{:S(2)}) async-start(f32[8,256,128]{2,1,0:T(8,128)} %broadcast_in_dim.10), calls=%async_computation.3 | async-start | bytes 2097152 | tf_op jit(solution)/shard_map/all_to_all | solution.py:292
  100.1 37.4 %reduce-scatter.2.cloned.1.call-start = ((), (), s32[]{:S(2)}) async-start(), calls=%async_computation.5 | async-start | bytes 655360 | tf_op jit(solution)/shard_map/reduce_scatter | solution.py:327
  121.9 15.0 %copy-start.2 = (f32[256,128]{1,0:T(8,128)S(1)}, f32[256,128]{1,0:T(8,128)}, u32[]{:S(2)}) copy-start(f32[256,128]{1,0:T(8,128)} %param.9) | copy-start | bytes 393220
  125.3 11.5 %all-to-all-start.3 = ((f32[4,256,128]{2,1,0:T(8,128)}), f32[4,256,128]{2,1,0:T(8,128)S(1)}, u32[]{:S(2)}, u32[]{:S(2)}) async-start(f32[4,256,128]{2,1,0:T(8,128)} %shard_map.81), calls=%async_computation.4 | async-start | bytes 1048576 | tf_op jit(solution)/shard_map/all_to_all | solution.py:292
Sparse Core Ops, SparseCore 0:
  10.1 44.1 all-gather.4
  57.0 49.7 all-gather.6
  110.7 23.7 reduce-scatter.1

commit v9 on v7

--- a/solution.py
+++ b/solution.py
@@ -120,58 +120,56 @@
     )(first, second)
 
 
-def couple(at, upper, columns, before=None):
-    def kernel(at_ref, upper_hbm, columns_hbm, *refs):
-        before_ref, (out_ref, left, right, ah, al, bh, bl, sems) = (
-            (None, refs) if before is None else (refs[0], refs[1:])
-        )
-        loads = [
-            pltpu.make_async_copy(columns_hbm, right, sems.at[0]),
-            pltpu.make_async_copy(upper_hbm.at[:, 256:512], left, sems.at[1]),
-        ]
-        for load in loads:
-            load.start()
-        _, _, core, _, x = device(at_ref)
-        odd = x & 1
-        side = core if before is None else 1 - core
-        loads[0].wait()
+def couple_kernel(
+    at_ref, gathered_hbm, own_hbm, other_hbm, out_ref, left, own, other, ah, al, bh, bl, sems
+):
+    loads = [
+        pltpu.make_async_copy(own_hbm, own, sems.at[0]),
+        pltpu.make_async_copy(other_hbm, other, sems.at[1]),
+        pltpu.make_async_copy(gathered_hbm.at[:, 256:512], left, sems.at[2]),
+    ]
+    for load in loads:
+        load.start()
+    _, _, core, _, x = device(at_ref)
+    odd = x & 1
+    for n, right in enumerate((own, other)):
+        loads[n].wait()
+        side = core if n == 0 else 1 - core
         for z in range(8):
             rows = slice(128 * z, 128 * (z + 1))
             for t in range(2):
-                cols = slice(128 * t, 128 * (t + 1))
+                cols = slice(256 * n + 128 * t, 256 * n + 128 * (t + 1))
                 bh[rows, cols], bl[rows, cols] = split2(right[z ^ (4 * side), t])
-        loads[1].wait()
-        for z in range(8):
-            rows = slice(128 * z, 128 * (z + 1))
-            ah[:, rows], al[:, rows] = split2(left[z])
-        part = three_pass(ah[...], al[...], bh[...], bl[...])
-        if before is None:
-            out_ref[0] = part[:, :128]
-            out_ref[1] = part[:, 128:]
-        else:
-            out_ref[odd] = before_ref[0]
-            out_ref[1 - odd] = before_ref[1]
-            out_ref[2 + odd] = part[:, :128]
-            out_ref[3 - odd] = part[:, 128:]
-
-    more = () if before is None else (before,)
-    return pl.pallas_call(
-        kernel,
-        out_shape=shape(2 + 2 * len(more), 256, 128),
-        in_specs=[SMEM, HBM, HBM] + [VMEM] * len(more),
+    loads[2].wait()
+    for z in range(8):
+        rows = slice(128 * z, 128 * (z + 1))
+        ah[:, rows], al[:, rows] = split2(left[z ^ (4 * core)])
+    for n in range(2):
+        cols = slice(256 * n, 256 * (n + 1))
+        part = three_pass(ah[...], al[...], bh[:, cols], bl[:, cols])
+        out_ref[2 * n + odd] = part[:, :128]
+        out_ref[2 * n + 1 - odd] = part[:, 128:]
+
+
+def couple(at, gathered, own, other):
+    return pl.pallas_call(
+        couple_kernel,
+        out_shape=shape(4, 256, 128),
+        in_specs=[SMEM, HBM, HBM, HBM],
         out_specs=VMEM,
         scratch_shapes=[
             pltpu.VMEM((8, 256, 128), F32),
             pltpu.VMEM((8, 2, 128, 128), F32),
-            pltpu.VMEM((256, 1024), BF16),
-            pltpu.VMEM((256, 1024), BF16),
-            pltpu.VMEM((1024, 256), BF16),
-            pltpu.VMEM((1024, 256), BF16),
-            DMA((2,)),
+            pltpu.VMEM((8, 2, 128, 128), F32),
+            pltpu.VMEM((256, 1024), BF16),
+            pltpu.VMEM((256, 1024), BF16),
+            pltpu.VMEM((1024, 512), BF16),
+            pltpu.VMEM((1024, 512), BF16),
+            DMA((3,)),
         ],
         compiler_params=NEAR,
-        cost_estimate=pl.CostEstimate(flops=3 << 28, bytes_accessed=3 << 20, transcendentals=0),
-    )(at, upper, columns, *more)
+        cost_estimate=pl.CostEstimate(flops=6 << 28, bytes_accessed=3 << 20, transcendentals=0),
+    )(at, gathered, own, other)
 
 
 def side_kernel(
@@ -179,16 +177,18 @@
 ):
     loads = [pltpu.make_async_copy(su_hbm.at[:, 0:256], sigma, sems.at[0])]
     for i in range(2):
-        rows = slice(8 * i, 8 * (i + 1))
-        loads.append(pltpu.make_async_copy(lower_hbm.at[rows], lower.at[rows], sems.at[1 + i]))
+        rows = slice(4 * i, 4 * (i + 1))
+        loads.append(
+            pltpu.make_async_copy(lower_hbm.at[:, rows], lower.at[:, rows], sems.at[1 + i])
+        )
     for load in loads:
         load.start()
-    _, _, _, _, x = device(at_ref)
+    _, _, core_at, _, x = device(at_ref)
     odd = x & 1
     loads[0].wait()
     for z in range(8):
         rows = slice(128 * z, 128 * (z + 1))
-        ah[:, rows], al[:, rows] = split2(sigma[z])
+        ah[:, rows], al[:, rows] = split2(sigma[z ^ (4 * core_at)])
     for z in range(8):
         if z % 4 == 0:
             loads[1 + z // 4].wait()
@@ -197,7 +197,7 @@
             for t in range(2):
                 cols = slice(256 * core + 128 * t, 256 * core + 128 * (t + 1))
                 place = 128 * (odd if t == 0 else 1 - odd)
-                value = lower[2 * z + core, pl.ds(pl.multiple_of(place, 128), 128), :]
+                value = lower[core, z, pl.ds(pl.multiple_of(place, 128), 128), :]
                 bh[rows, cols], bl[rows, cols] = split2(value)
     stores = [
         pltpu.make_async_copy(bh, hi_hbm, sems.at[3]),
@@ -210,8 +210,8 @@
         part = -three_pass(ah[...], al[...], bh[:, cols], bl[:, cols])
         out[2 * n] = part[:, :128]
         out[2 * n + 1] = part[:, 128:]
-        pair = slice(2 * n, 2 * n + 2)
-        stores.append(pltpu.make_async_copy(out.at[pair], out_hbm.at[pair], sems.at[5 + n]))
+        pair, place = slice(2 * n, 2 * n + 2), pl.ds(2 * (n ^ core_at), 2)
+        stores.append(pltpu.make_async_copy(out.at[pair], out_hbm.at[place], sems.at[5 + n]))
         stores[-1].start()
     for store in stores:
         store.wait()
@@ -225,7 +225,7 @@
         out_specs=(HBM,) * 3,
         scratch_shapes=[
             pltpu.VMEM((8, 256, 128), F32),
-            pltpu.VMEM((16, 256, 128), F32),
+            pltpu.VMEM((2, 8, 256, 128), F32),
             pltpu.VMEM((256, 1024), BF16),
             pltpu.VMEM((256, 1024), BF16),
             pltpu.VMEM((1024, 512), BF16),
@@ -285,12 +285,17 @@
     )(at, w, hi, lo)
 
 
-def exchange(v, axis, size):
+def rotated(axis, size):
     axes = (axis, "c") if axis == "y" else ("c", axis)
     groups = [
         [2 * p + c if axis == "y" else size * c + p for p in (i ^ (size // 2 * c) for i in range(size))]
         for c in range(2)
     ]
+    return axes, groups
+
+
+def exchange(v, axis, size):
+    axes, groups = rotated(axis, size)
     return lax.all_to_all(v, axes, 0, 0, tiled=True, axis_index_groups=groups)
 
 
@@ -306,7 +311,8 @@
 def shards(root_inverse, boundary_map, lower_factor, upper_factor, diagonal_inverse):
     at = lax.axis_index(("y", "c", "z", "x")).astype(jnp.int32).reshape(1)
     su, first, second = pick(at, boundary_map.reshape(32, 128), root_inverse, upper_factor)
-    gathered = lax.all_gather(su, "z", axis=0, tiled=False)
+    axes, groups = rotated("z", 8)
+    gathered = lax.all_gather(su, axes, axis=0, tiled=False, axis_index_groups=groups)
     copies = fan(deal(first, 0), deal(second, 1))
     copies, lower = lax.optimization_barrier((copies, lower_factor))
     odd = lax.axis_index("x") & 1
@@ -314,14 +320,19 @@
         deal(lax.dynamic_slice_in_dim(lower, 128 * (odd ^ t), 128), t) for t in range(2)
     ]
     lower = jnp.concatenate(lower, axis=0)
-    lower = lax.all_gather(lower, ("y", "c"), axis=0, tiled=False)
+    groups = [[2 * i + core for core in range(2) for i in range(8)]]
+    lower = lax.all_gather(lower, ("y", "c"), axis=0, tiled=False, axis_index_groups=groups)
+    lower = lower.reshape(2, 8, 256, 128)
     own = exchange(copies, "y", 8)
     other = turn(own, "c", 2, 1)
-    part = couple(at, gathered, other, couple(at, gathered, own))
+    part = couple(at, gathered, own, other)
     w = exchange(part, "x", 4).sum(axis=0)
     w_all = exchange(jnp.broadcast_to(w[None], (8, 256, 128)), "z", 8)
     sides, hi, lo = side(at, gathered, lower)
-    t = lax.psum_scatter(sides, "x", scatter_dimension=0, tiled=False)
+    axes, groups = rotated("x", 4)
+    t = lax.psum_scatter(
+        sides.reshape(1024, 128), axes, scatter_dimension=0, tiled=True, axis_index_groups=groups
+    )
     product = exchange(last(at, w_all, hi, lo), "x", 4).sum(axis=0)
     return (t, -w, diagonal_inverse + product)
 

time: 141 us -> 141 us (level)
  waiting for transfers between devices: 48.2 us -> 52.3 us
  starting transfers between devices: 51.5 us -> 48.7 us
  Pallas kernels: 14.4 us -> 12.9 us
    reduce_scatter x1, waiting for transfers between devices: 2.26 us -> 7.51 us  [shards(): lax.psum_scatter(sides.reshape(1024, 128), axes, scatter_dimension=0, til...]
    all_to_all x3, starting transfers between devices: 34.9 us -> 31.5 us  [exchange(): return lax.all_to_all(v, axes, 0, 0, tiled=True, axis_index_groups=groups)]
    ppermute x1, waiting for transfers between devices: 0.31 us -> 2.26 us  [turn(): return lax.ppermute(v, axis, [(i, (i + k) % size) for i in range(size)])]
    all_to_all x3, waiting for transfers between devices: 20.7 us -> 18.9 us  [exchange(): return lax.all_to_all(v, axes, 0, 0, tiled=True, axis_index_groups=groups)]
    pallas_call x2 -> x1, Pallas kernels: 3.85 us -> 2.39 us  [couple(): pl.pallas_call(couple_kernel, out_shape=shape(4, 256, 128), in_specs=[SME...]
  transfers between devices with their start and end apart: 11 -> 11, of which waited for: 9 -> 9; matrix products, arithmetic and copies ran while one was open for 2% -> 2% of each run, Pallas kernels for 9% -> 8%
where the time goes in v9:
time: 141 us; the launch traced here: 139 us
  waiting for transfers between devices  52.3 us (37%)
  starting transfers between devices  48.7 us (35%)
  between operations  13.9 us (10%)
  Pallas kernels  12.9 us (9%)
  blocking collectives  8.29 us (6%)
  other arithmetic  2.05 us (1%)
    all_to_all x3, starting transfers between devices, exchange(): return lax.all_to_all(v, axes, 0, 0, tiled=True, axis_index_groups=groups)  31.5 us
    all_to_all x3, waiting for transfers between devices, exchange(): return lax.all_to_all(v, axes, 0, 0, tiled=True, axis_index_groups=groups)  18.9 us
    all_gather x1, waiting for transfers between devices, shards(): lax.all_gather(lower, ('y', 'c'), axis=0, tiled=False, axis_index_groups=...  15.7 us
    ppermute x4, starting transfers between devices, deal(): return lax.ppermute(v, ('c', 'x'), moves)  14.1 us
    all_to_all x1, blocking collectives, exchange(): return lax.all_to_all(v, axes, 0, 0, tiled=True, axis_index_groups=groups)  8.29 us
    ppermute x4, waiting for transfers between devices, deal(): return lax.ppermute(v, ('c', 'x'), moves)  7.91 us
    reduce_scatter x1, waiting for transfers between devices, shards(): lax.psum_scatter(sides.reshape(1024, 128), axes, scatter_dimension=0, til...  7.51 us
    pallas_call x1, Pallas kernels, side(): pl.pallas_call(side_kernel, out_shape=(shape(4, 256, 128),) + (shape(1024...  3.71 us
  transfers between devices with their start and end apart: 11, of which 9 were waited for; matrix products, arithmetic and copies ran while one was open for 2% of the time, Pallas kernels for 8%

profile of v9, /device:TPU:1, one launch (start us, length us, event | category | flops | bytes accessed | tf_op | source)
XLA Modules:
  0.0 139.2 jit_solution(11896076132324002432)
XLA Ops:
  7.2 0.0 all-gather.5.cloned.1.call-start
  7.2 0.0 copy-start.1
  7.2 2.3 %shard_map.76 = (f32[512,128]{1,0:T(8,128)}, f32[128,128]{1,0:T(8,128)}, f32[128,128]{1,0:T(8,128)}) custom-call(s32[1]{0:T(128)} %bitcast.at_ref, s32[32,128]{1,0:T(8,128)} %bitcast.6, f32[512,256]{1,0:T(8,128)} %root_hbm.1, f32[256,128]{1,0:T(8,128)} %upper_hbm.1), custom_call_target="tpu_custom_call" | custom-call | tf_op jit(solution)/shard_map/pallas_call | solution.py:92
  9.6 0.0 all-gather.5.cloned.1.call-update
  9.6 6.0 %collective-permute-start = (f32[128,128]{1,0:T(8,128)}, f32[128,128]{1,0:T(8,128)S(1)}, u32[]{:S(2)}, u32[]{:S(2)}) collective-permute-start(f32[128,128]{1,0:T(8,128)} %get-tuple-element.12), channel_id=1, source_target_pairs={{0,0},{1,1},{2,32},{3,33},{32,2},{33,3},{34,34},{35,35},{4,4},{5,5... | collective-permute-start | bytes 196616 | tf_op jit(solution)/shard_map/ppermute | solution.py:304
  15.6 2.5 %collective-permute-start.1 = (f32[128,128]{1,0:T(8,128)}, f32[128,128]{1,0:T(8,128)S(1)}, u32[]{:S(2)}, u32[]{:S(2)}) collective-permute-start(f32[128,128]{1,0:T(8,128)} %get-tuple-element.13), channel_id=1, source_target_pairs={{0,1},{1,0},{2,33},{3,32},{32,3},{33,2},{34,35},{35,34},{4,5},{5,4... | collective-permute-start | bytes 196616 | tf_op jit(solution)/shard_map/ppermute | solution.py:304
  18.1 0.0 collective-permute-done.first_ref
  18.1 4.5 %collective-permute-done.1.second_ref = f32[128,128]{1,0:T(8,128)S(1)} collective-permute-done((f32[128,128]{1,0:T(8,128)}, f32[128,128]{1,0:T(8,128)S(1)}, u32[]{:S(2)}, u32[]{:S(2)}) %collective-permute-start.1) | collective-permute-done | bytes 65568 | tf_op jit(solution)/shard_map/ppermute | solution.py:304
  22.6 1.1 shard_map.77
  23.7 9.0 %all-to-all-start = ((f32[8,2,128,128]{3,2,1,0:T(8,128)}), f32[8,2,128,128]{3,2,1,0:T(8,128)S(1)}, u32[]{:S(2)}, u32[]{:S(2)}) async-start(f32[8,2,128,128]{3,2,1,0:T(8,128)} %shard_map.77), calls=%async_computation.1 | async-start | bytes 2097152 | tf_op jit(solution)/shard_map/all_to_all | solution.py:299
  32.7 0.0 all-gather.7.cloned.1.call-start
  32.7 0.0 copy-done.1
  32.7 1.9 %collective-permute-start.2 = (f32[128,128]{1,0:T(8,128)S(1)}, f32[128,128]{1,0:T(8,128)S(1)}, u32[]{:S(2)}, u32[]{:S(2)}) collective-permute-start(f32[128,128]{1,0:T(8,128)S(1)} %get-tuple-element.19), channel_id=1, source_target_pairs={{0,0},{1,1},{2,32},{3,33},{32,2},{33,3},{34,34},{35,35},{4,4},{5,5... | collective-permute-start | bytes 196616 | tf_op jit(solution)/shard_map/ppermute | solution.py:304
  34.7 3.7 %collective-permute-start.3 = (f32[128,128]{1,0:T(8,128)S(1)}, f32[128,128]{1,0:T(8,128)S(1)}, u32[]{:S(2)}, u32[]{:S(2)}) collective-permute-start(f32[128,128]{1,0:T(8,128)S(1)} %get-tuple-element.20), channel_id=1, source_target_pairs={{0,1},{1,0},{2,33},{3,32},{32,3},{33,2},{34,35},{35,34},{4,5},{5,4... | collective-permute-start | bytes 196616 | tf_op jit(solution)/shard_map/ppermute | solution.py:304
  38.4 1.8 %collective-permute-done.2 = f32[128,128]{1,0:T(8,128)S(1)} collective-permute-done((f32[128,128]{1,0:T(8,128)S(1)}, f32[128,128]{1,0:T(8,128)S(1)}, u32[]{:S(2)}, u32[]{:S(2)}) %collective-permute-start.2) | collective-permute-done | bytes 65568 | tf_op jit(solution)/shard_map/ppermute | solution.py:304
  40.1 1.6 %collective-permute-done.3 = f32[128,128]{1,0:T(8,128)S(1)} collective-permute-done((f32[128,128]{1,0:T(8,128)S(1)}, f32[128,128]{1,0:T(8,128)S(1)}, u32[]{:S(2)}, u32[]{:S(2)}) %collective-permute-start.3) | collective-permute-done | bytes 65568 | tf_op jit(solution)/shard_map/ppermute | solution.py:304
  41.8 0.7 pad_maximum_fusion
  42.4 0.0 all-gather.7.cloned.1.call-update
  42.4 11.0 %all-to-all-done.own_hbm = f32[8,2,128,128]{3,2,1,0:T(8,128)S(1)} async-done(((f32[8,2,128,128]{3,2,1,0:T(8,128)}), f32[8,2,128,128]{3,2,1,0:T(8,128)S(1)}, u32[]{:S(2)}, u32[]{:S(2)}) %all-to-all-start) | async-done | bytes 1048608 | tf_op jit(solution)/shard_map/all_to_all | solution.py:299
  53.5 3.0 %collective-permute-start.4 = (f32[8,2,128,128]{3,2,1,0:T(8,128)S(1)}, f32[8,2,128,128]{3,2,1,0:T(8,128)S(1)}, u32[]{:S(2)}, u32[]{:S(2)}) collective-permute-start(f32[8,2,128,128]{3,2,1,0:T(8,128)S(1)} %all-to-all-done.own_hbm), channel_id=1, source_target_pairs={{0,32},{32,0},{1,33},{33,1},{2,34},{34,2},{3,35},{35,3},{4,36},{36... | collective-permute-start | bytes 3145736 | tf_op jit(solution)/shard_map/ppermute | solution.py:308
  56.5 2.3 %collective-permute-done.4.other_hbm = f32[8,2,128,128]{3,2,1,0:T(8,128)S(1)} collective-permute-done((f32[8,2,128,128]{3,2,1,0:T(8,128)S(1)}, f32[8,2,128,128]{3,2,1,0:T(8,128)S(1)}, u32[]{:S(2)}, u32[]{:S(2)}) %collective-permute-start.4) | collective-permute-done | bytes 1048608 | tf_op jit(solution)/shard_map/ppermute | solution.py:308
  58.8 0.0 all-gather.5.cloned.1.call-done
  58.8 2.4 %shard_map.79 = f32[4,256,128]{2,1,0:T(8,128)S(1)} custom-call(s32[1]{0:T(128)} %bitcast.at_ref, f32[8,512,128]{2,1,0:T(8,128)} %bitcast.7, f32[8,2,128,128]{3,2,1,0:T(8,128)S(1)} %all-to-all-done.own_hbm, f32[8,2,128,128]{3,2,1,0:T(8,128)S(1)} %collective-permute-done.4.other_hbm), custom_call_target="tpu_custom_call" | custom-call | flops 1610612736 | bytes 3145728 | tf_op jit(solution)/shard_map/pallas_call | solution.py:155
  61.2 8.3 %all_to_all.20 = f32[4,256,128]{2,1,0:T(8,128)S(1)} all-to-all(f32[4,256,128]{2,1,0:T(8,128)S(1)} %shard_map.79), channel_id=1, replica_groups={{0,1,2,3},{34,35,32,33},{4,5,6,7},{38,39,36,37},{8,9,10,11},{42,43,40,4..., dimensions={0} | all-to-all | bytes 1048576 | tf_op jit(solution)/shard_map/all_to_all | solution.py:299
  69.5 1.1 broadcast_in_dim.2
  70.6 17.1 %all-to-all-start.2 = ((f32[8,256,128]{2,1,0:T(8,128)}), f32[8,256,128]{2,1,0:T(8,128)S(1)}, u32[]{:S(2)}, u32[]{:S(2)}) async-start(f32[8,256,128]{2,1,0:T(8,128)} %broadcast_in_dim.2), calls=%async_computation.3 | async-start | bytes 2097152 | tf_op jit(solution)/shard_map/all_to_all | solution.py:299
  87.6 0.0 reduce-scatter.2.cloned.1.call-start
  87.6 15.7 %all-gather.7.cloned.1.call-done = f32[4096,128]{1,0:T(8,128)} async-done(((f32[256,128]{1,0:T(8,128)}), f32[4096,128]{1,0:T(8,128)}) %all-gather.7.cloned.1.call-update) | async-done | bytes 2097168 | tf_op jit(solution)/shard_map/all_gather | solution.py:324
  103.4 3.7 %shard_map.78 = (f32[4,256,128]{2,1,0:T(8,128)}, bf16[1024,512]{1,0:T(8,128)(2,1)}, bf16[1024,512]{1,0:T(8,128)(2,1)}) custom-call(s32[1]{0:T(128)} %bitcast.at_ref, f32[8,512,128]{2,1,0:T(8,128)} %bitcast.8, f32[2,8,256,128]{3,2,1,0:T(8,128)} %bitcast.9), custom_call_target="tpu_custom_call" | custom-call | flops 1610612736 | bytes 6291456 | tf_op jit(solution)/shard_map/pallas_call | solution.py:221
  107.1 0.0 reduce-scatter.2.cloned.1.call-update
  107.1 1.9 %all-to-all-done.2.w_hbm = f32[8,256,128]{2,1,0:T(8,128)S(1)} async-done(((f32[8,256,128]{2,1,0:T(8,128)}), f32[8,256,128]{2,1,0:T(8,128)S(1)}, u32[]{:S(2)}, u32[]{:S(2)}) %all-to-all-start.2) | async-done | bytes 1048608 | tf_op jit(solution)/shard_map/all_to_all | solution.py:299
  109.0 0.0 copy-start
  109.0 3.4 %shard_map.80 = f32[4,256,128]{2,1,0:T(8,128)} custom-call(s32[1]{0:T(128)} %bitcast.at_ref, f32[8,256,128]{2,1,0:T(8,128)S(1)} %all-to-all-done.2.w_hbm, bf16[1024,512]{1,0:T(8,128)(2,1)} %get-tuple-element.17.hi_hbm, bf16[1024,512]{1,0:T(8,128)(2,1)} %get-tuple-element.18.lo_hbm), custom_call_target="tpu_custom_call" | custom-call | tf_op jit(solution)/shard_map/pallas_call | solution.py:270
  112.5 5.4 %all-to-all-start.3 = ((f32[4,256,128]{2,1,0:T(8,128)}), f32[4,256,128]{2,1,0:T(8,128)S(1)}, u32[]{:S(2)}, u32[]{:S(2)}) async-start(f32[4,256,128]{2,1,0:T(8,128)} %shard_map.80), calls=%async_computation.4 | async-start | bytes 1048576 | tf_op jit(solution)/shard_map/all_to_all | solution.py:299
  117.8 0.7 neg.3
  118.5 5.9 %all-to-all-done.3 = f32[4,256,128]{2,1,0:T(8,128)S(1)} async-done(((f32[4,256,128]{2,1,0:T(8,128)}), f32[4,256,128]{2,1,0:T(8,128)S(1)}, u32[]{:S(2)}, u32[]{:S(2)}) %all-to-all-start.3) | async-done | bytes 524320 | tf_op jit(solution)/shard_map/all_to_all | solution.py:299
  124.5 0.0 copy-done
  124.5 0.7 add.25
  125.2 7.5 %reduce-scatter.2.cloned.1.call-done = f32[256,128]{1,0:T(8,128)} async-done(((f32[1024,128]{1,0:T(8,128)}), f32[256,128]{1,0:T(8,128)}) %reduce-scatter.2.cloned.1.call-update) | async-done | bytes 131088 | tf_op jit(solution)/shard_map/reduce_scatter | solution.py:333
  (3 shorter events, 0.1 us)
Async XLA Ops:
  7.2 51.6 %all-gather.5.cloned.1.call-start = ((), (), s32[]{:S(2)}) async-start(), calls=%async_computation.6 | async-start | bytes 2359296 | tf_op jit(solution)/shard_map/all_gather | solution.py:315
  7.2 25.5 %copy-start.1 = (f32[256,128]{1,0:T(8,128)S(1)}, f32[256,128]{1,0:T(8,128)}, u32[]{:S(2)}) copy-start(f32[256,128]{1,0:T(8,128)} %param.7) | copy-start | bytes 393220
  9.6 8.5 %collective-permute-start = (f32[128,128]{1,0:T(8,128)}, f32[128,128]{1,0:T(8,128)S(1)}, u32[]{:S(2)}, u32[]{:S(2)}) collective-permute-start(f32[128,128]{1,0:T(8,128)} %get-tuple-element.12), channel_id=1, source_target_pairs={{0,0},{1,1},{2,32},{3,33},{32,2},{33,3},{34,34},{35,35},{4,4},{5,5... | collective-permute-start | bytes 196616 | tf_op jit(solution)/shard_map/ppermute | solution.py:304
  15.6 7.0 %collective-permute-start.1 = (f32[128,128]{1,0:T(8,128)}, f32[128,128]{1,0:T(8,128)S(1)}, u32[]{:S(2)}, u32[]{:S(2)}) collective-permute-start(f32[128,128]{1,0:T(8,128)} %get-tuple-element.13), channel_id=1, source_target_pairs={{0,1},{1,0},{2,33},{3,32},{32,3},{33,2},{34,35},{35,34},{4,5},{5,4... | collective-permute-start | bytes 196616 | tf_op jit(solution)/shard_map/ppermute | solution.py:304
  23.7 29.8 %all-to-all-start = ((f32[8,2,128,128]{3,2,1,0:T(8,128)}), f32[8,2,128,128]{3,2,1,0:T(8,128)S(1)}, u32[]{:S(2)}, u32[]{:S(2)}) async-start(f32[8,2,128,128]{3,2,1,0:T(8,128)} %shard_map.77), calls=%async_computation.1 | async-start | bytes 2097152 | tf_op jit(solution)/shard_map/all_to_all | solution.py:299
  32.7 70.7 %all-gather.7.cloned.1.call-start = ((), (), s32[]{:S(2)}) async-start(), calls=%async_computation.7 | async-start | bytes 2228224 | tf_op jit(solution)/shard_map/all_gather | solution.py:324
  32.7 7.4 %collective-permute-start.2 = (f32[128,128]{1,0:T(8,128)S(1)}, f32[128,128]{1,0:T(8,128)S(1)}, u32[]{:S(2)}, u32[]{:S(2)}) collective-permute-start(f32[128,128]{1,0:T(8,128)S(1)} %get-tuple-element.19), channel_id=1, source_target_pairs={{0,0},{1,1},{2,32},{3,33},{32,2},{33,3},{34,34},{35,35},{4,4},{5,5... | collective-permute-start | bytes 196616 | tf_op jit(solution)/shard_map/ppermute | solution.py:304
  34.7 7.1 %collective-permute-start.3 = (f32[128,128]{1,0:T(8,128)S(1)}, f32[128,128]{1,0:T(8,128)S(1)}, u32[]{:S(2)}, u32[]{:S(2)}) collective-permute-start(f32[128,128]{1,0:T(8,128)S(1)} %get-tuple-element.20), channel_id=1, source_target_pairs={{0,1},{1,0},{2,33},{3,32},{32,3},{33,2},{34,35},{35,34},{4,5},{5,4... | collective-permute-start | bytes 196616 | tf_op jit(solution)/shard_map/ppermute | solution.py:304
  53.5 5.3 %collective-permute-start.4 = (f32[8,2,128,128]{3,2,1,0:T(8,128)S(1)}, f32[8,2,128,128]{3,2,1,0:T(8,128)S(1)}, u32[]{:S(2)}, u32[]{:S(2)}) collective-permute-start(f32[8,2,128,128]{3,2,1,0:T(8,128)S(1)} %all-to-all-done.own_hbm), channel_id=1, source_target_pairs={{0,32},{32,0},{1,33},{33,1},{2,34},{34,2},{3,35},{35,3},{4,36},{36... | collective-permute-start | bytes 3145736 | tf_op jit(solution)/shard_map/ppermute | solution.py:308
  70.6 38.5 %all-to-all-start.2 = ((f32[8,256,128]{2,1,0:T(8,128)}), f32[8,256,128]{2,1,0:T(8,128)S(1)}, u32[]{:S(2)}, u32[]{:S(2)}) async-start(f32[8,256,128]{2,1,0:T(8,128)} %broadcast_in_dim.2), calls=%async_computation.3 | async-start | bytes 2097152 | tf_op jit(solution)/shard_map/all_to_all | solution.py:299
  87.6 45.0 %reduce-scatter.2.cloned.1.call-start = ((), (), s32[]{:S(2)}) async-start(), calls=%async_computation.5 | async-start | bytes 655360 | tf_op jit(solution)/shard_map/reduce_scatter | solution.py:333
  109.0 15.5 %copy-start = (f32[256,128]{1,0:T(8,128)S(1)}, f32[256,128]{1,0:T(8,128)}, u32[]{:S(2)}) copy-start(f32[256,128]{1,0:T(8,128)} %param.9) | copy-start | bytes 393220
  112.5 12.0 %all-to-all-start.3 = ((f32[4,256,128]{2,1,0:T(8,128)}), f32[4,256,128]{2,1,0:T(8,128)S(1)}, u32[]{:S(2)}, u32[]{:S(2)}) async-start(f32[4,256,128]{2,1,0:T(8,128)} %shard_map.80), calls=%async_computation.4 | async-start | bytes 1048576 | tf_op jit(solution)/shard_map/all_to_all | solution.py:299
Sparse Core Ops, SparseCore 0:
  10.1 46.0 all-gather.4
  58.9 44.4 all-gather.6
  107.2 25.3 reduce-scatter.1

commit v10 on v9

--- a/solution.py
+++ b/solution.py
@@ -14,7 +14,7 @@
 PARAMS = pltpu.CompilerParams(vmem_limit_bytes=32 * 1024 * 1024)
 WIDE = pltpu.CompilerParams(vmem_limit_bytes=62 * 1024 * 1024)
 NEAR = pltpu.CompilerParams(vmem_limit_bytes=51 * 1024 * 1024)
-MIDDLE = pltpu.CompilerParams(vmem_limit_bytes=52 * 1024 * 1024)
+MIDDLE = pltpu.CompilerParams(vmem_limit_bytes=52900 * 1024)
 DMA = pltpu.SemaphoreType.DMA
 
 
@@ -173,46 +173,43 @@
 
 
 def side_kernel(
-    at_ref, su_hbm, lower_hbm, out_hbm, hi_hbm, lo_hbm, sigma, lower, ah, al, bh, bl, out, sems
+    at_ref, su_hbm, lower_hbm, top_hbm, rest_hbm, hi_hbm, lo_hbm, sigma, lower, ah, al, bh, bl, out, sems
 ):
     loads = [pltpu.make_async_copy(su_hbm.at[:, 0:256], sigma, sems.at[0])]
-    for i in range(2):
-        rows = slice(4 * i, 4 * (i + 1))
-        loads.append(
-            pltpu.make_async_copy(lower_hbm.at[:, rows], lower.at[:, rows], sems.at[1 + i])
-        )
+    for n in range(2):
+        loads.append(pltpu.make_async_copy(lower_hbm.at[n], lower.at[n], sems.at[1 + n]))
     for load in loads:
         load.start()
-    _, _, core_at, _, x = device(at_ref)
+    _, _, core, _, x = device(at_ref)
     odd = x & 1
     loads[0].wait()
     for z in range(8):
         rows = slice(128 * z, 128 * (z + 1))
-        ah[:, rows], al[:, rows] = split2(sigma[z ^ (4 * core_at)])
-    for z in range(8):
-        if z % 4 == 0:
-            loads[1 + z // 4].wait()
-        rows = slice(128 * z, 128 * (z + 1))
-        for core in range(2):
+        ah[:, rows], al[:, rows] = split2(sigma[z ^ (4 * core)])
+    stores = []
+    for n in range(2):
+        loads[1 + n].wait()
+        for z in range(8):
+            rows = slice(128 * z, 128 * (z + 1))
             for t in range(2):
-                cols = slice(256 * core + 128 * t, 256 * core + 128 * (t + 1))
+                cols = slice(128 * t, 128 * (t + 1))
                 place = 128 * (odd if t == 0 else 1 - odd)
-                value = lower[core, z, pl.ds(pl.multiple_of(place, 128), 128), :]
-                bh[rows, cols], bl[rows, cols] = split2(value)
-    stores = [
-        pltpu.make_async_copy(bh, hi_hbm, sems.at[3]),
-        pltpu.make_async_copy(bl, lo_hbm, sems.at[4]),
-    ]
-    for store in stores:
-        store.start()
-    for n in range(2):
-        cols = slice(256 * n, 256 * (n + 1))
-        part = -three_pass(ah[...], al[...], bh[:, cols], bl[:, cols])
+                value = lower[n, z, pl.ds(pl.multiple_of(place, 128), 128), :]
+                bh[n, rows, cols], bl[n, rows, cols] = split2(value)
+        stores.append(pltpu.make_async_copy(bh.at[n], hi_hbm.at[n], sems.at[3 + n]))
+        stores.append(pltpu.make_async_copy(bl.at[n], lo_hbm.at[n], sems.at[5 + n]))
+        part = -three_pass(ah[...], al[...], bh[n], bl[n])
         out[2 * n] = part[:, :128]
         out[2 * n + 1] = part[:, 128:]
-        pair, place = slice(2 * n, 2 * n + 2), pl.ds(2 * (n ^ core_at), 2)
-        stores.append(pltpu.make_async_copy(out.at[pair], out_hbm.at[place], sems.at[5 + n]))
-        stores[-1].start()
+        pair, place = slice(2 * n, 2 * n + 2), pl.ds(2 * (n ^ core), 2)
+        stores.append(
+            pltpu.make_async_copy(out.at[pair, 0:128], top_hbm.at[place], sems.at[7 + n])
+        )
+        stores.append(
+            pltpu.make_async_copy(out.at[pair, 128:256], rest_hbm.at[place], sems.at[9 + n])
+        )
+        for store in stores[4 * n :]:
+            store.start()
     for store in stores:
         store.wait()
 
@@ -220,69 +217,70 @@
 def side(at, gathered, lower):
     return pl.pallas_call(
         side_kernel,
-        out_shape=(shape(4, 256, 128),) + (shape(1024, 512, dtype=BF16),) * 2,
+        out_shape=(shape(4, 128, 128),) * 2 + (shape(2, 1024, 256, dtype=BF16),) * 2,
         in_specs=[SMEM, HBM, HBM],
-        out_specs=(HBM,) * 3,
+        out_specs=(HBM,) * 4,
         scratch_shapes=[
             pltpu.VMEM((8, 256, 128), F32),
             pltpu.VMEM((2, 8, 256, 128), F32),
             pltpu.VMEM((256, 1024), BF16),
             pltpu.VMEM((256, 1024), BF16),
-            pltpu.VMEM((1024, 512), BF16),
-            pltpu.VMEM((1024, 512), BF16),
+            pltpu.VMEM((2, 1024, 256), BF16),
+            pltpu.VMEM((2, 1024, 256), BF16),
             pltpu.VMEM((4, 256, 128), F32),
-            DMA((7,)),
+            DMA((11,)),
         ],
         compiler_params=WIDE,
         cost_estimate=pl.CostEstimate(flops=6 << 28, bytes_accessed=6 << 20, transcendentals=0),
     )(at, gathered, lower)
 
 
-def last_kernel(at_ref, w_hbm, hi_hbm, lo_hbm, out_hbm, w, ah, al, bh, bl, out, sems):
-    loads = [
-        pltpu.make_async_copy(w_hbm, w, sems.at[0]),
-        pltpu.make_async_copy(hi_hbm, bh, sems.at[1]),
-        pltpu.make_async_copy(lo_hbm, bl, sems.at[2]),
-    ]
-    for load in loads:
+def last_kernel(at_ref, w_hbm, hi_hbm, lo_hbm, rest_hbm, out_hbm, w, ah, al, bh, bl, out, sems):
+    rest = pltpu.make_async_copy(rest_hbm, out_hbm.at[:, 256:384], sems.at[7])
+    loads = [pltpu.make_async_copy(w_hbm, w, sems.at[0])]
+    for n in range(2):
+        loads.append(pltpu.make_async_copy(hi_hbm.at[n], bh.at[n], sems.at[1 + n]))
+        loads.append(pltpu.make_async_copy(lo_hbm.at[n], bl.at[n], sems.at[3 + n]))
+    for load in loads + [rest]:
         load.start()
     core = device(at_ref)[2]
     loads[0].wait()
     for z in range(8):
         rows = slice(128 * z, 128 * (z + 1))
         ah[:, rows], al[:, rows] = split2(w[z ^ (4 * core)])
-    for load in loads[1:]:
-        load.wait()
-    stores = []
-    for n in range(2):
-        cols = slice(256 * n, 256 * (n + 1))
-        part = three_pass(ah[...], al[...], bh[:, cols], bl[:, cols])
+    stores = [rest]
+    for n in range(2):
+        for load in loads[1 + 2 * n : 3 + 2 * n]:
+            load.wait()
+        part = three_pass(ah[...], al[...], bh[n], bl[n])
         out[2 * n] = part[:, :128]
         out[2 * n + 1] = part[:, 128:]
         pair, place = slice(2 * n, 2 * n + 2), pl.ds(2 * (n ^ core), 2)
-        stores.append(pltpu.make_async_copy(out.at[pair], out_hbm.at[place], sems.at[3 + n]))
+        stores.append(
+            pltpu.make_async_copy(out.at[pair], out_hbm.at[place, 0:256], sems.at[5 + n])
+        )
         stores[-1].start()
     for store in stores:
         store.wait()
 
 
-def last(at, w, hi, lo):
+def last(at, w, hi, lo, rest):
     return pl.pallas_call(
         last_kernel,
-        out_shape=shape(4, 256, 128),
-        in_specs=[SMEM] + [HBM] * 3,
+        out_shape=shape(4, 384, 128),
+        in_specs=[SMEM] + [HBM] * 4,
         out_specs=HBM,
         scratch_shapes=[
             pltpu.VMEM((8, 256, 128), F32),
             pltpu.VMEM((256, 1024), BF16),
             pltpu.VMEM((256, 1024), BF16),
-            pltpu.VMEM((1024, 512), BF16),
-            pltpu.VMEM((1024, 512), BF16),
+            pltpu.VMEM((2, 1024, 256), BF16),
+            pltpu.VMEM((2, 1024, 256), BF16),
             pltpu.VMEM((4, 256, 128), F32),
-            DMA((5,)),
+            DMA((8,)),
         ],
         compiler_params=MIDDLE,
-    )(at, w, hi, lo)
+    )(at, w, hi, lo, rest)
 
 
 def rotated(axis, size):
@@ -328,13 +326,13 @@
     part = couple(at, gathered, own, other)
     w = exchange(part, "x", 4).sum(axis=0)
     w_all = exchange(jnp.broadcast_to(w[None], (8, 256, 128)), "z", 8)
-    sides, hi, lo = side(at, gathered, lower)
+    top, rest, hi, lo = side(at, gathered, lower)
     axes, groups = rotated("x", 4)
-    t = lax.psum_scatter(
-        sides.reshape(1024, 128), axes, scatter_dimension=0, tiled=True, axis_index_groups=groups
+    top = lax.psum_scatter(
+        top.reshape(512, 128), axes, scatter_dimension=0, tiled=True, axis_index_groups=groups
     )
-    product = exchange(last(at, w_all, hi, lo), "x", 4).sum(axis=0)
-    return (t, -w, diagonal_inverse + product)
+    sums = exchange(last(at, w_all, hi, lo, rest), "x", 4).sum(axis=0)
+    return (jnp.concatenate([top, sums[256:]], axis=0), -w, diagonal_inverse + sums[:256])
 
 
 def solution(mesh):

time: 141 us -> 154 us (1.092)
  waiting for transfers between devices: 52.3 us -> 61.8 us
    reduce_scatter x1, waiting for transfers between devices: 7.51 us -> 16.9 us  [shards(): lax.psum_scatter(top.reshape(512, 128), axes, scatter_dimension=0, tiled=...]
  transfers between devices with their start and end apart: 11 -> 11, of which waited for: 9 -> 9; matrix products, arithmetic and copies ran while one was open for 2% -> 2% of each run, Pallas kernels for 8% -> 5%
where the time goes in v10:
time: 154 us; the launch traced here: 152 us
  waiting for transfers between devices  61.8 us (40%)
  starting transfers between devices  48.8 us (32%)
  Pallas kernels  14.1 us (9%)
  between operations  13.9 us (9%)
  blocking collectives  8.29 us (5%)
  other arithmetic  3.57 us (2%)
  local copies, waits for them, and re-layouts  2.05 us (1%)
    all_to_all x3, starting transfers between devices, exchange(): return lax.all_to_all(v, axes, 0, 0, tiled=True, axis_index_groups=groups)  31.6 us
    all_to_all x3, waiting for transfers between devices, exchange(): return lax.all_to_all(v, axes, 0, 0, tiled=True, axis_index_groups=groups)  18.3 us
    reduce_scatter x1, waiting for transfers between devices, shards(): lax.psum_scatter(top.reshape(512, 128), axes, scatter_dimension=0, tiled=...  16.9 us
    all_gather x1, waiting for transfers between devices, shards(): lax.all_gather(lower, ('y', 'c'), axis=0, tiled=False, axis_index_groups=...  15.7 us
    ppermute x4, starting transfers between devices, deal(): return lax.ppermute(v, ('c', 'x'), moves)  14.1 us
    all_to_all x1, blocking collectives, exchange(): return lax.all_to_all(v, axes, 0, 0, tiled=True, axis_index_groups=groups)  8.29 us
    ppermute x4, waiting for transfers between devices, deal(): return lax.ppermute(v, ('c', 'x'), moves)  7.9 us
    pallas_call x1, Pallas kernels, side(): pl.pallas_call(side_kernel, out_shape=(shape(4, 128, 128),) * 2 + (shape(...  4.28 us
  transfers between devices with their start and end apart: 11, of which 9 were waited for; matrix products, arithmetic and copies ran while one was open for 2% of the time, Pallas kernels for 5%

profile of v10, /device:TPU:1, one launch (start us, length us, event | category | flops | bytes accessed | tf_op | source)
XLA Modules:
  0.0 152.5 jit_solution(13711027459618653453)
XLA Ops:
  7.2 0.0 all-gather.5.cloned.1.call-start
  7.2 0.0 copy-start.2
  7.2 2.3 %shard_map.76 = (f32[512,128]{1,0:T(8,128)}, f32[128,128]{1,0:T(8,128)}, f32[128,128]{1,0:T(8,128)}) custom-call(s32[1]{0:T(128)} %bitcast.at_ref, s32[32,128]{1,0:T(8,128)} %bitcast.6, f32[512,256]{1,0:T(8,128)} %root_hbm.1, f32[256,128]{1,0:T(8,128)} %upper_hbm.1), custom_call_target="tpu_custom_call" | custom-call | tf_op jit(solution)/shard_map/pallas_call | solution.py:92
  9.5 0.0 all-gather.5.cloned.1.call-update
  9.6 6.0 %collective-permute-start = (f32[128,128]{1,0:T(8,128)}, f32[128,128]{1,0:T(8,128)S(1)}, u32[]{:S(2)}, u32[]{:S(2)}) collective-permute-start(f32[128,128]{1,0:T(8,128)} %get-tuple-element.13), channel_id=1, source_target_pairs={{0,0},{1,1},{2,32},{3,33},{32,2},{33,3},{34,34},{35,35},{4,4},{5,5... | collective-permute-start | bytes 196616 | tf_op jit(solution)/shard_map/ppermute | solution.py:302
  15.6 2.5 %collective-permute-start.1 = (f32[128,128]{1,0:T(8,128)}, f32[128,128]{1,0:T(8,128)S(1)}, u32[]{:S(2)}, u32[]{:S(2)}) collective-permute-start(f32[128,128]{1,0:T(8,128)} %get-tuple-element.14), channel_id=1, source_target_pairs={{0,1},{1,0},{2,33},{3,32},{32,3},{33,2},{34,35},{35,34},{4,5},{5,4... | collective-permute-start | bytes 196616 | tf_op jit(solution)/shard_map/ppermute | solution.py:302
  18.1 0.0 collective-permute-done.first_ref
  18.1 4.5 %collective-permute-done.1.second_ref = f32[128,128]{1,0:T(8,128)S(1)} collective-permute-done((f32[128,128]{1,0:T(8,128)}, f32[128,128]{1,0:T(8,128)S(1)}, u32[]{:S(2)}, u32[]{:S(2)}) %collective-permute-start.1) | collective-permute-done | bytes 65568 | tf_op jit(solution)/shard_map/ppermute | solution.py:302
  22.6 1.0 shard_map.77
  23.7 9.0 %all-to-all-start = ((f32[8,2,128,128]{3,2,1,0:T(8,128)}), f32[8,2,128,128]{3,2,1,0:T(8,128)S(1)}, u32[]{:S(2)}, u32[]{:S(2)}) async-start(f32[8,2,128,128]{3,2,1,0:T(8,128)} %shard_map.77), calls=%async_computation.1 | async-start | bytes 2097152 | tf_op jit(solution)/shard_map/all_to_all | solution.py:297
  32.7 0.0 all-gather.7.cloned.1.call-start
  32.7 0.0 copy-done.2
  32.7 1.9 %collective-permute-start.2 = (f32[128,128]{1,0:T(8,128)S(1)}, f32[128,128]{1,0:T(8,128)S(1)}, u32[]{:S(2)}, u32[]{:S(2)}) collective-permute-start(f32[128,128]{1,0:T(8,128)S(1)} %get-tuple-element.21), channel_id=1, source_target_pairs={{0,0},{1,1},{2,32},{3,33},{32,2},{33,3},{34,34},{35,35},{4,4},{5,5... | collective-permute-start | bytes 196616 | tf_op jit(solution)/shard_map/ppermute | solution.py:302
  34.7 3.7 %collective-permute-start.3 = (f32[128,128]{1,0:T(8,128)S(1)}, f32[128,128]{1,0:T(8,128)S(1)}, u32[]{:S(2)}, u32[]{:S(2)}) collective-permute-start(f32[128,128]{1,0:T(8,128)S(1)} %get-tuple-element.22), channel_id=1, source_target_pairs={{0,1},{1,0},{2,33},{3,32},{32,3},{33,2},{34,35},{35,34},{4,5},{5,4... | collective-permute-start | bytes 196616 | tf_op jit(solution)/shard_map/ppermute | solution.py:302
  38.3 1.8 %collective-permute-done.2 = f32[128,128]{1,0:T(8,128)S(1)} collective-permute-done((f32[128,128]{1,0:T(8,128)S(1)}, f32[128,128]{1,0:T(8,128)S(1)}, u32[]{:S(2)}, u32[]{:S(2)}) %collective-permute-start.2) | collective-permute-done | bytes 65568 | tf_op jit(solution)/shard_map/ppermute | solution.py:302
  40.1 1.6 %collective-permute-done.3 = f32[128,128]{1,0:T(8,128)S(1)} collective-permute-done((f32[128,128]{1,0:T(8,128)S(1)}, f32[128,128]{1,0:T(8,128)S(1)}, u32[]{:S(2)}, u32[]{:S(2)}) %collective-permute-start.3) | collective-permute-done | bytes 65568 | tf_op jit(solution)/shard_map/ppermute | solution.py:302
  41.7 0.7 pad_maximum_fusion
  42.4 0.0 all-gather.7.cloned.1.call-update
  42.4 11.0 %all-to-all-done.own_hbm = f32[8,2,128,128]{3,2,1,0:T(8,128)S(1)} async-done(((f32[8,2,128,128]{3,2,1,0:T(8,128)}), f32[8,2,128,128]{3,2,1,0:T(8,128)S(1)}, u32[]{:S(2)}, u32[]{:S(2)}) %all-to-all-start) | async-done | bytes 1048608 | tf_op jit(solution)/shard_map/all_to_all | solution.py:297
  53.5 3.0 %collective-permute-start.4 = (f32[8,2,128,128]{3,2,1,0:T(8,128)S(1)}, f32[8,2,128,128]{3,2,1,0:T(8,128)S(1)}, u32[]{:S(2)}, u32[]{:S(2)}) collective-permute-start(f32[8,2,128,128]{3,2,1,0:T(8,128)S(1)} %all-to-all-done.own_hbm), channel_id=1, source_target_pairs={{0,32},{32,0},{1,33},{33,1},{2,34},{34,2},{3,35},{35,3},{4,36},{36... | collective-permute-start | bytes 3145736 | tf_op jit(solution)/shard_map/ppermute | solution.py:306
  56.5 2.3 %collective-permute-done.4.other_hbm = f32[8,2,128,128]{3,2,1,0:T(8,128)S(1)} collective-permute-done((f32[8,2,128,128]{3,2,1,0:T(8,128)S(1)}, f32[8,2,128,128]{3,2,1,0:T(8,128)S(1)}, u32[]{:S(2)}, u32[]{:S(2)}) %collective-permute-start.4) | collective-permute-done | bytes 1048608 | tf_op jit(solution)/shard_map/ppermute | solution.py:306
  58.8 0.0 all-gather.5.cloned.1.call-done
  58.8 2.4 %shard_map.79 = f32[4,256,128]{2,1,0:T(8,128)S(1)} custom-call(s32[1]{0:T(128)} %bitcast.at_ref, f32[8,512,128]{2,1,0:T(8,128)} %bitcast.7, f32[8,2,128,128]{3,2,1,0:T(8,128)S(1)} %all-to-all-done.own_hbm, f32[8,2,128,128]{3,2,1,0:T(8,128)S(1)} %collective-permute-done.4.other_hbm), custom_call_target="tpu_custom_call" | custom-call | flops 1610612736 | bytes 3145728 | tf_op jit(solution)/shard_map/pallas_call | solution.py:155
  61.2 8.3 %all_to_all.20 = f32[4,256,128]{2,1,0:T(8,128)S(1)} all-to-all(f32[4,256,128]{2,1,0:T(8,128)S(1)} %shard_map.79), channel_id=1, replica_groups={{0,1,2,3},{34,35,32,33},{4,5,6,7},{38,39,36,37},{8,9,10,11},{42,43,40,4..., dimensions={0} | all-to-all | bytes 1048576 | tf_op jit(solution)/shard_map/all_to_all | solution.py:297
  69.5 1.1 broadcast_in_dim.2
  70.5 17.1 %all-to-all-start.2 = ((f32[8,256,128]{2,1,0:T(8,128)}), f32[8,256,128]{2,1,0:T(8,128)S(1)}, u32[]{:S(2)}, u32[]{:S(2)}) async-start(f32[8,256,128]{2,1,0:T(8,128)} %broadcast_in_dim.2), calls=%async_computation.3 | async-start | bytes 2097152 | tf_op jit(solution)/shard_map/all_to_all | solution.py:297
  87.6 15.7 %all-gather.7.cloned.1.call-done = f32[4096,128]{1,0:T(8,128)} async-done(((f32[256,128]{1,0:T(8,128)}), f32[4096,128]{1,0:T(8,128)}) %all-gather.7.cloned.1.call-update) | async-done | bytes 2097168 | tf_op jit(solution)/shard_map/all_gather | solution.py:322
  103.4 4.3 %shard_map.78 = (f32[4,128,128]{2,1,0:T(8,128)}, f32[4,128,128]{2,1,0:T(8,128)}, bf16[2,1024,256]{2,1,0:T(8,128)(2,1)}, bf16[2,1024,256]{2,1,0:T(8,128)(2,1)}) custom-call(s32[1]{0:T(128)} %bitcast.at_ref, f32[8,512,128]{2,1,0:T(8,128)} %bitcast.8, f32[2,8,256,128]{3,2,1,0:T(8,128)} %bitcast.9), custom_call_target="tpu_custom_call" | custom-call | flops 1610612736 | bytes 6291456 | tf_op jit(solution)/shard_map/pallas_call | solution.py:218
  107.7 1.3 all-to-all-done.2.w_hbm
  109.0 0.0 copy-start
  109.0 0.9 copy-done
  110.0 4.0 %shard_map.80 = f32[4,384,128]{2,1,0:T(8,128)} custom-call(s32[1]{0:T(128)} %bitcast.at_ref, f32[8,256,128]{2,1,0:T(8,128)S(1)} %all-to-all-done.2.w_hbm, bf16[2,1024,256]{2,1,0:T(8,128)(2,1)} %get-tuple-element.18.hi_hbm, bf16[2,1024,256]{2,1,0:T(8,128)(2,1)} %get-tuple-element.19.lo_hbm, f32[4,128,128]{2,1,0:T(8,128)S(1)} %copy-done), custom_call_target="tpu_custom_call" | custom-call | tf_op jit(solution)/shard_map/pallas_call | solution.py:268
  114.0 0.0 copy-start.1
  114.0 5.5 %all-to-all-start.3 = ((f32[4,384,128]{2,1,0:T(8,128)}), f32[4,384,128]{2,1,0:T(8,128)S(1)}, u32[]{:S(2)}, u32[]{:S(2)}) async-start(f32[4,384,128]{2,1,0:T(8,128)} %shard_map.80), calls=%async_computation.4 | async-start | bytes 1572864 | tf_op jit(solution)/shard_map/all_to_all | solution.py:297
  119.6 0.0 reduce-scatter.2.cloned.1.call-start
  119.6 0.7 reduce-scatter.2.cloned.1.call-update
  120.3 0.7 neg.3
  121.0 5.9 %all-to-all-done.3 = f32[4,384,128]{2,1,0:T(8,128)S(1)} async-done(((f32[4,384,128]{2,1,0:T(8,128)}), f32[4,384,128]{2,1,0:T(8,128)S(1)}, u32[]{:S(2)}, u32[]{:S(2)}) %all-to-all-start.3) | async-done | bytes 786464 | tf_op jit(solution)/shard_map/all_to_all | solution.py:297
  126.9 0.0 copy-done.1
  126.9 0.7 slice_add_fusion
  127.6 16.9 %reduce-scatter.2.cloned.1.call-done = f32[128,128]{1,0:T(8,128)} async-done(((f32[512,128]{1,0:T(8,128)}), f32[128,128]{1,0:T(8,128)}) %reduce-scatter.2.cloned.1.call-update) | async-done | bytes 65552 | tf_op jit(solution)/shard_map/reduce_scatter | solution.py:331
  144.4 1.5 pad_maximum_fusion.1
  (4 shorter events, 0.1 us)
Async XLA Ops:
  7.2 51.6 %all-gather.5.cloned.1.call-start = ((), (), s32[]{:S(2)}) async-start(), calls=%async_computation.6 | async-start | bytes 2359296 | tf_op jit(solution)/shard_map/all_gather | solution.py:313
  7.2 25.5 %copy-start.2 = (f32[256,128]{1,0:T(8,128)S(1)}, f32[256,128]{1,0:T(8,128)}, u32[]{:S(2)}) copy-start(f32[256,128]{1,0:T(8,128)} %param.7) | copy-start | bytes 393220
  9.6 8.5 %collective-permute-start = (f32[128,128]{1,0:T(8,128)}, f32[128,128]{1,0:T(8,128)S(1)}, u32[]{:S(2)}, u32[]{:S(2)}) collective-permute-start(f32[128,128]{1,0:T(8,128)} %get-tuple-element.13), channel_id=1, source_target_pairs={{0,0},{1,1},{2,32},{3,33},{32,2},{33,3},{34,34},{35,35},{4,4},{5,5... | collective-permute-start | bytes 196616 | tf_op jit(solution)/shard_map/ppermute | solution.py:302
  15.6 7.0 %collective-permute-start.1 = (f32[128,128]{1,0:T(8,128)}, f32[128,128]{1,0:T(8,128)S(1)}, u32[]{:S(2)}, u32[]{:S(2)}) collective-permute-start(f32[128,128]{1,0:T(8,128)} %get-tuple-element.14), channel_id=1, source_target_pairs={{0,1},{1,0},{2,33},{3,32},{32,3},{33,2},{34,35},{35,34},{4,5},{5,4... | collective-permute-start | bytes 196616 | tf_op jit(solution)/shard_map/ppermute | solution.py:302
  23.7 29.8 %all-to-all-start = ((f32[8,2,128,128]{3,2,1,0:T(8,128)}), f32[8,2,128,128]{3,2,1,0:T(8,128)S(1)}, u32[]{:S(2)}, u32[]{:S(2)}) async-start(f32[8,2,128,128]{3,2,1,0:T(8,128)} %shard_map.77), calls=%async_computation.1 | async-start | bytes 2097152 | tf_op jit(solution)/shard_map/all_to_all | solution.py:297
  32.7 70.7 %all-gather.7.cloned.1.call-start = ((), (), s32[]{:S(2)}) async-start(), calls=%async_computation.7 | async-start | bytes 2228224 | tf_op jit(solution)/shard_map/all_gather | solution.py:322
  32.7 7.4 %collective-permute-start.2 = (f32[128,128]{1,0:T(8,128)S(1)}, f32[128,128]{1,0:T(8,128)S(1)}, u32[]{:S(2)}, u32[]{:S(2)}) collective-permute-start(f32[128,128]{1,0:T(8,128)S(1)} %get-tuple-element.21), channel_id=1, source_target_pairs={{0,0},{1,1},{2,32},{3,33},{32,2},{33,3},{34,34},{35,35},{4,4},{5,5... | collective-permute-start | bytes 196616 | tf_op jit(solution)/shard_map/ppermute | solution.py:302
  34.7 7.1 %collective-permute-start.3 = (f32[128,128]{1,0:T(8,128)S(1)}, f32[128,128]{1,0:T(8,128)S(1)}, u32[]{:S(2)}, u32[]{:S(2)}) collective-permute-start(f32[128,128]{1,0:T(8,128)S(1)} %get-tuple-element.22), channel_id=1, source_target_pairs={{0,1},{1,0},{2,33},{3,32},{32,3},{33,2},{34,35},{35,34},{4,5},{5,4... | collective-permute-start | bytes 196616 | tf_op jit(solution)/shard_map/ppermute | solution.py:302
  53.5 5.3 %collective-permute-start.4 = (f32[8,2,128,128]{3,2,1,0:T(8,128)S(1)}, f32[8,2,128,128]{3,2,1,0:T(8,128)S(1)}, u32[]{:S(2)}, u32[]{:S(2)}) collective-permute-start(f32[8,2,128,128]{3,2,1,0:T(8,128)S(1)} %all-to-all-done.own_hbm), channel_id=1, source_target_pairs={{0,32},{32,0},{1,33},{33,1},{2,34},{34,2},{3,35},{35,3},{4,36},{36... | collective-permute-start | bytes 3145736 | tf_op jit(solution)/shard_map/ppermute | solution.py:306
  70.5 38.5 %all-to-all-start.2 = ((f32[8,256,128]{2,1,0:T(8,128)}), f32[8,256,128]{2,1,0:T(8,128)S(1)}, u32[]{:S(2)}, u32[]{:S(2)}) async-start(f32[8,256,128]{2,1,0:T(8,128)} %broadcast_in_dim.2), calls=%async_computation.3 | async-start | bytes 2097152 | tf_op jit(solution)/shard_map/all_to_all | solution.py:297
  109.0 0.9 copy-start
  114.0 12.9 %copy-start.1 = (f32[256,128]{1,0:T(8,128)S(1)}, f32[256,128]{1,0:T(8,128)}, u32[]{:S(2)}) copy-start(f32[256,128]{1,0:T(8,128)} %param.9) | copy-start | bytes 393220
  114.0 12.8 %all-to-all-start.3 = ((f32[4,384,128]{2,1,0:T(8,128)}), f32[4,384,128]{2,1,0:T(8,128)S(1)}, u32[]{:S(2)}, u32[]{:S(2)}) async-start(f32[4,384,128]{2,1,0:T(8,128)} %shard_map.80), calls=%async_computation.4 | async-start | bytes 1572864 | tf_op jit(solution)/shard_map/all_to_all | solution.py:297
  119.6 24.9 %reduce-scatter.2.cloned.1.call-start = ((), (), s32[]{:S(2)}) async-start(), calls=%async_computation.5 | async-start | bytes 327680 | tf_op jit(solution)/shard_map/reduce_scatter | solution.py:331
Sparse Core Ops, SparseCore 0:
  10.1 46.0 all-gather.4
  58.9 44.4 all-gather.6
  123.2 21.1 reduce-scatter.1

commit v11 on v10

--- a/solution.py
+++ b/solution.py
@@ -14,7 +14,7 @@
 PARAMS = pltpu.CompilerParams(vmem_limit_bytes=32 * 1024 * 1024)
 WIDE = pltpu.CompilerParams(vmem_limit_bytes=62 * 1024 * 1024)
 NEAR = pltpu.CompilerParams(vmem_limit_bytes=51 * 1024 * 1024)
-MIDDLE = pltpu.CompilerParams(vmem_limit_bytes=52900 * 1024)
+MIDDLE = pltpu.CompilerParams(vmem_limit_bytes=51 * 1024 * 1024)
 DMA = pltpu.SemaphoreType.DMA
 
 
@@ -173,7 +173,7 @@
 
 
 def side_kernel(
-    at_ref, su_hbm, lower_hbm, top_hbm, rest_hbm, hi_hbm, lo_hbm, sigma, lower, ah, al, bh, bl, out, sems
+    at_ref, su_hbm, lower_hbm, rest_hbm, hi_hbm, lo_hbm, sigma, lower, ah, al, bh, bl, out, sems
 ):
     loads = [pltpu.make_async_copy(su_hbm.at[:, 0:256], sigma, sems.at[0])]
     for n in range(2):
@@ -202,13 +202,8 @@
         out[2 * n] = part[:, :128]
         out[2 * n + 1] = part[:, 128:]
         pair, place = slice(2 * n, 2 * n + 2), pl.ds(2 * (n ^ core), 2)
-        stores.append(
-            pltpu.make_async_copy(out.at[pair, 0:128], top_hbm.at[place], sems.at[7 + n])
-        )
-        stores.append(
-            pltpu.make_async_copy(out.at[pair, 128:256], rest_hbm.at[place], sems.at[9 + n])
-        )
-        for store in stores[4 * n :]:
+        stores.append(pltpu.make_async_copy(out.at[pair], rest_hbm.at[place], sems.at[7 + n]))
+        for store in stores[3 * n :]:
             store.start()
     for store in stores:
         store.wait()
@@ -217,9 +212,9 @@
 def side(at, gathered, lower):
     return pl.pallas_call(
         side_kernel,
-        out_shape=(shape(4, 128, 128),) * 2 + (shape(2, 1024, 256, dtype=BF16),) * 2,
+        out_shape=(shape(12, 256, 128),) + (shape(2, 1024, 256, dtype=BF16),) * 2,
         in_specs=[SMEM, HBM, HBM],
-        out_specs=(HBM,) * 4,
+        out_specs=(HBM,) * 3,
         scratch_shapes=[
             pltpu.VMEM((8, 256, 128), F32),
             pltpu.VMEM((2, 8, 256, 128), F32),
@@ -228,7 +223,7 @@
             pltpu.VMEM((2, 1024, 256), BF16),
             pltpu.VMEM((2, 1024, 256), BF16),
             pltpu.VMEM((4, 256, 128), F32),
-            DMA((11,)),
+            DMA((9,)),
         ],
         compiler_params=WIDE,
         cost_estimate=pl.CostEstimate(flops=6 << 28, bytes_accessed=6 << 20, transcendentals=0),
@@ -236,7 +231,7 @@
 
 
 def last_kernel(at_ref, w_hbm, hi_hbm, lo_hbm, rest_hbm, out_hbm, w, ah, al, bh, bl, out, sems):
-    rest = pltpu.make_async_copy(rest_hbm, out_hbm.at[:, 256:384], sems.at[7])
+    rest = pltpu.make_async_copy(rest_hbm.at[0:4], out_hbm.at[:, 256:512], sems.at[7])
     loads = [pltpu.make_async_copy(w_hbm, w, sems.at[0])]
     for n in range(2):
         loads.append(pltpu.make_async_copy(hi_hbm.at[n], bh.at[n], sems.at[1 + n]))
@@ -267,7 +262,7 @@
 def last(at, w, hi, lo, rest):
     return pl.pallas_call(
         last_kernel,
-        out_shape=shape(4, 384, 128),
+        out_shape=shape(4, 512, 128),
         in_specs=[SMEM] + [HBM] * 4,
         out_specs=HBM,
         scratch_shapes=[
@@ -326,13 +321,9 @@
     part = couple(at, gathered, own, other)
     w = exchange(part, "x", 4).sum(axis=0)
     w_all = exchange(jnp.broadcast_to(w[None], (8, 256, 128)), "z", 8)
-    top, rest, hi, lo = side(at, gathered, lower)
-    axes, groups = rotated("x", 4)
-    top = lax.psum_scatter(
-        top.reshape(512, 128), axes, scatter_dimension=0, tiled=True, axis_index_groups=groups
-    )
+    rest, hi, lo = side(at, gathered, lower)
     sums = exchange(last(at, w_all, hi, lo, rest), "x", 4).sum(axis=0)
-    return (jnp.concatenate([top, sums[256:]], axis=0), -w, diagonal_inverse + sums[:256])
+    return (sums[256:], -w, diagonal_inverse + sums[:256])
 
 
 def solution(mesh):

time: 154 us -> 154 us (level)
  the two profiles are of different devices: /device:TPU:1 before, /device:TPU:128 now
where the time goes in v11:
time: 154 us; the launch traced here: 153 us
  waiting for transfers between devices  65.3 us (42%)
  starting transfers between devices  32 us (21%)
  Pallas kernels  27.1 us (18%)
  between operations  14.2 us (9%)
  blocking collectives  11.4 us (7%)
  other arithmetic  2.15 us (1%)
    all_to_all x3, waiting for transfers between devices, exchange(): return lax.all_to_all(v, axes, 0, 0, tiled=True, axis_index_groups=groups)  40.1 us
    all_to_all x3, starting transfers between devices, exchange(): return lax.all_to_all(v, axes, 0, 0, tiled=True, axis_index_groups=groups)  21.1 us
    pallas_call x1, Pallas kernels, last(): pl.pallas_call(last_kernel, out_shape=shape(4, 512, 128), in_specs=[SMEM]...  17.1 us
    all_gather x1, waiting for transfers between devices, shards(): lax.all_gather(lower, ('y', 'c'), axis=0, tiled=False, axis_index_groups=...  16.5 us
    all_to_all x1, blocking collectives, exchange(): return lax.all_to_all(v, axes, 0, 0, tiled=True, axis_index_groups=groups)  11.4 us
    ppermute x4, starting transfers between devices, deal(): return lax.ppermute(v, ('c', 'x'), moves)  8.89 us
    ppermute x4, waiting for transfers between devices, deal(): return lax.ppermute(v, ('c', 'x'), moves)  5.99 us
    pallas_call x1, Pallas kernels, side(): pl.pallas_call(side_kernel, out_shape=(shape(12, 256, 128),) + (shape(2,...  4.25 us
  transfers between devices with their start and end apart: 10, of which 7 were waited for; matrix products, arithmetic and copies ran while one was open for 2% of the time, Pallas kernels for 5%

profile of v11, /device:TPU:128, one launch (start us, length us, event | category | flops | bytes accessed | tf_op | source)
XLA Modules:
  0.0 153.3 jit_solution(15079212740788100742)
XLA Ops:
  7.2 0.0 all-gather.5.cloned.1.call-start
  7.2 0.0 copy-start.1
  7.2 2.3 %shard_map.76 = (f32[512,128]{1,0:T(8,128)}, f32[128,128]{1,0:T(8,128)}, f32[128,128]{1,0:T(8,128)}) custom-call(s32[1]{0:T(128)} %bitcast.at_ref, s32[32,128]{1,0:T(8,128)} %bitcast.4, f32[512,256]{1,0:T(8,128)} %root_hbm.1, f32[256,128]{1,0:T(8,128)} %upper_hbm.1), custom_call_target="tpu_custom_call" | custom-call | tf_op jit(solution)/shard_map/pallas_call | solution.py:92
  9.6 0.0 all-gather.5.cloned.1.call-update
  9.6 1.5 collective-permute-start
  11.1 3.4 %collective-permute-start.1 = (f32[128,128]{1,0:T(8,128)}, f32[128,128]{1,0:T(8,128)S(1)}, u32[]{:S(2)}, u32[]{:S(2)}) collective-permute-start(f32[128,128]{1,0:T(8,128)} %get-tuple-element.13), channel_id=1, source_target_pairs={{0,1},{1,0},{2,33},{3,32},{32,3},{33,2},{34,35},{35,34},{4,5},{5,4... | collective-permute-start | bytes 196616 | tf_op jit(solution)/shard_map/ppermute | solution.py:297
  14.5 0.0 collective-permute-done.first_ref
  14.5 3.2 %collective-permute-done.1.second_ref = f32[128,128]{1,0:T(8,128)S(1)} collective-permute-done((f32[128,128]{1,0:T(8,128)}, f32[128,128]{1,0:T(8,128)S(1)}, u32[]{:S(2)}, u32[]{:S(2)}) %collective-permute-start.1) | collective-permute-done | bytes 65568 | tf_op jit(solution)/shard_map/ppermute | solution.py:297
  17.7 1.0 shard_map.77
  18.7 7.1 %all-to-all-start = ((f32[8,2,128,128]{3,2,1,0:T(8,128)}), f32[8,2,128,128]{3,2,1,0:T(8,128)S(1)}, u32[]{:S(2)}, u32[]{:S(2)}) async-start(f32[8,2,128,128]{3,2,1,0:T(8,128)} %shard_map.77), calls=%async_computation | async-start | bytes 2097152 | tf_op jit(solution)/shard_map/all_to_all | solution.py:292
  25.8 0.0 all-gather.7.cloned.1.call-start
  25.9 0.0 copy-done.1
  25.9 0.7 collective-permute-start.3
  26.6 3.3 %collective-permute-start.4 = (f32[128,128]{1,0:T(8,128)S(1)}, f32[128,128]{1,0:T(8,128)S(1)}, u32[]{:S(2)}, u32[]{:S(2)}) collective-permute-start(f32[128,128]{1,0:T(8,128)S(1)} %get-tuple-element.22), channel_id=1, source_target_pairs={{0,1},{1,0},{2,33},{3,32},{32,3},{33,2},{34,35},{35,34},{4,5},{5,4... | collective-permute-start | bytes 196616 | tf_op jit(solution)/shard_map/ppermute | solution.py:297
  29.9 0.0 collective-permute-done.3
  29.9 2.8 %collective-permute-done.4 = f32[128,128]{1,0:T(8,128)S(1)} collective-permute-done((f32[128,128]{1,0:T(8,128)S(1)}, f32[128,128]{1,0:T(8,128)S(1)}, u32[]{:S(2)}, u32[]{:S(2)}) %collective-permute-start.4) | collective-permute-done | bytes 65568 | tf_op jit(solution)/shard_map/ppermute | solution.py:297
  32.7 0.7 pad_maximum_fusion
  33.4 0.0 all-gather.7.cloned.1.call-update
  33.4 22.2 %all-to-all-done.own_hbm = f32[8,2,128,128]{3,2,1,0:T(8,128)S(1)} async-done(((f32[8,2,128,128]{3,2,1,0:T(8,128)}), f32[8,2,128,128]{3,2,1,0:T(8,128)S(1)}, u32[]{:S(2)}, u32[]{:S(2)}) %all-to-all-start) | async-done | bytes 1048608 | tf_op jit(solution)/shard_map/all_to_all | solution.py:292
  55.6 1.9 %collective-permute-start.2 = (f32[8,2,128,128]{3,2,1,0:T(8,128)S(1)}, f32[8,2,128,128]{3,2,1,0:T(8,128)S(1)}, u32[]{:S(2)}, u32[]{:S(2)}) collective-permute-start(f32[8,2,128,128]{3,2,1,0:T(8,128)S(1)} %all-to-all-done.own_hbm), channel_id=1, source_target_pairs={{0,32},{32,0},{1,33},{33,1},{2,34},{34,2},{3,35},{35,3},{4,36},{36... | collective-permute-start | bytes 3145736 | tf_op jit(solution)/shard_map/ppermute | solution.py:301
  57.5 2.6 %collective-permute-done.2.other_hbm = f32[8,2,128,128]{3,2,1,0:T(8,128)S(1)} collective-permute-done((f32[8,2,128,128]{3,2,1,0:T(8,128)S(1)}, f32[8,2,128,128]{3,2,1,0:T(8,128)S(1)}, u32[]{:S(2)}, u32[]{:S(2)}) %collective-permute-start.2) | collective-permute-done | bytes 1048608 | tf_op jit(solution)/shard_map/ppermute | solution.py:301
  60.1 0.0 all-gather.5.cloned.1.call-done
  60.1 2.4 %shard_map.78 = f32[4,256,128]{2,1,0:T(8,128)S(1)} custom-call(s32[1]{0:T(128)} %bitcast.at_ref, f32[8,512,128]{2,1,0:T(8,128)} %bitcast.5, f32[8,2,128,128]{3,2,1,0:T(8,128)S(1)} %all-to-all-done.own_hbm, f32[8,2,128,128]{3,2,1,0:T(8,128)S(1)} %collective-permute-done.2.other_hbm), custom_call_target="tpu_custom_call" | custom-call | flops 1610612736 | bytes 3145728 | tf_op jit(solution)/shard_map/pallas_call | solution.py:155
  62.5 11.4 %all_to_all.20 = f32[4,256,128]{2,1,0:T(8,128)S(1)} all-to-all(f32[4,256,128]{2,1,0:T(8,128)S(1)} %shard_map.78), channel_id=1, replica_groups={{0,1,2,3},{34,35,32,33},{4,5,6,7},{38,39,36,37},{8,9,10,11},{42,43,40,4..., dimensions={0} | all-to-all | bytes 1048576 | tf_op jit(solution)/shard_map/all_to_all | solution.py:292
  74.0 1.1 broadcast_in_dim.2
  75.1 9.1 %all-to-all-start.2 = ((f32[8,256,128]{2,1,0:T(8,128)}), f32[8,256,128]{2,1,0:T(8,128)S(1)}, u32[]{:S(2)}, u32[]{:S(2)}) async-start(f32[8,256,128]{2,1,0:T(8,128)} %broadcast_in_dim.2), calls=%async_computation.2 | async-start | bytes 2097152 | tf_op jit(solution)/shard_map/all_to_all | solution.py:292
  84.2 16.5 %all-gather.7.cloned.1.call-done = f32[4096,128]{1,0:T(8,128)} async-done(((f32[256,128]{1,0:T(8,128)}), f32[4096,128]{1,0:T(8,128)}) %all-gather.7.cloned.1.call-update) | async-done | bytes 2097168 | tf_op jit(solution)/shard_map/all_gather | solution.py:317
  100.7 4.3 %shard_map.79 = (f32[12,256,128]{2,1,0:T(8,128)}, bf16[2,1024,256]{2,1,0:T(8,128)(2,1)}, bf16[2,1024,256]{2,1,0:T(8,128)(2,1)}) custom-call(s32[1]{0:T(128)} %bitcast.at_ref, f32[8,512,128]{2,1,0:T(8,128)} %bitcast.6, f32[2,8,256,128]{3,2,1,0:T(8,128)} %bitcast.7), custom_call_target="tpu_custom_call" | custom-call | flops 1610612736 | bytes 6291456 | tf_op jit(solution)/shard_map/pallas_call | solution.py:213
  104.9 3.8 %all-to-all-done.2.w_hbm = f32[8,256,128]{2,1,0:T(8,128)S(1)} async-done(((f32[8,256,128]{2,1,0:T(8,128)}), f32[8,256,128]{2,1,0:T(8,128)S(1)}, u32[]{:S(2)}, u32[]{:S(2)}) %all-to-all-start.2) | async-done | bytes 1048608 | tf_op jit(solution)/shard_map/all_to_all | solution.py:292
  108.7 17.1 %shard_map.80 = f32[4,512,128]{2,1,0:T(8,128)} custom-call(s32[1]{0:T(128)} %bitcast.at_ref, f32[8,256,128]{2,1,0:T(8,128)S(1)} %all-to-all-done.2.w_hbm, bf16[2,1024,256]{2,1,0:T(8,128)(2,1)} %get-tuple-element.16.hi_hbm, bf16[2,1024,256]{2,1,0:T(8,128)(2,1)} %get-tuple-element.17.lo_hbm, f32[12,256,128]{2,1,0:T(8,128)} %get-tuple-element.18.rest_hbm), custom_call_target="tpu_custom_call" | custom-call | tf_op jit(solution)/shard_map/pallas_call | solution.py:263
  125.9 0.0 copy-start
  125.9 4.9 %all-to-all-start.3 = ((f32[4,512,128]{2,1,0:T(8,128)}), f32[4,512,128]{2,1,0:T(8,128)S(1)}, u32[]{:S(2)}, u32[]{:S(2)}) async-start(f32[4,512,128]{2,1,0:T(8,128)} %shard_map.80), calls=%async_computation.3 | async-start | bytes 2097152 | tf_op jit(solution)/shard_map/all_to_all | solution.py:292
  130.8 0.7 neg.3
  131.5 14.2 %all-to-all-done.3 = f32[4,512,128]{2,1,0:T(8,128)S(1)} async-done(((f32[4,512,128]{2,1,0:T(8,128)}), f32[4,512,128]{2,1,0:T(8,128)S(1)}, u32[]{:S(2)}, u32[]{:S(2)}) %all-to-all-start.3) | async-done | bytes 1048608 | tf_op jit(solution)/shard_map/all_to_all | solution.py:292
  145.6 0.1 reduce_sum.19
  145.7 0.0 copy-done
  145.7 0.7 slice_add_fusion
  (2 shorter events, 0.0 us)
Async XLA Ops:
  7.2 53.0 %all-gather.5.cloned.1.call-start = ((), (), s32[]{:S(2)}) async-start(), calls=%async_computation.4 | async-start | bytes 2359296 | tf_op jit(solution)/shard_map/all_gather | solution.py:308
  7.2 18.6 %copy-start.1 = (f32[256,128]{1,0:T(8,128)S(1)}, f32[256,128]{1,0:T(8,128)}, u32[]{:S(2)}) copy-start(f32[256,128]{1,0:T(8,128)} %param.7) | copy-start | bytes 393220
  9.6 4.9 %collective-permute-start = (f32[128,128]{1,0:T(8,128)}, f32[128,128]{1,0:T(8,128)S(1)}, u32[]{:S(2)}, u32[]{:S(2)}) collective-permute-start(f32[128,128]{1,0:T(8,128)} %get-tuple-element.12), channel_id=1, source_target_pairs={{0,0},{1,1},{2,32},{3,33},{32,2},{33,3},{34,34},{35,35},{4,4},{5,5... | collective-permute-start | bytes 196616 | tf_op jit(solution)/shard_map/ppermute | solution.py:297
  11.1 6.6 %collective-permute-start.1 = (f32[128,128]{1,0:T(8,128)}, f32[128,128]{1,0:T(8,128)S(1)}, u32[]{:S(2)}, u32[]{:S(2)}) collective-permute-start(f32[128,128]{1,0:T(8,128)} %get-tuple-element.13), channel_id=1, source_target_pairs={{0,1},{1,0},{2,33},{3,32},{32,3},{33,2},{34,35},{35,34},{4,5},{5,4... | collective-permute-start | bytes 196616 | tf_op jit(solution)/shard_map/ppermute | solution.py:297
  18.7 36.9 %all-to-all-start = ((f32[8,2,128,128]{3,2,1,0:T(8,128)}), f32[8,2,128,128]{3,2,1,0:T(8,128)S(1)}, u32[]{:S(2)}, u32[]{:S(2)}) async-start(f32[8,2,128,128]{3,2,1,0:T(8,128)} %shard_map.77), calls=%async_computation | async-start | bytes 2097152 | tf_op jit(solution)/shard_map/all_to_all | solution.py:292
  25.8 74.9 %all-gather.7.cloned.1.call-start = ((), (), s32[]{:S(2)}) async-start(), calls=%async_computation.5 | async-start | bytes 2228224 | tf_op jit(solution)/shard_map/all_gather | solution.py:317
  25.9 4.0 %collective-permute-start.3 = (f32[128,128]{1,0:T(8,128)S(1)}, f32[128,128]{1,0:T(8,128)S(1)}, u32[]{:S(2)}, u32[]{:S(2)}) collective-permute-start(f32[128,128]{1,0:T(8,128)S(1)} %get-tuple-element.21), channel_id=1, source_target_pairs={{0,0},{1,1},{2,32},{3,33},{32,2},{33,3},{34,34},{35,35},{4,4},{5,5... | collective-permute-start | bytes 196616 | tf_op jit(solution)/shard_map/ppermute | solution.py:297
  26.6 6.2 %collective-permute-start.4 = (f32[128,128]{1,0:T(8,128)S(1)}, f32[128,128]{1,0:T(8,128)S(1)}, u32[]{:S(2)}, u32[]{:S(2)}) collective-permute-start(f32[128,128]{1,0:T(8,128)S(1)} %get-tuple-element.22), channel_id=1, source_target_pairs={{0,1},{1,0},{2,33},{3,32},{32,3},{33,2},{34,35},{35,34},{4,5},{5,4... | collective-permute-start | bytes 196616 | tf_op jit(solution)/shard_map/ppermute | solution.py:297
  55.6 4.5 %collective-permute-start.2 = (f32[8,2,128,128]{3,2,1,0:T(8,128)S(1)}, f32[8,2,128,128]{3,2,1,0:T(8,128)S(1)}, u32[]{:S(2)}, u32[]{:S(2)}) collective-permute-start(f32[8,2,128,128]{3,2,1,0:T(8,128)S(1)} %all-to-all-done.own_hbm), channel_id=1, source_target_pairs={{0,32},{32,0},{1,33},{33,1},{2,34},{34,2},{3,35},{35,3},{4,36},{36... | collective-permute-start | bytes 3145736 | tf_op jit(solution)/shard_map/ppermute | solution.py:301
  75.1 33.6 %all-to-all-start.2 = ((f32[8,256,128]{2,1,0:T(8,128)}), f32[8,256,128]{2,1,0:T(8,128)S(1)}, u32[]{:S(2)}, u32[]{:S(2)}) async-start(f32[8,256,128]{2,1,0:T(8,128)} %broadcast_in_dim.2), calls=%async_computation.2 | async-start | bytes 2097152 | tf_op jit(solution)/shard_map/all_to_all | solution.py:292
  125.9 19.9 %copy-start = (f32[256,128]{1,0:T(8,128)S(1)}, f32[256,128]{1,0:T(8,128)}, u32[]{:S(2)}) copy-start(f32[256,128]{1,0:T(8,128)} %param.9) | copy-start | bytes 393220
  125.9 19.8 %all-to-all-start.3 = ((f32[4,512,128]{2,1,0:T(8,128)}), f32[4,512,128]{2,1,0:T(8,128)S(1)}, u32[]{:S(2)}, u32[]{:S(2)}) async-start(f32[4,512,128]{2,1,0:T(8,128)} %shard_map.80), calls=%async_computation.3 | async-start | bytes 2097152 | tf_op jit(solution)/shard_map/all_to_all | solution.py:292
Sparse Core Ops, SparseCore 0:
  10.1 46.1 all-gather.4
  59.0 41.6 all-gather.6

commit v12 on v11

--- a/solution.py
+++ b/solution.py
@@ -198,13 +198,14 @@
                 bh[n, rows, cols], bl[n, rows, cols] = split2(value)
         stores.append(pltpu.make_async_copy(bh.at[n], hi_hbm.at[n], sems.at[3 + n]))
         stores.append(pltpu.make_async_copy(bl.at[n], lo_hbm.at[n], sems.at[5 + n]))
+        for store in stores[-2:]:
+            store.start()
         part = -three_pass(ah[...], al[...], bh[n], bl[n])
         out[2 * n] = part[:, :128]
         out[2 * n + 1] = part[:, 128:]
         pair, place = slice(2 * n, 2 * n + 2), pl.ds(2 * (n ^ core), 2)
         stores.append(pltpu.make_async_copy(out.at[pair], rest_hbm.at[place], sems.at[7 + n]))
-        for store in stores[3 * n :]:
-            store.start()
+        stores[-1].start()
     for store in stores:
         store.wait()
 
@@ -230,26 +231,30 @@
     )(at, gathered, lower)
 
 
-def last_kernel(at_ref, w_hbm, hi_hbm, lo_hbm, rest_hbm, out_hbm, w, ah, al, bh, bl, out, sems):
-    rest = pltpu.make_async_copy(rest_hbm.at[0:4], out_hbm.at[:, 256:512], sems.at[7])
+def last_kernel(at_ref, w_hbm, hi_hbm, lo_hbm, rest_hbm, out_hbm, w, ah, al, bh, bl, out, rest, sems):
     loads = [pltpu.make_async_copy(w_hbm, w, sems.at[0])]
     for n in range(2):
         loads.append(pltpu.make_async_copy(hi_hbm.at[n], bh.at[n], sems.at[1 + n]))
         loads.append(pltpu.make_async_copy(lo_hbm.at[n], bl.at[n], sems.at[3 + n]))
-    for load in loads + [rest]:
+    loads.append(pltpu.make_async_copy(rest_hbm.at[0:4], rest, sems.at[7]))
+    for load in loads:
         load.start()
     core = device(at_ref)[2]
     loads[0].wait()
     for z in range(8):
         rows = slice(128 * z, 128 * (z + 1))
         ah[:, rows], al[:, rows] = split2(w[z ^ (4 * core)])
-    stores = [rest]
+    stores = []
     for n in range(2):
         for load in loads[1 + 2 * n : 3 + 2 * n]:
             load.wait()
         part = three_pass(ah[...], al[...], bh[n], bl[n])
         out[2 * n] = part[:, :128]
         out[2 * n + 1] = part[:, 128:]
+        if n == 0:
+            loads[5].wait()
+            stores.append(pltpu.make_async_copy(rest, out_hbm.at[:, 256:512], sems.at[8]))
+            stores[-1].start()
         pair, place = slice(2 * n, 2 * n + 2), pl.ds(2 * (n ^ core), 2)
         stores.append(
             pltpu.make_async_copy(out.at[pair], out_hbm.at[place, 0:256], sems.at[5 + n])
@@ -272,7 +277,8 @@
             pltpu.VMEM((2, 1024, 256), BF16),
             pltpu.VMEM((2, 1024, 256), BF16),
             pltpu.VMEM((4, 256, 128), F32),
-            DMA((8,)),
+            pltpu.VMEM((4, 256, 128), F32),
+            DMA((9,)),
         ],
         compiler_params=MIDDLE,
     )(at, w, hi, lo, rest)

time: 154 us -> 141 us (0.916)
  Pallas kernels: 27.1 us -> 14 us
    pallas_call x1, Pallas kernels: 17.1 us -> 3.97 us  [last(): pl.pallas_call(last_kernel, out_shape=shape(4, 512, 128), in_specs=[SMEM]...]
where the time goes in v12:
time: 141 us; the launch traced here: 140 us
  waiting for transfers between devices  65.3 us (46%)
  starting transfers between devices  32 us (23%)
  between operations  14.2 us (10%)
  Pallas kernels  14 us (10%)
  blocking collectives  11.4 us (8%)
  other arithmetic  2.15 us (2%)
    all_to_all x3, waiting for transfers between devices, exchange(): return lax.all_to_all(v, axes, 0, 0, tiled=True, axis_index_groups=groups)  40.1 us
    all_to_all x3, starting transfers between devices, exchange(): return lax.all_to_all(v, axes, 0, 0, tiled=True, axis_index_groups=groups)  21.1 us
    all_gather x1, waiting for transfers between devices, shards(): lax.all_gather(lower, ('y', 'c'), axis=0, tiled=False, axis_index_groups=...  16.5 us
    all_to_all x1, blocking collectives, exchange(): return lax.all_to_all(v, axes, 0, 0, tiled=True, axis_index_groups=groups)  11.4 us
    ppermute x4, starting transfers between devices, deal(): return lax.ppermute(v, ('c', 'x'), moves)  8.89 us
    ppermute x4, waiting for transfers between devices, deal(): return lax.ppermute(v, ('c', 'x'), moves)  5.99 us
    pallas_call x1, Pallas kernels, side(): pl.pallas_call(side_kernel, out_shape=(shape(12, 256, 128),) + (shape(2,...  4.25 us
    pallas_call x1, Pallas kernels, last(): pl.pallas_call(last_kernel, out_shape=shape(4, 512, 128), in_specs=[SMEM]...  3.97 us
  transfers between devices with their start and end apart: 10, of which 7 were waited for; matrix products, arithmetic and copies ran while one was open for 2% of the time, Pallas kernels for 5%

profile of v12, /device:TPU:128, one launch (start us, length us, event | category | flops | bytes accessed | tf_op | source)
XLA Modules:
  0.0 140.1 jit_solution(13084998679297160449)
XLA Ops:
  7.2 0.0 all-gather.5.cloned.1.call-start
  7.2 0.0 copy-start.1
  7.2 2.3 %shard_map.76 = (f32[512,128]{1,0:T(8,128)}, f32[128,128]{1,0:T(8,128)}, f32[128,128]{1,0:T(8,128)}) custom-call(s32[1]{0:T(128)} %bitcast.at_ref, s32[32,128]{1,0:T(8,128)} %bitcast.4, f32[512,256]{1,0:T(8,128)} %root_hbm.1, f32[256,128]{1,0:T(8,128)} %upper_hbm.1), custom_call_target="tpu_custom_call" | custom-call | tf_op jit(solution)/shard_map/pallas_call | solution.py:92
  9.6 0.0 all-gather.5.cloned.1.call-update
  9.6 1.5 %collective-permute-start = (f32[128,128]{1,0:T(8,128)}, f32[128,128]{1,0:T(8,128)S(1)}, u32[]{:S(2)}, u32[]{:S(2)}) collective-permute-start(f32[128,128]{1,0:T(8,128)} %get-tuple-element.12), channel_id=1, source_target_pairs={{0,0},{1,1},{2,32},{3,33},{32,2},{33,3},{34,34},{35,35},{4,4},{5,5... | collective-permute-start | bytes 196616 | tf_op jit(solution)/shard_map/ppermute | solution.py:303
  11.1 3.4 %collective-permute-start.1 = (f32[128,128]{1,0:T(8,128)}, f32[128,128]{1,0:T(8,128)S(1)}, u32[]{:S(2)}, u32[]{:S(2)}) collective-permute-start(f32[128,128]{1,0:T(8,128)} %get-tuple-element.13), channel_id=1, source_target_pairs={{0,1},{1,0},{2,33},{3,32},{32,3},{33,2},{34,35},{35,34},{4,5},{5,4... | collective-permute-start | bytes 196616 | tf_op jit(solution)/shard_map/ppermute | solution.py:303
  14.5 0.0 collective-permute-done.first_ref
  14.5 3.2 %collective-permute-done.1.second_ref = f32[128,128]{1,0:T(8,128)S(1)} collective-permute-done((f32[128,128]{1,0:T(8,128)}, f32[128,128]{1,0:T(8,128)S(1)}, u32[]{:S(2)}, u32[]{:S(2)}) %collective-permute-start.1) | collective-permute-done | bytes 65568 | tf_op jit(solution)/shard_map/ppermute | solution.py:303
  17.7 1.0 shard_map.77
  18.7 7.1 %all-to-all-start = ((f32[8,2,128,128]{3,2,1,0:T(8,128)}), f32[8,2,128,128]{3,2,1,0:T(8,128)S(1)}, u32[]{:S(2)}, u32[]{:S(2)}) async-start(f32[8,2,128,128]{3,2,1,0:T(8,128)} %shard_map.77), calls=%async_computation | async-start | bytes 2097152 | tf_op jit(solution)/shard_map/all_to_all | solution.py:298
  25.8 0.0 all-gather.7.cloned.1.call-start
  25.9 0.0 copy-done.1
  25.9 0.7 collective-permute-start.3
  26.6 3.3 %collective-permute-start.4 = (f32[128,128]{1,0:T(8,128)S(1)}, f32[128,128]{1,0:T(8,128)S(1)}, u32[]{:S(2)}, u32[]{:S(2)}) collective-permute-start(f32[128,128]{1,0:T(8,128)S(1)} %get-tuple-element.22), channel_id=1, source_target_pairs={{0,1},{1,0},{2,33},{3,32},{32,3},{33,2},{34,35},{35,34},{4,5},{5,4... | collective-permute-start | bytes 196616 | tf_op jit(solution)/shard_map/ppermute | solution.py:303
  29.9 0.0 collective-permute-done.3
  29.9 2.8 %collective-permute-done.4 = f32[128,128]{1,0:T(8,128)S(1)} collective-permute-done((f32[128,128]{1,0:T(8,128)S(1)}, f32[128,128]{1,0:T(8,128)S(1)}, u32[]{:S(2)}, u32[]{:S(2)}) %collective-permute-start.4) | collective-permute-done | bytes 65568 | tf_op jit(solution)/shard_map/ppermute | solution.py:303
  32.7 0.7 pad_maximum_fusion
  33.4 0.0 all-gather.7.cloned.1.call-update
  33.4 22.2 %all-to-all-done.own_hbm = f32[8,2,128,128]{3,2,1,0:T(8,128)S(1)} async-done(((f32[8,2,128,128]{3,2,1,0:T(8,128)}), f32[8,2,128,128]{3,2,1,0:T(8,128)S(1)}, u32[]{:S(2)}, u32[]{:S(2)}) %all-to-all-start) | async-done | bytes 1048608 | tf_op jit(solution)/shard_map/all_to_all | solution.py:298
  55.6 1.9 %collective-permute-start.2 = (f32[8,2,128,128]{3,2,1,0:T(8,128)S(1)}, f32[8,2,128,128]{3,2,1,0:T(8,128)S(1)}, u32[]{:S(2)}, u32[]{:S(2)}) collective-permute-start(f32[8,2,128,128]{3,2,1,0:T(8,128)S(1)} %all-to-all-done.own_hbm), channel_id=1, source_target_pairs={{0,32},{32,0},{1,33},{33,1},{2,34},{34,2},{3,35},{35,3},{4,36},{36... | collective-permute-start | bytes 3145736 | tf_op jit(solution)/shard_map/ppermute | solution.py:307
  57.5 2.6 %collective-permute-done.2.other_hbm = f32[8,2,128,128]{3,2,1,0:T(8,128)S(1)} collective-permute-done((f32[8,2,128,128]{3,2,1,0:T(8,128)S(1)}, f32[8,2,128,128]{3,2,1,0:T(8,128)S(1)}, u32[]{:S(2)}, u32[]{:S(2)}) %collective-permute-start.2) | collective-permute-done | bytes 1048608 | tf_op jit(solution)/shard_map/ppermute | solution.py:307
  60.1 0.0 all-gather.5.cloned.1.call-done
  60.1 2.4 %shard_map.78 = f32[4,256,128]{2,1,0:T(8,128)S(1)} custom-call(s32[1]{0:T(128)} %bitcast.at_ref, f32[8,512,128]{2,1,0:T(8,128)} %bitcast.5, f32[8,2,128,128]{3,2,1,0:T(8,128)S(1)} %all-to-all-done.own_hbm, f32[8,2,128,128]{3,2,1,0:T(8,128)S(1)} %collective-permute-done.2.other_hbm), custom_call_target="tpu_custom_call" | custom-call | flops 1610612736 | bytes 3145728 | tf_op jit(solution)/shard_map/pallas_call | solution.py:155
  62.5 11.4 %all_to_all.20 = f32[4,256,128]{2,1,0:T(8,128)S(1)} all-to-all(f32[4,256,128]{2,1,0:T(8,128)S(1)} %shard_map.78), channel_id=1, replica_groups={{0,1,2,3},{34,35,32,33},{4,5,6,7},{38,39,36,37},{8,9,10,11},{42,43,40,4..., dimensions={0} | all-to-all | bytes 1048576 | tf_op jit(solution)/shard_map/all_to_all | solution.py:298
  74.0 1.1 broadcast_in_dim.2
  75.1 9.1 %all-to-all-start.2 = ((f32[8,256,128]{2,1,0:T(8,128)}), f32[8,256,128]{2,1,0:T(8,128)S(1)}, u32[]{:S(2)}, u32[]{:S(2)}) async-start(f32[8,256,128]{2,1,0:T(8,128)} %broadcast_in_dim.2), calls=%async_computation.2 | async-start | bytes 2097152 | tf_op jit(solution)/shard_map/all_to_all | solution.py:298
  84.2 16.5 %all-gather.7.cloned.1.call-done = f32[4096,128]{1,0:T(8,128)} async-done(((f32[256,128]{1,0:T(8,128)}), f32[4096,128]{1,0:T(8,128)}) %all-gather.7.cloned.1.call-update) | async-done | bytes 2097168 | tf_op jit(solution)/shard_map/all_gather | solution.py:323
  100.7 4.3 %shard_map.79 = (f32[12,256,128]{2,1,0:T(8,128)}, bf16[2,1024,256]{2,1,0:T(8,128)(2,1)}, bf16[2,1024,256]{2,1,0:T(8,128)(2,1)}) custom-call(s32[1]{0:T(128)} %bitcast.at_ref, f32[8,512,128]{2,1,0:T(8,128)} %bitcast.6, f32[2,8,256,128]{3,2,1,0:T(8,128)} %bitcast.7), custom_call_target="tpu_custom_call" | custom-call | flops 1610612736 | bytes 6291456 | tf_op jit(solution)/shard_map/pallas_call | solution.py:214
  104.9 3.8 %all-to-all-done.2.w_hbm = f32[8,256,128]{2,1,0:T(8,128)S(1)} async-done(((f32[8,256,128]{2,1,0:T(8,128)}), f32[8,256,128]{2,1,0:T(8,128)S(1)}, u32[]{:S(2)}, u32[]{:S(2)}) %all-to-all-start.2) | async-done | bytes 1048608 | tf_op jit(solution)/shard_map/all_to_all | solution.py:298
  108.7 4.0 %shard_map.80 = f32[4,512,128]{2,1,0:T(8,128)} custom-call(s32[1]{0:T(128)} %bitcast.at_ref, f32[8,256,128]{2,1,0:T(8,128)S(1)} %all-to-all-done.2.w_hbm, bf16[2,1024,256]{2,1,0:T(8,128)(2,1)} %get-tuple-element.16.hi_hbm, bf16[2,1024,256]{2,1,0:T(8,128)(2,1)} %get-tuple-element.17.lo_hbm, f32[12,256,128]{2,1,0:T(8,128)} %get-tuple-element.18.rest_hbm), custom_call_target="tpu_custom_call" | custom-call | tf_op jit(solution)/shard_map/pallas_call | solution.py:268
  112.7 0.0 copy-start
  112.7 4.9 %all-to-all-start.3 = ((f32[4,512,128]{2,1,0:T(8,128)}), f32[4,512,128]{2,1,0:T(8,128)S(1)}, u32[]{:S(2)}, u32[]{:S(2)}) async-start(f32[4,512,128]{2,1,0:T(8,128)} %shard_map.80), calls=%async_computation.3 | async-start | bytes 2097152 | tf_op jit(solution)/shard_map/all_to_all | solution.py:298
  117.6 0.7 neg.3
  118.3 14.2 %all-to-all-done.3 = f32[4,512,128]{2,1,0:T(8,128)S(1)} async-done(((f32[4,512,128]{2,1,0:T(8,128)}), f32[4,512,128]{2,1,0:T(8,128)S(1)}, u32[]{:S(2)}, u32[]{:S(2)}) %all-to-all-start.3) | async-done | bytes 1048608 | tf_op jit(solution)/shard_map/all_to_all | solution.py:298
  132.5 0.1 reduce_sum.19
  132.5 0.0 copy-done
  132.6 0.7 slice_add_fusion
  (2 shorter events, 0.0 us)
Async XLA Ops:
  7.2 53.0 %all-gather.5.cloned.1.call-start = ((), (), s32[]{:S(2)}) async-start(), calls=%async_computation.4 | async-start | bytes 2359296 | tf_op jit(solution)/shard_map/all_gather | solution.py:314
  7.2 18.6 %copy-start.1 = (f32[256,128]{1,0:T(8,128)S(1)}, f32[256,128]{1,0:T(8,128)}, u32[]{:S(2)}) copy-start(f32[256,128]{1,0:T(8,128)} %param.7) | copy-start | bytes 393220
  9.6 4.9 %collective-permute-start = (f32[128,128]{1,0:T(8,128)}, f32[128,128]{1,0:T(8,128)S(1)}, u32[]{:S(2)}, u32[]{:S(2)}) collective-permute-start(f32[128,128]{1,0:T(8,128)} %get-tuple-element.12), channel_id=1, source_target_pairs={{0,0},{1,1},{2,32},{3,33},{32,2},{33,3},{34,34},{35,35},{4,4},{5,5... | collective-permute-start | bytes 196616 | tf_op jit(solution)/shard_map/ppermute | solution.py:303
  11.1 6.6 %collective-permute-start.1 = (f32[128,128]{1,0:T(8,128)}, f32[128,128]{1,0:T(8,128)S(1)}, u32[]{:S(2)}, u32[]{:S(2)}) collective-permute-start(f32[128,128]{1,0:T(8,128)} %get-tuple-element.13), channel_id=1, source_target_pairs={{0,1},{1,0},{2,33},{3,32},{32,3},{33,2},{34,35},{35,34},{4,5},{5,4... | collective-permute-start | bytes 196616 | tf_op jit(solution)/shard_map/ppermute | solution.py:303
  18.7 36.9 %all-to-all-start = ((f32[8,2,128,128]{3,2,1,0:T(8,128)}), f32[8,2,128,128]{3,2,1,0:T(8,128)S(1)}, u32[]{:S(2)}, u32[]{:S(2)}) async-start(f32[8,2,128,128]{3,2,1,0:T(8,128)} %shard_map.77), calls=%async_computation | async-start | bytes 2097152 | tf_op jit(solution)/shard_map/all_to_all | solution.py:298
  25.8 74.9 %all-gather.7.cloned.1.call-start = ((), (), s32[]{:S(2)}) async-start(), calls=%async_computation.5 | async-start | bytes 2228224 | tf_op jit(solution)/shard_map/all_gather | solution.py:323
  25.9 4.0 %collective-permute-start.3 = (f32[128,128]{1,0:T(8,128)S(1)}, f32[128,128]{1,0:T(8,128)S(1)}, u32[]{:S(2)}, u32[]{:S(2)}) collective-permute-start(f32[128,128]{1,0:T(8,128)S(1)} %get-tuple-element.21), channel_id=1, source_target_pairs={{0,0},{1,1},{2,32},{3,33},{32,2},{33,3},{34,34},{35,35},{4,4},{5,5... | collective-permute-start | bytes 196616 | tf_op jit(solution)/shard_map/ppermute | solution.py:303
  26.6 6.2 %collective-permute-start.4 = (f32[128,128]{1,0:T(8,128)S(1)}, f32[128,128]{1,0:T(8,128)S(1)}, u32[]{:S(2)}, u32[]{:S(2)}) collective-permute-start(f32[128,128]{1,0:T(8,128)S(1)} %get-tuple-element.22), channel_id=1, source_target_pairs={{0,1},{1,0},{2,33},{3,32},{32,3},{33,2},{34,35},{35,34},{4,5},{5,4... | collective-permute-start | bytes 196616 | tf_op jit(solution)/shard_map/ppermute | solution.py:303
  55.6 4.5 %collective-permute-start.2 = (f32[8,2,128,128]{3,2,1,0:T(8,128)S(1)}, f32[8,2,128,128]{3,2,1,0:T(8,128)S(1)}, u32[]{:S(2)}, u32[]{:S(2)}) collective-permute-start(f32[8,2,128,128]{3,2,1,0:T(8,128)S(1)} %all-to-all-done.own_hbm), channel_id=1, source_target_pairs={{0,32},{32,0},{1,33},{33,1},{2,34},{34,2},{3,35},{35,3},{4,36},{36... | collective-permute-start | bytes 3145736 | tf_op jit(solution)/shard_map/ppermute | solution.py:307
  75.1 33.6 %all-to-all-start.2 = ((f32[8,256,128]{2,1,0:T(8,128)}), f32[8,256,128]{2,1,0:T(8,128)S(1)}, u32[]{:S(2)}, u32[]{:S(2)}) async-start(f32[8,256,128]{2,1,0:T(8,128)} %broadcast_in_dim.2), calls=%async_computation.2 | async-start | bytes 2097152 | tf_op jit(solution)/shard_map/all_to_all | solution.py:298
  112.7 19.9 %copy-start = (f32[256,128]{1,0:T(8,128)S(1)}, f32[256,128]{1,0:T(8,128)}, u32[]{:S(2)}) copy-start(f32[256,128]{1,0:T(8,128)} %param.9) | copy-start | bytes 393220
  112.7 19.8 %all-to-all-start.3 = ((f32[4,512,128]{2,1,0:T(8,128)}), f32[4,512,128]{2,1,0:T(8,128)S(1)}, u32[]{:S(2)}, u32[]{:S(2)}) async-start(f32[4,512,128]{2,1,0:T(8,128)} %shard_map.80), calls=%async_computation.3 | async-start | bytes 2097152 | tf_op jit(solution)/shard_map/all_to_all | solution.py:298
Sparse Core Ops, SparseCore 0:
  10.1 46.1 all-gather.4
  59.0 41.6 all-gather.6

commit v13 on v10

--- a/solution.py
+++ b/solution.py
@@ -14,7 +14,7 @@
 PARAMS = pltpu.CompilerParams(vmem_limit_bytes=32 * 1024 * 1024)
 WIDE = pltpu.CompilerParams(vmem_limit_bytes=62 * 1024 * 1024)
 NEAR = pltpu.CompilerParams(vmem_limit_bytes=51 * 1024 * 1024)
-MIDDLE = pltpu.CompilerParams(vmem_limit_bytes=52900 * 1024)
+MIDDLE = pltpu.CompilerParams(vmem_limit_bytes=53248 * 1024)
 DMA = pltpu.SemaphoreType.DMA
 
 
@@ -198,17 +198,19 @@
                 bh[n, rows, cols], bl[n, rows, cols] = split2(value)
         stores.append(pltpu.make_async_copy(bh.at[n], hi_hbm.at[n], sems.at[3 + n]))
         stores.append(pltpu.make_async_copy(bl.at[n], lo_hbm.at[n], sems.at[5 + n]))
+        for store in stores[-2:]:
+            store.start()
         part = -three_pass(ah[...], al[...], bh[n], bl[n])
         out[2 * n] = part[:, :128]
         out[2 * n + 1] = part[:, 128:]
         pair, place = slice(2 * n, 2 * n + 2), pl.ds(2 * (n ^ core), 2)
         stores.append(
-            pltpu.make_async_copy(out.at[pair, 0:128], top_hbm.at[place], sems.at[7 + n])
+            pltpu.make_async_copy(out.at[pair, 0:192], top_hbm.at[place], sems.at[7 + n])
         )
         stores.append(
-            pltpu.make_async_copy(out.at[pair, 128:256], rest_hbm.at[place], sems.at[9 + n])
+            pltpu.make_async_copy(out.at[pair, 192:256], rest_hbm.at[place], sems.at[9 + n])
         )
-        for store in stores[4 * n :]:
+        for store in stores[-2:]:
             store.start()
     for store in stores:
         store.wait()
@@ -217,7 +219,7 @@
 def side(at, gathered, lower):
     return pl.pallas_call(
         side_kernel,
-        out_shape=(shape(4, 128, 128),) * 2 + (shape(2, 1024, 256, dtype=BF16),) * 2,
+        out_shape=(shape(4, 192, 128), shape(48, 64, 128)) + (shape(2, 1024, 256, dtype=BF16),) * 2,
         in_specs=[SMEM, HBM, HBM],
         out_specs=(HBM,) * 4,
         scratch_shapes=[
@@ -235,26 +237,30 @@
     )(at, gathered, lower)
 
 
-def last_kernel(at_ref, w_hbm, hi_hbm, lo_hbm, rest_hbm, out_hbm, w, ah, al, bh, bl, out, sems):
-    rest = pltpu.make_async_copy(rest_hbm, out_hbm.at[:, 256:384], sems.at[7])
+def last_kernel(at_ref, w_hbm, hi_hbm, lo_hbm, rest_hbm, out_hbm, w, ah, al, bh, bl, out, rest, sems):
     loads = [pltpu.make_async_copy(w_hbm, w, sems.at[0])]
     for n in range(2):
         loads.append(pltpu.make_async_copy(hi_hbm.at[n], bh.at[n], sems.at[1 + n]))
         loads.append(pltpu.make_async_copy(lo_hbm.at[n], bl.at[n], sems.at[3 + n]))
-    for load in loads + [rest]:
+    loads.append(pltpu.make_async_copy(rest_hbm.at[0:4], rest, sems.at[7]))
+    for load in loads:
         load.start()
     core = device(at_ref)[2]
     loads[0].wait()
     for z in range(8):
         rows = slice(128 * z, 128 * (z + 1))
         ah[:, rows], al[:, rows] = split2(w[z ^ (4 * core)])
-    stores = [rest]
+    stores = []
     for n in range(2):
         for load in loads[1 + 2 * n : 3 + 2 * n]:
             load.wait()
         part = three_pass(ah[...], al[...], bh[n], bl[n])
         out[2 * n] = part[:, :128]
         out[2 * n + 1] = part[:, 128:]
+        if n == 0:
+            loads[5].wait()
+            stores.append(pltpu.make_async_copy(rest, out_hbm.at[:, 256:320], sems.at[8]))
+            stores[-1].start()
         pair, place = slice(2 * n, 2 * n + 2), pl.ds(2 * (n ^ core), 2)
         stores.append(
             pltpu.make_async_copy(out.at[pair], out_hbm.at[place, 0:256], sems.at[5 + n])
@@ -267,7 +273,7 @@
 def last(at, w, hi, lo, rest):
     return pl.pallas_call(
         last_kernel,
-        out_shape=shape(4, 384, 128),
+        out_shape=shape(4, 320, 128),
         in_specs=[SMEM] + [HBM] * 4,
         out_specs=HBM,
         scratch_shapes=[
@@ -277,7 +283,8 @@
             pltpu.VMEM((2, 1024, 256), BF16),
             pltpu.VMEM((2, 1024, 256), BF16),
             pltpu.VMEM((4, 256, 128), F32),
-            DMA((8,)),
+            pltpu.VMEM((4, 64, 128), F32),
+            DMA((9,)),
         ],
         compiler_params=MIDDLE,
     )(at, w, hi, lo, rest)
@@ -329,7 +336,7 @@
     top, rest, hi, lo = side(at, gathered, lower)
     axes, groups = rotated("x", 4)
     top = lax.psum_scatter(
-        top.reshape(512, 128), axes, scatter_dimension=0, tiled=True, axis_index_groups=groups
+        top.reshape(768, 128), axes, scatter_dimension=0, tiled=True, axis_index_groups=groups
     )
     sums = exchange(last(at, w_all, hi, lo, rest), "x", 4).sum(axis=0)
     return (jnp.concatenate([top, sums[256:]], axis=0), -w, diagonal_inverse + sums[:256])

time: 154 us -> 144 us (0.935)
  the two profiles are of different devices: /device:TPU:1 before, /device:TPU:16 now
where the time goes in v13:
time: 144 us; the launch traced here: 143 us
  waiting for transfers between devices  67.5 us (47%)
  starting transfers between devices  31.3 us (22%)
  Pallas kernels  14 us (10%)
  between operations  13.9 us (10%)
  blocking collectives  11.5 us (8%)
  other arithmetic  3.62 us (3%)
    all_to_all x3, waiting for transfers between devices, exchange(): return lax.all_to_all(v, axes, 0, 0, tiled=True, axis_index_groups=groups)  35.4 us
    all_to_all x3, starting transfers between devices, exchange(): return lax.all_to_all(v, axes, 0, 0, tiled=True, axis_index_groups=groups)  21.8 us
    all_gather x1, waiting for transfers between devices, shards(): lax.all_gather(lower, ('y', 'c'), axis=0, tiled=False, axis_index_groups=...  17.5 us
    all_to_all x1, blocking collectives, exchange(): return lax.all_to_all(v, axes, 0, 0, tiled=True, axis_index_groups=groups)  11.5 us
    ppermute x4, waiting for transfers between devices, deal(): return lax.ppermute(v, ('c', 'x'), moves)  7.67 us
    ppermute x4, starting transfers between devices, deal(): return lax.ppermute(v, ('c', 'x'), moves)  7.47 us
    reduce_scatter x1, waiting for transfers between devices, shards(): lax.psum_scatter(top.reshape(768, 128), axes, scatter_dimension=0, tiled=...  4.36 us
    pallas_call x1, Pallas kernels, side(): pl.pallas_call(side_kernel, out_shape=(shape(4, 192, 128), shape(48, 64,...  4.29 us
  transfers between devices with their start and end apart: 11, of which 8 were waited for; matrix products, arithmetic and copies ran while one was open for 2% of the time, Pallas kernels for 8%

profile of v13, /device:TPU:16, one launch (start us, length us, event | category | flops | bytes accessed | tf_op | source)
XLA Modules:
  0.0 143.0 jit_solution(10181936218845817484)
XLA Ops:
  7.2 0.0 all-gather.5.cloned.1.call-start
  7.2 0.0 copy-start.1
  7.2 2.3 %shard_map.76 = (f32[512,128]{1,0:T(8,128)}, f32[128,128]{1,0:T(8,128)}, f32[128,128]{1,0:T(8,128)}) custom-call(s32[1]{0:T(128)} %bitcast.at_ref, s32[32,128]{1,0:T(8,128)} %bitcast.6, f32[512,256]{1,0:T(8,128)} %root_hbm.1, f32[256,128]{1,0:T(8,128)} %upper_hbm.1), custom_call_target="tpu_custom_call" | custom-call | tf_op jit(solution)/shard_map/pallas_call | solution.py:92
  9.6 0.0 all-gather.5.cloned.1.call-update
  9.6 1.5 %collective-permute-start = (f32[128,128]{1,0:T(8,128)}, f32[128,128]{1,0:T(8,128)S(1)}, u32[]{:S(2)}, u32[]{:S(2)}) collective-permute-start(f32[128,128]{1,0:T(8,128)} %get-tuple-element.13), channel_id=1, source_target_pairs={{0,0},{1,1},{2,32},{3,33},{32,2},{33,3},{34,34},{35,35},{4,4},{5,5... | collective-permute-start | bytes 196616 | tf_op jit(solution)/shard_map/ppermute | solution.py:309
  11.1 3.4 %collective-permute-start.1 = (f32[128,128]{1,0:T(8,128)}, f32[128,128]{1,0:T(8,128)S(1)}, u32[]{:S(2)}, u32[]{:S(2)}) collective-permute-start(f32[128,128]{1,0:T(8,128)} %get-tuple-element.14), channel_id=1, source_target_pairs={{0,1},{1,0},{2,33},{3,32},{32,3},{33,2},{34,35},{35,34},{4,5},{5,4... | collective-permute-start | bytes 196616 | tf_op jit(solution)/shard_map/ppermute | solution.py:309
  14.5 0.0 collective-permute-done.first_ref
  14.5 3.2 %collective-permute-done.1.second_ref = f32[128,128]{1,0:T(8,128)S(1)} collective-permute-done((f32[128,128]{1,0:T(8,128)}, f32[128,128]{1,0:T(8,128)S(1)}, u32[]{:S(2)}, u32[]{:S(2)}) %collective-permute-start.1) | collective-permute-done | bytes 65568 | tf_op jit(solution)/shard_map/ppermute | solution.py:309
  17.7 1.1 shard_map.77
  18.7 8.9 %all-to-all-start = ((f32[8,2,128,128]{3,2,1,0:T(8,128)}), f32[8,2,128,128]{3,2,1,0:T(8,128)S(1)}, u32[]{:S(2)}, u32[]{:S(2)}) async-start(f32[8,2,128,128]{3,2,1,0:T(8,128)} %shard_map.77), calls=%async_computation.1 | async-start | bytes 2097152 | tf_op jit(solution)/shard_map/all_to_all | solution.py:304
  27.7 0.0 all-gather.7.cloned.1.call-start
  27.7 0.0 copy-done.1
  27.7 0.7 collective-permute-start.2
  28.4 1.9 %collective-permute-start.3 = (f32[128,128]{1,0:T(8,128)S(1)}, f32[128,128]{1,0:T(8,128)S(1)}, u32[]{:S(2)}, u32[]{:S(2)}) collective-permute-start(f32[128,128]{1,0:T(8,128)S(1)} %get-tuple-element.22), channel_id=1, source_target_pairs={{0,1},{1,0},{2,33},{3,32},{32,3},{33,2},{34,35},{35,34},{4,5},{5,4... | collective-permute-start | bytes 196616 | tf_op jit(solution)/shard_map/ppermute | solution.py:309
  30.3 0.0 collective-permute-done.2
  30.3 4.5 %collective-permute-done.3 = f32[128,128]{1,0:T(8,128)S(1)} collective-permute-done((f32[128,128]{1,0:T(8,128)S(1)}, f32[128,128]{1,0:T(8,128)S(1)}, u32[]{:S(2)}, u32[]{:S(2)}) %collective-permute-start.3) | collective-permute-done | bytes 65568 | tf_op jit(solution)/shard_map/ppermute | solution.py:309
  34.8 0.7 pad_maximum_fusion
  35.5 0.0 all-gather.7.cloned.1.call-update
  35.5 19.8 %all-to-all-done.own_hbm = f32[8,2,128,128]{3,2,1,0:T(8,128)S(1)} async-done(((f32[8,2,128,128]{3,2,1,0:T(8,128)}), f32[8,2,128,128]{3,2,1,0:T(8,128)S(1)}, u32[]{:S(2)}, u32[]{:S(2)}) %all-to-all-start) | async-done | bytes 1048608 | tf_op jit(solution)/shard_map/all_to_all | solution.py:304
  55.3 2.0 %collective-permute-start.4 = (f32[8,2,128,128]{3,2,1,0:T(8,128)S(1)}, f32[8,2,128,128]{3,2,1,0:T(8,128)S(1)}, u32[]{:S(2)}, u32[]{:S(2)}) collective-permute-start(f32[8,2,128,128]{3,2,1,0:T(8,128)S(1)} %all-to-all-done.own_hbm), channel_id=1, source_target_pairs={{0,32},{32,0},{1,33},{33,1},{2,34},{34,2},{3,35},{35,3},{4,36},{36... | collective-permute-start | bytes 3145736 | tf_op jit(solution)/shard_map/ppermute | solution.py:313
  57.3 2.5 %collective-permute-done.4.other_hbm = f32[8,2,128,128]{3,2,1,0:T(8,128)S(1)} collective-permute-done((f32[8,2,128,128]{3,2,1,0:T(8,128)S(1)}, f32[8,2,128,128]{3,2,1,0:T(8,128)S(1)}, u32[]{:S(2)}, u32[]{:S(2)}) %collective-permute-start.4) | collective-permute-done | bytes 1048608 | tf_op jit(solution)/shard_map/ppermute | solution.py:313
  59.9 0.0 all-gather.5.cloned.1.call-done
  59.9 2.4 %shard_map.79 = f32[4,256,128]{2,1,0:T(8,128)S(1)} custom-call(s32[1]{0:T(128)} %bitcast.at_ref, f32[8,512,128]{2,1,0:T(8,128)} %bitcast.7, f32[8,2,128,128]{3,2,1,0:T(8,128)S(1)} %all-to-all-done.own_hbm, f32[8,2,128,128]{3,2,1,0:T(8,128)S(1)} %collective-permute-done.4.other_hbm), custom_call_target="tpu_custom_call" | custom-call | flops 1610612736 | bytes 3145728 | tf_op jit(solution)/shard_map/pallas_call | solution.py:155
  62.3 11.5 %all_to_all.20 = f32[4,256,128]{2,1,0:T(8,128)S(1)} all-to-all(f32[4,256,128]{2,1,0:T(8,128)S(1)} %shard_map.79), channel_id=1, replica_groups={{0,1,2,3},{34,35,32,33},{4,5,6,7},{38,39,36,37},{8,9,10,11},{42,43,40,4..., dimensions={0} | all-to-all | bytes 1048576 | tf_op jit(solution)/shard_map/all_to_all | solution.py:304
  73.8 1.1 broadcast_in_dim.2
  74.9 8.4 %all-to-all-start.2 = ((f32[8,256,128]{2,1,0:T(8,128)}), f32[8,256,128]{2,1,0:T(8,128)S(1)}, u32[]{:S(2)}, u32[]{:S(2)}) async-start(f32[8,256,128]{2,1,0:T(8,128)} %broadcast_in_dim.2), calls=%async_computation.3 | async-start | bytes 2097152 | tf_op jit(solution)/shard_map/all_to_all | solution.py:304
  83.3 0.0 reduce-scatter.2.cloned.1.call-start
  83.4 17.5 %all-gather.7.cloned.1.call-done = f32[4096,128]{1,0:T(8,128)} async-done(((f32[256,128]{1,0:T(8,128)}), f32[4096,128]{1,0:T(8,128)}) %all-gather.7.cloned.1.call-update) | async-done | bytes 2097168 | tf_op jit(solution)/shard_map/all_gather | solution.py:329
  100.9 4.3 %shard_map.78 = (f32[4,192,128]{2,1,0:T(8,128)}, f32[48,64,128]{2,1,0:T(8,128)}, bf16[2,1024,256]{2,1,0:T(8,128)(2,1)}, bf16[2,1024,256]{2,1,0:T(8,128)(2,1)}) custom-call(s32[1]{0:T(128)} %bitcast.at_ref, f32[8,512,128]{2,1,0:T(8,128)} %bitcast.8, f32[2,8,256,128]{3,2,1,0:T(8,128)} %bitcast.9), custom_call_target="tpu_custom_call" | custom-call | flops 1610612736 | bytes 6291456 | tf_op jit(solution)/shard_map/pallas_call | solution.py:220
  105.2 0.0 reduce-scatter.2.cloned.1.call-update
  105.2 3.5 %all-to-all-done.2.w_hbm = f32[8,256,128]{2,1,0:T(8,128)S(1)} async-done(((f32[8,256,128]{2,1,0:T(8,128)}), f32[8,256,128]{2,1,0:T(8,128)S(1)}, u32[]{:S(2)}, u32[]{:S(2)}) %all-to-all-start.2) | async-done | bytes 1048608 | tf_op jit(solution)/shard_map/all_to_all | solution.py:304
  108.7 4.0 %shard_map.80 = f32[4,320,128]{2,1,0:T(8,128)} custom-call(s32[1]{0:T(128)} %bitcast.at_ref, f32[8,256,128]{2,1,0:T(8,128)S(1)} %all-to-all-done.2.w_hbm, bf16[2,1024,256]{2,1,0:T(8,128)(2,1)} %get-tuple-element.18.hi_hbm, bf16[2,1024,256]{2,1,0:T(8,128)(2,1)} %get-tuple-element.19.lo_hbm, f32[48,64,128]{2,1,0:T(8,128)} %get-tuple-element.20.rest_hbm), custom_call_target="tpu_custom_call" | custom-call | tf_op jit(solution)/shard_map/pallas_call | solution.py:274
  112.7 0.0 copy-start
  112.7 4.4 %all-to-all-start.3 = ((f32[4,320,128]{2,1,0:T(8,128)}), f32[4,320,128]{2,1,0:T(8,128)S(1)}, u32[]{:S(2)}, u32[]{:S(2)}) async-start(f32[4,320,128]{2,1,0:T(8,128)} %shard_map.80), calls=%async_computation.4 | async-start | bytes 1310720 | tf_op jit(solution)/shard_map/all_to_all | solution.py:304
  117.1 0.7 neg.3
  117.8 12.0 %all-to-all-done.3 = f32[4,320,128]{2,1,0:T(8,128)S(1)} async-done(((f32[4,320,128]{2,1,0:T(8,128)}), f32[4,320,128]{2,1,0:T(8,128)S(1)}, u32[]{:S(2)}, u32[]{:S(2)}) %all-to-all-start.3) | async-done | bytes 655392 | tf_op jit(solution)/shard_map/all_to_all | solution.py:304
  129.9 0.0 copy-done
  129.9 0.7 slice_add_fusion
  130.5 4.4 %reduce-scatter.2.cloned.1.call-done = f32[192,128]{1,0:T(8,128)} async-done(((f32[768,128]{1,0:T(8,128)}), f32[192,128]{1,0:T(8,128)}) %reduce-scatter.2.cloned.1.call-update) | async-done | bytes 98320 | tf_op jit(solution)/shard_map/reduce_scatter | solution.py:338
  134.9 1.6 %pad_maximum_fusion.1 = f32[256,128]{1,0:T(8,128)} fusion(f32[64,128]{1,0:T(8,128)S(1)} %slice.8, f32[192,128]{1,0:T(8,128)} %reduce-scatter.2.cloned.1.call-done), kind=kLoop, calls=%fused_computation.2 | loop fusion | flops 32768 | bytes 262144 | tf_op jit(solution)/shard_map/concatenate | solution.py:342
  (4 shorter events, 0.1 us)
Async XLA Ops:
  7.2 52.7 %all-gather.5.cloned.1.call-start = ((), (), s32[]{:S(2)}) async-start(), calls=%async_computation.6 | async-start | bytes 2359296 | tf_op jit(solution)/shard_map/all_gather | solution.py:320
  7.2 20.4 %copy-start.1 = (f32[256,128]{1,0:T(8,128)S(1)}, f32[256,128]{1,0:T(8,128)}, u32[]{:S(2)}) copy-start(f32[256,128]{1,0:T(8,128)} %param.7) | copy-start | bytes 393220
  9.6 4.9 %collective-permute-start = (f32[128,128]{1,0:T(8,128)}, f32[128,128]{1,0:T(8,128)S(1)}, u32[]{:S(2)}, u32[]{:S(2)}) collective-permute-start(f32[128,128]{1,0:T(8,128)} %get-tuple-element.13), channel_id=1, source_target_pairs={{0,0},{1,1},{2,32},{3,33},{32,2},{33,3},{34,34},{35,35},{4,4},{5,5... | collective-permute-start | bytes 196616 | tf_op jit(solution)/shard_map/ppermute | solution.py:309
  11.1 6.6 %collective-permute-start.1 = (f32[128,128]{1,0:T(8,128)}, f32[128,128]{1,0:T(8,128)S(1)}, u32[]{:S(2)}, u32[]{:S(2)}) collective-permute-start(f32[128,128]{1,0:T(8,128)} %get-tuple-element.14), channel_id=1, source_target_pairs={{0,1},{1,0},{2,33},{3,32},{32,3},{33,2},{34,35},{35,34},{4,5},{5,4... | collective-permute-start | bytes 196616 | tf_op jit(solution)/shard_map/ppermute | solution.py:309
  18.7 36.6 %all-to-all-start = ((f32[8,2,128,128]{3,2,1,0:T(8,128)}), f32[8,2,128,128]{3,2,1,0:T(8,128)S(1)}, u32[]{:S(2)}, u32[]{:S(2)}) async-start(f32[8,2,128,128]{3,2,1,0:T(8,128)} %shard_map.77), calls=%async_computation.1 | async-start | bytes 2097152 | tf_op jit(solution)/shard_map/all_to_all | solution.py:304
  27.7 73.2 %all-gather.7.cloned.1.call-start = ((), (), s32[]{:S(2)}) async-start(), calls=%async_computation.7 | async-start | bytes 2228224 | tf_op jit(solution)/shard_map/all_gather | solution.py:329
  27.7 2.6 %collective-permute-start.2 = (f32[128,128]{1,0:T(8,128)S(1)}, f32[128,128]{1,0:T(8,128)S(1)}, u32[]{:S(2)}, u32[]{:S(2)}) collective-permute-start(f32[128,128]{1,0:T(8,128)S(1)} %get-tuple-element.21), channel_id=1, source_target_pairs={{0,0},{1,1},{2,32},{3,33},{32,2},{33,3},{34,34},{35,35},{4,4},{5,5... | collective-permute-start | bytes 196616 | tf_op jit(solution)/shard_map/ppermute | solution.py:309
  28.4 6.4 %collective-permute-start.3 = (f32[128,128]{1,0:T(8,128)S(1)}, f32[128,128]{1,0:T(8,128)S(1)}, u32[]{:S(2)}, u32[]{:S(2)}) collective-permute-start(f32[128,128]{1,0:T(8,128)S(1)} %get-tuple-element.22), channel_id=1, source_target_pairs={{0,1},{1,0},{2,33},{3,32},{32,3},{33,2},{34,35},{35,34},{4,5},{5,4... | collective-permute-start | bytes 196616 | tf_op jit(solution)/shard_map/ppermute | solution.py:309
  55.3 4.5 %collective-permute-start.4 = (f32[8,2,128,128]{3,2,1,0:T(8,128)S(1)}, f32[8,2,128,128]{3,2,1,0:T(8,128)S(1)}, u32[]{:S(2)}, u32[]{:S(2)}) collective-permute-start(f32[8,2,128,128]{3,2,1,0:T(8,128)S(1)} %all-to-all-done.own_hbm), channel_id=1, source_target_pairs={{0,32},{32,0},{1,33},{33,1},{2,34},{34,2},{3,35},{35,3},{4,36},{36... | collective-permute-start | bytes 3145736 | tf_op jit(solution)/shard_map/ppermute | solution.py:313
  74.9 33.8 %all-to-all-start.2 = ((f32[8,256,128]{2,1,0:T(8,128)}), f32[8,256,128]{2,1,0:T(8,128)S(1)}, u32[]{:S(2)}, u32[]{:S(2)}) async-start(f32[8,256,128]{2,1,0:T(8,128)} %broadcast_in_dim.2), calls=%async_computation.3 | async-start | bytes 2097152 | tf_op jit(solution)/shard_map/all_to_all | solution.py:304
  83.3 51.6 %reduce-scatter.2.cloned.1.call-start = ((), (), s32[]{:S(2)}) async-start(), calls=%async_computation.5 | async-start | bytes 491520 | tf_op jit(solution)/shard_map/reduce_scatter | solution.py:338
  112.7 17.2 %copy-start = (f32[256,128]{1,0:T(8,128)S(1)}, f32[256,128]{1,0:T(8,128)}, u32[]{:S(2)}) copy-start(f32[256,128]{1,0:T(8,128)} %param.9) | copy-start | bytes 393220
  112.7 17.1 %all-to-all-start.3 = ((f32[4,320,128]{2,1,0:T(8,128)}), f32[4,320,128]{2,1,0:T(8,128)S(1)}, u32[]{:S(2)}, u32[]{:S(2)}) async-start(f32[4,320,128]{2,1,0:T(8,128)} %shard_map.80), calls=%async_computation.4 | async-start | bytes 1310720 | tf_op jit(solution)/shard_map/all_to_all | solution.py:304
Sparse Core Ops, SparseCore 0:
  10.1 48.5 all-gather.4
  61.4 39.4 all-gather.6
  105.3 29.5 reduce-scatter.1

commit v14 on v9

--- a/solution.py
+++ b/solution.py
@@ -14,7 +14,7 @@
 PARAMS = pltpu.CompilerParams(vmem_limit_bytes=32 * 1024 * 1024)
 WIDE = pltpu.CompilerParams(vmem_limit_bytes=62 * 1024 * 1024)
 NEAR = pltpu.CompilerParams(vmem_limit_bytes=51 * 1024 * 1024)
-MIDDLE = pltpu.CompilerParams(vmem_limit_bytes=52 * 1024 * 1024)
+MIDDLE = pltpu.CompilerParams(vmem_limit_bytes=51 * 1024 * 1024)
 DMA = pltpu.SemaphoreType.DMA
 
 
@@ -220,7 +220,7 @@
 def side(at, gathered, lower):
     return pl.pallas_call(
         side_kernel,
-        out_shape=(shape(4, 256, 128),) + (shape(1024, 512, dtype=BF16),) * 2,
+        out_shape=(shape(12, 256, 128),) + (shape(1024, 512, dtype=BF16),) * 2,
         in_specs=[SMEM, HBM, HBM],
         out_specs=(HBM,) * 3,
         scratch_shapes=[
@@ -238,11 +238,14 @@
     )(at, gathered, lower)
 
 
-def last_kernel(at_ref, w_hbm, hi_hbm, lo_hbm, out_hbm, w, ah, al, bh, bl, out, sems):
+def last_kernel(
+    at_ref, w_hbm, hi_hbm, lo_hbm, rest_hbm, out_hbm, w, ah, al, bh, bl, out, rest, sems
+):
     loads = [
         pltpu.make_async_copy(w_hbm, w, sems.at[0]),
         pltpu.make_async_copy(hi_hbm, bh, sems.at[1]),
         pltpu.make_async_copy(lo_hbm, bl, sems.at[2]),
+        pltpu.make_async_copy(rest_hbm.at[0:4], rest, sems.at[5]),
     ]
     for load in loads:
         load.start()
@@ -253,24 +256,25 @@
         ah[:, rows], al[:, rows] = split2(w[z ^ (4 * core)])
     for load in loads[1:]:
         load.wait()
-    stores = []
+    stores = [pltpu.make_async_copy(rest, out_hbm.at[:, 256:512], sems.at[6])]
+    stores[0].start()
     for n in range(2):
         cols = slice(256 * n, 256 * (n + 1))
         part = three_pass(ah[...], al[...], bh[:, cols], bl[:, cols])
         out[2 * n] = part[:, :128]
         out[2 * n + 1] = part[:, 128:]
         pair, place = slice(2 * n, 2 * n + 2), pl.ds(2 * (n ^ core), 2)
-        stores.append(pltpu.make_async_copy(out.at[pair], out_hbm.at[place], sems.at[3 + n]))
+        stores.append(pltpu.make_async_copy(out.at[pair], out_hbm.at[place, 0:256], sems.at[3 + n]))
         stores[-1].start()
     for store in stores:
         store.wait()
 
 
-def last(at, w, hi, lo):
+def last(at, w, hi, lo, rest):
     return pl.pallas_call(
         last_kernel,
-        out_shape=shape(4, 256, 128),
-        in_specs=[SMEM] + [HBM] * 3,
+        out_shape=shape(4, 512, 128),
+        in_specs=[SMEM] + [HBM] * 4,
         out_specs=HBM,
         scratch_shapes=[
             pltpu.VMEM((8, 256, 128), F32),
@@ -279,10 +283,11 @@
             pltpu.VMEM((1024, 512), BF16),
             pltpu.VMEM((1024, 512), BF16),
             pltpu.VMEM((4, 256, 128), F32),
-            DMA((5,)),
+            pltpu.VMEM((4, 256, 128), F32),
+            DMA((7,)),
         ],
         compiler_params=MIDDLE,
-    )(at, w, hi, lo)
+    )(at, w, hi, lo, rest)
 
 
 def rotated(axis, size):
@@ -328,13 +333,9 @@
     part = couple(at, gathered, own, other)
     w = exchange(part, "x", 4).sum(axis=0)
     w_all = exchange(jnp.broadcast_to(w[None], (8, 256, 128)), "z", 8)
-    sides, hi, lo = side(at, gathered, lower)
-    axes, groups = rotated("x", 4)
-    t = lax.psum_scatter(
-        sides.reshape(1024, 128), axes, scatter_dimension=0, tiled=True, axis_index_groups=groups
-    )
-    product = exchange(last(at, w_all, hi, lo), "x", 4).sum(axis=0)
-    return (t, -w, diagonal_inverse + product)
+    rest, hi, lo = side(at, gathered, lower)
+    sums = exchange(last(at, w_all, hi, lo, rest), "x", 4).sum(axis=0)
+    return (sums[256:], -w, diagonal_inverse + sums[:256])
 
 
 def solution(mesh):

time: 141 us -> 140 us (level)
  the two profiles are of different devices: /device:TPU:1 before, /device:TPU:128 now
where the time goes in v14:
time: 140 us
  waiting for transfers between devices  65.9 us (47%)
  starting transfers between devices  32 us (23%)
  between operations  14.2 us (10%)
  Pallas kernels  13 us (9%)
  blocking collectives  11.4 us (8%)
  other arithmetic  2.15 us (2%)
    all_to_all x3, waiting for transfers between devices, exchange(): return lax.all_to_all(v, axes, 0, 0, tiled=True, axis_index_groups=groups)  40.7 us
    all_to_all x3, starting transfers between devices, exchange(): return lax.all_to_all(v, axes, 0, 0, tiled=True, axis_index_groups=groups)  21.1 us
    all_gather x1, waiting for transfers between devices, shards(): lax.all_gather(lower, ('y', 'c'), axis=0, tiled=False, axis_index_groups=...  16.5 us
    all_to_all x1, blocking collectives, exchange(): return lax.all_to_all(v, axes, 0, 0, tiled=True, axis_index_groups=groups)  11.4 us
    ppermute x4, starting transfers between devices, deal(): return lax.ppermute(v, ('c', 'x'), moves)  8.89 us
    ppermute x4, waiting for transfers between devices, deal(): return lax.ppermute(v, ('c', 'x'), moves)  5.99 us
    pallas_call x1, Pallas kernels, side(): pl.pallas_call(side_kernel, out_shape=(shape(12, 256, 128),) + (shape(102...  3.71 us
    pallas_call x1, Pallas kernels, last(): pl.pallas_call(last_kernel, out_shape=shape(4, 512, 128), in_specs=[SMEM]...  3.59 us
  transfers between devices with their start and end apart: 10, of which 7 were waited for; matrix products, arithmetic and copies ran while one was open for 2% of the time, Pallas kernels for 5%

profile of v14, /device:TPU:128, one launch (start us, length us, event | category | flops | bytes accessed | tf_op | source)
XLA Modules:
  0.0 139.7 jit_solution(3095766072921730454)
XLA Ops:
  7.2 0.0 all-gather.5.cloned.1.call-start
  7.2 0.0 copy-start.1
  7.2 2.3 %shard_map.76 = (f32[512,128]{1,0:T(8,128)}, f32[128,128]{1,0:T(8,128)}, f32[128,128]{1,0:T(8,128)}) custom-call(s32[1]{0:T(128)} %bitcast.at_ref, s32[32,128]{1,0:T(8,128)} %bitcast.4, f32[512,256]{1,0:T(8,128)} %root_hbm.1, f32[256,128]{1,0:T(8,128)} %upper_hbm.1), custom_call_target="tpu_custom_call" | custom-call | tf_op jit(solution)/shard_map/pallas_call | solution.py:92
  9.6 0.0 all-gather.5.cloned.1.call-update
  9.6 1.5 %collective-permute-start = (f32[128,128]{1,0:T(8,128)}, f32[128,128]{1,0:T(8,128)S(1)}, u32[]{:S(2)}, u32[]{:S(2)}) collective-permute-start(f32[128,128]{1,0:T(8,128)} %get-tuple-element.12), channel_id=1, source_target_pairs={{0,0},{1,1},{2,32},{3,33},{32,2},{33,3},{34,34},{35,35},{4,4},{5,5... | collective-permute-start | bytes 196616 | tf_op jit(solution)/shard_map/ppermute | solution.py:309
  11.1 3.4 %collective-permute-start.1 = (f32[128,128]{1,0:T(8,128)}, f32[128,128]{1,0:T(8,128)S(1)}, u32[]{:S(2)}, u32[]{:S(2)}) collective-permute-start(f32[128,128]{1,0:T(8,128)} %get-tuple-element.13), channel_id=1, source_target_pairs={{0,1},{1,0},{2,33},{3,32},{32,3},{33,2},{34,35},{35,34},{4,5},{5,4... | collective-permute-start | bytes 196616 | tf_op jit(solution)/shard_map/ppermute | solution.py:309
  14.5 0.0 collective-permute-done.first_ref
  14.5 3.2 %collective-permute-done.1.second_ref = f32[128,128]{1,0:T(8,128)S(1)} collective-permute-done((f32[128,128]{1,0:T(8,128)}, f32[128,128]{1,0:T(8,128)S(1)}, u32[]{:S(2)}, u32[]{:S(2)}) %collective-permute-start.1) | collective-permute-done | bytes 65568 | tf_op jit(solution)/shard_map/ppermute | solution.py:309
  17.7 1.0 shard_map.77
  18.7 7.1 %all-to-all-start = ((f32[8,2,128,128]{3,2,1,0:T(8,128)}), f32[8,2,128,128]{3,2,1,0:T(8,128)S(1)}, u32[]{:S(2)}, u32[]{:S(2)}) async-start(f32[8,2,128,128]{3,2,1,0:T(8,128)} %shard_map.77), calls=%async_computation | async-start | bytes 2097152 | tf_op jit(solution)/shard_map/all_to_all | solution.py:304
  25.8 0.0 all-gather.7.cloned.1.call-start
  25.9 0.0 copy-done.1
  25.9 0.7 collective-permute-start.3
  26.6 3.3 %collective-permute-start.4 = (f32[128,128]{1,0:T(8,128)S(1)}, f32[128,128]{1,0:T(8,128)S(1)}, u32[]{:S(2)}, u32[]{:S(2)}) collective-permute-start(f32[128,128]{1,0:T(8,128)S(1)} %get-tuple-element.22), channel_id=1, source_target_pairs={{0,1},{1,0},{2,33},{3,32},{32,3},{33,2},{34,35},{35,34},{4,5},{5,4... | collective-permute-start | bytes 196616 | tf_op jit(solution)/shard_map/ppermute | solution.py:309
  29.9 0.0 collective-permute-done.3
  29.9 2.8 %collective-permute-done.4 = f32[128,128]{1,0:T(8,128)S(1)} collective-permute-done((f32[128,128]{1,0:T(8,128)S(1)}, f32[128,128]{1,0:T(8,128)S(1)}, u32[]{:S(2)}, u32[]{:S(2)}) %collective-permute-start.4) | collective-permute-done | bytes 65568 | tf_op jit(solution)/shard_map/ppermute | solution.py:309
  32.7 0.7 pad_maximum_fusion
  33.4 0.0 all-gather.7.cloned.1.call-update
  33.4 22.2 %all-to-all-done.own_hbm = f32[8,2,128,128]{3,2,1,0:T(8,128)S(1)} async-done(((f32[8,2,128,128]{3,2,1,0:T(8,128)}), f32[8,2,128,128]{3,2,1,0:T(8,128)S(1)}, u32[]{:S(2)}, u32[]{:S(2)}) %all-to-all-start) | async-done | bytes 1048608 | tf_op jit(solution)/shard_map/all_to_all | solution.py:304
  55.6 1.9 %collective-permute-start.2 = (f32[8,2,128,128]{3,2,1,0:T(8,128)S(1)}, f32[8,2,128,128]{3,2,1,0:T(8,128)S(1)}, u32[]{:S(2)}, u32[]{:S(2)}) collective-permute-start(f32[8,2,128,128]{3,2,1,0:T(8,128)S(1)} %all-to-all-done.own_hbm), channel_id=1, source_target_pairs={{0,32},{32,0},{1,33},{33,1},{2,34},{34,2},{3,35},{35,3},{4,36},{36... | collective-permute-start | bytes 3145736 | tf_op jit(solution)/shard_map/ppermute | solution.py:313
  57.5 2.6 %collective-permute-done.2.other_hbm = f32[8,2,128,128]{3,2,1,0:T(8,128)S(1)} collective-permute-done((f32[8,2,128,128]{3,2,1,0:T(8,128)S(1)}, f32[8,2,128,128]{3,2,1,0:T(8,128)S(1)}, u32[]{:S(2)}, u32[]{:S(2)}) %collective-permute-start.2) | collective-permute-done | bytes 1048608 | tf_op jit(solution)/shard_map/ppermute | solution.py:313
  60.1 0.0 all-gather.5.cloned.1.call-done
  60.1 2.4 %shard_map.78 = f32[4,256,128]{2,1,0:T(8,128)S(1)} custom-call(s32[1]{0:T(128)} %bitcast.at_ref, f32[8,512,128]{2,1,0:T(8,128)} %bitcast.5, f32[8,2,128,128]{3,2,1,0:T(8,128)S(1)} %all-to-all-done.own_hbm, f32[8,2,128,128]{3,2,1,0:T(8,128)S(1)} %collective-permute-done.2.other_hbm), custom_call_target="tpu_custom_call" | custom-call | flops 1610612736 | bytes 3145728 | tf_op jit(solution)/shard_map/pallas_call | solution.py:155
  62.5 11.4 %all_to_all.20 = f32[4,256,128]{2,1,0:T(8,128)S(1)} all-to-all(f32[4,256,128]{2,1,0:T(8,128)S(1)} %shard_map.78), channel_id=1, replica_groups={{0,1,2,3},{34,35,32,33},{4,5,6,7},{38,39,36,37},{8,9,10,11},{42,43,40,4..., dimensions={0} | all-to-all | bytes 1048576 | tf_op jit(solution)/shard_map/all_to_all | solution.py:304
  74.0 1.1 broadcast_in_dim.2
  75.1 9.1 %all-to-all-start.2 = ((f32[8,256,128]{2,1,0:T(8,128)}), f32[8,256,128]{2,1,0:T(8,128)S(1)}, u32[]{:S(2)}, u32[]{:S(2)}) async-start(f32[8,256,128]{2,1,0:T(8,128)} %broadcast_in_dim.2), calls=%async_computation.2 | async-start | bytes 2097152 | tf_op jit(solution)/shard_map/all_to_all | solution.py:304
  84.2 16.5 %all-gather.7.cloned.1.call-done = f32[4096,128]{1,0:T(8,128)} async-done(((f32[256,128]{1,0:T(8,128)}), f32[4096,128]{1,0:T(8,128)}) %all-gather.7.cloned.1.call-update) | async-done | bytes 2097168 | tf_op jit(solution)/shard_map/all_gather | solution.py:329
  100.7 3.7 %shard_map.79 = (f32[12,256,128]{2,1,0:T(8,128)}, bf16[1024,512]{1,0:T(8,128)(2,1)}, bf16[1024,512]{1,0:T(8,128)(2,1)}) custom-call(s32[1]{0:T(128)} %bitcast.at_ref, f32[8,512,128]{2,1,0:T(8,128)} %bitcast.6, f32[2,8,256,128]{3,2,1,0:T(8,128)} %bitcast.7), custom_call_target="tpu_custom_call" | custom-call | flops 1610612736 | bytes 6291456 | tf_op jit(solution)/shard_map/pallas_call | solution.py:221
  104.4 4.3 %all-to-all-done.2.w_hbm = f32[8,256,128]{2,1,0:T(8,128)S(1)} async-done(((f32[8,256,128]{2,1,0:T(8,128)}), f32[8,256,128]{2,1,0:T(8,128)S(1)}, u32[]{:S(2)}, u32[]{:S(2)}) %all-to-all-start.2) | async-done | bytes 1048608 | tf_op jit(solution)/shard_map/all_to_all | solution.py:304
  108.7 3.6 %shard_map.80 = f32[4,512,128]{2,1,0:T(8,128)} custom-call(s32[1]{0:T(128)} %bitcast.at_ref, f32[8,256,128]{2,1,0:T(8,128)S(1)} %all-to-all-done.2.w_hbm, bf16[1024,512]{1,0:T(8,128)(2,1)} %get-tuple-element.16.hi_hbm, bf16[1024,512]{1,0:T(8,128)(2,1)} %get-tuple-element.17.lo_hbm, f32[12,256,128]{2,1,0:T(8,128)} %get-tuple-element.18.rest_hbm), custom_call_target="tpu_custom_call" | custom-call | tf_op jit(solution)/shard_map/pallas_call | solution.py:274
  112.3 0.0 copy-start
  112.3 4.9 %all-to-all-start.3 = ((f32[4,512,128]{2,1,0:T(8,128)}), f32[4,512,128]{2,1,0:T(8,128)S(1)}, u32[]{:S(2)}, u32[]{:S(2)}) async-start(f32[4,512,128]{2,1,0:T(8,128)} %shard_map.80), calls=%async_computation.3 | async-start | bytes 2097152 | tf_op jit(solution)/shard_map/all_to_all | solution.py:304
  117.2 0.7 neg.3
  117.9 14.2 %all-to-all-done.3 = f32[4,512,128]{2,1,0:T(8,128)S(1)} async-done(((f32[4,512,128]{2,1,0:T(8,128)}), f32[4,512,128]{2,1,0:T(8,128)S(1)}, u32[]{:S(2)}, u32[]{:S(2)}) %all-to-all-start.3) | async-done | bytes 1048608 | tf_op jit(solution)/shard_map/all_to_all | solution.py:304
  132.1 0.1 reduce_sum.19
  132.2 0.0 copy-done
  132.2 0.7 slice_add_fusion
  (2 shorter events, 0.0 us)
Async XLA Ops:
  7.2 53.0 %all-gather.5.cloned.1.call-start = ((), (), s32[]{:S(2)}) async-start(), calls=%async_computation.4 | async-start | bytes 2359296 | tf_op jit(solution)/shard_map/all_gather | solution.py:320
  7.2 18.6 %copy-start.1 = (f32[256,128]{1,0:T(8,128)S(1)}, f32[256,128]{1,0:T(8,128)}, u32[]{:S(2)}) copy-start(f32[256,128]{1,0:T(8,128)} %param.7) | copy-start | bytes 393220
  9.6 4.9 %collective-permute-start = (f32[128,128]{1,0:T(8,128)}, f32[128,128]{1,0:T(8,128)S(1)}, u32[]{:S(2)}, u32[]{:S(2)}) collective-permute-start(f32[128,128]{1,0:T(8,128)} %get-tuple-element.12), channel_id=1, source_target_pairs={{0,0},{1,1},{2,32},{3,33},{32,2},{33,3},{34,34},{35,35},{4,4},{5,5... | collective-permute-start | bytes 196616 | tf_op jit(solution)/shard_map/ppermute | solution.py:309
  11.1 6.6 %collective-permute-start.1 = (f32[128,128]{1,0:T(8,128)}, f32[128,128]{1,0:T(8,128)S(1)}, u32[]{:S(2)}, u32[]{:S(2)}) collective-permute-start(f32[128,128]{1,0:T(8,128)} %get-tuple-element.13), channel_id=1, source_target_pairs={{0,1},{1,0},{2,33},{3,32},{32,3},{33,2},{34,35},{35,34},{4,5},{5,4... | collective-permute-start | bytes 196616 | tf_op jit(solution)/shard_map/ppermute | solution.py:309
  18.7 36.9 %all-to-all-start = ((f32[8,2,128,128]{3,2,1,0:T(8,128)}), f32[8,2,128,128]{3,2,1,0:T(8,128)S(1)}, u32[]{:S(2)}, u32[]{:S(2)}) async-start(f32[8,2,128,128]{3,2,1,0:T(8,128)} %shard_map.77), calls=%async_computation | async-start | bytes 2097152 | tf_op jit(solution)/shard_map/all_to_all | solution.py:304
  25.8 74.9 %all-gather.7.cloned.1.call-start = ((), (), s32[]{:S(2)}) async-start(), calls=%async_computation.5 | async-start | bytes 2228224 | tf_op jit(solution)/shard_map/all_gather | solution.py:329
  25.9 4.0 %collective-permute-start.3 = (f32[128,128]{1,0:T(8,128)S(1)}, f32[128,128]{1,0:T(8,128)S(1)}, u32[]{:S(2)}, u32[]{:S(2)}) collective-permute-start(f32[128,128]{1,0:T(8,128)S(1)} %get-tuple-element.21), channel_id=1, source_target_pairs={{0,0},{1,1},{2,32},{3,33},{32,2},{33,3},{34,34},{35,35},{4,4},{5,5... | collective-permute-start | bytes 196616 | tf_op jit(solution)/shard_map/ppermute | solution.py:309
  26.6 6.2 %collective-permute-start.4 = (f32[128,128]{1,0:T(8,128)S(1)}, f32[128,128]{1,0:T(8,128)S(1)}, u32[]{:S(2)}, u32[]{:S(2)}) collective-permute-start(f32[128,128]{1,0:T(8,128)S(1)} %get-tuple-element.22), channel_id=1, source_target_pairs={{0,1},{1,0},{2,33},{3,32},{32,3},{33,2},{34,35},{35,34},{4,5},{5,4... | collective-permute-start | bytes 196616 | tf_op jit(solution)/shard_map/ppermute | solution.py:309
  55.6 4.5 %collective-permute-start.2 = (f32[8,2,128,128]{3,2,1,0:T(8,128)S(1)}, f32[8,2,128,128]{3,2,1,0:T(8,128)S(1)}, u32[]{:S(2)}, u32[]{:S(2)}) collective-permute-start(f32[8,2,128,128]{3,2,1,0:T(8,128)S(1)} %all-to-all-done.own_hbm), channel_id=1, source_target_pairs={{0,32},{32,0},{1,33},{33,1},{2,34},{34,2},{3,35},{35,3},{4,36},{36... | collective-permute-start | bytes 3145736 | tf_op jit(solution)/shard_map/ppermute | solution.py:313
  75.1 33.6 %all-to-all-start.2 = ((f32[8,256,128]{2,1,0:T(8,128)}), f32[8,256,128]{2,1,0:T(8,128)S(1)}, u32[]{:S(2)}, u32[]{:S(2)}) async-start(f32[8,256,128]{2,1,0:T(8,128)} %broadcast_in_dim.2), calls=%async_computation.2 | async-start | bytes 2097152 | tf_op jit(solution)/shard_map/all_to_all | solution.py:304
  112.3 19.9 %copy-start = (f32[256,128]{1,0:T(8,128)S(1)}, f32[256,128]{1,0:T(8,128)}, u32[]{:S(2)}) copy-start(f32[256,128]{1,0:T(8,128)} %param.9) | copy-start | bytes 393220
  112.3 19.8 %all-to-all-start.3 = ((f32[4,512,128]{2,1,0:T(8,128)}), f32[4,512,128]{2,1,0:T(8,128)S(1)}, u32[]{:S(2)}, u32[]{:S(2)}) async-start(f32[4,512,128]{2,1,0:T(8,128)} %shard_map.80), calls=%async_computation.3 | async-start | bytes 2097152 | tf_op jit(solution)/shard_map/all_to_all | solution.py:304
Sparse Core Ops, SparseCore 0:
  10.1 46.1 all-gather.4
  59.0 41.6 all-gather.6

commit v15 on v14

--- a/solution.py
+++ b/solution.py
@@ -121,26 +121,20 @@
 
 
 def couple_kernel(
-    at_ref, gathered_hbm, own_hbm, other_hbm, out_ref, left, own, other, ah, al, bh, bl, sems
+    at_ref, gathered_hbm, own, other, out_ref, left, ah, al, bh, bl, sem
 ):
-    loads = [
-        pltpu.make_async_copy(own_hbm, own, sems.at[0]),
-        pltpu.make_async_copy(other_hbm, other, sems.at[1]),
-        pltpu.make_async_copy(gathered_hbm.at[:, 256:512], left, sems.at[2]),
-    ]
-    for load in loads:
-        load.start()
+    load = pltpu.make_async_copy(gathered_hbm.at[:, 256:512], left, sem)
+    load.start()
     _, _, core, _, x = device(at_ref)
     odd = x & 1
     for n, right in enumerate((own, other)):
-        loads[n].wait()
         side = core if n == 0 else 1 - core
         for z in range(8):
             rows = slice(128 * z, 128 * (z + 1))
             for t in range(2):
                 cols = slice(256 * n + 128 * t, 256 * n + 128 * (t + 1))
                 bh[rows, cols], bl[rows, cols] = split2(right[z ^ (4 * side), t])
-    loads[2].wait()
+    load.wait()
     for z in range(8):
         rows = slice(128 * z, 128 * (z + 1))
         ah[:, rows], al[:, rows] = split2(left[z ^ (4 * core)])
@@ -155,17 +149,15 @@
     return pl.pallas_call(
         couple_kernel,
         out_shape=shape(4, 256, 128),
-        in_specs=[SMEM, HBM, HBM, HBM],
+        in_specs=[SMEM, HBM, VMEM, VMEM],
         out_specs=VMEM,
         scratch_shapes=[
             pltpu.VMEM((8, 256, 128), F32),
-            pltpu.VMEM((8, 2, 128, 128), F32),
-            pltpu.VMEM((8, 2, 128, 128), F32),
-            pltpu.VMEM((256, 1024), BF16),
-            pltpu.VMEM((256, 1024), BF16),
-            pltpu.VMEM((1024, 512), BF16),
-            pltpu.VMEM((1024, 512), BF16),
-            DMA((3,)),
+            pltpu.VMEM((256, 1024), BF16),
+            pltpu.VMEM((256, 1024), BF16),
+            pltpu.VMEM((1024, 512), BF16),
+            pltpu.VMEM((1024, 512), BF16),
+            DMA,
         ],
         compiler_params=NEAR,
         cost_estimate=pl.CostEstimate(flops=6 << 28, bytes_accessed=3 << 20, transcendentals=0),
@@ -239,24 +231,22 @@
 
 
 def last_kernel(
-    at_ref, w_hbm, hi_hbm, lo_hbm, rest_hbm, out_hbm, w, ah, al, bh, bl, out, rest, sems
+    at_ref, w, hi_hbm, lo_hbm, rest_hbm, out_hbm, ah, al, bh, bl, out, rest, sems
 ):
     loads = [
-        pltpu.make_async_copy(w_hbm, w, sems.at[0]),
         pltpu.make_async_copy(hi_hbm, bh, sems.at[1]),
         pltpu.make_async_copy(lo_hbm, bl, sems.at[2]),
-        pltpu.make_async_copy(rest_hbm.at[0:4], rest, sems.at[5]),
+        pltpu.make_async_copy(rest_hbm.at[0:4], rest, sems.at[0]),
     ]
     for load in loads:
         load.start()
     core = device(at_ref)[2]
-    loads[0].wait()
     for z in range(8):
         rows = slice(128 * z, 128 * (z + 1))
         ah[:, rows], al[:, rows] = split2(w[z ^ (4 * core)])
-    for load in loads[1:]:
+    for load in loads:
         load.wait()
-    stores = [pltpu.make_async_copy(rest, out_hbm.at[:, 256:512], sems.at[6])]
+    stores = [pltpu.make_async_copy(rest, out_hbm.at[:, 256:512], sems.at[5])]
     stores[0].start()
     for n in range(2):
         cols = slice(256 * n, 256 * (n + 1))
@@ -274,17 +264,16 @@
     return pl.pallas_call(
         last_kernel,
         out_shape=shape(4, 512, 128),
-        in_specs=[SMEM] + [HBM] * 4,
+        in_specs=[SMEM, VMEM] + [HBM] * 3,
         out_specs=HBM,
         scratch_shapes=[
-            pltpu.VMEM((8, 256, 128), F32),
             pltpu.VMEM((256, 1024), BF16),
             pltpu.VMEM((256, 1024), BF16),
             pltpu.VMEM((1024, 512), BF16),
             pltpu.VMEM((1024, 512), BF16),
             pltpu.VMEM((4, 256, 128), F32),
             pltpu.VMEM((4, 256, 128), F32),
-            DMA((7,)),
+            DMA((6,)),
         ],
         compiler_params=MIDDLE,
     )(at, w, hi, lo, rest)

time: 140 us -> 141 us (level)
  the two profiles are of different devices: /device:TPU:128 before, /device:TPU:1 now
where the time goes in v15:
time: 141 us; the launch traced here: 140 us
  starting transfers between devices  52.6 us (37%)
  waiting for transfers between devices  49 us (35%)
  between operations  14.2 us (10%)
  Pallas kernels  12.8 us (9%)
  blocking collectives  8.29 us (6%)
  other arithmetic  2.15 us (2%)
    all_to_all x3, starting transfers between devices, exchange(): return lax.all_to_all(v, axes, 0, 0, tiled=True, axis_index_groups=groups)  35.5 us
    all_to_all x3, waiting for transfers between devices, exchange(): return lax.all_to_all(v, axes, 0, 0, tiled=True, axis_index_groups=groups)  22.9 us
    all_gather x1, waiting for transfers between devices, shards(): lax.all_gather(lower, ('y', 'c'), axis=0, tiled=False, axis_index_groups=...  15.9 us
    ppermute x4, starting transfers between devices, deal(): return lax.ppermute(v, ('c', 'x'), moves)  14.1 us
    all_to_all x1, blocking collectives, exchange(): return lax.all_to_all(v, axes, 0, 0, tiled=True, axis_index_groups=groups)  8.29 us
    ppermute x4, waiting for transfers between devices, deal(): return lax.ppermute(v, ('c', 'x'), moves)  7.9 us
    pallas_call x1, Pallas kernels, side(): pl.pallas_call(side_kernel, out_shape=(shape(12, 256, 128),) + (shape(102...  3.71 us
    pallas_call x1, Pallas kernels, last(): pl.pallas_call(last_kernel, out_shape=shape(4, 512, 128), in_specs=[SMEM,...  3.51 us
  transfers between devices with their start and end apart: 10, of which 8 were waited for; matrix products, arithmetic and copies ran while one was open for 2% of the time, Pallas kernels for 5%

profile of v15, /device:TPU:1, one launch (start us, length us, event | category | flops | bytes accessed | tf_op | source)
XLA Modules:
  0.0 140.2 jit_solution(3266922320974303415)
XLA Ops:
  7.2 0.0 all-gather.5.cloned.1.call-start
  7.2 0.0 copy-start.1
  7.2 2.3 %shard_map.76 = (f32[512,128]{1,0:T(8,128)}, f32[128,128]{1,0:T(8,128)}, f32[128,128]{1,0:T(8,128)}) custom-call(s32[1]{0:T(128)} %bitcast.at_ref, s32[32,128]{1,0:T(8,128)} %bitcast.4, f32[512,256]{1,0:T(8,128)} %root_hbm.1, f32[256,128]{1,0:T(8,128)} %upper_hbm.1), custom_call_target="tpu_custom_call" | custom-call | tf_op jit(solution)/shard_map/pallas_call | solution.py:92
  9.5 0.0 all-gather.5.cloned.1.call-update
  9.6 6.0 %collective-permute-start = (f32[128,128]{1,0:T(8,128)}, f32[128,128]{1,0:T(8,128)S(1)}, u32[]{:S(2)}, u32[]{:S(2)}) collective-permute-start(f32[128,128]{1,0:T(8,128)} %get-tuple-element.12), channel_id=1, source_target_pairs={{0,0},{1,1},{2,32},{3,33},{32,2},{33,3},{34,34},{35,35},{4,4},{5,5... | collective-permute-start | bytes 196616 | tf_op jit(solution)/shard_map/ppermute | solution.py:298
  15.6 2.5 %collective-permute-start.1 = (f32[128,128]{1,0:T(8,128)}, f32[128,128]{1,0:T(8,128)S(1)}, u32[]{:S(2)}, u32[]{:S(2)}) collective-permute-start(f32[128,128]{1,0:T(8,128)} %get-tuple-element.13), channel_id=1, source_target_pairs={{0,1},{1,0},{2,33},{3,32},{32,3},{33,2},{34,35},{35,34},{4,5},{5,4... | collective-permute-start | bytes 196616 | tf_op jit(solution)/shard_map/ppermute | solution.py:298
  18.1 0.0 collective-permute-done.first_ref
  18.1 4.5 %collective-permute-done.1.second_ref = f32[128,128]{1,0:T(8,128)S(1)} collective-permute-done((f32[128,128]{1,0:T(8,128)}, f32[128,128]{1,0:T(8,128)S(1)}, u32[]{:S(2)}, u32[]{:S(2)}) %collective-permute-start.1) | collective-permute-done | bytes 65568 | tf_op jit(solution)/shard_map/ppermute | solution.py:298
  22.6 1.0 shard_map.77
  23.7 9.0 %all-to-all-start = ((f32[8,2,128,128]{3,2,1,0:T(8,128)}), f32[8,2,128,128]{3,2,1,0:T(8,128)S(1)}, u32[]{:S(2)}, u32[]{:S(2)}) async-start(f32[8,2,128,128]{3,2,1,0:T(8,128)} %shard_map.77), calls=%async_computation | async-start | bytes 2097152 | tf_op jit(solution)/shard_map/all_to_all | solution.py:293
  32.7 0.0 all-gather.7.cloned.1.call-start
  32.7 0.0 copy-done.1
  32.7 1.9 %collective-permute-start.3 = (f32[128,128]{1,0:T(8,128)S(1)}, f32[128,128]{1,0:T(8,128)S(1)}, u32[]{:S(2)}, u32[]{:S(2)}) collective-permute-start(f32[128,128]{1,0:T(8,128)S(1)} %get-tuple-element.21), channel_id=1, source_target_pairs={{0,0},{1,1},{2,32},{3,33},{32,2},{33,3},{34,34},{35,35},{4,4},{5,5... | collective-permute-start | bytes 196616 | tf_op jit(solution)/shard_map/ppermute | solution.py:298
  34.7 3.7 %collective-permute-start.4 = (f32[128,128]{1,0:T(8,128)S(1)}, f32[128,128]{1,0:T(8,128)S(1)}, u32[]{:S(2)}, u32[]{:S(2)}) collective-permute-start(f32[128,128]{1,0:T(8,128)S(1)} %get-tuple-element.22), channel_id=1, source_target_pairs={{0,1},{1,0},{2,33},{3,32},{32,3},{33,2},{34,35},{35,34},{4,5},{5,4... | collective-permute-start | bytes 196616 | tf_op jit(solution)/shard_map/ppermute | solution.py:298
  38.3 1.8 %collective-permute-done.3 = f32[128,128]{1,0:T(8,128)S(1)} collective-permute-done((f32[128,128]{1,0:T(8,128)S(1)}, f32[128,128]{1,0:T(8,128)S(1)}, u32[]{:S(2)}, u32[]{:S(2)}) %collective-permute-start.3) | collective-permute-done | bytes 65568 | tf_op jit(solution)/shard_map/ppermute | solution.py:298
  40.1 1.6 %collective-permute-done.4 = f32[128,128]{1,0:T(8,128)S(1)} collective-permute-done((f32[128,128]{1,0:T(8,128)S(1)}, f32[128,128]{1,0:T(8,128)S(1)}, u32[]{:S(2)}, u32[]{:S(2)}) %collective-permute-start.4) | collective-permute-done | bytes 65568 | tf_op jit(solution)/shard_map/ppermute | solution.py:298
  41.7 0.7 pad_maximum_fusion
  42.4 0.0 all-gather.7.cloned.1.call-update
  42.4 11.0 %all-to-all-done.own = f32[8,2,128,128]{3,2,1,0:T(8,128)S(1)} async-done(((f32[8,2,128,128]{3,2,1,0:T(8,128)}), f32[8,2,128,128]{3,2,1,0:T(8,128)S(1)}, u32[]{:S(2)}, u32[]{:S(2)}) %all-to-all-start) | async-done | bytes 1048608 | tf_op jit(solution)/shard_map/all_to_all | solution.py:293
  53.5 3.0 %collective-permute-start.2 = (f32[8,2,128,128]{3,2,1,0:T(8,128)S(1)}, f32[8,2,128,128]{3,2,1,0:T(8,128)S(1)}, u32[]{:S(2)}, u32[]{:S(2)}) collective-permute-start(f32[8,2,128,128]{3,2,1,0:T(8,128)S(1)} %all-to-all-done.own), channel_id=1, source_target_pairs={{0,32},{32,0},{1,33},{33,1},{2,34},{34,2},{3,35},{35,3},{4,36},{36... | collective-permute-start | bytes 3145736 | tf_op jit(solution)/shard_map/ppermute | solution.py:302
  56.5 2.3 %collective-permute-done.2.other = f32[8,2,128,128]{3,2,1,0:T(8,128)S(1)} collective-permute-done((f32[8,2,128,128]{3,2,1,0:T(8,128)S(1)}, f32[8,2,128,128]{3,2,1,0:T(8,128)S(1)}, u32[]{:S(2)}, u32[]{:S(2)}) %collective-permute-start.2) | collective-permute-done | bytes 1048608 | tf_op jit(solution)/shard_map/ppermute | solution.py:302
  58.8 0.0 all-gather.5.cloned.1.call-done
  58.8 2.2 %shard_map.78 = f32[4,256,128]{2,1,0:T(8,128)S(1)} custom-call(s32[1]{0:T(128)} %bitcast.at_ref, f32[8,512,128]{2,1,0:T(8,128)} %bitcast.5, f32[8,2,128,128]{3,2,1,0:T(8,128)S(1)} %all-to-all-done.own, f32[8,2,128,128]{3,2,1,0:T(8,128)S(1)} %collective-permute-done.2.other), custom_call_target="tpu_custom_call" | custom-call | flops 1610612736 | bytes 3145728 | tf_op jit(solution)/shard_map/pallas_call | solution.py:149
  61.0 8.3 %all_to_all.20 = f32[4,256,128]{2,1,0:T(8,128)S(1)} all-to-all(f32[4,256,128]{2,1,0:T(8,128)S(1)} %shard_map.78), channel_id=1, replica_groups={{0,1,2,3},{34,35,32,33},{4,5,6,7},{38,39,36,37},{8,9,10,11},{42,43,40,4..., dimensions={0} | all-to-all | bytes 1048576 | tf_op jit(solution)/shard_map/all_to_all | solution.py:293
  69.3 1.1 broadcast_in_dim.2
  70.4 17.1 %all-to-all-start.2 = ((f32[8,256,128]{2,1,0:T(8,128)}), f32[8,256,128]{2,1,0:T(8,128)S(1)}, u32[]{:S(2)}, u32[]{:S(2)}) async-start(f32[8,256,128]{2,1,0:T(8,128)} %broadcast_in_dim.2), calls=%async_computation.2 | async-start | bytes 2097152 | tf_op jit(solution)/shard_map/all_to_all | solution.py:293
  87.5 15.9 %all-gather.7.cloned.1.call-done = f32[4096,128]{1,0:T(8,128)} async-done(((f32[256,128]{1,0:T(8,128)}), f32[4096,128]{1,0:T(8,128)}) %all-gather.7.cloned.1.call-update) | async-done | bytes 2097168 | tf_op jit(solution)/shard_map/all_gather | solution.py:318
  103.4 3.7 %shard_map.79 = (f32[12,256,128]{2,1,0:T(8,128)}, bf16[1024,512]{1,0:T(8,128)(2,1)}, bf16[1024,512]{1,0:T(8,128)(2,1)}) custom-call(s32[1]{0:T(128)} %bitcast.at_ref, f32[8,512,128]{2,1,0:T(8,128)} %bitcast.6, f32[2,8,256,128]{3,2,1,0:T(8,128)} %bitcast.7), custom_call_target="tpu_custom_call" | custom-call | flops 1610612736 | bytes 6291456 | tf_op jit(solution)/shard_map/pallas_call | solution.py:213
  107.1 1.8 %all-to-all-done.2.w = f32[8,256,128]{2,1,0:T(8,128)S(1)} async-done(((f32[8,256,128]{2,1,0:T(8,128)}), f32[8,256,128]{2,1,0:T(8,128)S(1)}, u32[]{:S(2)}, u32[]{:S(2)}) %all-to-all-start.2) | async-done | bytes 1048608 | tf_op jit(solution)/shard_map/all_to_all | solution.py:293
  108.9 3.5 %shard_map.80 = f32[4,512,128]{2,1,0:T(8,128)} custom-call(s32[1]{0:T(128)} %bitcast.at_ref, f32[8,256,128]{2,1,0:T(8,128)S(1)} %all-to-all-done.2.w, bf16[1024,512]{1,0:T(8,128)(2,1)} %get-tuple-element.16.hi_hbm, bf16[1024,512]{1,0:T(8,128)(2,1)} %get-tuple-element.17.lo_hbm, f32[12,256,128]{2,1,0:T(8,128)} %get-tuple-element.18.rest_hbm), custom_call_target="tpu_custom_call" | custom-call | tf_op jit(solution)/shard_map/pallas_call | solution.py:264
  112.4 0.0 copy-start
  112.4 9.3 %all-to-all-start.3 = ((f32[4,512,128]{2,1,0:T(8,128)}), f32[4,512,128]{2,1,0:T(8,128)S(1)}, u32[]{:S(2)}, u32[]{:S(2)}) async-start(f32[4,512,128]{2,1,0:T(8,128)} %shard_map.80), calls=%async_computation.3 | async-start | bytes 2097152 | tf_op jit(solution)/shard_map/all_to_all | solution.py:293
  121.8 0.7 neg.3
  122.4 10.1 %all-to-all-done.3 = f32[4,512,128]{2,1,0:T(8,128)S(1)} async-done(((f32[4,512,128]{2,1,0:T(8,128)}), f32[4,512,128]{2,1,0:T(8,128)S(1)}, u32[]{:S(2)}, u32[]{:S(2)}) %all-to-all-start.3) | async-done | bytes 1048608 | tf_op jit(solution)/shard_map/all_to_all | solution.py:293
  132.6 0.1 reduce_sum.19
  132.6 0.0 copy-done
  132.6 0.7 slice_add_fusion
  (2 shorter events, 0.0 us)
Async XLA Ops:
  7.2 51.6 %all-gather.5.cloned.1.call-start = ((), (), s32[]{:S(2)}) async-start(), calls=%async_computation.4 | async-start | bytes 2359296 | tf_op jit(solution)/shard_map/all_gather | solution.py:309
  7.2 25.5 %copy-start.1 = (f32[256,128]{1,0:T(8,128)S(1)}, f32[256,128]{1,0:T(8,128)}, u32[]{:S(2)}) copy-start(f32[256,128]{1,0:T(8,128)} %param.7) | copy-start | bytes 393220
  9.6 8.5 %collective-permute-start = (f32[128,128]{1,0:T(8,128)}, f32[128,128]{1,0:T(8,128)S(1)}, u32[]{:S(2)}, u32[]{:S(2)}) collective-permute-start(f32[128,128]{1,0:T(8,128)} %get-tuple-element.12), channel_id=1, source_target_pairs={{0,0},{1,1},{2,32},{3,33},{32,2},{33,3},{34,34},{35,35},{4,4},{5,5... | collective-permute-start | bytes 196616 | tf_op jit(solution)/shard_map/ppermute | solution.py:298
  15.6 7.0 %collective-permute-start.1 = (f32[128,128]{1,0:T(8,128)}, f32[128,128]{1,0:T(8,128)S(1)}, u32[]{:S(2)}, u32[]{:S(2)}) collective-permute-start(f32[128,128]{1,0:T(8,128)} %get-tuple-element.13), channel_id=1, source_target_pairs={{0,1},{1,0},{2,33},{3,32},{32,3},{33,2},{34,35},{35,34},{4,5},{5,4... | collective-permute-start | bytes 196616 | tf_op jit(solution)/shard_map/ppermute | solution.py:298
  23.7 29.8 %all-to-all-start = ((f32[8,2,128,128]{3,2,1,0:T(8,128)}), f32[8,2,128,128]{3,2,1,0:T(8,128)S(1)}, u32[]{:S(2)}, u32[]{:S(2)}) async-start(f32[8,2,128,128]{3,2,1,0:T(8,128)} %shard_map.77), calls=%async_computation | async-start | bytes 2097152 | tf_op jit(solution)/shard_map/all_to_all | solution.py:293
  32.7 70.7 %all-gather.7.cloned.1.call-start = ((), (), s32[]{:S(2)}) async-start(), calls=%async_computation.5 | async-start | bytes 2228224 | tf_op jit(solution)/shard_map/all_gather | solution.py:318
  32.7 7.4 %collective-permute-start.3 = (f32[128,128]{1,0:T(8,128)S(1)}, f32[128,128]{1,0:T(8,128)S(1)}, u32[]{:S(2)}, u32[]{:S(2)}) collective-permute-start(f32[128,128]{1,0:T(8,128)S(1)} %get-tuple-element.21), channel_id=1, source_target_pairs={{0,0},{1,1},{2,32},{3,33},{32,2},{33,3},{34,34},{35,35},{4,4},{5,5... | collective-permute-start | bytes 196616 | tf_op jit(solution)/shard_map/ppermute | solution.py:298
  34.7 7.1 %collective-permute-start.4 = (f32[128,128]{1,0:T(8,128)S(1)}, f32[128,128]{1,0:T(8,128)S(1)}, u32[]{:S(2)}, u32[]{:S(2)}) collective-permute-start(f32[128,128]{1,0:T(8,128)S(1)} %get-tuple-element.22), channel_id=1, source_target_pairs={{0,1},{1,0},{2,33},{3,32},{32,3},{33,2},{34,35},{35,34},{4,5},{5,4... | collective-permute-start | bytes 196616 | tf_op jit(solution)/shard_map/ppermute | solution.py:298
  53.5 5.3 %collective-permute-start.2 = (f32[8,2,128,128]{3,2,1,0:T(8,128)S(1)}, f32[8,2,128,128]{3,2,1,0:T(8,128)S(1)}, u32[]{:S(2)}, u32[]{:S(2)}) collective-permute-start(f32[8,2,128,128]{3,2,1,0:T(8,128)S(1)} %all-to-all-done.own), channel_id=1, source_target_pairs={{0,32},{32,0},{1,33},{33,1},{2,34},{34,2},{3,35},{35,3},{4,36},{36... | collective-permute-start | bytes 3145736 | tf_op jit(solution)/shard_map/ppermute | solution.py:302
  70.4 38.5 %all-to-all-start.2 = ((f32[8,256,128]{2,1,0:T(8,128)}), f32[8,256,128]{2,1,0:T(8,128)S(1)}, u32[]{:S(2)}, u32[]{:S(2)}) async-start(f32[8,256,128]{2,1,0:T(8,128)} %broadcast_in_dim.2), calls=%async_computation.2 | async-start | bytes 2097152 | tf_op jit(solution)/shard_map/all_to_all | solution.py:293
  112.4 20.2 %copy-start = (f32[256,128]{1,0:T(8,128)S(1)}, f32[256,128]{1,0:T(8,128)}, u32[]{:S(2)}) copy-start(f32[256,128]{1,0:T(8,128)} %param.9) | copy-start | bytes 393220
  112.4 20.1 %all-to-all-start.3 = ((f32[4,512,128]{2,1,0:T(8,128)}), f32[4,512,128]{2,1,0:T(8,128)S(1)}, u32[]{:S(2)}, u32[]{:S(2)}) async-start(f32[4,512,128]{2,1,0:T(8,128)} %shard_map.80), calls=%async_computation.3 | async-start | bytes 2097152 | tf_op jit(solution)/shard_map/all_to_all | solution.py:293
Sparse Core Ops, SparseCore 0:
  10.1 46.0 all-gather.4
  58.9 44.4 all-gather.6

commit v16 on v15

--- a/solution.py
+++ b/solution.py
@@ -244,10 +244,9 @@
     for z in range(8):
         rows = slice(128 * z, 128 * (z + 1))
         ah[:, rows], al[:, rows] = split2(w[z ^ (4 * core)])
-    for load in loads:
+    for load in loads[:2]:
         load.wait()
-    stores = [pltpu.make_async_copy(rest, out_hbm.at[:, 256:512], sems.at[5])]
-    stores[0].start()
+    stores = []
     for n in range(2):
         cols = slice(256 * n, 256 * (n + 1))
         part = three_pass(ah[...], al[...], bh[:, cols], bl[:, cols])
@@ -256,6 +255,10 @@
         pair, place = slice(2 * n, 2 * n + 2), pl.ds(2 * (n ^ core), 2)
         stores.append(pltpu.make_async_copy(out.at[pair], out_hbm.at[place, 0:256], sems.at[3 + n]))
         stores[-1].start()
+        if n == 0:
+            loads[2].wait()
+            stores.append(pltpu.make_async_copy(rest, out_hbm.at[:, 256:512], sems.at[5]))
+            stores[-1].start()
     for store in stores:
         store.wait()
 

time: 141 us -> 142 us (level)
  no operation moved by 1% of the time
where the time goes in v16:
time: 142 us; the launch traced here: 141 us
  starting transfers between devices  52.7 us (37%)
  waiting for transfers between devices  49 us (35%)
  between operations  14.2 us (10%)
  Pallas kernels  13.5 us (10%)
  blocking collectives  8.29 us (6%)
  other arithmetic  2.15 us (2%)
    all_to_all x3, starting transfers between devices, exchange(): return lax.all_to_all(v, axes, 0, 0, tiled=True, axis_index_groups=groups)  35.5 us
    all_to_all x3, waiting for transfers between devices, exchange(): return lax.all_to_all(v, axes, 0, 0, tiled=True, axis_index_groups=groups)  22.9 us
    all_gather x1, waiting for transfers between devices, shards(): lax.all_gather(lower, ('y', 'c'), axis=0, tiled=False, axis_index_groups=...  15.9 us
    ppermute x4, starting transfers between devices, deal(): return lax.ppermute(v, ('c', 'x'), moves)  14.1 us
    all_to_all x1, blocking collectives, exchange(): return lax.all_to_all(v, axes, 0, 0, tiled=True, axis_index_groups=groups)  8.29 us
    ppermute x4, waiting for transfers between devices, deal(): return lax.ppermute(v, ('c', 'x'), moves)  7.9 us
    pallas_call x1, Pallas kernels, last(): pl.pallas_call(last_kernel, out_shape=shape(4, 512, 128), in_specs=[SMEM,...  4.21 us
    pallas_call x1, Pallas kernels, side(): pl.pallas_call(side_kernel, out_shape=(shape(12, 256, 128),) + (shape(102...  3.71 us
  transfers between devices with their start and end apart: 10, of which 8 were waited for; matrix products, arithmetic and copies ran while one was open for 2% of the time, Pallas kernels for 5%

profile of v16, /device:TPU:1, one launch (start us, length us, event | category | flops | bytes accessed | tf_op | source)
XLA Modules:
  0.0 140.9 jit_solution(1417554862344709124)
XLA Ops:
  7.2 0.0 all-gather.5.cloned.1.call-start
  7.2 0.0 copy-start.1
  7.2 2.3 %shard_map.76 = (f32[512,128]{1,0:T(8,128)}, f32[128,128]{1,0:T(8,128)}, f32[128,128]{1,0:T(8,128)}) custom-call(s32[1]{0:T(128)} %bitcast.at_ref, s32[32,128]{1,0:T(8,128)} %bitcast.4, f32[512,256]{1,0:T(8,128)} %root_hbm.1, f32[256,128]{1,0:T(8,128)} %upper_hbm.1), custom_call_target="tpu_custom_call" | custom-call | tf_op jit(solution)/shard_map/pallas_call | solution.py:92
  9.5 0.0 all-gather.5.cloned.1.call-update
  9.6 6.0 %collective-permute-start = (f32[128,128]{1,0:T(8,128)}, f32[128,128]{1,0:T(8,128)S(1)}, u32[]{:S(2)}, u32[]{:S(2)}) collective-permute-start(f32[128,128]{1,0:T(8,128)} %get-tuple-element.12), channel_id=1, source_target_pairs={{0,0},{1,1},{2,32},{3,33},{32,2},{33,3},{34,34},{35,35},{4,4},{5,5... | collective-permute-start | bytes 196616 | tf_op jit(solution)/shard_map/ppermute | solution.py:301
  15.6 2.5 %collective-permute-start.1 = (f32[128,128]{1,0:T(8,128)}, f32[128,128]{1,0:T(8,128)S(1)}, u32[]{:S(2)}, u32[]{:S(2)}) collective-permute-start(f32[128,128]{1,0:T(8,128)} %get-tuple-element.13), channel_id=1, source_target_pairs={{0,1},{1,0},{2,33},{3,32},{32,3},{33,2},{34,35},{35,34},{4,5},{5,4... | collective-permute-start | bytes 196616 | tf_op jit(solution)/shard_map/ppermute | solution.py:301
  18.1 0.0 collective-permute-done.first_ref
  18.1 4.5 %collective-permute-done.1.second_ref = f32[128,128]{1,0:T(8,128)S(1)} collective-permute-done((f32[128,128]{1,0:T(8,128)}, f32[128,128]{1,0:T(8,128)S(1)}, u32[]{:S(2)}, u32[]{:S(2)}) %collective-permute-start.1) | collective-permute-done | bytes 65568 | tf_op jit(solution)/shard_map/ppermute | solution.py:301
  22.6 1.0 shard_map.77
  23.7 9.0 %all-to-all-start = ((f32[8,2,128,128]{3,2,1,0:T(8,128)}), f32[8,2,128,128]{3,2,1,0:T(8,128)S(1)}, u32[]{:S(2)}, u32[]{:S(2)}) async-start(f32[8,2,128,128]{3,2,1,0:T(8,128)} %shard_map.77), calls=%async_computation | async-start | bytes 2097152 | tf_op jit(solution)/shard_map/all_to_all | solution.py:296
  32.7 0.0 all-gather.7.cloned.1.call-start
  32.7 0.0 copy-done.1
  32.7 1.9 %collective-permute-start.3 = (f32[128,128]{1,0:T(8,128)S(1)}, f32[128,128]{1,0:T(8,128)S(1)}, u32[]{:S(2)}, u32[]{:S(2)}) collective-permute-start(f32[128,128]{1,0:T(8,128)S(1)} %get-tuple-element.21), channel_id=1, source_target_pairs={{0,0},{1,1},{2,32},{3,33},{32,2},{33,3},{34,34},{35,35},{4,4},{5,5... | collective-permute-start | bytes 196616 | tf_op jit(solution)/shard_map/ppermute | solution.py:301
  34.7 3.7 %collective-permute-start.4 = (f32[128,128]{1,0:T(8,128)S(1)}, f32[128,128]{1,0:T(8,128)S(1)}, u32[]{:S(2)}, u32[]{:S(2)}) collective-permute-start(f32[128,128]{1,0:T(8,128)S(1)} %get-tuple-element.22), channel_id=1, source_target_pairs={{0,1},{1,0},{2,33},{3,32},{32,3},{33,2},{34,35},{35,34},{4,5},{5,4... | collective-permute-start | bytes 196616 | tf_op jit(solution)/shard_map/ppermute | solution.py:301
  38.3 1.8 %collective-permute-done.3 = f32[128,128]{1,0:T(8,128)S(1)} collective-permute-done((f32[128,128]{1,0:T(8,128)S(1)}, f32[128,128]{1,0:T(8,128)S(1)}, u32[]{:S(2)}, u32[]{:S(2)}) %collective-permute-start.3) | collective-permute-done | bytes 65568 | tf_op jit(solution)/shard_map/ppermute | solution.py:301
  40.1 1.6 %collective-permute-done.4 = f32[128,128]{1,0:T(8,128)S(1)} collective-permute-done((f32[128,128]{1,0:T(8,128)S(1)}, f32[128,128]{1,0:T(8,128)S(1)}, u32[]{:S(2)}, u32[]{:S(2)}) %collective-permute-start.4) | collective-permute-done | bytes 65568 | tf_op jit(solution)/shard_map/ppermute | solution.py:301
  41.7 0.7 pad_maximum_fusion
  42.4 0.0 all-gather.7.cloned.1.call-update
  42.4 11.0 %all-to-all-done.own = f32[8,2,128,128]{3,2,1,0:T(8,128)S(1)} async-done(((f32[8,2,128,128]{3,2,1,0:T(8,128)}), f32[8,2,128,128]{3,2,1,0:T(8,128)S(1)}, u32[]{:S(2)}, u32[]{:S(2)}) %all-to-all-start) | async-done | bytes 1048608 | tf_op jit(solution)/shard_map/all_to_all | solution.py:296
  53.5 3.0 %collective-permute-start.2 = (f32[8,2,128,128]{3,2,1,0:T(8,128)S(1)}, f32[8,2,128,128]{3,2,1,0:T(8,128)S(1)}, u32[]{:S(2)}, u32[]{:S(2)}) collective-permute-start(f32[8,2,128,128]{3,2,1,0:T(8,128)S(1)} %all-to-all-done.own), channel_id=1, source_target_pairs={{0,32},{32,0},{1,33},{33,1},{2,34},{34,2},{3,35},{35,3},{4,36},{36... | collective-permute-start | bytes 3145736 | tf_op jit(solution)/shard_map/ppermute | solution.py:305
  56.5 2.3 %collective-permute-done.2.other = f32[8,2,128,128]{3,2,1,0:T(8,128)S(1)} collective-permute-done((f32[8,2,128,128]{3,2,1,0:T(8,128)S(1)}, f32[8,2,128,128]{3,2,1,0:T(8,128)S(1)}, u32[]{:S(2)}, u32[]{:S(2)}) %collective-permute-start.2) | collective-permute-done | bytes 1048608 | tf_op jit(solution)/shard_map/ppermute | solution.py:305
  58.8 0.0 all-gather.5.cloned.1.call-done
  58.8 2.2 %shard_map.78 = f32[4,256,128]{2,1,0:T(8,128)S(1)} custom-call(s32[1]{0:T(128)} %bitcast.at_ref, f32[8,512,128]{2,1,0:T(8,128)} %bitcast.5, f32[8,2,128,128]{3,2,1,0:T(8,128)S(1)} %all-to-all-done.own, f32[8,2,128,128]{3,2,1,0:T(8,128)S(1)} %collective-permute-done.2.other), custom_call_target="tpu_custom_call" | custom-call | flops 1610612736 | bytes 3145728 | tf_op jit(solution)/shard_map/pallas_call | solution.py:149
  61.0 8.3 %all_to_all.20 = f32[4,256,128]{2,1,0:T(8,128)S(1)} all-to-all(f32[4,256,128]{2,1,0:T(8,128)S(1)} %shard_map.78), channel_id=1, replica_groups={{0,1,2,3},{34,35,32,33},{4,5,6,7},{38,39,36,37},{8,9,10,11},{42,43,40,4..., dimensions={0} | all-to-all | bytes 1048576 | tf_op jit(solution)/shard_map/all_to_all | solution.py:296
  69.3 1.1 broadcast_in_dim.2
  70.4 17.1 %all-to-all-start.2 = ((f32[8,256,128]{2,1,0:T(8,128)}), f32[8,256,128]{2,1,0:T(8,128)S(1)}, u32[]{:S(2)}, u32[]{:S(2)}) async-start(f32[8,256,128]{2,1,0:T(8,128)} %broadcast_in_dim.2), calls=%async_computation.2 | async-start | bytes 2097152 | tf_op jit(solution)/shard_map/all_to_all | solution.py:296
  87.5 15.9 %all-gather.7.cloned.1.call-done = f32[4096,128]{1,0:T(8,128)} async-done(((f32[256,128]{1,0:T(8,128)}), f32[4096,128]{1,0:T(8,128)}) %all-gather.7.cloned.1.call-update) | async-done | bytes 2097168 | tf_op jit(solution)/shard_map/all_gather | solution.py:321
  103.4 3.7 %shard_map.79 = (f32[12,256,128]{2,1,0:T(8,128)}, bf16[1024,512]{1,0:T(8,128)(2,1)}, bf16[1024,512]{1,0:T(8,128)(2,1)}) custom-call(s32[1]{0:T(128)} %bitcast.at_ref, f32[8,512,128]{2,1,0:T(8,128)} %bitcast.6, f32[2,8,256,128]{3,2,1,0:T(8,128)} %bitcast.7), custom_call_target="tpu_custom_call" | custom-call | flops 1610612736 | bytes 6291456 | tf_op jit(solution)/shard_map/pallas_call | solution.py:213
  107.1 1.8 %all-to-all-done.2.w = f32[8,256,128]{2,1,0:T(8,128)S(1)} async-done(((f32[8,256,128]{2,1,0:T(8,128)}), f32[8,256,128]{2,1,0:T(8,128)S(1)}, u32[]{:S(2)}, u32[]{:S(2)}) %all-to-all-start.2) | async-done | bytes 1048608 | tf_op jit(solution)/shard_map/all_to_all | solution.py:296
  108.9 4.2 %shard_map.80 = f32[4,512,128]{2,1,0:T(8,128)} custom-call(s32[1]{0:T(128)} %bitcast.at_ref, f32[8,256,128]{2,1,0:T(8,128)S(1)} %all-to-all-done.2.w, bf16[1024,512]{1,0:T(8,128)(2,1)} %get-tuple-element.16.hi_hbm, bf16[1024,512]{1,0:T(8,128)(2,1)} %get-tuple-element.17.lo_hbm, f32[12,256,128]{2,1,0:T(8,128)} %get-tuple-element.18.rest_hbm), custom_call_target="tpu_custom_call" | custom-call | tf_op jit(solution)/shard_map/pallas_call | solution.py:267
  113.1 0.0 copy-start
  113.1 9.3 %all-to-all-start.3 = ((f32[4,512,128]{2,1,0:T(8,128)}), f32[4,512,128]{2,1,0:T(8,128)S(1)}, u32[]{:S(2)}, u32[]{:S(2)}) async-start(f32[4,512,128]{2,1,0:T(8,128)} %shard_map.80), calls=%async_computation.3 | async-start | bytes 2097152 | tf_op jit(solution)/shard_map/all_to_all | solution.py:296
  122.5 0.7 neg.3
  123.1 10.1 %all-to-all-done.3 = f32[4,512,128]{2,1,0:T(8,128)S(1)} async-done(((f32[4,512,128]{2,1,0:T(8,128)}), f32[4,512,128]{2,1,0:T(8,128)S(1)}, u32[]{:S(2)}, u32[]{:S(2)}) %all-to-all-start.3) | async-done | bytes 1048608 | tf_op jit(solution)/shard_map/all_to_all | solution.py:296
  133.3 0.1 reduce_sum.19
  133.3 0.0 copy-done
  133.3 0.7 slice_add_fusion
  (2 shorter events, 0.0 us)
Async XLA Ops:
  7.2 51.6 %all-gather.5.cloned.1.call-start = ((), (), s32[]{:S(2)}) async-start(), calls=%async_computation.4 | async-start | bytes 2359296 | tf_op jit(solution)/shard_map/all_gather | solution.py:312
  7.2 25.5 %copy-start.1 = (f32[256,128]{1,0:T(8,128)S(1)}, f32[256,128]{1,0:T(8,128)}, u32[]{:S(2)}) copy-start(f32[256,128]{1,0:T(8,128)} %param.7) | copy-start | bytes 393220
  9.6 8.5 %collective-permute-start = (f32[128,128]{1,0:T(8,128)}, f32[128,128]{1,0:T(8,128)S(1)}, u32[]{:S(2)}, u32[]{:S(2)}) collective-permute-start(f32[128,128]{1,0:T(8,128)} %get-tuple-element.12), channel_id=1, source_target_pairs={{0,0},{1,1},{2,32},{3,33},{32,2},{33,3},{34,34},{35,35},{4,4},{5,5... | collective-permute-start | bytes 196616 | tf_op jit(solution)/shard_map/ppermute | solution.py:301
  15.6 7.0 %collective-permute-start.1 = (f32[128,128]{1,0:T(8,128)}, f32[128,128]{1,0:T(8,128)S(1)}, u32[]{:S(2)}, u32[]{:S(2)}) collective-permute-start(f32[128,128]{1,0:T(8,128)} %get-tuple-element.13), channel_id=1, source_target_pairs={{0,1},{1,0},{2,33},{3,32},{32,3},{33,2},{34,35},{35,34},{4,5},{5,4... | collective-permute-start | bytes 196616 | tf_op jit(solution)/shard_map/ppermute | solution.py:301
  23.7 29.8 %all-to-all-start = ((f32[8,2,128,128]{3,2,1,0:T(8,128)}), f32[8,2,128,128]{3,2,1,0:T(8,128)S(1)}, u32[]{:S(2)}, u32[]{:S(2)}) async-start(f32[8,2,128,128]{3,2,1,0:T(8,128)} %shard_map.77), calls=%async_computation | async-start | bytes 2097152 | tf_op jit(solution)/shard_map/all_to_all | solution.py:296
  32.7 70.7 %all-gather.7.cloned.1.call-start = ((), (), s32[]{:S(2)}) async-start(), calls=%async_computation.5 | async-start | bytes 2228224 | tf_op jit(solution)/shard_map/all_gather | solution.py:321
  32.7 7.4 %collective-permute-start.3 = (f32[128,128]{1,0:T(8,128)S(1)}, f32[128,128]{1,0:T(8,128)S(1)}, u32[]{:S(2)}, u32[]{:S(2)}) collective-permute-start(f32[128,128]{1,0:T(8,128)S(1)} %get-tuple-element.21), channel_id=1, source_target_pairs={{0,0},{1,1},{2,32},{3,33},{32,2},{33,3},{34,34},{35,35},{4,4},{5,5... | collective-permute-start | bytes 196616 | tf_op jit(solution)/shard_map/ppermute | solution.py:301
  34.7 7.1 %collective-permute-start.4 = (f32[128,128]{1,0:T(8,128)S(1)}, f32[128,128]{1,0:T(8,128)S(1)}, u32[]{:S(2)}, u32[]{:S(2)}) collective-permute-start(f32[128,128]{1,0:T(8,128)S(1)} %get-tuple-element.22), channel_id=1, source_target_pairs={{0,1},{1,0},{2,33},{3,32},{32,3},{33,2},{34,35},{35,34},{4,5},{5,4... | collective-permute-start | bytes 196616 | tf_op jit(solution)/shard_map/ppermute | solution.py:301
  53.5 5.3 %collective-permute-start.2 = (f32[8,2,128,128]{3,2,1,0:T(8,128)S(1)}, f32[8,2,128,128]{3,2,1,0:T(8,128)S(1)}, u32[]{:S(2)}, u32[]{:S(2)}) collective-permute-start(f32[8,2,128,128]{3,2,1,0:T(8,128)S(1)} %all-to-all-done.own), channel_id=1, source_target_pairs={{0,32},{32,0},{1,33},{33,1},{2,34},{34,2},{3,35},{35,3},{4,36},{36... | collective-permute-start | bytes 3145736 | tf_op jit(solution)/shard_map/ppermute | solution.py:305
  70.4 38.5 %all-to-all-start.2 = ((f32[8,256,128]{2,1,0:T(8,128)}), f32[8,256,128]{2,1,0:T(8,128)S(1)}, u32[]{:S(2)}, u32[]{:S(2)}) async-start(f32[8,256,128]{2,1,0:T(8,128)} %broadcast_in_dim.2), calls=%async_computation.2 | async-start | bytes 2097152 | tf_op jit(solution)/shard_map/all_to_all | solution.py:296
  113.1 20.2 %copy-start = (f32[256,128]{1,0:T(8,128)S(1)}, f32[256,128]{1,0:T(8,128)}, u32[]{:S(2)}) copy-start(f32[256,128]{1,0:T(8,128)} %param.9) | copy-start | bytes 393220
  113.1 20.1 %all-to-all-start.3 = ((f32[4,512,128]{2,1,0:T(8,128)}), f32[4,512,128]{2,1,0:T(8,128)S(1)}, u32[]{:S(2)}, u32[]{:S(2)}) async-start(f32[4,512,128]{2,1,0:T(8,128)} %shard_map.80), calls=%async_computation.3 | async-start | bytes 2097152 | tf_op jit(solution)/shard_map/all_to_all | solution.py:296
Sparse Core Ops, SparseCore 0:
  10.1 46.0 all-gather.4
  58.9 44.4 all-gather.6
